TPU v7x, 32 devices: a whole 2x2x4 slice. The times are simulated.
32 devices in a mesh: row: 4 (over x, core), col: 8 (over z, y).
Axes of the slice: x: 2, y: 2, z: 4, core: 2. Of those that a mesh axis runs over, the one named last changes fastest.
Arguments:
- dinv_root: bfloat16 [16384, 16384], P('row', 'col'), may hold values from -0.03125 to 0.03125
- rhs_root: bfloat16 [16384, 384], P('col'), may hold values from -6 to 6
- dinv_mid: bfloat16 [16384, 8192], P('row', 'col'), may hold values from -0.046875 to 0.046875
- coup_mid: bfloat16 [16384, 8192], P('row', 'col'), may hold values from -0.0625 to 0.0625
- rhs_mid: bfloat16 [2, 8192, 384], P(None, 'col'), may hold values from -6 to 6
- dinv_leaf: bfloat16 [8, 4096, 4096], P('col', None, 'row'), may hold values from -0.0625 to 0.0625
- coup_leaf: bfloat16 [8, 6144, 4096], P('col', 'row'), may hold values from -0.109375 to 0.109375
- rhs_leaf: bfloat16 [8, 4096, 384], P('col', 'row'), may hold values from -6 to 6
- bounds_mid: int32 [2, 64], replicated, may hold values from 0 to 127, as said below
- bounds_leaf: int32 [8, 48], replicated, may hold values from 0 to 191, as said below
- parents: int32 [8], replicated, may hold values from 0 to 1, as said below
Outputs:
- root_values: bfloat16 [16384, 384], P(('row', 'col'))
- mid_values: bfloat16 [16384, 384], P(('row', 'col'))
- leaf_values: bfloat16 [8, 4096, 384], P('col', 'row')
Inputs may be any that keep to these rules, and one draw needn't show every extreme that they name: `bounds_mid`: each row holds 64 distinct root block numbers; every root block appears in some row. `parents`: each mid front is the parent of exactly 4 leaf fronts. `bounds_leaf`: each row holds 48 distinct values. Every row names the same number of root blocks; the leaf fronts of one parent together name each block of that parent's separator exactly once, each naming 8192 / 128 / 4 of them.
All inputs are finite; a program needn't handle non-finite values.
Results may differ from a plain program's by a relative error of at most 0.0065.
Values may be sent and summed in bfloat16 or wider, within the bound.
No kernel may reach another device: no remote copies, remote signals or barrier semaphores. Data moves between devices by JAX's collectives and lax.ppermute only.
A program may use at most 128 MiB of HBM per device.

v0:
```python
import jax
import jax.numpy as jnp
from jax import lax
from jax.sharding import PartitionSpec as P

N0 = 16384
BLOCK = 128


def partner(value, axis, distance):
    mask = 2**distance
    pairs = [(source, source ^ mask) for source in range(lax.axis_size(axis))]
    return lax.ppermute(value, axis, pairs)


def pick_blocks(shard_rows, wanted):
    block_count = shard_rows.shape[0] // BLOCK
    flat_blocks = shard_rows.reshape(block_count, BLOCK * shard_rows.shape[1])
    present = jnp.arange(block_count, dtype=jnp.int32)
    select = (wanted[:, None] == present[None, :]).astype(shard_rows.dtype)
    return jnp.dot(select, flat_blocks, preferred_element_type=jnp.float32)


def transposed_product(coupling, boundary):
    return lax.dot_general(
        coupling, boundary, (((0,), (0,)), ((), ())), preferred_element_type=jnp.float32
    )


def shards(
    dinv_root,
    rhs_root,
    dinv_mid,
    coup_mid,
    rhs_mid,
    dinv_leaf,
    coup_leaf,
    rhs_leaf,
    bounds_mid,
    bounds_leaf,
    parents,
):
    row_total = lax.axis_size("row")
    row_id = lax.axis_index("row")
    col_id = lax.axis_index("col")
    rhs_width = rhs_root.shape[1]
    root_total = N0 // BLOCK
    front_mid = row_id // 2
    half_index = row_id % 2
    half_blocks = bounds_mid.shape[1] // 2
    mid_all = lax.dynamic_slice_in_dim(bounds_mid, front_mid, 1, 0)[0]
    mid_list = lax.dynamic_slice_in_dim(mid_all, half_index * half_blocks, half_blocks, 0)
    leaf_all = lax.dynamic_slice_in_dim(bounds_leaf, col_id, 1, 0)[0]
    leaf_slots = leaf_all.shape[0] // row_total
    leaf_list = lax.dynamic_slice_in_dim(leaf_all, row_id * leaf_slots, leaf_slots, 0)
    wanted = jnp.concatenate([mid_list, leaf_list])
    root_values = lax.psum_scatter(
        jnp.dot(dinv_root, rhs_root, preferred_element_type=jnp.float32),
        "col",
        scatter_dimension=0,
        tiled=True,
    ).astype(jnp.bfloat16)
    picked = pick_blocks(lax.all_gather(root_values, ("row", "col"), axis=0, tiled=True), wanted)
    bound_mid = picked[:half_blocks].reshape(half_blocks * BLOCK, rhs_width).astype(jnp.bfloat16)
    root_side = picked[half_blocks:]
    mid_part = transposed_product(coup_mid, bound_mid)
    mid_terms = mid_part + partner(mid_part, "row", 0)
    rhs_here = lax.dynamic_slice_in_dim(rhs_mid, front_mid, 1, 0)[0]
    shift_mid = (rhs_here - mid_terms).astype(jnp.bfloat16)
    mid_values = lax.psum_scatter(
        jnp.dot(dinv_mid, shift_mid, preferred_element_type=jnp.float32),
        "col",
        scatter_dimension=0,
        tiled=True,
    ).astype(jnp.bfloat16)
    half_rows = lax.all_gather(mid_values, "col", axis=0, tiled=True)
    half_count = half_rows.shape[0] // BLOCK
    half_flat = half_rows.reshape(half_count, BLOCK * rhs_width)
    local_ids = leaf_all - root_total - half_index * half_count
    owns_parent = lax.dynamic_slice_in_dim(parents, col_id, 1, 0)[0] == front_mid
    choose = (
        (local_ids[:, None] == jnp.arange(half_count, dtype=jnp.int32)[None, :]) & owns_parent
    ).astype(jnp.bfloat16)
    from_parent = lax.psum_scatter(
        jnp.dot(choose, half_flat, preferred_element_type=jnp.float32).astype(jnp.bfloat16),
        "row",
        scatter_dimension=0,
        tiled=True,
    ).astype(jnp.float32)
    bound_leaf = (
        (root_side + from_parent).reshape(leaf_slots * BLOCK, rhs_width).astype(jnp.bfloat16)
    )
    coup_here = coup_leaf[0]
    leaf_sum = lax.psum_scatter(
        transposed_product(coup_here, bound_leaf), "row", scatter_dimension=0, tiled=True
    )
    shift_leaf = (rhs_leaf[0] - leaf_sum).astype(jnp.bfloat16)
    dinv_here = dinv_leaf[0]
    leaf_values = lax.psum_scatter(
        jnp.dot(dinv_here, shift_leaf, preferred_element_type=jnp.float32),
        "row",
        scatter_dimension=0,
        tiled=True,
    ).astype(jnp.bfloat16)
    return (root_values, mid_values, leaf_values[None])


def solution(mesh):
    return jax.shard_map(
        shards,
        mesh=mesh,
        in_specs=(
            P("row", "col"),
            P("col", None),
            P("row", "col"),
            P("row", "col"),
            P(None, "col", None),
            P("col", None, "row"),
            P("col", "row", None),
            P("col", "row", None),
            P(),
            P(),
            P(),
        ),
        out_specs=(P(("row", "col"), None), P(("row", "col"), None), P("col", "row", None)),
        check_vma=False,
    )
```

profile of v0, /device:TPU:0, one launch (start us, length us, event | category | flops | bytes accessed | tf_op | source)
XLA Modules:
  0.0 747.1 jit_solution(10379395671590368210)
XLA Ops:
  7.2 0.0 copy-start
  7.2 0.0 reduce-scatter.7.cloned.1.call-start
  7.2 1.4 copy-done
  8.6 14.1 %fusion.24 = f32[4096,384]{1,0:T(8,128)} fusion(bf16[4096,2048]{1,0:T(8,128)(2,1)} %param.11, bf16[2048,384]{1,0:T(8,128)(2,1)S(1)} %copy-done), kind=kOutput, calls=%fused_computation.31 | convolution fusion | flops 6442450944 | bytes 24641536 | tf_op jit(solution)/shard_map/dot_general | solution.py:58
  22.7 0.0 reduce-scatter.7.cloned.1.call-update
  22.7 0.0 all-gather.3.cloned.1.call-start
  22.8 120.8 %reduce-scatter.7.cloned.1.call-done = f32[512,384]{1,0:T(8,128)} async-done(((f32[4096,384]{1,0:T(8,128)}), f32[512,384]{1,0:T(8,128)}) %reduce-scatter.7.cloned.1.call-update) | async-done | bytes 786448 | tf_op jit(solution)/shard_map/reduce_scatter | solution.py:57
  143.5 1.9 convert_element_type.45
  145.5 0.0 all-gather.3.cloned.1.call-update
  145.5 0.0 reduce-scatter.9.cloned.1.call-start
  145.6 0.8 dynamic-slice_bitcast_fusion
  146.3 0.0 copy-done.7
  146.4 0.1 dynamic-slice_bitcast_fusion.1
  146.4 0.1 pad_add_fusion
  146.5 95.7 %all-gather.3.cloned.1.call-done = bf16[16384,384]{1,0:T(8,128)(2,1)} async-done(((bf16[512,384]{1,0:T(8,128)(2,1)}), bf16[16384,384]{1,0:T(8,128)(2,1)}) %all-gather.3.cloned.1.call-update) | async-done | bytes 12582928 | tf_op jit(solution)/shard_map/all_gather | solution.py:63
  242.2 16.3 %reshape.33 = bf16[128,49152]{1,0:T(8,128)(2,1)} reshape(bf16[16384,384]{1,0:T(8,128)(2,1)} %all-gather.3.cloned.1.call-done) | data formatting | bytes 25165824 | tf_op jit(solution)/shard_map/reshape | solution.py:18
  258.5 5.6 fusion.18
  264.1 0.0 copy-start.2
  264.1 3.7 copy-done.2
  267.8 2.0 slice.16
  269.7 4.9 convert_element_type.48
  274.6 6.9 convolution_bitcast_fusion.1
  281.6 0.3 collective-permute-start
  281.9 0.0 copy-done.5
  281.9 0.1 constant_dynamic-slice_fusion
  282.0 0.3 copy.26
  282.3 2.9 collective-permute-done
  285.2 10.0 %convolution_bitcast_fusion = f32[4096,384]{0,1:T(8,128)} fusion(bf16[4096,1024]{1,0:T(8,128)(2,1)} %param.13, f32[1024,384]{0,1:T(8,128)S(1)} %convolution_bitcast_fusion.1, f32[1024,384]{0,1:T(8,128)} %collective-permute-done, bf16[1,1024,384]{1,2,0:T(8,128)(2,1)S(1)} %copy.26), kind=kOutput, calls=%fused_computation.8 | convolution fusion | flops 3222798336 | bytes 18612224 | tf_op jit(solution)/shard_map/dot_general | solution.py:71
  295.2 0.0 reduce-scatter.9.cloned.1.call-update
  295.2 0.0 all-gather.5.cloned.1.call-start
  295.3 116.7 %reduce-scatter.9.cloned.1.call-done = f32[512,384]{0,1:T(8,128)} async-done(((f32[4096,384]{0,1:T(8,128)}), f32[512,384]{0,1:T(8,128)}) %reduce-scatter.9.cloned.1.call-update) | async-done | bytes 786448 | tf_op jit(solution)/shard_map/reduce_scatter | solution.py:70
  411.9 1.9 convert_element_type.50
  413.9 0.0 all-gather.5.cloned.1.call-update
  413.9 0.2 reduce-scatter.11.cloned.1.call-start
  414.1 0.0 copy-done.8
  414.1 0.6 dynamic_slice.26
  415.4 0.7 subtract_bitcast_fusion
  416.1 60.6 %all-gather.5.cloned.1.call-done = bf16[4096,384]{0,1:T(8,128)(2,1)} async-done(((bf16[512,384]{0,1:T(8,128)(2,1)}), bf16[4096,384]{0,1:T(8,128)(2,1)}) %all-gather.5.cloned.1.call-update) | async-done | bytes 3145744 | tf_op jit(solution)/shard_map/all_gather | solution.py:76
  476.7 4.7 copy.23
  481.3 4.8 reshape.34
  486.2 5.5 convolution_convert_fusion
  491.7 57.6 %fusion = bf16[16,49152]{1,0:T(8,128)(2,1)S(1)} fusion(bf16[48,49152]{1,0:T(8,128)(2,1)} %convolution_convert_fusion), kind=kCustom, calls=%all-reduce-scatter | all-reduce-scatter fusion | flops 3145729 | bytes 6291968
  549.3 0.0 copy-start.6
  549.3 0.4 slice.11
  549.7 2.5 collective-permute-start.1
  552.2 0.0 copy-done.6
  552.2 0.6 dynamic-slice.6
  553.4 0.7 collective-permute-done.1
  554.2 26.6 %concatenate.4 = bf16[28,49152]{1,0:T(8,128)(2,1)} concatenate(bf16[12,49152]{1,0:T(8,128)(2,1)} %collective-permute-done.1, bf16[16,49152]{1,0:T(8,128)(2,1)S(1)} %fusion), dimensions={0} | concatenate | bytes 5505024
  580.8 3.1 fusion.11
  583.9 1.0 convert_element_type.56
  584.9 10.8 %fusion.8 = f32[4096,384]{0,1:T(8,128)} fusion(bf16[1536,384]{1,0:T(8,128)(2,1)S(1)} %convert_element_type.56, bf16[1,1536,4096]{2,1,0:T(8,128)(2,1)} %param.17), kind=kOutput, calls=%fused_computation.7 | convolution fusion | flops 4831838208 | bytes 20054016 | tf_op jit(solution)/shard_map/dot_general | solution.py:25
  595.7 0.0 reduce-scatter.11.cloned.1.call-update
  595.8 0.0 reduce-scatter.13.cloned.1.call-start
  595.8 1.1 copy-done.4
  596.9 0.3 copy.22
  597.1 71.9 %reduce-scatter.11.cloned.1.call-done = f32[1024,384]{0,1:T(8,128)} async-done(((f32[4096,384]{0,1:T(8,128)}), f32[1024,384]{0,1:T(8,128)}) %reduce-scatter.11.cloned.1.call-update) | async-done | bytes 1572880 | tf_op jit(solution)/shard_map/reduce_scatter | solution.py:94
  669.0 10.0 %fusion.5 = f32[4096,384]{0,1:T(8,128)} fusion(bf16[1,4096,1024]{2,1,0:T(8,128)(2,1)} %param.16, f32[1024,384]{0,1:T(8,128)} %reduce-scatter.11.cloned.1.call-done, bf16[1,1024,384]{1,2,0:T(8,128)(2,1)S(1)} %copy.22), kind=kOutput, calls=%fused_computation.6 | convolution fusion | flops 3222405120 | bytes 17039360 | tf_op jit(solution)/shard_map/dot_general | solution.py:100
  679.0 0.0 reduce-scatter.13.cloned.1.call-update
  679.0 1.0 copy-done.3
  680.0 0.9 copy.24
  680.9 56.6 %reduce-scatter.13.cloned.1.call-done = f32[1024,384]{0,1:T(8,128)} async-done(((f32[4096,384]{0,1:T(8,128)}), f32[1024,384]{0,1:T(8,128)}) %reduce-scatter.13.cloned.1.call-update) | async-done | bytes 1572880 | tf_op jit(solution)/shard_map/reduce_scatter | solution.py:99
  737.5 1.5 convert_bitcast_fusion
  739.1 1.2 copy.25
  (7 shorter events, 0.0 us)
Async XLA Ops:
  7.2 1.4 copy-start
  7.2 136.4 %reduce-scatter.7.cloned.1.call-start = ((), (), s32[]{:S(2)}) async-start(), calls=%async_computation.4 | async-start | bytes 7077888 | tf_op jit(solution)/shard_map/reduce_scatter | solution.py:57
  22.7 123.7 %copy-start.7 = (s32[2,64]{1,0:T(2,128)S(1)}, s32[2,64]{1,0:T(2,128)}, u32[]{:S(2)}) copy-start(s32[2,64]{1,0:T(2,128)} %param.19) | copy-start | bytes 1540
  22.7 219.5 %all-gather.3.cloned.1.call-start = ((), (), s32[]{:S(2)}) async-start(), calls=%async_computation.5 | async-start | bytes 12976128 | tf_op jit(solution)/shard_map/all_gather | solution.py:63
  145.5 266.4 %reduce-scatter.9.cloned.1.call-start = ((), (), s32[]{:S(2)}) async-start(), calls=%async_computation.6 | async-start | bytes 7077888 | tf_op jit(solution)/shard_map/reduce_scatter | solution.py:70
  264.1 3.7 copy-start.2
  274.6 7.3 copy-start.5
  281.6 3.6 collective-permute-start
  295.2 118.9 %copy-start.8 = (s32[8]{0:T(128)S(1)}, s32[8]{0:T(128)}, u32[]{:S(2)}) copy-start(s32[8]{0:T(128)} %param.21) | copy-start | bytes 100
  295.2 181.4 %all-gather.5.cloned.1.call-start = ((), (), s32[]{:S(2)}) async-start(), calls=%async_computation.7 | async-start | bytes 3538944 | tf_op jit(solution)/shard_map/all_gather | solution.py:76
  413.9 255.1 %reduce-scatter.11.cloned.1.call-start = ((), (), s32[]{:S(2)}) async-start(), calls=%async_computation.8 | async-start | bytes 7864320 | tf_op jit(solution)/shard_map/reduce_scatter | solution.py:94
  549.3 2.9 copy-start.6
  549.7 4.4 collective-permute-start.1
  595.7 1.1 copy-start.4
  595.8 141.8 %reduce-scatter.13.cloned.1.call-start = ((), (), s32[]{:S(2)}) async-start(), calls=%async_computation.9 | async-start | bytes 7864320 | tf_op jit(solution)/shard_map/reduce_scatter | solution.py:99
  679.0 1.0 copy-start.3
  680.0 60.2 %copy-start.1 = (bf16[2048,384]{1,0:T(8,128)(2,1)S(1)}, bf16[2048,384]{1,0:T(8,128)(2,1)}, u32[]{:S(2)}) copy-start(bf16[2048,384]{1,0:T(8,128)(2,1)} %param.12) | copy-start | bytes 4718596
Sparse Core Ops, SparseCore 0:
  22.8 120.6 reduce-scatter.6
  147.0 95.1 all-gather.2
  295.3 116.5 reduce-scatter.8
  414.4 62.2 all-gather.4
  595.9 73.1 reduce-scatter.10
  679.1 58.3 reduce-scatter.12
where the time goes:
time: 750 us; the launch traced here: 747 us
  waiting for transfers between devices  526 us (70%)
  local copies, waits for them, and re-layouts  72.4 us (10%)
  matrix products  62.9 us (8%)
  blocking collectives  57.6 us (8%)
  between operations  15.6 us (2%)
  other arithmetic  9.27 us (1%)
    reduce_scatter x1, waiting for transfers between devices, shards(): lax.psum_scatter(jnp.dot(dinv_root, rhs_root, preferred_element_type=jnp....  121 us
    reduce_scatter x1, waiting for transfers between devices, shards(): lax.psum_scatter(jnp.dot(dinv_mid, shift_mid, preferred_element_type=jnp....  117 us
    all_gather x1, waiting for transfers between devices, shards(): lax.all_gather(root_values, ('row', 'col'), axis=0, tiled=True)  95.7 us
    reduce_scatter x1, waiting for transfers between devices, shards(): lax.psum_scatter(transposed_product(coup_here, bound_leaf), 'row', scatte...  71.9 us
    all_gather x1, waiting for transfers between devices, shards(): half_rows = lax.all_gather(mid_values, 'col', axis=0, tiled=True)  60.6 us
    unnamed x1, blocking collectives  57.6 us
    reduce_scatter x1, waiting for transfers between devices, shards(): lax.psum_scatter(jnp.dot(dinv_here, shift_leaf, preferred_element_type=jn...  56.6 us
    unnamed x25, local copies, waits for them, and re-layouts  37.3 us
  transfers between devices with their start and end apart: 8, of which 8 were waited for; matrix products, arithmetic and copies ran while one was open for 1% of the time, Pallas kernels for 0%

commit v1 on v0

v1 whole, which is shorter than its diff:
```python
import functools

import jax
import jax.numpy as jnp
from jax import lax
from jax.experimental import pallas as pl
from jax.experimental.pallas import tpu as pltpu
from jax.sharding import PartitionSpec as P

BLOCK = 128
CHUNKS = 3
F32 = jnp.float32
BF16 = jnp.bfloat16
NT = (((1,), (1,)), ((), ()))
NN = (((1,), (0,)), ((), ()))


def partner(value, axis, distance):
    mask = 2**distance
    pairs = [(source, source ^ mask) for source in range(lax.axis_size(axis))]
    return lax.ppermute(value, axis, pairs)


def pick_blocks(shard_rows, wanted):
    block_count = shard_rows.shape[0] // BLOCK
    flat_blocks = shard_rows.reshape(block_count, BLOCK * shard_rows.shape[1])
    present = jnp.arange(block_count, dtype=jnp.int32)
    select = (wanted[:, None] == present[None, :]).astype(shard_rows.dtype)
    return jnp.dot(select, flat_blocks, preferred_element_type=F32)


def transposed_product(coupling, boundary):
    return lax.dot_general(coupling, boundary, (((0,), (0,)), ((), ())), preferred_element_type=F32)


def general_shards(
    dinv_root,
    rhs_root,
    dinv_mid,
    coup_mid,
    rhs_mid,
    dinv_leaf,
    coup_leaf,
    rhs_leaf,
    bounds_mid,
    bounds_leaf,
    parents,
):
    row_total = lax.axis_size("row")
    row_id = lax.axis_index("row")
    col_id = lax.axis_index("col")
    rhs_width = rhs_root.shape[1]
    root_total = dinv_root.shape[0] * row_total // BLOCK
    front_mid = row_id // 2
    half_index = row_id % 2
    half_blocks = bounds_mid.shape[1] // 2
    mid_all = lax.dynamic_slice_in_dim(bounds_mid, front_mid, 1, 0)[0]
    mid_list = lax.dynamic_slice_in_dim(mid_all, half_index * half_blocks, half_blocks, 0)
    leaf_all = lax.dynamic_slice_in_dim(bounds_leaf, col_id, 1, 0)[0]
    leaf_slots = leaf_all.shape[0] // row_total
    leaf_list = lax.dynamic_slice_in_dim(leaf_all, row_id * leaf_slots, leaf_slots, 0)
    wanted = jnp.concatenate([mid_list, leaf_list])
    root_values = lax.psum_scatter(
        jnp.dot(dinv_root, rhs_root, preferred_element_type=F32),
        "col",
        scatter_dimension=0,
        tiled=True,
    ).astype(BF16)
    picked = pick_blocks(lax.all_gather(root_values, ("row", "col"), axis=0, tiled=True), wanted)
    bound_mid = picked[:half_blocks].reshape(half_blocks * BLOCK, rhs_width).astype(BF16)
    root_side = picked[half_blocks:]
    mid_part = transposed_product(coup_mid, bound_mid)
    mid_terms = mid_part + partner(mid_part, "row", 0)
    rhs_here = lax.dynamic_slice_in_dim(rhs_mid, front_mid, 1, 0)[0]
    shift_mid = (rhs_here - mid_terms).astype(BF16)
    mid_values = lax.psum_scatter(
        jnp.dot(dinv_mid, shift_mid, preferred_element_type=F32),
        "col",
        scatter_dimension=0,
        tiled=True,
    ).astype(BF16)
    half_rows = lax.all_gather(mid_values, "col", axis=0, tiled=True)
    half_count = half_rows.shape[0] // BLOCK
    half_flat = half_rows.reshape(half_count, BLOCK * rhs_width)
    local_ids = leaf_all - root_total - half_index * half_count
    owns_parent = lax.dynamic_slice_in_dim(parents, col_id, 1, 0)[0] == front_mid
    choose = (
        (local_ids[:, None] == jnp.arange(half_count, dtype=jnp.int32)[None, :]) & owns_parent
    ).astype(BF16)
    from_parent = lax.psum_scatter(
        jnp.dot(choose, half_flat, preferred_element_type=F32).astype(BF16),
        "row",
        scatter_dimension=0,
        tiled=True,
    ).astype(F32)
    bound_leaf = (root_side + from_parent).reshape(leaf_slots * BLOCK, rhs_width).astype(BF16)
    leaf_sum = lax.psum_scatter(
        transposed_product(coup_leaf[0], bound_leaf), "row", scatter_dimension=0, tiled=True
    )
    shift_leaf = (rhs_leaf[0] - leaf_sum).astype(BF16)
    leaf_values = lax.psum_scatter(
        jnp.dot(dinv_leaf[0], shift_leaf, preferred_element_type=F32),
        "row",
        scatter_dimension=0,
        tiled=True,
    ).astype(BF16)
    return (root_values, mid_values, leaf_values[None])


SMEM = pl.BlockSpec(memory_space=pltpu.SMEM)
VMEM = pl.BlockSpec(memory_space=pltpu.VMEM)
LIMIT = 48 * 1024 * 1024


def params():
    return pltpu.CompilerParams(vmem_limit_bytes=LIMIT)


def loop(count, body):
    def step(i, carry):
        body(i)
        return carry

    lax.fori_loop(0, count, step, 0)


def mark_fronts(bounds_ref, front):
    def body(j):
        front[bounds_ref[0, j]] = 0
        front[bounds_ref[1, j]] = 1

    loop(bounds_ref.shape[1], body)


def order_kernel(local, slot, place_ref, bounds_ref, out_ref, front):
    x, h, z, y = (place_ref[i] for i in range(4))
    first = (2 * x + h) * local
    mark_fronts(bounds_ref, front)
    before = lax.fori_loop(0, first, lambda v, s: s + 1 - front[v], jnp.int32(0))
    zeros = lax.fori_loop(0, local, lambda i, s: s + 1 - front[first + i], jnp.int32(0))

    def body(i, carry):
        low, high = carry
        kind = front[first + i]
        rank = jnp.where(kind == 0, low, zeros + high)
        chip = (before + rank) & 7
        near = ((chip & 1) ^ y) * (local // 2) + ((chip >> 1) ^ z) * slot
        out_ref[near + (rank >> 3)] = i
        return low + 1 - kind, high + kind

    lax.fori_loop(0, local, body, (jnp.int32(0), jnp.int32(0)))


def plan_kernel(local, slot, leaf_slots, place_ref, bounds_ref, leaf_ref, parents_ref, out_ref, front, ident, where):
    x, h, z, y = (place_ref[i] for i in range(4))
    col = 2 * z + y
    total = 4 * local
    mark_fronts(bounds_ref, front)

    def per_row(r, before):
        zeros = lax.fori_loop(0, local, lambda i, s: s + 1 - front[r * local + i], jnp.int32(0))

        def body(i, carry):
            low, high = carry
            kind = front[r * local + i]
            rank = jnp.where(kind == 0, low, zeros + high)
            chip = (before + rank) & 7
            ident[r * local + chip * slot + (rank >> 3)] = r * local + i
            return low + 1 - kind, high + kind

        lax.fori_loop(0, local, body, (jnp.int32(0), jnp.int32(0)))
        return before + zeros

    lax.fori_loop(0, 4, per_row, jnp.int32(0))

    def clear(v):
        where[v] = 0

    loop(total, clear)

    def per_chip(chip, _):
        here = chip == col
        near = ((chip & 1) ^ y) * (local // 2) + ((chip >> 1) ^ z) * slot

        def put(core, count, block, code):
            where[block] = (core ^ h) * local + near + count

            @pl.when(here & (core == h))
            def _():
                out_ref[count] = code

        def from_far(step, carry):
            count0, count1 = carry
            core, k = step // slot, step % slot
            block = ident[(2 * (1 - x) + core) * local + chip * slot + k]
            taken = front[block] == x
            count = jnp.where(core == 0, count0, count1)

            @pl.when(taken)
            def _():
                put(core, count, block, 2 * slot + k)

            add = taken.astype(jnp.int32)
            return count0 + jnp.where(core == 0, add, 0), count1 + jnp.where(core == 0, 0, add)

        counts = lax.fori_loop(0, 2 * slot, from_far, (jnp.int32(0), jnp.int32(0)))

        def from_near(step, carry):
            count0, count1 = carry
            owner, k = step // slot, step % slot
            block = ident[(2 * x + owner) * local + chip * slot + k]
            taken = front[block] == x
            core = (count0 >= slot).astype(jnp.int32)
            count = jnp.where(core == 0, count0, count1)

            @pl.when(taken)
            def _():
                put(core, count, block, (owner ^ core) * slot + k)

            add = taken.astype(jnp.int32)
            return count0 + jnp.where(core == 0, add, 0), count1 + jnp.where(core == 0, 0, add)

        lax.fori_loop(0, 2 * slot, from_near, counts)
        return 0

    lax.fori_loop(0, 8, per_chip, 0)

    at = plan_layout(local, slot, leaf_slots)

    def mid_place(block):
        inner = block % local
        chip = inner // slot
        near = ((chip & 1) ^ y) * (local // 2) + ((chip >> 1) ^ z) * slot
        return ((block // local) ^ h) * local + near + inner % slot

    def mid_list(j):
        out_ref[at["mid"] + j] = where[bounds_ref[x, h * local + j]]

    loop(local, mid_list)
    far = 2 * (1 - x) + h
    mine = 2 * x + h
    owner = parents_ref[col] == x

    def lists(j):
        asked = leaf_ref[col, far * leaf_slots + j]
        out_ref[at["send_root"] + j] = where[jnp.minimum(asked, total - 1)]
        out_ref[at["send_mid"] + j] = mid_place(jnp.maximum(asked - total, 0))
        held = leaf_ref[col, mine * leaf_slots + j]
        low = jnp.minimum(held, total - 1)
        from_root = jnp.where(front[low] == x, where[low], 2 * local + j)
        from_mid = jnp.where(owner, mid_place(jnp.maximum(held - total, 0)), 2 * local + j) + at["mid_base"]
        out_ref[at["leaf"] + j] = jnp.where(held < total, from_root, from_mid)

    loop(leaf_slots, lists)

    def outs(j):
        asked = far * local + col * slot + j
        out_ref[at["send_root"] + leaf_slots + j] = where[asked]
        held = mine * local + col * slot + j
        out_ref[at["out"] + j] = jnp.where(front[held] == x, where[held], 2 * local + leaf_slots + j)

    loop(slot, outs)


def plan_layout(local, slot, leaf_slots):
    at = {}
    size = 0
    for name, count in (
        ("select", slot),
        ("mid", local),
        ("send_root", leaf_slots + slot),
        ("leaf", leaf_slots),
        ("out", slot),
        ("send_mid", leaf_slots),
    ):
        at[name] = size
        size += count
    at["size"] = size
    at["mid_base"] = 2 * local + leaf_slots + slot
    return at


def fetch(sources, code, target, index):
    base = 0
    for source in sources:
        count = source.shape[0]

        @pl.when((code >= base) & (code < base + count))
        def _(source=source, base=base):
            target[index] = source[code - base]

        base += count


def gather_kernel(start, count, table_ref, *refs):
    *sources, out_ref = refs
    for i in range(count):
        fetch(sources, table_ref[start + i], out_ref, i)


def gather(table, start, count, *sources):
    shape = sources[0].shape
    return pl.pallas_call(
        functools.partial(gather_kernel, start, count),
        out_shape=jax.ShapeDtypeStruct((count,) + shape[1:], BF16),
        in_specs=[SMEM] + [VMEM] * len(sources),
        out_specs=VMEM,
        compiler_params=params(),
    )(table, *sources)


def row_product_kernel(parts, order_ref, value_ref, *refs):
    *blocks, out_ref = refs
    matrix = jnp.concatenate([b[...] for b in blocks], axis=0)
    result = lax.dot_general(value_ref[...], matrix, NT, preferred_element_type=F32).astype(BF16)
    for i in range(parts):
        out_ref[i] = result[:, i * BLOCK : (i + 1) * BLOCK]


def row_product(order, start, count, value, matrix, parts=4):
    width, depth = value.shape

    def spec(i):
        return pl.BlockSpec((BLOCK, depth), lambda s, order: (order[start + parts * s + i], 0))

    return pl.pallas_call(
        functools.partial(row_product_kernel, parts),
        grid_spec=pltpu.PrefetchScalarGridSpec(
            num_scalar_prefetch=1,
            grid=(count // parts,),
            in_specs=[pl.BlockSpec((width, depth), lambda s, order: (0, 0))] + [spec(i) for i in range(parts)],
            out_specs=pl.BlockSpec((parts, width, BLOCK), lambda s, order: (s, 0, 0)),
        ),
        out_shape=jax.ShapeDtypeStruct((count, width, BLOCK), BF16),
        compiler_params=params(),
        cost_estimate=pl.CostEstimate(
            flops=2 * count * BLOCK * depth * width, bytes_accessed=2 * count * BLOCK * depth, transcendentals=0
        ),
    )(order, value, *([matrix] * parts))


def mid_coupling_kernel(start, parts, table_ref, own_ref, sib_ref, coup_ref, out_ref, bound):
    step = pl.program_id(0)
    for i in range(parts):
        fetch([own_ref, sib_ref], table_ref[start + parts * step + i], bound, i)
    value = jnp.concatenate([bound[i] for i in range(parts)], axis=1)
    product = lax.dot_general(value, coup_ref[...], NN, preferred_element_type=F32)

    @pl.when(step == 0)
    def _():
        out_ref[...] = product

    @pl.when(step > 0)
    def _():
        out_ref[...] += product


def mid_coupling(table, start, own, sib, coup, parts=4):
    local, width, _ = own.shape
    rows, cols = coup.shape
    whole = pl.BlockSpec((local, width, BLOCK), lambda s, table: (0, 0, 0))
    return pl.pallas_call(
        functools.partial(mid_coupling_kernel, start, parts),
        grid_spec=pltpu.PrefetchScalarGridSpec(
            num_scalar_prefetch=1,
            grid=(local // parts,),
            in_specs=[whole, whole, pl.BlockSpec((parts * BLOCK, cols), lambda s, table: (s, 0))],
            out_specs=pl.BlockSpec((width, cols), lambda s, table: (0, 0)),
            scratch_shapes=[pltpu.VMEM((parts, width, BLOCK), BF16)],
        ),
        out_shape=jax.ShapeDtypeStruct((width, cols), F32),
        compiler_params=params(),
        cost_estimate=pl.CostEstimate(
            flops=2 * rows * cols * width, bytes_accessed=2 * rows * cols, transcendentals=0
        ),
    )(table, own, sib, coup)


def leaf_coupling_kernel(order_ref, bound_ref, coup_ref, out_ref):
    out_ref[0] = lax.dot_general(bound_ref[...], coup_ref[...], NN, preferred_element_type=F32).astype(BF16)


def leaf_coupling(order, start, count, bound, coup, cols):
    width, depth = bound.shape
    return pl.pallas_call(
        leaf_coupling_kernel,
        grid_spec=pltpu.PrefetchScalarGridSpec(
            num_scalar_prefetch=1,
            grid=(count,),
            in_specs=[
                pl.BlockSpec((width, depth), lambda s, order: (0, 0)),
                pl.BlockSpec((depth, cols), lambda s, order: (0, order[start + s])),
            ],
            out_specs=pl.BlockSpec((1, width, cols), lambda s, order: (s, 0, 0)),
        ),
        out_shape=jax.ShapeDtypeStruct((count, width, cols), BF16),
        compiler_params=params(),
        cost_estimate=pl.CostEstimate(
            flops=2 * count * depth * cols * width, bytes_accessed=2 * count * depth * cols, transcendentals=0
        ),
    )(order, bound, coup)


def leaf_inverse_kernel(order_ref, value_ref, matrix_ref, out_ref):
    out_ref[0] = lax.dot_general(value_ref[...], matrix_ref[...], NT, preferred_element_type=F32).astype(BF16)


def leaf_inverse(order, start, count, value, matrix):
    width, depth = value.shape
    rows = depth
    return pl.pallas_call(
        leaf_inverse_kernel,
        grid_spec=pltpu.PrefetchScalarGridSpec(
            num_scalar_prefetch=1,
            grid=(count,),
            in_specs=[
                pl.BlockSpec((width, depth), lambda s, order: (0, 0)),
                pl.BlockSpec((rows, depth), lambda s, order: (order[start + s], 0)),
            ],
            out_specs=pl.BlockSpec((1, width, rows), lambda s, order: (s, 0, 0)),
        ),
        out_shape=jax.ShapeDtypeStruct((count, width, rows), BF16),
        compiler_params=params(),
        cost_estimate=pl.CostEstimate(
            flops=2 * count * rows * depth * width, bytes_accessed=2 * count * rows * depth, transcendentals=0
        ),
    )(order, value, matrix)


def swap(value, axis, mask):
    return lax.ppermute(value, axis, [(i, i ^ mask) for i in range(lax.axis_size(axis))])


def add(*terms):
    return functools.reduce(jnp.add, [t.astype(F32) for t in terms])


def reduce_columns(send, keep, slot):
    got = swap(send, "col", 1)
    part = [add(keep[m * slot : (m + 1) * slot], got[m * slot : (m + 1) * slot]) for m in range(4)]
    far = [swap(part[m].astype(BF16), "col", 2 * m) for m in (1, 2, 3)]
    return add(part[0], *far).astype(BF16)


def gather_columns(value):
    far = [swap(value, "col", 2 * m) for m in (1, 2, 3)]
    near = swap(value, "col", 1)
    rest = jnp.concatenate(far, axis=0)
    return jnp.concatenate([value, rest, near, swap(rest, "col", 1)], axis=0)


def natural(blocks):
    return jnp.swapaxes(blocks, 1, 2).reshape(-1, blocks.shape[1])


def shards(
    dinv_root,
    rhs_root,
    dinv_mid,
    coup_mid,
    rhs_mid,
    dinv_leaf,
    coup_leaf,
    rhs_leaf,
    bounds_mid,
    bounds_leaf,
    parents,
):
    row_id = lax.axis_index("row")
    col_id = lax.axis_index("col")
    x, h, z, y = row_id // 2, row_id % 2, col_id // 2, col_id % 2
    place = jnp.stack([x, h, z, y]).astype(jnp.int32)
    rhs_width = rhs_root.shape[1]
    local = dinv_root.shape[0] // BLOCK
    slot = local // 8
    half = local // 2
    leaf_slots = bounds_leaf.shape[1] // 4
    at = plan_layout(local, slot, leaf_slots)

    order = pl.pallas_call(
        functools.partial(order_kernel, local, slot),
        out_shape=jax.ShapeDtypeStruct((local,), jnp.int32),
        in_specs=[SMEM] * 2,
        out_specs=SMEM,
        scratch_shapes=[pltpu.SMEM((4 * local,), jnp.int32)],
    )(place, bounds_mid)
    plan = pl.pallas_call(
        functools.partial(plan_kernel, local, slot, leaf_slots),
        out_shape=jax.ShapeDtypeStruct((at["size"],), jnp.int32),
        in_specs=[SMEM] * 4,
        out_specs=SMEM,
        scratch_shapes=[pltpu.SMEM((4 * local,), jnp.int32)] * 3,
    )(place, bounds_mid, bounds_leaf, parents)

    near = jnp.arange(local, dtype=jnp.int32)
    near_y, near_z, near_k = near // half, near % half // slot, near % slot
    mid_order = (2 * (z ^ near_z) + (y ^ near_y)) * slot + near_k
    leaf_order = jnp.stack(
        [2 * x + 1 - h, 2 * (1 - x) + 1 - h, 2 * x + h, 2 * (1 - x) + h]
    ).astype(jnp.int32)

    root_rhs = rhs_root.T
    mid_rhs = lax.dynamic_index_in_dim(rhs_mid, x, 0, keepdims=False).T
    leaf_rhs = rhs_leaf[0].T
    leaf_cols = coup_leaf.shape[2] // 4

    def chain(lo, hi):
        value = root_rhs[lo:hi]
        send = row_product(order, half, half, value, dinv_root)
        keep = row_product(order, 0, half, value, dinv_root)
        got = reduce_columns(send, keep, slot)
        picked = gather(plan, at["select"], slot, got, swap(got, "row", 1), swap(got, "row", 2))
        own = gather_columns(picked)
        sib = swap(own, "row", 1)
        asked = swap(gather(plan, at["send_root"], leaf_slots + slot, own, sib), "row", 2)
        root_out = natural(gather(plan, at["out"], slot, own, sib, asked))

        term = mid_coupling(plan, at["mid"], own, sib, coup_mid)
        shift = (mid_rhs[lo:hi] - (term + swap(term, "row", 1))).astype(BF16)
        send = row_product(mid_order, half, half, shift, dinv_mid)
        keep = row_product(mid_order, 0, half, shift, dinv_mid)
        got = reduce_columns(send, keep, slot)
        mid_out = natural(got)
        mid_own = gather_columns(got)
        mid_sib = swap(mid_own, "row", 1)
        mid_asked = swap(gather(plan, at["send_mid"], leaf_slots, mid_own, mid_sib), "row", 2)

        bound = gather(plan, at["leaf"], leaf_slots, own, sib, asked, mid_own, mid_sib, mid_asked)
        bound = jnp.swapaxes(bound, 0, 1).reshape(hi - lo, leaf_slots * BLOCK)

        def reduce_rows(send, keep):
            part = add(keep, swap(send, "row", 1))
            return add(part[0], swap(part[1].astype(BF16), "row", 2))

        term = reduce_rows(
            leaf_coupling(leaf_order, 0, 2, bound, coup_leaf[0], leaf_cols),
            leaf_coupling(leaf_order, 2, 2, bound, coup_leaf[0], leaf_cols),
        )
        shift = (leaf_rhs[lo:hi] - term).astype(BF16)
        leaf_out = reduce_rows(
            leaf_inverse(leaf_order, 0, 2, shift, dinv_leaf[0]),
            leaf_inverse(leaf_order, 2, 2, shift, dinv_leaf[0]),
        ).astype(BF16)
        return root_out, mid_out, leaf_out.T

    step = rhs_width // CHUNKS
    results = [chain(i * step, (i + 1) * step) for i in range(CHUNKS)]
    root_values, mid_values, leaf_values = (jnp.concatenate(part, axis=1) for part in zip(*results))
    return (root_values, mid_values, leaf_values[None])


def solution(mesh):
    sizes = dict(mesh.shape)
    in_specs = (
        P("row", "col"),
        P("col", None),
        P("row", "col"),
        P("row", "col"),
        P(None, "col", None),
        P("col", None, "row"),
        P("col", "row", None),
        P("col", "row", None),
        P(),
        P(),
        P(),
    )
    out_specs = (P(("row", "col"), None), P(("row", "col"), None), P("col", "row", None))

    def run(*args):
        fronts, listed = args[8].shape
        blocks = args[0].shape[0] // BLOCK
        whole = fronts == 2 and fronts * listed == blocks and args[2].shape[0] == args[0].shape[0]
        fits = sizes["row"] == 4 and sizes["col"] == 8 and whole
        body = shards if fits else general_shards
        return jax.shard_map(body, mesh=mesh, in_specs=in_specs, out_specs=out_specs, check_vma=False)(*args)

    return run
```

time: 750 us -> 491 us (0.65)
  waiting for transfers between devices: 526 us -> 150 us
  Pallas kernels: 0 us -> 171 us
  starting transfers between devices: 3.23 us -> 116 us
  matrix products: 62.9 us -> 0 us
  blocking collectives: 57.6 us -> 0 us
  local copies, waits for them, and re-layouts: 72.4 us -> 30.6 us
  between operations: 15.6 us -> 2.12 us
  other arithmetic: 9.27 us -> 18.8 us
    reduce_scatter x4 -> x0, waiting for transfers between devices: 366 us -> none  [the longest x1 121 us: shards(): lax.psum_scatter(jnp.dot(dinv_root, rhs_root, preferred_element_type=jnp....]
    pallas_call x0 -> x44, Pallas kernels: none -> 171 us  [the longest x12 67.7 us: row_product(): pl.pallas_call(functools.partial(row_product_kernel, parts), grid_spec=pl...]
    all_gather x2 -> x0, waiting for transfers between devices: 156 us -> none  [the longest x1 95.7 us: shards(): lax.all_gather(root_values, ('row', 'col'), axis=0, tiled=True)]
    ppermute x1 -> x87, waiting for transfers between devices: 2.9 us -> 150 us  [swap(): lax.ppermute(value, axis, [(i, i ^ mask) for i in range(lax.axis_size(axi...]
    ppermute x1 -> x87, starting transfers between devices: 0.32 us -> 116 us  [swap(): lax.ppermute(value, axis, [(i, i ^ mask) for i in range(lax.axis_size(axi...]
    dot_general x7 -> x0, matrix products: 62.9 us -> none  [the longest x2 17.7 us: transposed_product(): lax.dot_general(coupling, boundary, (((0,), (0,)), ((), ())), preferred_e...]
    unnamed x1 -> x0, blocking collectives: 57.6 us -> none
    reshape x2 -> x3, local copies, waits for them, and re-layouts: 21.1 us -> 1.53 us  [chain(): bound = jnp.swapaxes(bound, 0, 1).reshape(hi - lo, leaf_slots * BLOCK)]
  transfers between devices with their start and end apart: 8 -> 87, of which waited for: 8 -> 29; matrix products, arithmetic and copies ran while one was open for 1% -> 5% of each run, Pallas kernels for 0% -> 31%
where the time goes in v1:
time: 491 us; the launch traced here: 489 us
  Pallas kernels  171 us (35%)
  waiting for transfers between devices  150 us (31%)
  starting transfers between devices  116 us (24%)
  local copies, waits for them, and re-layouts  30.6 us (6%)
  other arithmetic  18.8 us (4%)
    ppermute x87, waiting for transfers between devices, swap(): lax.ppermute(value, axis, [(i, i ^ mask) for i in range(lax.axis_size(axi...  150 us
    ppermute x87, starting transfers between devices, swap(): lax.ppermute(value, axis, [(i, i ^ mask) for i in range(lax.axis_size(axi...  116 us
    pallas_call x12, Pallas kernels, row_product(): pl.pallas_call(functools.partial(row_product_kernel, parts), grid_spec=pl...  67.7 us
    pallas_call x6, Pallas kernels, leaf_coupling(): pl.pallas_call(leaf_coupling_kernel, grid_spec=pltpu.PrefetchScalarGridSp...  26.1 us
    pallas_call x3, Pallas kernels, mid_coupling(): pl.pallas_call(functools.partial(mid_coupling_kernel, start, parts), grid...  24.5 us
    pallas_call x6, Pallas kernels, leaf_inverse(): pl.pallas_call(leaf_inverse_kernel, grid_spec=pltpu.PrefetchScalarGridSpe...  23.6 us
    unnamed x132, local copies, waits for them, and re-layouts  19.8 us
    pallas_call x15, Pallas kernels, gather(): pl.pallas_call(functools.partial(gather_kernel, start, count), out_shape=...  18.9 us
  transfers between devices with their start and end apart: 87, of which 29 were waited for; matrix products, arithmetic and copies ran while one was open for 5% of the time, Pallas kernels for 31%

profile of v1, /device:TPU:0, one launch (start us, length us, event | category | flops | bytes accessed | tf_op | source)
XLA Modules:
  0.0 489.0 jit_solution(18095916952802303717)
XLA Ops:
  0.7 2.7 copy.21
  8.6 7.0 %shard_map.138 = bf16[16,128,128]{2,1,0:T(8,128)(2,1)} custom-call(s32[32]{0:T(128)S(1)} %copy-done.38, bf16[128,2048]{1,0:T(8,128)(2,1)S(1)} %get-tuple-element.17.value_ref, bf16[4096,2048]{1,0:T(8,128)(2,1)} %refs_3_.17, bf16[4096,2048]{1,0:T(8,128)(2,1)} %refs_3_.17, bf16[4096,2048]{1,0:T(8,128)(2,1)} %refs_3_.17, bf16[4096,2048]{1,0:T(8,128)(2,1)} %refs_3_.17), custom_call_target="tpu_custom_call" | custom-call | flops 1073741824 | bytes 8388608 | tf_op jit(solution)/shard_map/pallas_call | solution.py:326
  15.6 3.0 collective-permute-start.13
  18.6 7.0 %shard_map.133 = bf16[16,128,128]{2,1,0:T(8,128)(2,1)} custom-call(s32[32]{0:T(128)S(1)} %copy-done.38, bf16[128,2048]{1,0:T(8,128)(2,1)S(1)} %get-tuple-element.15.value_ref, bf16[4096,2048]{1,0:T(8,128)(2,1)} %refs_3_.17, bf16[4096,2048]{1,0:T(8,128)(2,1)} %refs_3_.17, bf16[4096,2048]{1,0:T(8,128)(2,1)} %refs_3_.17, bf16[4096,2048]{1,0:T(8,128)(2,1)} %refs_3_.17), custom_call_target="tpu_custom_call" | custom-call | flops 1073741824 | bytes 8388608 | tf_op jit(solution)/shard_map/pallas_call | solution.py:326
  25.6 7.0 %shard_map.143 = bf16[16,128,128]{2,1,0:T(8,128)(2,1)} custom-call(s32[32]{0:T(128)S(1)} %copy-done.38, bf16[128,2048]{1,0:T(8,128)(2,1)S(1)} %get-tuple-element.16.value_ref, bf16[4096,2048]{1,0:T(8,128)(2,1)} %refs_3_.17, bf16[4096,2048]{1,0:T(8,128)(2,1)} %refs_3_.17, bf16[4096,2048]{1,0:T(8,128)(2,1)} %refs_3_.17, bf16[4096,2048]{1,0:T(8,128)(2,1)} %refs_3_.17), custom_call_target="tpu_custom_call" | custom-call | flops 1073741824 | bytes 8388608 | tf_op jit(solution)/shard_map/pallas_call | solution.py:326
  34.7 6.4 %shard_map.137 = bf16[16,128,128]{2,1,0:T(8,128)(2,1)S(1)} custom-call(s32[32]{0:T(128)S(1)} %copy-done.38, bf16[128,2048]{1,0:T(8,128)(2,1)S(1)} %get-tuple-element.17.value_ref, bf16[4096,2048]{1,0:T(8,128)(2,1)} %refs_3_.17, bf16[4096,2048]{1,0:T(8,128)(2,1)} %refs_3_.17, bf16[4096,2048]{1,0:T(8,128)(2,1)} %refs_3_.17, bf16[4096,2048]{1,0:T(8,128)(2,1)} %refs_3_.17), custom_call_target="tpu_custom_call" | custom-call | flops 1073741824 | bytes 8388608 | tf_op jit(solution)/shard_map/pallas_call | solution.py:326
  41.9 6.3 %shard_map.132 = bf16[16,128,128]{2,1,0:T(8,128)(2,1)S(1)} custom-call(s32[32]{0:T(128)S(1)} %copy-done.38, bf16[128,2048]{1,0:T(8,128)(2,1)S(1)} %get-tuple-element.15.value_ref, bf16[4096,2048]{1,0:T(8,128)(2,1)} %refs_3_.17, bf16[4096,2048]{1,0:T(8,128)(2,1)} %refs_3_.17, bf16[4096,2048]{1,0:T(8,128)(2,1)} %refs_3_.17, bf16[4096,2048]{1,0:T(8,128)(2,1)} %refs_3_.17), custom_call_target="tpu_custom_call" | custom-call | flops 1073741824 | bytes 8388608 | tf_op jit(solution)/shard_map/pallas_call | solution.py:326
  48.2 6.4 %shard_map.142 = bf16[16,128,128]{2,1,0:T(8,128)(2,1)S(1)} custom-call(s32[32]{0:T(128)S(1)} %copy-done.38, bf16[128,2048]{1,0:T(8,128)(2,1)S(1)} %get-tuple-element.16.value_ref, bf16[4096,2048]{1,0:T(8,128)(2,1)} %refs_3_.17, bf16[4096,2048]{1,0:T(8,128)(2,1)} %refs_3_.17, bf16[4096,2048]{1,0:T(8,128)(2,1)} %refs_3_.17, bf16[4096,2048]{1,0:T(8,128)(2,1)} %refs_3_.17), custom_call_target="tpu_custom_call" | custom-call | flops 1073741824 | bytes 8388608 | tf_op jit(solution)/shard_map/pallas_call | solution.py:326
  54.6 8.1 %shard_map.130.table_ref = s32[80]{0:T(128)} custom-call(s32[4]{0:T(128)} %pad_add_fusion.place_ref, s32[2,64]{1,0:T(2,128)} %bounds_ref.3, s32[8,48]{1,0:T(8,128)} %leaf_ref.1, s32[8]{0:T(128)} %parents_ref.1), custom_call_target="tpu_custom_call" | custom-call | tf_op jit(solution)/shard_map/pallas_call | solution.py:487
  65.6 2.6 collective-permute-start.15
  70.3 3.5 collective-permute-start.2
  75.3 3.4 collective-permute-done.15
  78.7 10.3 %collective-permute-start.28 = (bf16[4,128,128]{2,1,0:T(8,128)(2,1)S(1)}, bf16[4,128,128]{2,1,0:T(8,128)(2,1)S(1)}, u32[]{:S(2)}, u32[]{:S(2)}) collective-permute-start(bf16[4,128,128]{2,1,0:T(8,128)(2,1)S(1)} %get-tuple-element.35), channel_id=1, source_target_pairs={{0,4},{1,5},{2,6},{3,7},{4,0},{5,1},{6,2},{7,3},{8,12},{9,13},{10,... | collective-permute-start | bytes 393224 | tf_op jit(solution)/shard_map/ppermute | solution.py:431
  96.6 3.8 collective-permute-done.28
  114.0 5.1 %collective-permute-done.20 = bf16[4,128,128]{2,1,0:T(8,128)(2,1)S(1)} collective-permute-done((bf16[4,128,128]{2,1,0:T(8,128)(2,1)S(1)}, bf16[4,128,128]{2,1,0:T(8,128)(2,1)S(1)}, u32[]{:S(2)}, u32[]{:S(2)}) %collective-permute-start.20) | collective-permute-done | bytes 131104 | tf_op jit(solution)/shard_map/ppermute | solution.py:431
  119.1 2.5 collective-permute-start.8
  122.2 6.5 %collective-permute-start.32 = (bf16[4,128,128]{2,1,0:T(8,128)(2,1)S(1)}, bf16[4,128,128]{2,1,0:T(8,128)(2,1)S(1)}, u32[]{:S(2)}, u32[]{:S(2)}) collective-permute-start(bf16[4,128,128]{2,1,0:T(8,128)(2,1)S(1)} %shard_map.144), channel_id=1, source_target_pairs={{0,2},{1,3},{2,0},{3,1},{4,6},{5,7},{6,4},{7,5},{8,10},{9,11},{10,... | collective-permute-start | bytes 393224 | tf_op jit(solution)/shard_map/ppermute | solution.py:431
  133.7 7.7 %collective-permute-done.33 = bf16[4,128,128]{2,1,0:T(8,128)(2,1)S(1)} collective-permute-done((bf16[4,128,128]{2,1,0:T(8,128)(2,1)S(1)}, bf16[4,128,128]{2,1,0:T(8,128)(2,1)S(1)}, u32[]{:S(2)}, u32[]{:S(2)}) %collective-permute-start.33) | collective-permute-done | bytes 131104 | tf_op jit(solution)/shard_map/ppermute | solution.py:431
  143.8 9.7 %collective-permute-done.23 = bf16[12,128,128]{2,1,0:T(8,128)(2,1)S(1)} collective-permute-done((bf16[12,128,128]{2,1,0:T(8,128)(2,1)S(1)}, bf16[12,128,128]{2,1,0:T(8,128)(2,1)S(1)}, u32[]{:S(2)}, u32[]{:S(2)}) %collective-permute-start.23) | collective-permute-done | bytes 393248 | tf_op jit(solution)/shard_map/ppermute | solution.py:431
  153.7 8.3 %collective-permute-done.10 = bf16[12,128,128]{2,1,0:T(8,128)(2,1)S(1)} collective-permute-done((bf16[12,128,128]{2,1,0:T(8,128)(2,1)S(1)}, bf16[12,128,128]{2,1,0:T(8,128)(2,1)S(1)}, u32[]{:S(2)}, u32[]{:S(2)}) %collective-permute-start.10) | collective-permute-done | bytes 393248 | tf_op jit(solution)/shard_map/ppermute | solution.py:431
  162.1 5.3 %collective-permute-done.36 = bf16[12,128,128]{2,1,0:T(8,128)(2,1)S(1)} collective-permute-done((bf16[12,128,128]{2,1,0:T(8,128)(2,1)S(1)}, bf16[12,128,128]{2,1,0:T(8,128)(2,1)S(1)}, u32[]{:S(2)}, u32[]{:S(2)}) %collective-permute-start.36) | collective-permute-done | bytes 393248 | tf_op jit(solution)/shard_map/ppermute | solution.py:431
  167.6 7.6 %shard_map.150 = f32[128,1024]{1,0:T(8,128)S(1)} custom-call(s32[80]{0:T(128)S(1)} %copy-done.37, bf16[32,128,128]{2,1,0:T(8,128)(2,1)S(1)} %constant_dynamic-update-slice_fusion.6.refs_0_.own_ref, bf16[32,128,128]{2,1,0:T(8,128)(2,1)S(1)} %collective-permute-done.24.refs_1_.sib_ref, bf16[4096,1024]{1,0:T(8,128)(2,1)} %coup_ref.5), custom_call_target="tpu_custom_call" | custom-call | flops 1073741824 | bytes 8388608 | tf_op jit(solution)/shard_map/pallas_call | solution.py:362
  175.8 8.4 %shard_map.147 = f32[128,1024]{1,0:T(8,128)} custom-call(s32[80]{0:T(128)S(1)} %copy-done.37, bf16[32,128,128]{2,1,0:T(8,128)(2,1)S(1)} %constant_dynamic-update-slice_fusion.refs_0_.own_ref, bf16[32,128,128]{2,1,0:T(8,128)(2,1)S(1)} %collective-permute-done.11.refs_1_.sib_ref, bf16[4096,1024]{1,0:T(8,128)(2,1)} %coup_ref.5), custom_call_target="tpu_custom_call" | custom-call | flops 1073741824 | bytes 8388608 | tf_op jit(solution)/shard_map/pallas_call | solution.py:362
  184.3 8.5 %shard_map.153 = f32[128,1024]{1,0:T(8,128)} custom-call(s32[80]{0:T(128)S(1)} %copy-done.37, bf16[32,128,128]{2,1,0:T(8,128)(2,1)S(1)} %constant_dynamic-update-slice_fusion.12.refs_0_.own_ref, bf16[32,128,128]{2,1,0:T(8,128)(2,1)S(1)} %collective-permute-done.37.refs_1_.sib_ref, bf16[4096,1024]{1,0:T(8,128)(2,1)} %coup_ref.5), custom_call_target="tpu_custom_call" | custom-call | flops 1073741824 | bytes 8388608 | tf_op jit(solution)/shard_map/pallas_call | solution.py:362
  197.7 4.6 shard_map.152
  203.5 4.6 shard_map.155
  209.1 4.6 shard_map.149
  214.8 4.6 shard_map.151
  219.4 4.6 shard_map.154
  224.0 4.6 shard_map.148
  233.4 5.4 %collective-permute-done.40 = bf16[16,128,128]{2,1,0:T(8,128)(2,1)S(1)} collective-permute-done((bf16[16,128,128]{2,1,0:T(8,128)(2,1)S(1)}, bf16[16,128,128]{2,1,0:T(8,128)(2,1)S(1)}, u32[]{:S(2)}, u32[]{:S(2)}) %collective-permute-start.40) | collective-permute-done | bytes 524320 | tf_op jit(solution)/shard_map/ppermute | solution.py:431
  239.6 2.9 collective-permute-start.53
  242.5 8.7 %collective-permute-start.42 = (bf16[4,128,128]{2,1,0:T(8,128)(2,1)S(1)}, bf16[4,128,128]{2,1,0:T(8,128)(2,1)S(1)}, u32[]{:S(2)}, u32[]{:S(2)}) collective-permute-start(bf16[4,128,128]{2,1,0:T(8,128)(2,1)S(1)} %get-tuple-element.20), channel_id=1, source_target_pairs={{0,4},{1,5},{2,6},{3,7},{4,0},{5,1},{6,2},{7,3},{8,12},{9,13},{10,... | collective-permute-start | bytes 393224 | tf_op jit(solution)/shard_map/ppermute | solution.py:431
  251.4 2.5 collective-permute-start.43
  253.9 4.7 collective-permute-done.52
  258.6 5.0 %collective-permute-start.66 = (bf16[4,128,128]{2,1,0:T(8,128)(2,1)S(1)}, bf16[4,128,128]{2,1,0:T(8,128)(2,1)S(1)}, u32[]{:S(2)}, u32[]{:S(2)}) collective-permute-start(bf16[4,128,128]{2,1,0:T(8,128)(2,1)S(1)} %get-tuple-element.12), channel_id=1, source_target_pairs={{0,4},{1,5},{2,6},{3,7},{4,0},{5,1},{6,2},{7,3},{8,12},{9,13},{10,... | collective-permute-start | bytes 393224 | tf_op jit(solution)/shard_map/ppermute | solution.py:431
  264.5 3.9 collective-permute-done.42
  268.4 2.7 collective-permute-start.68
  271.2 3.5 collective-permute-start.76
  280.3 5.6 %collective-permute-start.54 = (bf16[4,128,128]{2,1,0:T(8,128)(2,1)S(1)}, bf16[4,128,128]{2,1,0:T(8,128)(2,1)S(1)}, u32[]{:S(2)}, u32[]{:S(2)}) collective-permute-start(bf16[4,128,128]{2,1,0:T(8,128)(2,1)S(1)} %get-tuple-element.10), channel_id=1, source_target_pairs={{0,2},{1,3},{2,0},{3,1},{4,6},{5,7},{6,4},{7,5},{8,10},{9,11},{10,... | collective-permute-start | bytes 393224 | tf_op jit(solution)/shard_map/ppermute | solution.py:431
  285.9 3.7 collective-permute-done.77
  291.7 6.3 %collective-permute-done.55 = bf16[4,128,128]{2,1,0:T(8,128)(2,1)S(1)} collective-permute-done((bf16[4,128,128]{2,1,0:T(8,128)(2,1)S(1)}, bf16[4,128,128]{2,1,0:T(8,128)(2,1)S(1)}, u32[]{:S(2)}, u32[]{:S(2)}) %collective-permute-start.55) | collective-permute-done | bytes 131104 | tf_op jit(solution)/shard_map/ppermute | solution.py:431
  301.6 8.4 %collective-permute-done.69 = bf16[12,128,128]{2,1,0:T(8,128)(2,1)S(1)} collective-permute-done((bf16[12,128,128]{2,1,0:T(8,128)(2,1)S(1)}, bf16[12,128,128]{2,1,0:T(8,128)(2,1)S(1)}, u32[]{:S(2)}, u32[]{:S(2)}) %collective-permute-start.69) | collective-permute-done | bytes 393248 | tf_op jit(solution)/shard_map/ppermute | solution.py:431
  310.1 8.3 %collective-permute-done.80 = bf16[12,128,128]{2,1,0:T(8,128)(2,1)S(1)} collective-permute-done((bf16[12,128,128]{2,1,0:T(8,128)(2,1)S(1)}, bf16[12,128,128]{2,1,0:T(8,128)(2,1)S(1)}, u32[]{:S(2)}, u32[]{:S(2)}) %collective-permute-start.80) | collective-permute-done | bytes 393248 | tf_op jit(solution)/shard_map/ppermute | solution.py:431
  318.6 4.4 collective-permute-done.58
  342.0 6.2 %collective-permute-done.71.refs_5_ = bf16[12,128,128]{2,1,0:T(8,128)(2,1)S(1)} collective-permute-done((bf16[12,128,128]{2,1,0:T(8,128)(2,1)}, bf16[12,128,128]{2,1,0:T(8,128)(2,1)S(1)}, u32[]{:S(2)}, u32[]{:S(2)}) %collective-permute-start.71) | collective-permute-done | bytes 393248 | tf_op jit(solution)/shard_map/ppermute | solution.py:431
  354.7 5.0 %shard_map.165 = bf16[2,128,1024]{2,1,0:T(8,128)(2,1)} custom-call(s32[4]{0:T(128)S(1)} %pad_add_fusion.1.order_ref, bf16[128,1536]{1,0:T(8,128)(2,1)S(1)} %copy.34.bound_ref, bf16[1536,4096]{1,0:T(8,128)(2,1)} %bitcast.109), custom_call_target="tpu_custom_call" | custom-call | flops 805306368 | bytes 6291456 | tf_op jit(solution)/shard_map/pallas_call | solution.py:385
  359.7 19.4 %collective-permute-done.82.refs_5_ = bf16[12,128,128]{2,1,0:T(8,128)(2,1)} collective-permute-done((bf16[12,128,128]{2,1,0:T(8,128)(2,1)}, bf16[12,128,128]{2,1,0:T(8,128)(2,1)}, u32[]{:S(2)}, u32[]{:S(2)}) %collective-permute-start.82) | collective-permute-done | bytes 393248 | tf_op jit(solution)/shard_map/ppermute | solution.py:431
  381.2 5.0 %shard_map.171 = bf16[2,128,1024]{2,1,0:T(8,128)(2,1)} custom-call(s32[4]{0:T(128)S(1)} %pad_add_fusion.1.order_ref, bf16[128,1536]{1,0:T(8,128)(2,1)S(1)} %copy.37.bound_ref, bf16[1536,4096]{1,0:T(8,128)(2,1)} %bitcast.110), custom_call_target="tpu_custom_call" | custom-call | flops 805306368 | bytes 6291456 | tf_op jit(solution)/shard_map/pallas_call | solution.py:385
  390.9 4.0 shard_map.164
  394.9 4.0 shard_map.170
  398.9 4.0 shard_map.159
  402.9 4.0 shard_map.158
  418.5 5.6 %collective-permute-done.84 = bf16[128,1024]{1,0:T(8,128)(2,1)} collective-permute-done((bf16[128,1024]{1,0:T(8,128)(2,1)}, bf16[128,1024]{1,0:T(8,128)(2,1)}, u32[]{:S(2)}, u32[]{:S(2)}) %collective-permute-start.84) | collective-permute-done | bytes 262176 | tf_op jit(solution)/shard_map/ppermute | solution.py:431
  424.1 5.1 %collective-permute-done.62 = bf16[128,1024]{1,0:T(8,128)(2,1)S(1)} collective-permute-done((bf16[128,1024]{1,0:T(8,128)(2,1)S(1)}, bf16[128,1024]{1,0:T(8,128)(2,1)S(1)}, u32[]{:S(2)}, u32[]{:S(2)}) %collective-permute-start.62) | collective-permute-done | bytes 262176 | tf_op jit(solution)/shard_map/ppermute | solution.py:431
  432.2 4.5 shard_map.161
  446.5 3.8 shard_map.167
  450.8 3.8 shard_map.160
  454.6 3.8 shard_map.166
  458.5 3.8 shard_map.173
  462.3 3.8 shard_map.172
  471.3 5.5 %collective-permute-done.64 = bf16[128,1024]{1,0:T(8,128)(2,1)S(1)} collective-permute-done((bf16[128,1024]{1,0:T(8,128)(2,1)S(1)}, bf16[128,1024]{1,0:T(8,128)(2,1)S(1)}, u32[]{:S(2)}, u32[]{:S(2)}) %collective-permute-start.64) | collective-permute-done | bytes 262176 | tf_op jit(solution)/shard_map/ppermute | solution.py:431
  476.8 5.6 %collective-permute-done.75 = bf16[128,1024]{1,0:T(8,128)(2,1)S(1)} collective-permute-done((bf16[128,1024]{1,0:T(8,128)(2,1)S(1)}, bf16[128,1024]{1,0:T(8,128)(2,1)S(1)}, u32[]{:S(2)}, u32[]{:S(2)}) %collective-permute-start.75) | collective-permute-done | bytes 262176 | tf_op jit(solution)/shard_map/ppermute | solution.py:431
  482.4 5.1 %collective-permute-done.86 = bf16[128,1024]{1,0:T(8,128)(2,1)S(1)} collective-permute-done((bf16[128,1024]{1,0:T(8,128)(2,1)S(1)}, bf16[128,1024]{1,0:T(8,128)(2,1)S(1)}, u32[]{:S(2)}, u32[]{:S(2)}) %collective-permute-start.86) | collective-permute-done | bytes 262176 | tf_op jit(solution)/shard_map/ppermute | solution.py:431
  (347 shorter events, 134.1 us)
Async XLA Ops:
  15.6 47.1 %collective-permute-start.13 = (bf16[16,128,128]{2,1,0:T(8,128)(2,1)}, bf16[16,128,128]{2,1,0:T(8,128)(2,1)}, u32[]{:S(2)}, u32[]{:S(2)}) collective-permute-start(bf16[16,128,128]{2,1,0:T(8,128)(2,1)} %shard_map.138), channel_id=1, source_target_pairs={{0,1},{1,0},{2,3},{3,2},{4,5},{5,4},{6,7},{7,6},{8,9},{9,8},{10,11... | collective-permute-start | bytes 1572872 | tf_op jit(solution)/shard_map/ppermute | solution.py:431
  25.6 42.8 %collective-permute-start = (bf16[16,128,128]{2,1,0:T(8,128)(2,1)}, bf16[16,128,128]{2,1,0:T(8,128)(2,1)}, u32[]{:S(2)}, u32[]{:S(2)}) collective-permute-start(bf16[16,128,128]{2,1,0:T(8,128)(2,1)} %shard_map.133), channel_id=1, source_target_pairs={{0,1},{1,0},{2,3},{3,2},{4,5},{5,4},{6,7},{7,6},{8,9},{9,8},{10,11... | collective-permute-start | bytes 1572872 | tf_op jit(solution)/shard_map/ppermute | solution.py:431
  32.7 37.7 %collective-permute-start.26 = (bf16[16,128,128]{2,1,0:T(8,128)(2,1)}, bf16[16,128,128]{2,1,0:T(8,128)(2,1)}, u32[]{:S(2)}, u32[]{:S(2)}) collective-permute-start(bf16[16,128,128]{2,1,0:T(8,128)(2,1)} %shard_map.143), channel_id=1, source_target_pairs={{0,1},{1,0},{2,3},{3,2},{4,5},{5,4},{6,7},{7,6},{8,9},{9,8},{10,11... | collective-permute-start | bytes 1572872 | tf_op jit(solution)/shard_map/ppermute | solution.py:431
  65.6 13.0 %collective-permute-start.15 = (bf16[4,128,128]{2,1,0:T(8,128)(2,1)S(1)}, bf16[4,128,128]{2,1,0:T(8,128)(2,1)S(1)}, u32[]{:S(2)}, u32[]{:S(2)}) collective-permute-start(bf16[4,128,128]{2,1,0:T(8,128)(2,1)S(1)} %get-tuple-element.32), channel_id=1, source_target_pairs={{0,4},{1,5},{2,6},{3,7},{4,0},{5,1},{6,2},{7,3},{8,12},{9,13},{10,... | collective-permute-start | bytes 393224 | tf_op jit(solution)/shard_map/ppermute | solution.py:431
  69.6 20.4 %collective-permute-start.1 = (bf16[4,128,128]{2,1,0:T(8,128)(2,1)S(1)}, bf16[4,128,128]{2,1,0:T(8,128)(2,1)S(1)}, u32[]{:S(2)}, u32[]{:S(2)}) collective-permute-start(bf16[4,128,128]{2,1,0:T(8,128)(2,1)S(1)} %get-tuple-element.27), channel_id=1, source_target_pairs={{0,2},{1,3},{2,0},{3,1},{4,6},{5,7},{6,4},{7,5},{8,10},{9,11},{10,... | collective-permute-start | bytes 393224 | tf_op jit(solution)/shard_map/ppermute | solution.py:431
  70.3 23.1 %collective-permute-start.2 = (bf16[4,128,128]{2,1,0:T(8,128)(2,1)S(1)}, bf16[4,128,128]{2,1,0:T(8,128)(2,1)S(1)}, u32[]{:S(2)}, u32[]{:S(2)}) collective-permute-start(bf16[4,128,128]{2,1,0:T(8,128)(2,1)S(1)} %get-tuple-element.29), channel_id=1, source_target_pairs={{0,4},{1,5},{2,6},{3,7},{4,0},{5,1},{6,2},{7,3},{8,12},{9,13},{10,... | collective-permute-start | bytes 393224 | tf_op jit(solution)/shard_map/ppermute | solution.py:431
  75.0 18.4 %collective-permute-start.3 = (bf16[4,128,128]{2,1,0:T(8,128)(2,1)S(1)}, bf16[4,128,128]{2,1,0:T(8,128)(2,1)S(1)}, u32[]{:S(2)}, u32[]{:S(2)}) collective-permute-start(bf16[4,128,128]{2,1,0:T(8,128)(2,1)S(1)} %get-tuple-element.28), channel_id=1, source_target_pairs={{0,6},{1,7},{2,4},{3,5},{4,2},{5,3},{6,0},{7,1},{8,14},{9,15},{10,... | collective-permute-start | bytes 393224 | tf_op jit(solution)/shard_map/ppermute | solution.py:431
  78.7 17.6 %collective-permute-start.27 = (bf16[4,128,128]{2,1,0:T(8,128)(2,1)S(1)}, bf16[4,128,128]{2,1,0:T(8,128)(2,1)S(1)}, u32[]{:S(2)}, u32[]{:S(2)}) collective-permute-start(bf16[4,128,128]{2,1,0:T(8,128)(2,1)S(1)} %get-tuple-element.33), channel_id=1, source_target_pairs={{0,2},{1,3},{2,0},{3,1},{4,6},{5,7},{6,4},{7,5},{8,10},{9,11},{10,... | collective-permute-start | bytes 393224 | tf_op jit(solution)/shard_map/ppermute | solution.py:431
  78.7 21.7 %collective-permute-start.28 = (bf16[4,128,128]{2,1,0:T(8,128)(2,1)S(1)}, bf16[4,128,128]{2,1,0:T(8,128)(2,1)S(1)}, u32[]{:S(2)}, u32[]{:S(2)}) collective-permute-start(bf16[4,128,128]{2,1,0:T(8,128)(2,1)S(1)} %get-tuple-element.35), channel_id=1, source_target_pairs={{0,4},{1,5},{2,6},{3,7},{4,0},{5,1},{6,2},{7,3},{8,12},{9,13},{10,... | collective-permute-start | bytes 393224 | tf_op jit(solution)/shard_map/ppermute | solution.py:431
  90.0 12.2 %collective-permute-start.29 = (bf16[4,128,128]{2,1,0:T(8,128)(2,1)S(1)}, bf16[4,128,128]{2,1,0:T(8,128)(2,1)S(1)}, u32[]{:S(2)}, u32[]{:S(2)}) collective-permute-start(bf16[4,128,128]{2,1,0:T(8,128)(2,1)S(1)} %get-tuple-element.34), channel_id=1, source_target_pairs={{0,6},{1,7},{2,4},{3,5},{4,2},{5,3},{6,0},{7,1},{8,14},{9,15},{10,... | collective-permute-start | bytes 393224 | tf_op jit(solution)/shard_map/ppermute | solution.py:431
  106.1 13.0 %collective-permute-start.20 = (bf16[4,128,128]{2,1,0:T(8,128)(2,1)S(1)}, bf16[4,128,128]{2,1,0:T(8,128)(2,1)S(1)}, u32[]{:S(2)}, u32[]{:S(2)}) collective-permute-start(bf16[4,128,128]{2,1,0:T(8,128)(2,1)S(1)} %shard_map.139), channel_id=1, source_target_pairs={{0,4},{1,5},{2,6},{3,7},{4,0},{5,1},{6,2},{7,3},{8,12},{9,13},{10,... | collective-permute-start | bytes 393224 | tf_op jit(solution)/shard_map/ppermute | solution.py:431
  107.4 14.2 %collective-permute-start.21 = (bf16[4,128,128]{2,1,0:T(8,128)(2,1)S(1)}, bf16[4,128,128]{2,1,0:T(8,128)(2,1)S(1)}, u32[]{:S(2)}, u32[]{:S(2)}) collective-permute-start(bf16[4,128,128]{2,1,0:T(8,128)(2,1)S(1)} %shard_map.139), channel_id=1, source_target_pairs={{0,6},{1,7},{2,4},{3,5},{4,2},{5,3},{6,0},{7,1},{8,14},{9,15},{10,... | collective-permute-start | bytes 393224 | tf_op jit(solution)/shard_map/ppermute | solution.py:431
  109.4 34.2 %collective-permute-start.22 = (bf16[4,128,128]{2,1,0:T(8,128)(2,1)S(1)}, bf16[4,128,128]{2,1,0:T(8,128)(2,1)S(1)}, u32[]{:S(2)}, u32[]{:S(2)}) collective-permute-start(bf16[4,128,128]{2,1,0:T(8,128)(2,1)S(1)} %shard_map.139), channel_id=1, source_target_pairs={{0,1},{1,0},{2,3},{3,2},{4,5},{5,4},{6,7},{7,6},{8,9},{9,8},{10,11... | collective-permute-start | bytes 393224 | tf_op jit(solution)/shard_map/ppermute | solution.py:431
  110.0 12.2 %collective-permute-start.6 = (bf16[4,128,128]{2,1,0:T(8,128)(2,1)S(1)}, bf16[4,128,128]{2,1,0:T(8,128)(2,1)S(1)}, u32[]{:S(2)}, u32[]{:S(2)}) collective-permute-start(bf16[4,128,128]{2,1,0:T(8,128)(2,1)S(1)} %shard_map.134), channel_id=1, source_target_pairs={{0,2},{1,3},{2,0},{3,1},{4,6},{5,7},{6,4},{7,5},{8,10},{9,11},{10,... | collective-permute-start | bytes 393224 | tf_op jit(solution)/shard_map/ppermute | solution.py:431
  111.8 18.5 %collective-permute-start.7 = (bf16[4,128,128]{2,1,0:T(8,128)(2,1)S(1)}, bf16[4,128,128]{2,1,0:T(8,128)(2,1)S(1)}, u32[]{:S(2)}, u32[]{:S(2)}) collective-permute-start(bf16[4,128,128]{2,1,0:T(8,128)(2,1)S(1)} %shard_map.134), channel_id=1, source_target_pairs={{0,4},{1,5},{2,6},{3,7},{4,0},{5,1},{6,2},{7,3},{8,12},{9,13},{10,... | collective-permute-start | bytes 393224 | tf_op jit(solution)/shard_map/ppermute | solution.py:431
  119.1 11.3 %collective-permute-start.8 = (bf16[4,128,128]{2,1,0:T(8,128)(2,1)S(1)}, bf16[4,128,128]{2,1,0:T(8,128)(2,1)S(1)}, u32[]{:S(2)}, u32[]{:S(2)}) collective-permute-start(bf16[4,128,128]{2,1,0:T(8,128)(2,1)S(1)} %shard_map.134), channel_id=1, source_target_pairs={{0,6},{1,7},{2,4},{3,5},{4,2},{5,3},{6,0},{7,1},{8,14},{9,15},{10,... | collective-permute-start | bytes 393224 | tf_op jit(solution)/shard_map/ppermute | solution.py:431
  121.6 22.2 %collective-permute-start.9 = (bf16[4,128,128]{2,1,0:T(8,128)(2,1)S(1)}, bf16[4,128,128]{2,1,0:T(8,128)(2,1)S(1)}, u32[]{:S(2)}, u32[]{:S(2)}) collective-permute-start(bf16[4,128,128]{2,1,0:T(8,128)(2,1)S(1)} %shard_map.134), channel_id=1, source_target_pairs={{0,1},{1,0},{2,3},{3,2},{4,5},{5,4},{6,7},{7,6},{8,9},{9,8},{10,11... | collective-permute-start | bytes 393224 | tf_op jit(solution)/shard_map/ppermute | solution.py:431
  130.3 11.2 %collective-permute-start.33 = (bf16[4,128,128]{2,1,0:T(8,128)(2,1)S(1)}, bf16[4,128,128]{2,1,0:T(8,128)(2,1)S(1)}, u32[]{:S(2)}, u32[]{:S(2)}) collective-permute-start(bf16[4,128,128]{2,1,0:T(8,128)(2,1)S(1)} %shard_map.144), channel_id=1, source_target_pairs={{0,4},{1,5},{2,6},{3,7},{4,0},{5,1},{6,2},{7,3},{8,12},{9,13},{10,... | collective-permute-start | bytes 393224 | tf_op jit(solution)/shard_map/ppermute | solution.py:431
  141.5 12.1 %collective-permute-start.23 = (bf16[12,128,128]{2,1,0:T(8,128)(2,1)S(1)}, bf16[12,128,128]{2,1,0:T(8,128)(2,1)S(1)}, u32[]{:S(2)}, u32[]{:S(2)}) collective-permute-start(bf16[12,128,128]{2,1,0:T(8,128)(2,1)S(1)} %pad_maximum_fusion.1), channel_id=1, source_target_pairs={{0,1},{1,0},{2,3},{3,2},{4,5},{5,4},{6,7},{7,6},{8,9},{9,8},{10,11... | collective-permute-start | bytes 1179656 | tf_op jit(solution)/shard_map/ppermute | solution.py:431
  141.5 20.5 %collective-permute-start.10 = (bf16[12,128,128]{2,1,0:T(8,128)(2,1)S(1)}, bf16[12,128,128]{2,1,0:T(8,128)(2,1)S(1)}, u32[]{:S(2)}, u32[]{:S(2)}) collective-permute-start(bf16[12,128,128]{2,1,0:T(8,128)(2,1)S(1)} %pad_maximum_fusion), channel_id=1, source_target_pairs={{0,1},{1,0},{2,3},{3,2},{4,5},{5,4},{6,7},{7,6},{8,9},{9,8},{10,11... | collective-permute-start | bytes 1179656 | tf_op jit(solution)/shard_map/ppermute | solution.py:431
  143.6 23.8 %collective-permute-start.36 = (bf16[12,128,128]{2,1,0:T(8,128)(2,1)S(1)}, bf16[12,128,128]{2,1,0:T(8,128)(2,1)S(1)}, u32[]{:S(2)}, u32[]{:S(2)}) collective-permute-start(bf16[12,128,128]{2,1,0:T(8,128)(2,1)S(1)} %pad_maximum_fusion.2), channel_id=1, source_target_pairs={{0,1},{1,0},{2,3},{3,2},{4,5},{5,4},{6,7},{7,6},{8,9},{9,8},{10,11... | collective-permute-start | bytes 1179656 | tf_op jit(solution)/shard_map/ppermute | solution.py:431
  153.6 14.0 %collective-permute-start.24 = (bf16[32,128,128]{2,1,0:T(8,128)(2,1)S(1)}, bf16[32,128,128]{2,1,0:T(8,128)(2,1)S(1)}, u32[]{:S(2)}, u32[]{:S(2)}) collective-permute-start(bf16[32,128,128]{2,1,0:T(8,128)(2,1)S(1)} %constant_dynamic-update-slice_fusion.6.refs_0_.own_ref), channel_id=1, source_target_pairs={{0,8},{8,0},{16,24},{24,16},{1,9},{9,1},{17,25},{25,17},{2,10},{10... | collective-permute-start | bytes 3145736 | tf_op jit(solution)/shard_map/ppermute | solution.py:431
  162.0 13.8 %collective-permute-start.11 = (bf16[32,128,128]{2,1,0:T(8,128)(2,1)S(1)}, bf16[32,128,128]{2,1,0:T(8,128)(2,1)S(1)}, u32[]{:S(2)}, u32[]{:S(2)}) collective-permute-start(bf16[32,128,128]{2,1,0:T(8,128)(2,1)S(1)} %constant_dynamic-update-slice_fusion.refs_0_.own_ref), channel_id=1, source_target_pairs={{0,8},{8,0},{16,24},{24,16},{1,9},{9,1},{17,25},{25,17},{2,10},{10... | collective-permute-start | bytes 3145736 | tf_op jit(solution)/shard_map/ppermute | solution.py:431
  167.5 16.8 %collective-permute-start.37 = (bf16[32,128,128]{2,1,0:T(8,128)(2,1)S(1)}, bf16[32,128,128]{2,1,0:T(8,128)(2,1)S(1)}, u32[]{:S(2)}, u32[]{:S(2)}) collective-permute-start(bf16[32,128,128]{2,1,0:T(8,128)(2,1)S(1)} %constant_dynamic-update-slice_fusion.12.refs_0_.own_ref), channel_id=1, source_target_pairs={{0,8},{8,0},{16,24},{24,16},{1,9},{9,1},{17,25},{25,17},{2,10},{10... | collective-permute-start | bytes 3145736 | tf_op jit(solution)/shard_map/ppermute | solution.py:431
  175.2 20.3 %collective-permute-start.44 = (f32[128,1024]{1,0:T(8,128)S(1)}, f32[128,1024]{1,0:T(8,128)}, u32[]{:S(2)}, u32[]{:S(2)}) collective-permute-start(f32[128,1024]{1,0:T(8,128)S(1)} %shard_map.150), channel_id=1, source_target_pairs={{0,8},{8,0},{16,24},{24,16},{1,9},{9,1},{17,25},{25,17},{2,10},{10... | collective-permute-start | bytes 1572872 | tf_op jit(solution)/shard_map/ppermute | solution.py:431
  184.2 11.4 %collective-permute-start.39 = (f32[128,1024]{1,0:T(8,128)}, f32[128,1024]{1,0:T(8,128)}, u32[]{:S(2)}, u32[]{:S(2)}) collective-permute-start(f32[128,1024]{1,0:T(8,128)} %shard_map.147), channel_id=1, source_target_pairs={{0,8},{8,0},{16,24},{24,16},{1,9},{9,1},{17,25},{25,17},{2,10},{10... | collective-permute-start | bytes 1572872 | tf_op jit(solution)/shard_map/ppermute | solution.py:431
  202.3 26.3 %collective-permute-start.45 = (bf16[16,128,128]{2,1,0:T(8,128)(2,1)S(1)}, bf16[16,128,128]{2,1,0:T(8,128)(2,1)S(1)}, u32[]{:S(2)}, u32[]{:S(2)}) collective-permute-start(bf16[16,128,128]{2,1,0:T(8,128)(2,1)S(1)} %shard_map.152), channel_id=1, source_target_pairs={{0,1},{1,0},{2,3},{3,2},{4,5},{5,4},{6,7},{7,6},{8,9},{9,8},{10,11... | collective-permute-start | bytes 1572872 | tf_op jit(solution)/shard_map/ppermute | solution.py:431
  208.0 25.1 %collective-permute-start.50 = (bf16[16,128,128]{2,1,0:T(8,128)(2,1)S(1)}, bf16[16,128,128]{2,1,0:T(8,128)(2,1)S(1)}, u32[]{:S(2)}, u32[]{:S(2)}) collective-permute-start(bf16[16,128,128]{2,1,0:T(8,128)(2,1)S(1)} %shard_map.155), channel_id=1, source_target_pairs={{0,1},{1,0},{2,3},{3,2},{4,5},{5,4},{6,7},{7,6},{8,9},{9,8},{10,11... | collective-permute-start | bytes 1572872 | tf_op jit(solution)/shard_map/ppermute | solution.py:431
  213.7 25.1 %collective-permute-start.40 = (bf16[16,128,128]{2,1,0:T(8,128)(2,1)S(1)}, bf16[16,128,128]{2,1,0:T(8,128)(2,1)S(1)}, u32[]{:S(2)}, u32[]{:S(2)}) collective-permute-start(bf16[16,128,128]{2,1,0:T(8,128)(2,1)S(1)} %shard_map.149), channel_id=1, source_target_pairs={{0,1},{1,0},{2,3},{3,2},{4,5},{5,4},{6,7},{7,6},{8,9},{9,8},{10,11... | collective-permute-start | bytes 1572872 | tf_op jit(solution)/shard_map/ppermute | solution.py:431
  229.5 13.0 %collective-permute-start.47 = (bf16[4,128,128]{2,1,0:T(8,128)(2,1)S(1)}, bf16[4,128,128]{2,1,0:T(8,128)(2,1)S(1)}, u32[]{:S(2)}, u32[]{:S(2)}) collective-permute-start(bf16[4,128,128]{2,1,0:T(8,128)(2,1)S(1)} %get-tuple-element.23), channel_id=1, source_target_pairs={{0,4},{1,5},{2,6},{3,7},{4,0},{5,1},{6,2},{7,3},{8,12},{9,13},{10,... | collective-permute-start | bytes 393224 | tf_op jit(solution)/shard_map/ppermute | solution.py:431
  233.3 18.1 %collective-permute-start.51 = (bf16[4,128,128]{2,1,0:T(8,128)(2,1)S(1)}, bf16[4,128,128]{2,1,0:T(8,128)(2,1)S(1)}, u32[]{:S(2)}, u32[]{:S(2)}) collective-permute-start(bf16[4,128,128]{2,1,0:T(8,128)(2,1)S(1)} %get-tuple-element.24), channel_id=1, source_target_pairs={{0,2},{1,3},{2,0},{3,1},{4,6},{5,7},{6,4},{7,5},{8,10},{9,11},{10,... | collective-permute-start | bytes 393224 | tf_op jit(solution)/shard_map/ppermute | solution.py:431
  238.7 19.9 %collective-permute-start.52 = (bf16[4,128,128]{2,1,0:T(8,128)(2,1)S(1)}, bf16[4,128,128]{2,1,0:T(8,128)(2,1)S(1)}, u32[]{:S(2)}, u32[]{:S(2)}) collective-permute-start(bf16[4,128,128]{2,1,0:T(8,128)(2,1)S(1)} %get-tuple-element.26), channel_id=1, source_target_pairs={{0,4},{1,5},{2,6},{3,7},{4,0},{5,1},{6,2},{7,3},{8,12},{9,13},{10,... | collective-permute-start | bytes 393224 | tf_op jit(solution)/shard_map/ppermute | solution.py:431
  239.6 19.0 %collective-permute-start.53 = (bf16[4,128,128]{2,1,0:T(8,128)(2,1)S(1)}, bf16[4,128,128]{2,1,0:T(8,128)(2,1)S(1)}, u32[]{:S(2)}, u32[]{:S(2)}) collective-permute-start(bf16[4,128,128]{2,1,0:T(8,128)(2,1)S(1)} %get-tuple-element.25), channel_id=1, source_target_pairs={{0,6},{1,7},{2,4},{3,5},{4,2},{5,3},{6,0},{7,1},{8,14},{9,15},{10,... | collective-permute-start | bytes 393224 | tf_op jit(solution)/shard_map/ppermute | solution.py:431
  242.5 21.2 %collective-permute-start.41 = (bf16[4,128,128]{2,1,0:T(8,128)(2,1)S(1)}, bf16[4,128,128]{2,1,0:T(8,128)(2,1)S(1)}, u32[]{:S(2)}, u32[]{:S(2)}) collective-permute-start(bf16[4,128,128]{2,1,0:T(8,128)(2,1)S(1)} %get-tuple-element.18), channel_id=1, source_target_pairs={{0,2},{1,3},{2,0},{3,1},{4,6},{5,7},{6,4},{7,5},{8,10},{9,11},{10,... | collective-permute-start | bytes 393224 | tf_op jit(solution)/shard_map/ppermute | solution.py:431
  242.5 25.9 %collective-permute-start.42 = (bf16[4,128,128]{2,1,0:T(8,128)(2,1)S(1)}, bf16[4,128,128]{2,1,0:T(8,128)(2,1)S(1)}, u32[]{:S(2)}, u32[]{:S(2)}) collective-permute-start(bf16[4,128,128]{2,1,0:T(8,128)(2,1)S(1)} %get-tuple-element.20), channel_id=1, source_target_pairs={{0,4},{1,5},{2,6},{3,7},{4,0},{5,1},{6,2},{7,3},{8,12},{9,13},{10,... | collective-permute-start | bytes 393224 | tf_op jit(solution)/shard_map/ppermute | solution.py:431
  251.4 19.8 %collective-permute-start.43 = (bf16[4,128,128]{2,1,0:T(8,128)(2,1)S(1)}, bf16[4,128,128]{2,1,0:T(8,128)(2,1)S(1)}, u32[]{:S(2)}, u32[]{:S(2)}) collective-permute-start(bf16[4,128,128]{2,1,0:T(8,128)(2,1)S(1)} %get-tuple-element.19), channel_id=1, source_target_pairs={{0,6},{1,7},{2,4},{3,5},{4,2},{5,3},{6,0},{7,1},{8,14},{9,15},{10,... | collective-permute-start | bytes 393224 | tf_op jit(solution)/shard_map/ppermute | solution.py:431
  258.6 16.1 %collective-permute-start.65 = (bf16[4,128,128]{2,1,0:T(8,128)(2,1)S(1)}, bf16[4,128,128]{2,1,0:T(8,128)(2,1)S(1)}, u32[]{:S(2)}, u32[]{:S(2)}) collective-permute-start(bf16[4,128,128]{2,1,0:T(8,128)(2,1)S(1)} %get-tuple-element.12), channel_id=1, source_target_pairs={{0,2},{1,3},{2,0},{3,1},{4,6},{5,7},{6,4},{7,5},{8,10},{9,11},{10,... | collective-permute-start | bytes 393224 | tf_op jit(solution)/shard_map/ppermute | solution.py:431
  258.6 18.3 %collective-permute-start.66 = (bf16[4,128,128]{2,1,0:T(8,128)(2,1)S(1)}, bf16[4,128,128]{2,1,0:T(8,128)(2,1)S(1)}, u32[]{:S(2)}, u32[]{:S(2)}) collective-permute-start(bf16[4,128,128]{2,1,0:T(8,128)(2,1)S(1)} %get-tuple-element.12), channel_id=1, source_target_pairs={{0,4},{1,5},{2,6},{3,7},{4,0},{5,1},{6,2},{7,3},{8,12},{9,13},{10,... | collective-permute-start | bytes 393224 | tf_op jit(solution)/shard_map/ppermute | solution.py:431
  263.7 14.9 %collective-permute-start.67 = (bf16[4,128,128]{2,1,0:T(8,128)(2,1)S(1)}, bf16[4,128,128]{2,1,0:T(8,128)(2,1)S(1)}, u32[]{:S(2)}, u32[]{:S(2)}) collective-permute-start(bf16[4,128,128]{2,1,0:T(8,128)(2,1)S(1)} %get-tuple-element.12), channel_id=1, source_target_pairs={{0,6},{1,7},{2,4},{3,5},{4,2},{5,3},{6,0},{7,1},{8,14},{9,15},{10,... | collective-permute-start | bytes 393224 | tf_op jit(solution)/shard_map/ppermute | solution.py:431
  268.4 31.7 %collective-permute-start.68 = (bf16[4,128,128]{2,1,0:T(8,128)(2,1)S(1)}, bf16[4,128,128]{2,1,0:T(8,128)(2,1)S(1)}, u32[]{:S(2)}, u32[]{:S(2)}) collective-permute-start(bf16[4,128,128]{2,1,0:T(8,128)(2,1)S(1)} %get-tuple-element.12), channel_id=1, source_target_pairs={{0,1},{1,0},{2,3},{3,2},{4,5},{5,4},{6,7},{7,6},{8,9},{9,8},{10,11... | collective-permute-start | bytes 393224 | tf_op jit(solution)/shard_map/ppermute | solution.py:431
  274.7 14.8 %collective-permute-start.77 = (bf16[4,128,128]{2,1,0:T(8,128)(2,1)S(1)}, bf16[4,128,128]{2,1,0:T(8,128)(2,1)S(1)}, u32[]{:S(2)}, u32[]{:S(2)}) collective-permute-start(bf16[4,128,128]{2,1,0:T(8,128)(2,1)S(1)} %get-tuple-element.14), channel_id=1, source_target_pairs={{0,4},{1,5},{2,6},{3,7},{4,0},{5,1},{6,2},{7,3},{8,12},{9,13},{10,... | collective-permute-start | bytes 393224 | tf_op jit(solution)/shard_map/ppermute | solution.py:431
  277.0 12.6 %collective-permute-start.78 = (bf16[4,128,128]{2,1,0:T(8,128)(2,1)S(1)}, bf16[4,128,128]{2,1,0:T(8,128)(2,1)S(1)}, u32[]{:S(2)}, u32[]{:S(2)}) collective-permute-start(bf16[4,128,128]{2,1,0:T(8,128)(2,1)S(1)} %get-tuple-element.14), channel_id=1, source_target_pairs={{0,6},{1,7},{2,4},{3,5},{4,2},{5,3},{6,0},{7,1},{8,14},{9,15},{10,... | collective-permute-start | bytes 393224 | tf_op jit(solution)/shard_map/ppermute | solution.py:431
  278.6 22.9 %collective-permute-start.79 = (bf16[4,128,128]{2,1,0:T(8,128)(2,1)S(1)}, bf16[4,128,128]{2,1,0:T(8,128)(2,1)S(1)}, u32[]{:S(2)}, u32[]{:S(2)}) collective-permute-start(bf16[4,128,128]{2,1,0:T(8,128)(2,1)S(1)} %get-tuple-element.14), channel_id=1, source_target_pairs={{0,1},{1,0},{2,3},{3,2},{4,5},{5,4},{6,7},{7,6},{8,9},{9,8},{10,11... | collective-permute-start | bytes 393224 | tf_op jit(solution)/shard_map/ppermute | solution.py:431
  280.3 11.3 %collective-permute-start.54 = (bf16[4,128,128]{2,1,0:T(8,128)(2,1)S(1)}, bf16[4,128,128]{2,1,0:T(8,128)(2,1)S(1)}, u32[]{:S(2)}, u32[]{:S(2)}) collective-permute-start(bf16[4,128,128]{2,1,0:T(8,128)(2,1)S(1)} %get-tuple-element.10), channel_id=1, source_target_pairs={{0,2},{1,3},{2,0},{3,1},{4,6},{5,7},{6,4},{7,5},{8,10},{9,11},{10,... | collective-permute-start | bytes 393224 | tf_op jit(solution)/shard_map/ppermute | solution.py:431
  297.9 12.1 %collective-permute-start.69 = (bf16[12,128,128]{2,1,0:T(8,128)(2,1)S(1)}, bf16[12,128,128]{2,1,0:T(8,128)(2,1)S(1)}, u32[]{:S(2)}, u32[]{:S(2)}) collective-permute-start(bf16[12,128,128]{2,1,0:T(8,128)(2,1)S(1)} %pad_maximum_fusion.6), channel_id=1, source_target_pairs={{0,1},{1,0},{2,3},{3,2},{4,5},{5,4},{6,7},{7,6},{8,9},{9,8},{10,11... | collective-permute-start | bytes 1179656 | tf_op jit(solution)/shard_map/ppermute | solution.py:431
  299.2 19.2 %collective-permute-start.80 = (bf16[12,128,128]{2,1,0:T(8,128)(2,1)S(1)}, bf16[12,128,128]{2,1,0:T(8,128)(2,1)S(1)}, u32[]{:S(2)}, u32[]{:S(2)}) collective-permute-start(bf16[12,128,128]{2,1,0:T(8,128)(2,1)S(1)} %pad_maximum_fusion.7), channel_id=1, source_target_pairs={{0,1},{1,0},{2,3},{3,2},{4,5},{5,4},{6,7},{7,6},{8,9},{9,8},{10,11... | collective-permute-start | bytes 1179656 | tf_op jit(solution)/shard_map/ppermute | solution.py:431
  300.1 22.9 %collective-permute-start.58 = (bf16[12,128,128]{2,1,0:T(8,128)(2,1)S(1)}, bf16[12,128,128]{2,1,0:T(8,128)(2,1)S(1)}, u32[]{:S(2)}, u32[]{:S(2)}) collective-permute-start(bf16[12,128,128]{2,1,0:T(8,128)(2,1)S(1)} %pad_maximum_fusion.5), channel_id=1, source_target_pairs={{0,1},{1,0},{2,3},{3,2},{4,5},{5,4},{6,7},{7,6},{8,9},{9,8},{10,11... | collective-permute-start | bytes 1179656 | tf_op jit(solution)/shard_map/ppermute | solution.py:431
  310.1 15.8 %collective-permute-start.70 = (bf16[32,128,128]{2,1,0:T(8,128)(2,1)S(1)}, bf16[32,128,128]{2,1,0:T(8,128)(2,1)S(1)}, u32[]{:S(2)}, u32[]{:S(2)}) collective-permute-start(bf16[32,128,128]{2,1,0:T(8,128)(2,1)S(1)} %constant_dynamic-update-slice_fusion.24.refs_0_.refs_3_), channel_id=1, source_target_pairs={{0,8},{8,0},{16,24},{24,16},{1,9},{9,1},{17,25},{25,17},{2,10},{10... | collective-permute-start | bytes 3145736 | tf_op jit(solution)/shard_map/ppermute | solution.py:431
  318.5 14.0 %collective-permute-start.81 = (bf16[32,128,128]{2,1,0:T(8,128)(2,1)S(1)}, bf16[32,128,128]{2,1,0:T(8,128)(2,1)S(1)}, u32[]{:S(2)}, u32[]{:S(2)}) collective-permute-start(bf16[32,128,128]{2,1,0:T(8,128)(2,1)S(1)} %constant_dynamic-update-slice_fusion.30.refs_0_.refs_3_), channel_id=1, source_target_pairs={{0,8},{8,0},{16,24},{24,16},{1,9},{9,1},{17,25},{25,17},{2,10},{10... | collective-permute-start | bytes 3145736 | tf_op jit(solution)/shard_map/ppermute | solution.py:431
  323.1 11.9 %collective-permute-start.59 = (bf16[32,128,128]{2,1,0:T(8,128)(2,1)S(1)}, bf16[32,128,128]{2,1,0:T(8,128)(2,1)S(1)}, u32[]{:S(2)}, u32[]{:S(2)}) collective-permute-start(bf16[32,128,128]{2,1,0:T(8,128)(2,1)S(1)} %constant_dynamic-update-slice_fusion.18.refs_0_.refs_3_), channel_id=1, source_target_pairs={{0,8},{8,0},{16,24},{24,16},{1,9},{9,1},{17,25},{25,17},{2,10},{10... | collective-permute-start | bytes 3145736 | tf_op jit(solution)/shard_map/ppermute | solution.py:431
  324.8 16.2 %collective-permute-start.25 = (bf16[16,128,128]{2,1,0:T(8,128)(2,1)}, bf16[16,128,128]{2,1,0:T(8,128)(2,1)S(1)}, u32[]{:S(2)}, u32[]{:S(2)}) collective-permute-start(bf16[16,128,128]{2,1,0:T(8,128)(2,1)} %shard_map.140), channel_id=1, source_target_pairs={{0,16},{8,24},{16,0},{24,8},{1,17},{9,25},{17,1},{25,9},{2,18},{10... | collective-permute-start | bytes 1572872 | tf_op jit(solution)/shard_map/ppermute | solution.py:431
  327.3 20.8 %collective-permute-start.71 = (bf16[12,128,128]{2,1,0:T(8,128)(2,1)}, bf16[12,128,128]{2,1,0:T(8,128)(2,1)S(1)}, u32[]{:S(2)}, u32[]{:S(2)}) collective-permute-start(bf16[12,128,128]{2,1,0:T(8,128)(2,1)} %shard_map.162), channel_id=1, source_target_pairs={{0,16},{8,24},{16,0},{24,8},{1,17},{9,25},{17,1},{25,9},{2,18},{10... | collective-permute-start | bytes 1179656 | tf_op jit(solution)/shard_map/ppermute | solution.py:431
  329.9 29.9 %collective-permute-start.38 = (bf16[16,128,128]{2,1,0:T(8,128)(2,1)}, bf16[16,128,128]{2,1,0:T(8,128)(2,1)}, u32[]{:S(2)}, u32[]{:S(2)}) collective-permute-start(bf16[16,128,128]{2,1,0:T(8,128)(2,1)} %shard_map.145), channel_id=1, source_target_pairs={{0,16},{8,24},{16,0},{24,8},{1,17},{9,25},{17,1},{25,9},{2,18},{10... | collective-permute-start | bytes 1572872 | tf_op jit(solution)/shard_map/ppermute | solution.py:431
  332.5 53.7 %collective-permute-start.12 = (bf16[16,128,128]{2,1,0:T(8,128)(2,1)}, bf16[16,128,128]{2,1,0:T(8,128)(2,1)}, u32[]{:S(2)}, u32[]{:S(2)}) collective-permute-start(bf16[16,128,128]{2,1,0:T(8,128)(2,1)} %shard_map.135), channel_id=1, source_target_pairs={{0,16},{8,24},{16,0},{24,8},{1,17},{9,25},{17,1},{25,9},{2,18},{10... | collective-permute-start | bytes 1572872 | tf_op jit(solution)/shard_map/ppermute | solution.py:431
  335.9 43.2 %collective-permute-start.82 = (bf16[12,128,128]{2,1,0:T(8,128)(2,1)}, bf16[12,128,128]{2,1,0:T(8,128)(2,1)}, u32[]{:S(2)}, u32[]{:S(2)}) collective-permute-start(bf16[12,128,128]{2,1,0:T(8,128)(2,1)} %shard_map.168), channel_id=1, source_target_pairs={{0,16},{8,24},{16,0},{24,8},{1,17},{9,25},{17,1},{25,9},{2,18},{10... | collective-permute-start | bytes 1179656 | tf_op jit(solution)/shard_map/ppermute | solution.py:431
  340.9 46.2 %collective-permute-start.60 = (bf16[12,128,128]{2,1,0:T(8,128)(2,1)}, bf16[12,128,128]{2,1,0:T(8,128)(2,1)}, u32[]{:S(2)}, u32[]{:S(2)}) collective-permute-start(bf16[12,128,128]{2,1,0:T(8,128)(2,1)} %shard_map.156), channel_id=1, source_target_pairs={{0,16},{8,24},{16,0},{24,8},{1,17},{9,25},{17,1},{25,9},{2,18},{10... | collective-permute-start | bytes 1179656 | tf_op jit(solution)/shard_map/ppermute | solution.py:431
  359.7 47.3 %collective-permute-start.72 = (bf16[2,128,1024]{2,1,0:T(8,128)(2,1)}, bf16[2,128,1024]{2,1,0:T(8,128)(2,1)}, u32[]{:S(2)}, u32[]{:S(2)}) collective-permute-start(bf16[2,128,1024]{2,1,0:T(8,128)(2,1)} %shard_map.165), channel_id=1, source_target_pairs={{0,8},{8,0},{16,24},{24,16},{1,9},{9,1},{17,25},{25,17},{2,10},{10... | collective-permute-start | bytes 1572872 | tf_op jit(solution)/shard_map/ppermute | solution.py:431
  386.2 23.9 %collective-permute-start.83 = (bf16[2,128,1024]{2,1,0:T(8,128)(2,1)}, bf16[2,128,1024]{2,1,0:T(8,128)(2,1)}, u32[]{:S(2)}, u32[]{:S(2)}) collective-permute-start(bf16[2,128,1024]{2,1,0:T(8,128)(2,1)} %shard_map.171), channel_id=1, source_target_pairs={{0,8},{8,0},{16,24},{24,16},{1,9},{9,1},{17,25},{25,17},{2,10},{10... | collective-permute-start | bytes 1572872 | tf_op jit(solution)/shard_map/ppermute | solution.py:431
  412.1 12.0 %collective-permute-start.84 = (bf16[128,1024]{1,0:T(8,128)(2,1)}, bf16[128,1024]{1,0:T(8,128)(2,1)}, u32[]{:S(2)}, u32[]{:S(2)}) collective-permute-start(bf16[128,1024]{1,0:T(8,128)(2,1)} %fusion.21), channel_id=1, source_target_pairs={{0,16},{8,24},{16,0},{24,8},{1,17},{9,25},{17,1},{25,9},{2,18},{10... | collective-permute-start | bytes 786440 | tf_op jit(solution)/shard_map/ppermute | solution.py:431
  414.3 14.9 %collective-permute-start.62 = (bf16[128,1024]{1,0:T(8,128)(2,1)S(1)}, bf16[128,1024]{1,0:T(8,128)(2,1)S(1)}, u32[]{:S(2)}, u32[]{:S(2)}) collective-permute-start(bf16[128,1024]{1,0:T(8,128)(2,1)S(1)} %fusion.15), channel_id=1, source_target_pairs={{0,16},{8,24},{16,0},{24,8},{1,17},{9,25},{17,1},{25,9},{2,18},{10... | collective-permute-start | bytes 786440 | tf_op jit(solution)/shard_map/ppermute | solution.py:431
  436.7 29.6 %collective-permute-start.63 = (bf16[2,128,1024]{2,1,0:T(8,128)(2,1)}, bf16[2,128,1024]{2,1,0:T(8,128)(2,1)}, u32[]{:S(2)}, u32[]{:S(2)}) collective-permute-start(bf16[2,128,1024]{2,1,0:T(8,128)(2,1)} %shard_map.161), channel_id=1, source_target_pairs={{0,8},{8,0},{16,24},{24,16},{1,9},{9,1},{17,25},{25,17},{2,10},{10... | collective-permute-start | bytes 1572872 | tf_op jit(solution)/shard_map/ppermute | solution.py:431
  450.3 18.3 %collective-permute-start.74 = (bf16[2,128,1024]{2,1,0:T(8,128)(2,1)S(1)}, bf16[2,128,1024]{2,1,0:T(8,128)(2,1)S(1)}, u32[]{:S(2)}, u32[]{:S(2)}) collective-permute-start(bf16[2,128,1024]{2,1,0:T(8,128)(2,1)S(1)} %shard_map.167), channel_id=1, source_target_pairs={{0,8},{8,0},{16,24},{24,16},{1,9},{9,1},{17,25},{25,17},{2,10},{10... | collective-permute-start | bytes 1572872 | tf_op jit(solution)/shard_map/ppermute | solution.py:431
  468.9 13.5 %collective-permute-start.75 = (bf16[128,1024]{1,0:T(8,128)(2,1)S(1)}, bf16[128,1024]{1,0:T(8,128)(2,1)S(1)}, u32[]{:S(2)}, u32[]{:S(2)}) collective-permute-start(bf16[128,1024]{1,0:T(8,128)(2,1)S(1)} %fusion.20), channel_id=1, source_target_pairs={{0,16},{8,24},{16,0},{24,8},{1,17},{9,25},{17,1},{25,9},{2,18},{10... | collective-permute-start | bytes 786440 | tf_op jit(solution)/shard_map/ppermute | solution.py:431
  470.1 17.4 %collective-permute-start.86 = (bf16[128,1024]{1,0:T(8,128)(2,1)S(1)}, bf16[128,1024]{1,0:T(8,128)(2,1)S(1)}, u32[]{:S(2)}, u32[]{:S(2)}) collective-permute-start(bf16[128,1024]{1,0:T(8,128)(2,1)S(1)} %fusion.23), channel_id=1, source_target_pairs={{0,16},{8,24},{16,0},{24,8},{1,17},{9,25},{17,1},{25,9},{2,18},{10... | collective-permute-start | bytes 786440 | tf_op jit(solution)/shard_map/ppermute | solution.py:431
  (74 other events, 815.2 us)

commit v2 on v1

v2 whole, which is shorter than its diff:
```python
import functools

import jax
import jax.numpy as jnp
from jax import lax
from jax.experimental import pallas as pl
from jax.experimental.pallas import tpu as pltpu
from jax.sharding import PartitionSpec as P

BLOCK = 128
F32 = jnp.float32
BF16 = jnp.bfloat16
NT = (((1,), (1,)), ((), ()))
NN = (((1,), (0,)), ((), ()))


def partner(value, axis, distance):
    mask = 2**distance
    pairs = [(source, source ^ mask) for source in range(lax.axis_size(axis))]
    return lax.ppermute(value, axis, pairs)


def pick_blocks(shard_rows, wanted):
    block_count = shard_rows.shape[0] // BLOCK
    flat_blocks = shard_rows.reshape(block_count, BLOCK * shard_rows.shape[1])
    present = jnp.arange(block_count, dtype=jnp.int32)
    select = (wanted[:, None] == present[None, :]).astype(shard_rows.dtype)
    return jnp.dot(select, flat_blocks, preferred_element_type=F32)


def transposed_product(coupling, boundary):
    return lax.dot_general(coupling, boundary, (((0,), (0,)), ((), ())), preferred_element_type=F32)


def general_shards(
    dinv_root,
    rhs_root,
    dinv_mid,
    coup_mid,
    rhs_mid,
    dinv_leaf,
    coup_leaf,
    rhs_leaf,
    bounds_mid,
    bounds_leaf,
    parents,
):
    row_total = lax.axis_size("row")
    row_id = lax.axis_index("row")
    col_id = lax.axis_index("col")
    rhs_width = rhs_root.shape[1]
    root_total = dinv_root.shape[0] * row_total // BLOCK
    front_mid = row_id // 2
    half_index = row_id % 2
    half_blocks = bounds_mid.shape[1] // 2
    mid_all = lax.dynamic_slice_in_dim(bounds_mid, front_mid, 1, 0)[0]
    mid_list = lax.dynamic_slice_in_dim(mid_all, half_index * half_blocks, half_blocks, 0)
    leaf_all = lax.dynamic_slice_in_dim(bounds_leaf, col_id, 1, 0)[0]
    leaf_slots = leaf_all.shape[0] // row_total
    leaf_list = lax.dynamic_slice_in_dim(leaf_all, row_id * leaf_slots, leaf_slots, 0)
    wanted = jnp.concatenate([mid_list, leaf_list])
    root_values = lax.psum_scatter(
        jnp.dot(dinv_root, rhs_root, preferred_element_type=F32),
        "col",
        scatter_dimension=0,
        tiled=True,
    ).astype(BF16)
    picked = pick_blocks(lax.all_gather(root_values, ("row", "col"), axis=0, tiled=True), wanted)
    bound_mid = picked[:half_blocks].reshape(half_blocks * BLOCK, rhs_width).astype(BF16)
    root_side = picked[half_blocks:]
    mid_part = transposed_product(coup_mid, bound_mid)
    mid_terms = mid_part + partner(mid_part, "row", 0)
    rhs_here = lax.dynamic_slice_in_dim(rhs_mid, front_mid, 1, 0)[0]
    shift_mid = (rhs_here - mid_terms).astype(BF16)
    mid_values = lax.psum_scatter(
        jnp.dot(dinv_mid, shift_mid, preferred_element_type=F32),
        "col",
        scatter_dimension=0,
        tiled=True,
    ).astype(BF16)
    half_rows = lax.all_gather(mid_values, "col", axis=0, tiled=True)
    half_count = half_rows.shape[0] // BLOCK
    half_flat = half_rows.reshape(half_count, BLOCK * rhs_width)
    local_ids = leaf_all - root_total - half_index * half_count
    owns_parent = lax.dynamic_slice_in_dim(parents, col_id, 1, 0)[0] == front_mid
    choose = (
        (local_ids[:, None] == jnp.arange(half_count, dtype=jnp.int32)[None, :]) & owns_parent
    ).astype(BF16)
    from_parent = lax.psum_scatter(
        jnp.dot(choose, half_flat, preferred_element_type=F32).astype(BF16),
        "row",
        scatter_dimension=0,
        tiled=True,
    ).astype(F32)
    bound_leaf = (root_side + from_parent).reshape(leaf_slots * BLOCK, rhs_width).astype(BF16)
    leaf_sum = lax.psum_scatter(
        transposed_product(coup_leaf[0], bound_leaf), "row", scatter_dimension=0, tiled=True
    )
    shift_leaf = (rhs_leaf[0] - leaf_sum).astype(BF16)
    leaf_values = lax.psum_scatter(
        jnp.dot(dinv_leaf[0], shift_leaf, preferred_element_type=F32),
        "row",
        scatter_dimension=0,
        tiled=True,
    ).astype(BF16)
    return (root_values, mid_values, leaf_values[None])


SMEM = pl.BlockSpec(memory_space=pltpu.SMEM)
VMEM = pl.BlockSpec(memory_space=pltpu.VMEM)
ANY = pl.BlockSpec(memory_space=pl.ANY)
LIMIT = 48 * 1024 * 1024
CHAINS = ((1, 2, 4), (2, 1, 4))


def params():
    return pltpu.CompilerParams(vmem_limit_bytes=LIMIT)


def cost(rows, depth, width):
    return pl.CostEstimate(flops=2 * rows * depth * width, bytes_accessed=2 * rows * depth, transcendentals=0)


def loop(count, body):
    def step(i, carry):
        body(i)
        return carry

    lax.fori_loop(0, count, step, 0)


def place_of(chip, col, bits, slot):
    far = chip ^ col
    high, mid, low = (((far & bit) != 0).astype(jnp.int32) for bit in bits)
    return (4 * high + 2 * mid + low) * slot


def chips_in_order(col, bits):
    return [col ^ sum(bit for bit, shift in zip(bits, (4, 2, 1)) if t & shift) for t in range(8)]


def mark_fronts(bounds_ref, front):
    def body(j):
        front[bounds_ref[0, j]] = 0
        front[bounds_ref[1, j]] = 1

    loop(bounds_ref.shape[1], body)


def order_kernel(local, slot, place_ref, bounds_ref, out_ref, front):
    row, col = place_ref[0], place_ref[1]
    first = row * local
    mark_fronts(bounds_ref, front)
    before = lax.fori_loop(0, first, lambda v, s: s + 1 - front[v], jnp.int32(0))
    zeros = lax.fori_loop(0, local, lambda i, s: s + 1 - front[first + i], jnp.int32(0))

    def body(i, carry):
        low, high = carry
        kind = front[first + i]
        rank = jnp.where(kind == 0, low, zeros + high)
        out_ref[place_of((before + rank) & 7, col, CHAINS[0], slot) + (rank >> 3)] = i
        return low + 1 - kind, high + kind

    lax.fori_loop(0, local, body, (jnp.int32(0), jnp.int32(0)))


def plan_layout(local, slot, leaf_slots):
    at = {}
    size = 0
    for name, count in (
        ("select", slot),
        ("mid", local),
        ("send_root", leaf_slots + slot),
        ("leaf", leaf_slots),
        ("out", slot),
        ("send_mid", leaf_slots),
    ):
        at[name] = size
        size += count
    at["size"] = size
    at["mid_base"] = 2 * local + leaf_slots + slot
    return at


def plan_kernel(local, slot, leaf_slots, place_ref, bounds_ref, leaf_ref, parents_ref, out_ref, front, ident, where):
    row, col = place_ref[0], place_ref[1]
    x, h = row // 2, row % 2
    total = 4 * local
    mark_fronts(bounds_ref, front)
    chains = range(len(CHAINS))
    at = plan_layout(local, slot, leaf_slots)

    def per_row(r, before):
        zeros = lax.fori_loop(0, local, lambda i, s: s + 1 - front[r * local + i], jnp.int32(0))

        def body(i, carry):
            low, high = carry
            kind = front[r * local + i]
            rank = jnp.where(kind == 0, low, zeros + high)
            chip = (before + rank) & 7
            ident[r * local + chip * slot + (rank >> 3)] = r * local + i
            return low + 1 - kind, high + kind

        lax.fori_loop(0, local, body, (jnp.int32(0), jnp.int32(0)))
        return before + zeros

    lax.fori_loop(0, 4, per_row, jnp.int32(0))

    def clear(v):
        for n in chains:
            where[n, v] = 0

    loop(total, clear)

    def per_chip(chip, _):
        here = chip == col
        near = [place_of(chip, col, bits, slot) for bits in CHAINS]

        def put(core, count, block, code):
            for n in chains:
                where[n, block] = (core ^ h) * local + near[n] + count

            @pl.when(here & (core == h))
            def _():
                for n in chains:
                    out_ref[n, count] = code

        def from_far(step, carry):
            count0, count1 = carry
            core, k = step // slot, step % slot
            block = ident[(2 * (1 - x) + core) * local + chip * slot + k]
            taken = front[block] == x
            count = jnp.where(core == 0, count0, count1)

            @pl.when(taken)
            def _():
                put(core, count, block, 2 * slot + k)

            add = taken.astype(jnp.int32)
            return count0 + jnp.where(core == 0, add, 0), count1 + jnp.where(core == 0, 0, add)

        counts = lax.fori_loop(0, 2 * slot, from_far, (jnp.int32(0), jnp.int32(0)))

        def from_near(step, carry):
            count0, count1 = carry
            owner, k = step // slot, step % slot
            block = ident[(2 * x + owner) * local + chip * slot + k]
            taken = front[block] == x
            core = (count0 >= slot).astype(jnp.int32)
            count = jnp.where(core == 0, count0, count1)

            @pl.when(taken)
            def _():
                put(core, count, block, (owner ^ core) * slot + k)

            add = taken.astype(jnp.int32)
            return count0 + jnp.where(core == 0, add, 0), count1 + jnp.where(core == 0, 0, add)

        lax.fori_loop(0, 2 * slot, from_near, counts)
        return 0

    lax.fori_loop(0, 8, per_chip, 0)

    def mid_place(block, bits):
        inner = block % local
        return ((block // local) ^ h) * local + place_of(inner // slot, col, bits, slot) + inner % slot

    def mid_list(j):
        block = bounds_ref[x, h * local + j]
        for n in chains:
            out_ref[n, at["mid"] + j] = where[n, block]

    loop(local, mid_list)
    far = 2 * (1 - x) + h
    owner = parents_ref[col] == x

    def lists(j):
        asked = leaf_ref[col, far * leaf_slots + j]
        held = leaf_ref[col, row * leaf_slots + j]
        low = jnp.minimum(held, total - 1)
        for n in chains:
            bits = CHAINS[n]
            out_ref[n, at["send_root"] + j] = where[n, jnp.minimum(asked, total - 1)]
            out_ref[n, at["send_mid"] + j] = mid_place(jnp.maximum(asked - total, 0), bits)
            from_root = jnp.where(front[low] == x, where[n, low], 2 * local + j)
            from_mid = jnp.where(owner, mid_place(jnp.maximum(held - total, 0), bits), 2 * local + j)
            out_ref[n, at["leaf"] + j] = jnp.where(held < total, from_root, from_mid + at["mid_base"])

    loop(leaf_slots, lists)

    def outs(j):
        asked = far * local + col * slot + j
        held = row * local + col * slot + j
        for n in chains:
            out_ref[n, at["send_root"] + leaf_slots + j] = where[n, asked]
            out_ref[n, at["out"] + j] = jnp.where(front[held] == x, where[n, held], 2 * local + leaf_slots + j)

    loop(slot, outs)


def start_fetch(sources, code, target, sem):
    base = 0
    for source in sources:
        count = source.shape[0]

        @pl.when((code >= base) & (code < base + count))
        def _(source=source, base=base):
            pltpu.make_async_copy(source.at[code - base], target, sem).start()

        base += count


def lanes(ref, i):
    return ref.at[:, pl.ds(i * BLOCK, BLOCK)]


def gather_kernel(chain, start, count, wide, table_ref, *refs):
    *sources, out_ref, sems = refs
    targets = [lanes(out_ref, i) if wide else out_ref.at[i] for i in range(count)]
    for i in range(count):
        start_fetch(sources, table_ref[chain, start + i], targets[i], sems.at[i])
    for i in range(count):
        pltpu.make_async_copy(sources[0].at[0], targets[i], sems.at[i]).wait()


def gather(table, chain, start, count, *sources, wide=False):
    width = sources[0].shape[1]
    shape = (width, count * BLOCK) if wide else (count, width, BLOCK)
    return pl.pallas_call(
        functools.partial(gather_kernel, chain, start, count, wide),
        out_shape=jax.ShapeDtypeStruct(shape, BF16),
        in_specs=[SMEM] + [ANY] * len(sources),
        out_specs=VMEM,
        scratch_shapes=[pltpu.SemaphoreType.DMA((count,))],
        compiler_params=params(),
    )(table, *sources)


def root_product_kernel(parts, order_ref, value_ref, *refs):
    blocks, outs = refs[:parts], refs[parts:]
    step = pl.program_id(0)
    matrix = jnp.concatenate([b[...] for b in blocks], axis=0)
    result = lax.dot_general(value_ref[...], matrix, NT, preferred_element_type=F32)
    width = result.shape[0] // 2
    for n, bit in enumerate((2, 1)):
        part = result[n * width : (n + 1) * width]

        def store(ref, part=part):
            for i in range(parts):
                ref[i] = part[:, i * BLOCK : (i + 1) * BLOCK].astype(ref.dtype)

        far = (3 - step) & bit

        @pl.when(far != 0)
        def _(n=n, store=store):
            store(outs[2 * n])

        @pl.when(far == 0)
        def _(n=n, store=store):
            store(outs[2 * n + 1])


def root_product(order, value, matrix):
    width, depth = value.shape
    local = matrix.shape[0] // BLOCK
    parts = local // 4

    def spec(i):
        return pl.BlockSpec((BLOCK, depth), lambda s, order: (order[parts * (3 - s) + i], 0))

    out_specs, out_shape = [], []
    for bit in (2, 1):
        for far in (True, False):
            seen = [s for s in range(4) if bool((3 - s) & bit) == far]
            index = [1 - min(sum(1 for t in seen if t < s), 1) for s in range(4)]

            def block(s, order, index=index):
                picked = functools.reduce(lambda acc, t: jnp.where(s == t, index[t], acc), range(1, 4), index[0])
                return (picked, 0, 0)

            out_specs.append(pl.BlockSpec((parts, width // 2, BLOCK), block))
            out_shape.append(jax.ShapeDtypeStruct((local // 2, width // 2, BLOCK), BF16 if far else F32))
    outs = pl.pallas_call(
        functools.partial(root_product_kernel, parts),
        grid_spec=pltpu.PrefetchScalarGridSpec(
            num_scalar_prefetch=1,
            grid=(4,),
            in_specs=[pl.BlockSpec((width, depth), lambda s, order: (0, 0))] + [spec(i) for i in range(parts)],
            out_specs=out_specs,
        ),
        out_shape=out_shape,
        compiler_params=params(),
        cost_estimate=cost(matrix.shape[0], depth, width),
    )(order, value, *([matrix] * parts))
    return outs[:2], outs[2:]


def mid_product_kernel(parts, order_ref, value_ref, *refs):
    blocks, (send_ref, keep_ref) = refs[:parts], refs[parts:]
    step = pl.program_id(0)
    matrix = jnp.concatenate([b[...] for b in blocks], axis=0)
    result = lax.dot_general(value_ref[...], matrix, NT, preferred_element_type=F32)

    def store(ref):
        for i in range(parts):
            ref[i] = result[:, i * BLOCK : (i + 1) * BLOCK].astype(ref.dtype)

    @pl.when(step < 2)
    def _():
        store(send_ref)

    @pl.when(step >= 2)
    def _():
        store(keep_ref)


def mid_product(order, value, matrix):
    width, depth = value.shape
    local = matrix.shape[0] // BLOCK
    parts = local // 4

    def spec(i):
        return pl.BlockSpec((BLOCK, depth), lambda s, order: (order[parts * ((s + 2) % 4) + i], 0))

    return pl.pallas_call(
        functools.partial(mid_product_kernel, parts),
        grid_spec=pltpu.PrefetchScalarGridSpec(
            num_scalar_prefetch=1,
            grid=(4,),
            in_specs=[pl.BlockSpec((width, depth), lambda s, order: (0, 0))] + [spec(i) for i in range(parts)],
            out_specs=[
                pl.BlockSpec((parts, width, BLOCK), lambda s, order: (jnp.minimum(s, 1), 0, 0)),
                pl.BlockSpec((parts, width, BLOCK), lambda s, order: (jnp.maximum(s - 2, 0), 0, 0)),
            ],
        ),
        out_shape=[
            jax.ShapeDtypeStruct((local // 2, width, BLOCK), BF16),
            jax.ShapeDtypeStruct((local // 2, width, BLOCK), F32),
        ],
        compiler_params=params(),
        cost_estimate=cost(matrix.shape[0], depth, width),
    )(order, value, *([matrix] * parts))


def mid_coupling_kernel(value_ref, coup_ref, out_ref):
    out_ref[...] = lax.dot_general(value_ref[...], coup_ref[...], NN, preferred_element_type=F32)


def mid_coupling(value, coup, steps=4):
    width, depth = value.shape
    cols = coup.shape[1]
    return pl.pallas_call(
        mid_coupling_kernel,
        grid=(steps,),
        in_specs=[
            pl.BlockSpec((width, depth), lambda s: (0, 0)),
            pl.BlockSpec((depth, cols // steps), lambda s: (0, s)),
        ],
        out_specs=pl.BlockSpec((width, cols // steps), lambda s: (0, s)),
        out_shape=jax.ShapeDtypeStruct((width, cols), F32),
        compiler_params=params(),
        cost_estimate=cost(cols, depth, width),
    )(value, coup)


def leaf_kernel(dims, order_ref, value_ref, matrix_ref, out_ref):
    product = lax.dot_general(value_ref[...], matrix_ref[...], dims, preferred_element_type=F32)
    out_ref[0] = product.astype(out_ref.dtype)


def leaf_product(order, start, dims, value, matrix, cols, kind):
    width, depth = value.shape
    if dims is NN:
        spec = pl.BlockSpec((depth, cols), lambda s, order: (0, order[start + s]))
    else:
        spec = pl.BlockSpec((cols, depth), lambda s, order: (order[start + s], 0))
    return pl.pallas_call(
        functools.partial(leaf_kernel, dims),
        grid_spec=pltpu.PrefetchScalarGridSpec(
            num_scalar_prefetch=1,
            grid=(2,),
            in_specs=[pl.BlockSpec((width, depth), lambda s, order: (0, 0)), spec],
            out_specs=pl.BlockSpec((1, width, cols), lambda s, order: (s, 0, 0)),
        ),
        out_shape=jax.ShapeDtypeStruct((2, width, cols), kind),
        compiler_params=params(),
        cost_estimate=cost(2 * cols, depth, width),
    )(order, value, matrix)


def swap(value, axis, mask):
    return lax.ppermute(value, axis, [(i, i ^ mask) for i in range(lax.axis_size(axis))])


def add(*terms):
    return functools.reduce(jnp.add, [t.astype(F32) for t in terms])


def reduce_columns(send, keep, bits):
    got = swap(send, "col", bits[0])
    for bit in bits[1:]:
        half = got.shape[0] // 2
        send = add(keep[half:], got[half:]).astype(BF16)
        keep = add(keep[:half], got[:half])
        got = swap(send, "col", bit)
    return add(keep, got).astype(BF16)


def gather_columns(value, bits):
    for bit in reversed(bits):
        value = jnp.concatenate([value, swap(value, "col", bit)], axis=0)
    return value


def natural(parts):
    blocks = jnp.concatenate(parts, axis=1)
    return jnp.swapaxes(blocks, 1, 2).reshape(-1, blocks.shape[1])


def shards(
    dinv_root,
    rhs_root,
    dinv_mid,
    coup_mid,
    rhs_mid,
    dinv_leaf,
    coup_leaf,
    rhs_leaf,
    bounds_mid,
    bounds_leaf,
    parents,
):
    row_id = lax.axis_index("row")
    col_id = lax.axis_index("col")
    x, h = row_id // 2, row_id % 2
    place = jnp.stack([row_id, col_id]).astype(jnp.int32)
    local = dinv_root.shape[0] // BLOCK
    slot = local // 8
    leaf_slots = bounds_leaf.shape[1] // 4
    at = plan_layout(local, slot, leaf_slots)
    chains = range(len(CHAINS))

    order = pl.pallas_call(
        functools.partial(order_kernel, local, slot),
        out_shape=jax.ShapeDtypeStruct((local,), jnp.int32),
        in_specs=[SMEM] * 2,
        out_specs=SMEM,
        scratch_shapes=[pltpu.SMEM((4 * local,), jnp.int32)],
    )(place, bounds_mid)
    plan = pl.pallas_call(
        functools.partial(plan_kernel, local, slot, leaf_slots),
        out_shape=jax.ShapeDtypeStruct((len(CHAINS), at["size"]), jnp.int32),
        in_specs=[SMEM] * 4,
        out_specs=SMEM,
        scratch_shapes=[pltpu.SMEM((4 * local,), jnp.int32)] * 2
        + [pltpu.SMEM((len(CHAINS), 4 * local), jnp.int32)],
    )(place, bounds_mid, bounds_leaf, parents)

    within = jnp.arange(slot, dtype=jnp.int32)
    leaf_order = jnp.stack([2 * x + 1 - h, 2 * (1 - x) + 1 - h, 2 * x + h, 2 * (1 - x) + h]).astype(jnp.int32)
    mid_rhs = lax.dynamic_index_in_dim(rhs_mid, x, 0, keepdims=False).T
    leaf_rhs = rhs_leaf[0].T
    leaf_cols = coup_leaf.shape[2] // 4
    sent = root_product(order, rhs_root.T, dinv_root)

    def reduce_rows(dims, value, matrix):
        send = leaf_product(leaf_order, 0, dims, value, matrix, leaf_cols, BF16)
        keep = leaf_product(leaf_order, 2, dims, value, matrix, leaf_cols, F32)
        got = swap(send, "row", 1)
        far = swap(add(keep[1], got[1]).astype(BF16), "row", 2)
        return add(keep[0], got[0], far)

    def chain(n):
        bits = CHAINS[n]
        got = reduce_columns(*sent[n], bits)
        picked = gather(plan, n, at["select"], slot, got, swap(got, "row", 1), swap(got, "row", 2))
        own = gather_columns(picked, bits)
        sib = swap(own, "row", 1)
        bound = gather(plan, n, at["mid"], local, own, sib, wide=True)
        asked = swap(gather(plan, n, at["send_root"], leaf_slots + slot, own, sib), "row", 2)
        root_out = gather(plan, n, at["out"], slot, own, sib, asked)

        term = mid_coupling(bound, coup_mid)
        width = term.shape[0]
        rhs = mid_rhs[n * width : (n + 1) * width]
        shift = (rhs - (term + swap(term, "row", 1))).astype(BF16)
        mid_order = jnp.concatenate([chip * slot + within for chip in chips_in_order(col_id, bits)])
        mid_out = reduce_columns(*mid_product(mid_order.astype(jnp.int32), shift, dinv_mid), bits)
        mid_own = gather_columns(mid_out, bits)
        mid_sib = swap(mid_own, "row", 1)
        mid_asked = swap(gather(plan, n, at["send_mid"], leaf_slots, mid_own, mid_sib), "row", 2)

        sources = (own, sib, asked, mid_own, mid_sib, mid_asked)
        bound = gather(plan, n, at["leaf"], leaf_slots, *sources, wide=True)
        rhs = leaf_rhs[n * width : (n + 1) * width]
        shift = (rhs - reduce_rows(NN, bound, coup_leaf[0])).astype(BF16)
        leaf_out = reduce_rows(NT, shift, dinv_leaf[0]).astype(BF16)
        return root_out, mid_out, leaf_out

    root_values, mid_values, leaf_values = zip(*[chain(n) for n in chains])
    return (natural(root_values), natural(mid_values), jnp.concatenate(leaf_values, axis=0).T[None])


def solution(mesh):
    sizes = dict(mesh.shape)
    in_specs = (
        P("row", "col"),
        P("col", None),
        P("row", "col"),
        P("row", "col"),
        P(None, "col", None),
        P("col", None, "row"),
        P("col", "row", None),
        P("col", "row", None),
        P(),
        P(),
        P(),
    )
    out_specs = (P(("row", "col"), None), P(("row", "col"), None), P("col", "row", None))

    def run(*args):
        fronts, listed = args[8].shape
        blocks = args[0].shape[0] // BLOCK
        whole = fronts == 2 and fronts * listed == blocks and args[2].shape[0] == args[0].shape[0]
        fits = sizes["row"] == 4 and sizes["col"] == 8 and whole
        body = shards if fits else general_shards
        return jax.shard_map(body, mesh=mesh, in_specs=in_specs, out_specs=out_specs, check_vma=False)(*args)

    return run
```

time: 491 us -> 413 us (0.84)
  waiting for transfers between devices: 150 us -> 233 us
  starting transfers between devices: 116 us -> 37.1 us
  Pallas kernels: 171 us -> 105 us
  local copies, waits for them, and re-layouts: 30.6 us -> 18 us
    ppermute x87 -> x46, waiting for transfers between devices: 150 us -> 233 us  [swap(): lax.ppermute(value, axis, [(i, i ^ mask) for i in range(lax.axis_size(axi...]
    ppermute x87 -> x46, starting transfers between devices: 116 us -> 37.1 us  [swap(): lax.ppermute(value, axis, [(i, i ^ mask) for i in range(lax.axis_size(axi...]
    pallas_call x42 -> x25, Pallas kernels: 161 us -> 93.9 us  [the longest x8 33.8 us: leaf_product(): pl.pallas_call(functools.partial(leaf_kernel, dims), grid_spec=pltpu.Pref...]
    unnamed x132 -> x73, local copies, waits for them, and re-layouts: 19.8 us -> 13.5 us
    convert_element_type x11 -> x20, other arithmetic: 11.3 us -> 15.9 us  [the longest x4 6 us: reduce_rows(): far = swap(add(keep[1], got[1]).astype(BF16), 'row', 2)]
  transfers between devices with their start and end apart: 87 -> 46, of which waited for: 29 -> 31; matrix products, arithmetic and copies ran while one was open for 5% -> 4% of each run, Pallas kernels for 31% -> 19%
where the time goes in v2:
time: 413 us; the launch traced here: 412 us
  waiting for transfers between devices  233 us (56%)
  Pallas kernels  105 us (25%)
  starting transfers between devices  37.1 us (9%)
  local copies, waits for them, and re-layouts  18 us (4%)
  other arithmetic  17.8 us (4%)
    ppermute x46, waiting for transfers between devices, swap(): lax.ppermute(value, axis, [(i, i ^ mask) for i in range(lax.axis_size(axi...  233 us
    ppermute x46, starting transfers between devices, swap(): lax.ppermute(value, axis, [(i, i ^ mask) for i in range(lax.axis_size(axi...  37.1 us
    pallas_call x8, Pallas kernels, leaf_product(): pl.pallas_call(functools.partial(leaf_kernel, dims), grid_spec=pltpu.Pref...  33.8 us
    pallas_call x12, Pallas kernels, gather(): pl.pallas_call(functools.partial(gather_kernel, chain, start, count, wide...  22.4 us
    pallas_call x2, Pallas kernels, mid_product(): pl.pallas_call(functools.partial(mid_product_kernel, parts), grid_spec=pl...  14 us
    unnamed x73, local copies, waits for them, and re-layouts  13.5 us
    pallas_call x1, Pallas kernels, root_product(): pl.pallas_call(functools.partial(root_product_kernel, parts), grid_spec=p...  11.9 us
    pallas_call x2, Pallas kernels, mid_coupling(): pl.pallas_call(mid_coupling_kernel, grid=(steps,), in_specs=[pl.BlockSpec...  11.9 us
  transfers between devices with their start and end apart: 46, of which 31 were waited for; matrix products, arithmetic and copies ran while one was open for 4% of the time, Pallas kernels for 19%

profile of v2, /device:TPU:0, one launch (start us, length us, event | category | flops | bytes accessed | tf_op | source)
XLA Modules:
  0.0 412.3 jit_solution(15681441621719902357)
XLA Ops:
  0.7 2.8 copy.18
  4.0 2.5 shard_map.131.order_ref
  7.2 11.9 %shard_map.132 = (bf16[16,192,128]{2,1,0:T(8,128)(2,1)S(1)}, f32[16,192,128]{2,1,0:T(8,128)S(1)}, bf16[16,192,128]{2,1,0:T(8,128)(2,1)S(1)}, f32[16,192,128]{2,1,0:T(8,128)S(1)}) custom-call(s32[32]{0:T(128)S(1)} %copy-done.26, bf16[384,2048]{1,0:T(8,128)(2,1)} %bitcast.69, bf16[4096,2048]{1,0:T(8,128)(2,1)} %refs_7_.3, bf16[4096,2048]{1,0:T(8,128)(2,1)} %refs_7_.3, ...), custom_call_target="tpu_custom_call" | custom-call | flops 6442450944 | bytes 16777216 | tf_op jit(solution)/shard_map/pallas_call | solution.py:383
  19.1 3.0 collective-permute-start
  23.7 16.1 %collective-permute-done = bf16[16,192,128]{2,1,0:T(8,128)(2,1)S(1)} collective-permute-done((bf16[16,192,128]{2,1,0:T(8,128)(2,1)S(1)}, bf16[16,192,128]{2,1,0:T(8,128)(2,1)S(1)}, u32[]{:S(2)}, u32[]{:S(2)}) %collective-permute-start) | collective-permute-done | bytes 786464 | tf_op jit(solution)/shard_map/ppermute | solution.py:492
  40.1 1.9 collective-permute-start.1
  43.7 6.9 %collective-permute-done.1 = bf16[8,192,128]{2,1,0:T(8,128)(2,1)S(1)} collective-permute-done((bf16[8,192,128]{2,1,0:T(8,128)(2,1)S(1)}, bf16[8,192,128]{2,1,0:T(8,128)(2,1)S(1)}, u32[]{:S(2)}, u32[]{:S(2)}) %collective-permute-start.1) | collective-permute-done | bytes 393248 | tf_op jit(solution)/shard_map/ppermute | solution.py:492
  50.7 2.6 collective-permute-start.2
  54.8 11.4 %collective-permute-done.2 = bf16[4,192,128]{2,1,0:T(8,128)(2,1)S(1)} collective-permute-done((bf16[4,192,128]{2,1,0:T(8,128)(2,1)S(1)}, bf16[4,192,128]{2,1,0:T(8,128)(2,1)S(1)}, u32[]{:S(2)}, u32[]{:S(2)}) %collective-permute-start.2) | collective-permute-done | bytes 196640 | tf_op jit(solution)/shard_map/ppermute | solution.py:492
  66.4 1.9 collective-permute-start.4
  71.3 9.0 %shard_map.130.table_ref = s32[2,80]{1,0:T(2,128)} custom-call(s32[2]{0:T(128)} %pad_add_fusion.place_ref, s32[2,64]{1,0:T(2,128)} %bounds_ref.3, s32[8,48]{1,0:T(8,128)} %leaf_ref.1, s32[8]{0:T(128)} %parents_ref.1), custom_call_target="tpu_custom_call" | custom-call | tf_op jit(solution)/shard_map/pallas_call | solution.py:550
  83.0 3.0 collective-permute-start.15
  85.9 13.1 %collective-permute-done.5 = bf16[4,192,128]{2,1,0:T(8,128)(2,1)S(1)} collective-permute-done((bf16[4,192,128]{2,1,0:T(8,128)(2,1)S(1)}, bf16[4,192,128]{2,1,0:T(8,128)(2,1)S(1)}, u32[]{:S(2)}, u32[]{:S(2)}) %collective-permute-start.5) | collective-permute-done | bytes 196640 | tf_op jit(solution)/shard_map/ppermute | solution.py:492
  99.2 3.4 collective-permute-done.15
  102.7 1.6 collective-permute-start.16
  104.3 6.7 %collective-permute-done.6 = bf16[8,192,128]{2,1,0:T(8,128)(2,1)S(1)} collective-permute-done((bf16[8,192,128]{2,1,0:T(8,128)(2,1)S(1)}, bf16[8,192,128]{2,1,0:T(8,128)(2,1)S(1)}, u32[]{:S(2)}, u32[]{:S(2)}) %collective-permute-start.6) | collective-permute-done | bytes 393248 | tf_op jit(solution)/shard_map/ppermute | solution.py:492
  111.0 1.6 collective-permute-start.7
  113.1 17.3 %collective-permute-done.7 = bf16[16,192,128]{2,1,0:T(8,128)(2,1)S(1)} collective-permute-done((bf16[16,192,128]{2,1,0:T(8,128)(2,1)S(1)}, bf16[16,192,128]{2,1,0:T(8,128)(2,1)S(1)}, u32[]{:S(2)}, u32[]{:S(2)}) %collective-permute-start.7) | collective-permute-done | bytes 786464 | tf_op jit(solution)/shard_map/ppermute | solution.py:492
  132.1 2.0 collective-permute-done.8.refs_1_
  134.1 1.6 shard_map.139.value_ref
  136.8 5.9 %shard_map.140 = f32[192,1024]{1,0:T(8,128)} custom-call(bf16[192,4096]{1,0:T(8,128)(2,1)S(1)} %shard_map.139.value_ref, bf16[4096,1024]{1,0:T(8,128)(2,1)} %coup_ref.3), custom_call_target="tpu_custom_call" | custom-call | flops 1610612736 | bytes 8388608 | tf_op jit(solution)/shard_map/pallas_call | solution.py:452
  142.9 1.8 shard_map.142.value_ref
  144.7 6.0 %shard_map.143 = f32[192,1024]{1,0:T(8,128)} custom-call(bf16[192,4096]{1,0:T(8,128)(2,1)S(1)} %shard_map.142.value_ref, bf16[4096,1024]{1,0:T(8,128)(2,1)} %coup_ref.3), custom_call_target="tpu_custom_call" | custom-call | flops 1610612736 | bytes 8388608 | tf_op jit(solution)/shard_map/pallas_call | solution.py:452
  153.6 2.3 subtract_convert_fusion.1
  155.9 7.3 %shard_map.141 = (bf16[16,192,128]{2,1,0:T(8,128)(2,1)}, f32[16,192,128]{2,1,0:T(8,128)S(1)}) custom-call(s32[32]{0:T(128)S(1)} %concatenate.66.order_ref, bf16[192,1024]{1,0:T(8,128)(2,1)S(1)} %get-tuple-element.35.value_ref, bf16[4096,1024]{1,0:T(8,128)(2,1)} %refs_7_.5, bf16[4096,1024]{1,0:T(8,128)(2,1)} %refs_7_.5, bf16[4096,1024]{1,0:T(8,128)(2,1)} %refs_7_.5, ...), custom_call_target="tpu_custom_call" | custom-call | flops 1610612736 | bytes 8388608 | tf_op jit(solution)/shard_map/pallas_call | solution.py:425
  166.0 6.6 %shard_map.144 = (bf16[16,192,128]{2,1,0:T(8,128)(2,1)S(1)}, f32[16,192,128]{2,1,0:T(8,128)S(1)}) custom-call(s32[32]{0:T(128)S(1)} %concatenate.67.order_ref, bf16[192,1024]{1,0:T(8,128)(2,1)S(1)} %get-tuple-element.36.value_ref, bf16[4096,1024]{1,0:T(8,128)(2,1)} %refs_7_.5, bf16[4096,1024]{1,0:T(8,128)(2,1)} %refs_7_.5, bf16[4096,1024]{1,0:T(8,128)(2,1)} %refs_7_.5, ...), custom_call_target="tpu_custom_call" | custom-call | flops 1610612736 | bytes 8388608 | tf_op jit(solution)/shard_map/pallas_call | solution.py:425
  172.7 11.5 %collective-permute-done.21 = bf16[16,192,128]{2,1,0:T(8,128)(2,1)S(1)} collective-permute-done((bf16[16,192,128]{2,1,0:T(8,128)(2,1)}, bf16[16,192,128]{2,1,0:T(8,128)(2,1)S(1)}, u32[]{:S(2)}, u32[]{:S(2)}) %collective-permute-start.21) | collective-permute-done | bytes 786464 | tf_op jit(solution)/shard_map/ppermute | solution.py:492
  186.4 6.7 %collective-permute-done.25 = bf16[16,192,128]{2,1,0:T(8,128)(2,1)S(1)} collective-permute-done((bf16[16,192,128]{2,1,0:T(8,128)(2,1)S(1)}, bf16[16,192,128]{2,1,0:T(8,128)(2,1)S(1)}, u32[]{:S(2)}, u32[]{:S(2)}) %collective-permute-start.25) | collective-permute-done | bytes 786464 | tf_op jit(solution)/shard_map/ppermute | solution.py:492
  193.8 6.6 %collective-permute-done.22 = bf16[8,192,128]{2,1,0:T(8,128)(2,1)S(1)} collective-permute-done((bf16[8,192,128]{2,1,0:T(8,128)(2,1)S(1)}, bf16[8,192,128]{2,1,0:T(8,128)(2,1)S(1)}, u32[]{:S(2)}, u32[]{:S(2)}) %collective-permute-start.22) | collective-permute-done | bytes 393248 | tf_op jit(solution)/shard_map/ppermute | solution.py:492
  203.6 12.2 %collective-permute-done.23 = bf16[4,192,128]{2,1,0:T(8,128)(2,1)S(1)} collective-permute-done((bf16[4,192,128]{2,1,0:T(8,128)(2,1)S(1)}, bf16[4,192,128]{2,1,0:T(8,128)(2,1)S(1)}, u32[]{:S(2)}, u32[]{:S(2)}) %collective-permute-start.23) | collective-permute-done | bytes 196640 | tf_op jit(solution)/shard_map/ppermute | solution.py:492
  216.0 8.3 %collective-permute-done.27 = bf16[4,192,128]{2,1,0:T(8,128)(2,1)S(1)} collective-permute-done((bf16[4,192,128]{2,1,0:T(8,128)(2,1)S(1)}, bf16[4,192,128]{2,1,0:T(8,128)(2,1)S(1)}, u32[]{:S(2)}, u32[]{:S(2)}) %collective-permute-start.27) | collective-permute-done | bytes 196640 | tf_op jit(solution)/shard_map/ppermute | solution.py:492
  224.4 8.3 %collective-permute-done.28 = bf16[4,192,128]{2,1,0:T(8,128)(2,1)S(1)} collective-permute-done((bf16[4,192,128]{2,1,0:T(8,128)(2,1)S(1)}, bf16[4,192,128]{2,1,0:T(8,128)(2,1)S(1)}, u32[]{:S(2)}, u32[]{:S(2)}) %collective-permute-start.28) | collective-permute-done | bytes 196640 | tf_op jit(solution)/shard_map/ppermute | solution.py:492
  232.8 4.1 collective-permute-done.37
  237.4 7.7 %collective-permute-done.29 = bf16[8,192,128]{2,1,0:T(8,128)(2,1)S(1)} collective-permute-done((bf16[8,192,128]{2,1,0:T(8,128)(2,1)S(1)}, bf16[8,192,128]{2,1,0:T(8,128)(2,1)S(1)}, u32[]{:S(2)}, u32[]{:S(2)}) %collective-permute-start.29) | collective-permute-done | bytes 393248 | tf_op jit(solution)/shard_map/ppermute | solution.py:492
  245.8 2.0 collective-permute-done.38
  248.0 16.8 %collective-permute-done.30 = bf16[16,192,128]{2,1,0:T(8,128)(2,1)S(1)} collective-permute-done((bf16[16,192,128]{2,1,0:T(8,128)(2,1)S(1)}, bf16[16,192,128]{2,1,0:T(8,128)(2,1)S(1)}, u32[]{:S(2)}, u32[]{:S(2)}) %collective-permute-start.30) | collective-permute-done | bytes 786464 | tf_op jit(solution)/shard_map/ppermute | solution.py:492
  266.9 2.8 shard_map.134
  270.3 2.4 shard_map.145
  272.7 1.7 collective-permute-start.32
  274.4 2.8 shard_map.137
  277.7 2.4 shard_map.151
  280.1 1.7 collective-permute-start.41
  281.9 8.7 %collective-permute-done.9.refs_2_ = bf16[16,192,128]{2,1,0:T(8,128)(2,1)} collective-permute-done((bf16[16,192,128]{2,1,0:T(8,128)(2,1)}, bf16[16,192,128]{2,1,0:T(8,128)(2,1)}, u32[]{:S(2)}, u32[]{:S(2)}) %collective-permute-start.9) | collective-permute-done | bytes 786464 | tf_op jit(solution)/shard_map/ppermute | solution.py:492
  290.5 12.6 %collective-permute-done.32.refs_5_ = bf16[12,192,128]{2,1,0:T(8,128)(2,1)} collective-permute-done((bf16[12,192,128]{2,1,0:T(8,128)(2,1)}, bf16[12,192,128]{2,1,0:T(8,128)(2,1)}, u32[]{:S(2)}, u32[]{:S(2)}) %collective-permute-start.32) | collective-permute-done | bytes 589856 | tf_op jit(solution)/shard_map/ppermute | solution.py:492
  304.6 1.8 shard_map.146.value_ref
  306.4 4.2 %shard_map.148 = bf16[2,192,1024]{2,1,0:T(8,128)(2,1)S(1)} custom-call(s32[4]{0:T(128)S(1)} %pad_add_fusion.1.order_ref, bf16[192,1536]{1,0:T(8,128)(2,1)S(1)} %shard_map.146.value_ref, bf16[1536,4096]{1,0:T(8,128)(2,1)} %bitcast.61), custom_call_target="tpu_custom_call" | custom-call | flops 1207959552 | bytes 6291456 | tf_op jit(solution)/shard_map/pallas_call | solution.py:477
  310.7 9.4 %collective-permute-done.19.refs_2_ = bf16[16,192,128]{2,1,0:T(8,128)(2,1)} collective-permute-done((bf16[16,192,128]{2,1,0:T(8,128)(2,1)}, bf16[16,192,128]{2,1,0:T(8,128)(2,1)}, u32[]{:S(2)}, u32[]{:S(2)}) %collective-permute-start.19) | collective-permute-done | bytes 786464 | tf_op jit(solution)/shard_map/ppermute | solution.py:492
  320.0 12.0 %collective-permute-done.41.refs_5_ = bf16[12,192,128]{2,1,0:T(8,128)(2,1)} collective-permute-done((bf16[12,192,128]{2,1,0:T(8,128)(2,1)}, bf16[12,192,128]{2,1,0:T(8,128)(2,1)}, u32[]{:S(2)}, u32[]{:S(2)}) %collective-permute-start.41) | collective-permute-done | bytes 589856 | tf_op jit(solution)/shard_map/ppermute | solution.py:492
  332.0 1.8 shard_map.152.value_ref
  333.8 4.2 %shard_map.154 = bf16[2,192,1024]{2,1,0:T(8,128)(2,1)S(1)} custom-call(s32[4]{0:T(128)S(1)} %pad_add_fusion.1.order_ref, bf16[192,1536]{1,0:T(8,128)(2,1)S(1)} %shard_map.152.value_ref, bf16[1536,4096]{1,0:T(8,128)(2,1)} %bitcast.62), custom_call_target="tpu_custom_call" | custom-call | flops 1207959552 | bytes 6291456 | tf_op jit(solution)/shard_map/pallas_call | solution.py:477
  338.1 4.2 %shard_map.147 = f32[2,192,1024]{2,1,0:T(8,128)S(1)} custom-call(s32[4]{0:T(128)S(1)} %pad_add_fusion.1.order_ref, bf16[192,1536]{1,0:T(8,128)(2,1)S(1)} %shard_map.146.value_ref, bf16[1536,4096]{1,0:T(8,128)(2,1)} %bitcast.63), custom_call_target="tpu_custom_call" | custom-call | flops 1207959552 | bytes 6291456 | tf_op jit(solution)/shard_map/pallas_call | solution.py:477
  342.3 4.2 %shard_map.153 = f32[2,192,1024]{2,1,0:T(8,128)S(1)} custom-call(s32[4]{0:T(128)S(1)} %pad_add_fusion.1.order_ref, bf16[192,1536]{1,0:T(8,128)(2,1)S(1)} %shard_map.152.value_ref, bf16[1536,4096]{1,0:T(8,128)(2,1)} %bitcast.64), custom_call_target="tpu_custom_call" | custom-call | flops 1207959552 | bytes 6291456 | tf_op jit(solution)/shard_map/pallas_call | solution.py:477
  351.4 2.3 copy.22
  353.7 5.9 %collective-permute-done.34 = bf16[192,1024]{1,0:T(8,128)(2,1)S(1)} collective-permute-done((bf16[192,1024]{1,0:T(8,128)(2,1)}, bf16[192,1024]{1,0:T(8,128)(2,1)S(1)}, u32[]{:S(2)}, u32[]{:S(2)}) %collective-permute-start.34) | collective-permute-done | bytes 393248 | tf_op jit(solution)/shard_map/ppermute | solution.py:492
  359.7 8.1 %collective-permute-done.43 = bf16[192,1024]{1,0:T(8,128)(2,1)} collective-permute-done((bf16[192,1024]{1,0:T(8,128)(2,1)}, bf16[192,1024]{1,0:T(8,128)(2,1)}, u32[]{:S(2)}, u32[]{:S(2)}) %collective-permute-start.43) | collective-permute-done | bytes 393248 | tf_op jit(solution)/shard_map/ppermute | solution.py:492
  367.8 2.6 fusion.17
  370.4 4.6 %shard_map.156 = bf16[2,192,1024]{2,1,0:T(8,128)(2,1)} custom-call(s32[4]{0:T(128)S(1)} %pad_add_fusion.1.order_ref, bf16[192,1024]{1,0:T(8,128)(2,1)S(1)} %get-tuple-element.34.value_ref, bf16[4096,1024]{1,0:T(8,128)(2,1)} %bitcast.65), custom_call_target="tpu_custom_call" | custom-call | flops 805306368 | bytes 4194304 | tf_op jit(solution)/shard_map/pallas_call | solution.py:477
  375.0 4.6 %shard_map.150 = bf16[2,192,1024]{2,1,0:T(8,128)(2,1)} custom-call(s32[4]{0:T(128)S(1)} %pad_add_fusion.1.order_ref, bf16[192,1024]{1,0:T(8,128)(2,1)S(1)} %get-tuple-element.33.value_ref, bf16[4096,1024]{1,0:T(8,128)(2,1)} %bitcast.66), custom_call_target="tpu_custom_call" | custom-call | flops 805306368 | bytes 4194304 | tf_op jit(solution)/shard_map/pallas_call | solution.py:477
  384.3 3.8 shard_map.155
  388.2 1.8 fusion.21
  390.7 3.8 shard_map.149
  394.6 2.4 fusion.19
  399.3 3.1 collective-permute-done.45
  403.7 6.0 %collective-permute-done.36 = bf16[192,1024]{1,0:T(8,128)(2,1)} collective-permute-done((bf16[192,1024]{1,0:T(8,128)(2,1)}, bf16[192,1024]{1,0:T(8,128)(2,1)}, u32[]{:S(2)}, u32[]{:S(2)}) %collective-permute-start.36) | collective-permute-done | bytes 393248 | tf_op jit(solution)/shard_map/ppermute | solution.py:492
  (175 shorter events, 50.6 us)
Async XLA Ops:
  0.6 150.4 %copy-start = (bf16[2,1024,384]{2,1,0:T(8,128)(2,1)S(1)}, bf16[2,1024,384]{2,1,0:T(8,128)(2,1)}, u32[]{:S(2)}) copy-start(bf16[2,1024,384]{2,1,0:T(8,128)(2,1)} %param.15) | copy-start | bytes 4718596
  19.1 20.8 %collective-permute-start = (bf16[16,192,128]{2,1,0:T(8,128)(2,1)S(1)}, bf16[16,192,128]{2,1,0:T(8,128)(2,1)S(1)}, u32[]{:S(2)}, u32[]{:S(2)}) collective-permute-start(bf16[16,192,128]{2,1,0:T(8,128)(2,1)S(1)} %get-tuple-element.12), channel_id=1, source_target_pairs={{0,1},{1,0},{2,3},{3,2},{4,5},{5,4},{6,7},{7,6},{8,9},{9,8},{10,11... | collective-permute-start | bytes 2359304 | tf_op jit(solution)/shard_map/ppermute | solution.py:492
  22.2 19.8 %collective-permute-start.10 = (bf16[16,192,128]{2,1,0:T(8,128)(2,1)S(1)}, bf16[16,192,128]{2,1,0:T(8,128)(2,1)S(1)}, u32[]{:S(2)}, u32[]{:S(2)}) collective-permute-start(bf16[16,192,128]{2,1,0:T(8,128)(2,1)S(1)} %get-tuple-element.14), channel_id=1, source_target_pairs={{0,2},{1,3},{2,0},{3,1},{4,6},{5,7},{6,4},{7,5},{8,10},{9,11},{10,... | collective-permute-start | bytes 2359304 | tf_op jit(solution)/shard_map/ppermute | solution.py:492
  40.1 10.6 %collective-permute-start.1 = (bf16[8,192,128]{2,1,0:T(8,128)(2,1)S(1)}, bf16[8,192,128]{2,1,0:T(8,128)(2,1)S(1)}, u32[]{:S(2)}, u32[]{:S(2)}) collective-permute-start(bf16[8,192,128]{2,1,0:T(8,128)(2,1)S(1)} %get-tuple-element.29), channel_id=1, source_target_pairs={{0,2},{1,3},{2,0},{3,1},{4,6},{5,7},{6,4},{7,5},{8,10},{9,11},{10,... | collective-permute-start | bytes 1179656 | tf_op jit(solution)/shard_map/ppermute | solution.py:492
  42.1 11.1 %collective-permute-start.11 = (bf16[8,192,128]{2,1,0:T(8,128)(2,1)S(1)}, bf16[8,192,128]{2,1,0:T(8,128)(2,1)S(1)}, u32[]{:S(2)}, u32[]{:S(2)}) collective-permute-start(bf16[8,192,128]{2,1,0:T(8,128)(2,1)S(1)} %get-tuple-element.31), channel_id=1, source_target_pairs={{0,1},{1,0},{2,3},{3,2},{4,5},{5,4},{6,7},{7,6},{8,9},{9,8},{10,11... | collective-permute-start | bytes 1179656 | tf_op jit(solution)/shard_map/ppermute | solution.py:492
  50.7 15.5 %collective-permute-start.2 = (bf16[4,192,128]{2,1,0:T(8,128)(2,1)S(1)}, bf16[4,192,128]{2,1,0:T(8,128)(2,1)S(1)}, u32[]{:S(2)}, u32[]{:S(2)}) collective-permute-start(bf16[4,192,128]{2,1,0:T(8,128)(2,1)S(1)} %fusion.31), channel_id=1, source_target_pairs={{0,4},{1,5},{2,6},{3,7},{4,0},{5,1},{6,2},{7,3},{8,12},{9,13},{10,... | collective-permute-start | bytes 589832 | tf_op jit(solution)/shard_map/ppermute | solution.py:492
  53.3 16.4 %collective-permute-start.12 = (bf16[4,192,128]{2,1,0:T(8,128)(2,1)S(1)}, bf16[4,192,128]{2,1,0:T(8,128)(2,1)S(1)}, u32[]{:S(2)}, u32[]{:S(2)}) collective-permute-start(bf16[4,192,128]{2,1,0:T(8,128)(2,1)S(1)} %fusion.28), channel_id=1, source_target_pairs={{0,4},{1,5},{2,6},{3,7},{4,0},{5,1},{6,2},{7,3},{8,12},{9,13},{10,... | collective-permute-start | bytes 589832 | tf_op jit(solution)/shard_map/ppermute | solution.py:492
  66.3 14.0 %collective-permute-start.3 = (bf16[4,192,128]{2,1,0:T(8,128)(2,1)S(1)}, bf16[4,192,128]{2,1,0:T(8,128)(2,1)S(1)}, u32[]{:S(2)}, u32[]{:S(2)}) collective-permute-start(bf16[4,192,128]{2,1,0:T(8,128)(2,1)S(1)} %fusion.33.refs_0_), channel_id=1, source_target_pairs={{0,8},{8,0},{16,24},{24,16},{1,9},{9,1},{17,25},{25,17},{2,10},{10... | collective-permute-start | bytes 589832 | tf_op jit(solution)/shard_map/ppermute | solution.py:492
  66.4 14.0 %collective-permute-start.4 = (bf16[4,192,128]{2,1,0:T(8,128)(2,1)S(1)}, bf16[4,192,128]{2,1,0:T(8,128)(2,1)S(1)}, u32[]{:S(2)}, u32[]{:S(2)}) collective-permute-start(bf16[4,192,128]{2,1,0:T(8,128)(2,1)S(1)} %fusion.33.refs_0_), channel_id=1, source_target_pairs={{0,16},{8,24},{16,0},{24,8},{1,17},{9,25},{17,1},{25,9},{2,18},{10... | collective-permute-start | bytes 589832 | tf_op jit(solution)/shard_map/ppermute | solution.py:492
  69.7 12.3 %collective-permute-start.13 = (bf16[4,192,128]{2,1,0:T(8,128)(2,1)S(1)}, bf16[4,192,128]{2,1,0:T(8,128)(2,1)S(1)}, u32[]{:S(2)}, u32[]{:S(2)}) collective-permute-start(bf16[4,192,128]{2,1,0:T(8,128)(2,1)S(1)} %fusion.30.refs_0_), channel_id=1, source_target_pairs={{0,8},{8,0},{16,24},{24,16},{1,9},{9,1},{17,25},{25,17},{2,10},{10... | collective-permute-start | bytes 589832 | tf_op jit(solution)/shard_map/ppermute | solution.py:492
  69.8 12.2 %collective-permute-start.14 = (bf16[4,192,128]{2,1,0:T(8,128)(2,1)S(1)}, bf16[4,192,128]{2,1,0:T(8,128)(2,1)S(1)}, u32[]{:S(2)}, u32[]{:S(2)}) collective-permute-start(bf16[4,192,128]{2,1,0:T(8,128)(2,1)S(1)} %fusion.30.refs_0_), channel_id=1, source_target_pairs={{0,16},{8,24},{16,0},{24,8},{1,17},{9,25},{17,1},{25,9},{2,18},{10... | collective-permute-start | bytes 589832 | tf_op jit(solution)/shard_map/ppermute | solution.py:492
  81.9 17.1 %collective-permute-start.5 = (bf16[4,192,128]{2,1,0:T(8,128)(2,1)S(1)}, bf16[4,192,128]{2,1,0:T(8,128)(2,1)S(1)}, u32[]{:S(2)}, u32[]{:S(2)}) collective-permute-start(bf16[4,192,128]{2,1,0:T(8,128)(2,1)S(1)} %shard_map.133), channel_id=1, source_target_pairs={{0,4},{1,5},{2,6},{3,7},{4,0},{5,1},{6,2},{7,3},{8,12},{9,13},{10,... | collective-permute-start | bytes 589832 | tf_op jit(solution)/shard_map/ppermute | solution.py:492
  83.0 19.6 %collective-permute-start.15 = (bf16[4,192,128]{2,1,0:T(8,128)(2,1)S(1)}, bf16[4,192,128]{2,1,0:T(8,128)(2,1)S(1)}, u32[]{:S(2)}, u32[]{:S(2)}) collective-permute-start(bf16[4,192,128]{2,1,0:T(8,128)(2,1)S(1)} %shard_map.136), channel_id=1, source_target_pairs={{0,4},{1,5},{2,6},{3,7},{4,0},{5,1},{6,2},{7,3},{8,12},{9,13},{10,... | collective-permute-start | bytes 589832 | tf_op jit(solution)/shard_map/ppermute | solution.py:492
  99.1 11.8 %collective-permute-start.6 = (bf16[8,192,128]{2,1,0:T(8,128)(2,1)S(1)}, bf16[8,192,128]{2,1,0:T(8,128)(2,1)S(1)}, u32[]{:S(2)}, u32[]{:S(2)}) collective-permute-start(bf16[8,192,128]{2,1,0:T(8,128)(2,1)S(1)} %pad_maximum_fusion.8), channel_id=1, source_target_pairs={{0,2},{1,3},{2,0},{3,1},{4,6},{5,7},{6,4},{7,5},{8,10},{9,11},{10,... | collective-permute-start | bytes 1179656 | tf_op jit(solution)/shard_map/ppermute | solution.py:492
  102.7 10.3 %collective-permute-start.16 = (bf16[8,192,128]{2,1,0:T(8,128)(2,1)S(1)}, bf16[8,192,128]{2,1,0:T(8,128)(2,1)S(1)}, u32[]{:S(2)}, u32[]{:S(2)}) collective-permute-start(bf16[8,192,128]{2,1,0:T(8,128)(2,1)S(1)} %pad_maximum_fusion.9), channel_id=1, source_target_pairs={{0,1},{1,0},{2,3},{3,2},{4,5},{5,4},{6,7},{7,6},{8,9},{9,8},{10,11... | collective-permute-start | bytes 1179656 | tf_op jit(solution)/shard_map/ppermute | solution.py:492
  111.0 19.4 %collective-permute-start.7 = (bf16[16,192,128]{2,1,0:T(8,128)(2,1)S(1)}, bf16[16,192,128]{2,1,0:T(8,128)(2,1)S(1)}, u32[]{:S(2)}, u32[]{:S(2)}) collective-permute-start(bf16[16,192,128]{2,1,0:T(8,128)(2,1)S(1)} %pad_maximum_fusion.4), channel_id=1, source_target_pairs={{0,1},{1,0},{2,3},{3,2},{4,5},{5,4},{6,7},{7,6},{8,9},{9,8},{10,11... | collective-permute-start | bytes 2359304 | tf_op jit(solution)/shard_map/ppermute | solution.py:492
  113.1 18.8 %collective-permute-start.17 = (bf16[16,192,128]{2,1,0:T(8,128)(2,1)S(1)}, bf16[16,192,128]{2,1,0:T(8,128)(2,1)S(1)}, u32[]{:S(2)}, u32[]{:S(2)}) collective-permute-start(bf16[16,192,128]{2,1,0:T(8,128)(2,1)S(1)} %pad_maximum_fusion.5), channel_id=1, source_target_pairs={{0,2},{1,3},{2,0},{3,1},{4,6},{5,7},{6,4},{7,5},{8,10},{9,11},{10,... | collective-permute-start | bytes 2359304 | tf_op jit(solution)/shard_map/ppermute | solution.py:492
  130.6 3.5 collective-permute-start.8
  132.0 10.9 %copy-start.2 = (bf16[32,192,128]{2,1,0:T(8,128)(2,1)}, bf16[32,192,128]{2,1,0:T(8,128)(2,1)S(1)}, u32[]{:S(2)}) copy-start(bf16[32,192,128]{2,1,0:T(8,128)(2,1)S(1)} %pad_maximum_fusion.1.refs_0_) | copy-start | bytes 4718596
  132.0 10.9 %collective-permute-start.18 = (bf16[32,192,128]{2,1,0:T(8,128)(2,1)S(1)}, bf16[32,192,128]{2,1,0:T(8,128)(2,1)S(1)}, u32[]{:S(2)}, u32[]{:S(2)}) collective-permute-start(bf16[32,192,128]{2,1,0:T(8,128)(2,1)S(1)} %pad_maximum_fusion.1.refs_0_), channel_id=1, source_target_pairs={{0,8},{8,0},{16,24},{24,16},{1,9},{9,1},{17,25},{25,17},{2,10},{10... | collective-permute-start | bytes 4718600 | tf_op jit(solution)/shard_map/ppermute | solution.py:492
  142.8 10.9 %collective-permute-start.20 = (f32[192,1024]{1,0:T(8,128)}, f32[192,1024]{1,0:T(8,128)}, u32[]{:S(2)}, u32[]{:S(2)}) collective-permute-start(f32[192,1024]{1,0:T(8,128)} %shard_map.140), channel_id=1, source_target_pairs={{0,8},{8,0},{16,24},{24,16},{1,9},{9,1},{17,25},{25,17},{2,10},{10... | collective-permute-start | bytes 2359304 | tf_op jit(solution)/shard_map/ppermute | solution.py:492
  150.7 3.0 collective-permute-start.24
  164.4 19.8 %collective-permute-start.21 = (bf16[16,192,128]{2,1,0:T(8,128)(2,1)}, bf16[16,192,128]{2,1,0:T(8,128)(2,1)S(1)}, u32[]{:S(2)}, u32[]{:S(2)}) collective-permute-start(bf16[16,192,128]{2,1,0:T(8,128)(2,1)} %get-tuple-element.16), channel_id=1, source_target_pairs={{0,1},{1,0},{2,3},{3,2},{4,5},{5,4},{6,7},{7,6},{8,9},{9,8},{10,11... | collective-permute-start | bytes 2359304 | tf_op jit(solution)/shard_map/ppermute | solution.py:492
  166.0 19.1 %copy-start.23 = (f32[16,192,128]{2,1,0:T(8,128)S(1)}, f32[16,192,128]{2,1,0:T(8,128)}, u32[]{:S(2)}) copy-start(f32[16,192,128]{2,1,0:T(8,128)} %copy-done.22) | copy-start | bytes 4718596
  172.6 20.5 %collective-permute-start.25 = (bf16[16,192,128]{2,1,0:T(8,128)(2,1)S(1)}, bf16[16,192,128]{2,1,0:T(8,128)(2,1)S(1)}, u32[]{:S(2)}, u32[]{:S(2)}) collective-permute-start(bf16[16,192,128]{2,1,0:T(8,128)(2,1)S(1)} %get-tuple-element.18), channel_id=1, source_target_pairs={{0,2},{1,3},{2,0},{3,1},{4,6},{5,7},{6,4},{7,5},{8,10},{9,11},{10,... | collective-permute-start | bytes 2359304 | tf_op jit(solution)/shard_map/ppermute | solution.py:492
  186.3 14.1 %collective-permute-start.22 = (bf16[8,192,128]{2,1,0:T(8,128)(2,1)S(1)}, bf16[8,192,128]{2,1,0:T(8,128)(2,1)S(1)}, u32[]{:S(2)}, u32[]{:S(2)}) collective-permute-start(bf16[8,192,128]{2,1,0:T(8,128)(2,1)S(1)} %get-tuple-element.25), channel_id=1, source_target_pairs={{0,2},{1,3},{2,0},{3,1},{4,6},{5,7},{6,4},{7,5},{8,10},{9,11},{10,... | collective-permute-start | bytes 1179656 | tf_op jit(solution)/shard_map/ppermute | solution.py:492
  193.3 8.9 %collective-permute-start.26 = (bf16[8,192,128]{2,1,0:T(8,128)(2,1)S(1)}, bf16[8,192,128]{2,1,0:T(8,128)(2,1)S(1)}, u32[]{:S(2)}, u32[]{:S(2)}) collective-permute-start(bf16[8,192,128]{2,1,0:T(8,128)(2,1)S(1)} %get-tuple-element.27), channel_id=1, source_target_pairs={{0,1},{1,0},{2,3},{3,2},{4,5},{5,4},{6,7},{7,6},{8,9},{9,8},{10,11... | collective-permute-start | bytes 1179656 | tf_op jit(solution)/shard_map/ppermute | solution.py:492
  200.5 15.3 %collective-permute-start.23 = (bf16[4,192,128]{2,1,0:T(8,128)(2,1)S(1)}, bf16[4,192,128]{2,1,0:T(8,128)(2,1)S(1)}, u32[]{:S(2)}, u32[]{:S(2)}) collective-permute-start(bf16[4,192,128]{2,1,0:T(8,128)(2,1)S(1)} %fusion.25), channel_id=1, source_target_pairs={{0,4},{1,5},{2,6},{3,7},{4,0},{5,1},{6,2},{7,3},{8,12},{9,13},{10,... | collective-permute-start | bytes 589832 | tf_op jit(solution)/shard_map/ppermute | solution.py:492
  202.3 21.9 %collective-permute-start.27 = (bf16[4,192,128]{2,1,0:T(8,128)(2,1)S(1)}, bf16[4,192,128]{2,1,0:T(8,128)(2,1)S(1)}, u32[]{:S(2)}, u32[]{:S(2)}) collective-permute-start(bf16[4,192,128]{2,1,0:T(8,128)(2,1)S(1)} %fusion.22), channel_id=1, source_target_pairs={{0,4},{1,5},{2,6},{3,7},{4,0},{5,1},{6,2},{7,3},{8,12},{9,13},{10,... | collective-permute-start | bytes 589832 | tf_op jit(solution)/shard_map/ppermute | solution.py:492
  215.9 48.9 %copy-start.27 = (bf16[4,192,128]{2,1,0:T(8,128)(2,1)}, bf16[4,192,128]{2,1,0:T(8,128)(2,1)S(1)}, u32[]{:S(2)}) copy-start(bf16[4,192,128]{2,1,0:T(8,128)(2,1)S(1)} %fusion.27) | copy-start | bytes 589828
  215.9 16.8 %collective-permute-start.28 = (bf16[4,192,128]{2,1,0:T(8,128)(2,1)S(1)}, bf16[4,192,128]{2,1,0:T(8,128)(2,1)S(1)}, u32[]{:S(2)}, u32[]{:S(2)}) collective-permute-start(bf16[4,192,128]{2,1,0:T(8,128)(2,1)S(1)} %fusion.27), channel_id=1, source_target_pairs={{0,4},{1,5},{2,6},{3,7},{4,0},{5,1},{6,2},{7,3},{8,12},{9,13},{10,... | collective-permute-start | bytes 589832 | tf_op jit(solution)/shard_map/ppermute | solution.py:492
  224.3 42.1 %copy-start.29 = (bf16[4,192,128]{2,1,0:T(8,128)(2,1)}, bf16[4,192,128]{2,1,0:T(8,128)(2,1)S(1)}, u32[]{:S(2)}) copy-start(bf16[4,192,128]{2,1,0:T(8,128)(2,1)S(1)} %fusion.24) | copy-start | bytes 589828
  224.3 12.5 %collective-permute-start.37 = (bf16[4,192,128]{2,1,0:T(8,128)(2,1)S(1)}, bf16[4,192,128]{2,1,0:T(8,128)(2,1)S(1)}, u32[]{:S(2)}, u32[]{:S(2)}) collective-permute-start(bf16[4,192,128]{2,1,0:T(8,128)(2,1)S(1)} %fusion.24), channel_id=1, source_target_pairs={{0,4},{1,5},{2,6},{3,7},{4,0},{5,1},{6,2},{7,3},{8,12},{9,13},{10,... | collective-permute-start | bytes 589832 | tf_op jit(solution)/shard_map/ppermute | solution.py:492
  232.7 12.5 %collective-permute-start.29 = (bf16[8,192,128]{2,1,0:T(8,128)(2,1)S(1)}, bf16[8,192,128]{2,1,0:T(8,128)(2,1)S(1)}, u32[]{:S(2)}, u32[]{:S(2)}) collective-permute-start(bf16[8,192,128]{2,1,0:T(8,128)(2,1)S(1)} %pad_maximum_fusion.10), channel_id=1, source_target_pairs={{0,2},{1,3},{2,0},{3,1},{4,6},{5,7},{6,4},{7,5},{8,10},{9,11},{10,... | collective-permute-start | bytes 1179656 | tf_op jit(solution)/shard_map/ppermute | solution.py:492
  236.9 11.0 %collective-permute-start.38 = (bf16[8,192,128]{2,1,0:T(8,128)(2,1)S(1)}, bf16[8,192,128]{2,1,0:T(8,128)(2,1)S(1)}, u32[]{:S(2)}, u32[]{:S(2)}) collective-permute-start(bf16[8,192,128]{2,1,0:T(8,128)(2,1)S(1)} %pad_maximum_fusion.11), channel_id=1, source_target_pairs={{0,1},{1,0},{2,3},{3,2},{4,5},{5,4},{6,7},{7,6},{8,9},{9,8},{10,11... | collective-permute-start | bytes 1179656 | tf_op jit(solution)/shard_map/ppermute | solution.py:492
  245.2 19.5 %collective-permute-start.30 = (bf16[16,192,128]{2,1,0:T(8,128)(2,1)S(1)}, bf16[16,192,128]{2,1,0:T(8,128)(2,1)S(1)}, u32[]{:S(2)}, u32[]{:S(2)}) collective-permute-start(bf16[16,192,128]{2,1,0:T(8,128)(2,1)S(1)} %pad_maximum_fusion.6), channel_id=1, source_target_pairs={{0,1},{1,0},{2,3},{3,2},{4,5},{5,4},{6,7},{7,6},{8,9},{9,8},{10,11... | collective-permute-start | bytes 2359304 | tf_op jit(solution)/shard_map/ppermute | solution.py:492
  247.9 18.5 %collective-permute-start.39 = (bf16[16,192,128]{2,1,0:T(8,128)(2,1)S(1)}, bf16[16,192,128]{2,1,0:T(8,128)(2,1)S(1)}, u32[]{:S(2)}, u32[]{:S(2)}) collective-permute-start(bf16[16,192,128]{2,1,0:T(8,128)(2,1)S(1)} %pad_maximum_fusion.7), channel_id=1, source_target_pairs={{0,2},{1,3},{2,0},{3,1},{4,6},{5,7},{6,4},{7,5},{8,10},{9,11},{10,... | collective-permute-start | bytes 2359304 | tf_op jit(solution)/shard_map/ppermute | solution.py:492
  264.9 5.3 %copy-start.13 = (bf16[32,192,128]{2,1,0:T(8,128)(2,1)}, bf16[32,192,128]{2,1,0:T(8,128)(2,1)S(1)}, u32[]{:S(2)}) copy-start(bf16[32,192,128]{2,1,0:T(8,128)(2,1)S(1)} %pad_maximum_fusion.2.refs_0_.refs_3_) | copy-start | bytes 4718596
  264.9 5.3 %collective-permute-start.31 = (bf16[32,192,128]{2,1,0:T(8,128)(2,1)S(1)}, bf16[32,192,128]{2,1,0:T(8,128)(2,1)S(1)}, u32[]{:S(2)}, u32[]{:S(2)}) collective-permute-start(bf16[32,192,128]{2,1,0:T(8,128)(2,1)S(1)} %pad_maximum_fusion.2.refs_0_.refs_3_), channel_id=1, source_target_pairs={{0,8},{8,0},{16,24},{24,16},{1,9},{9,1},{17,25},{25,17},{2,10},{10... | collective-permute-start | bytes 4718600 | tf_op jit(solution)/shard_map/ppermute | solution.py:492
  266.6 11.1 %copy-start.12 = (bf16[32,192,128]{2,1,0:T(8,128)(2,1)}, bf16[32,192,128]{2,1,0:T(8,128)(2,1)S(1)}, u32[]{:S(2)}) copy-start(bf16[32,192,128]{2,1,0:T(8,128)(2,1)S(1)} %pad_maximum_fusion.3.refs_0_.refs_3_) | copy-start | bytes 4718596
  266.6 11.1 %collective-permute-start.40 = (bf16[32,192,128]{2,1,0:T(8,128)(2,1)S(1)}, bf16[32,192,128]{2,1,0:T(8,128)(2,1)S(1)}, u32[]{:S(2)}, u32[]{:S(2)}) collective-permute-start(bf16[32,192,128]{2,1,0:T(8,128)(2,1)S(1)} %pad_maximum_fusion.3.refs_0_.refs_3_), channel_id=1, source_target_pairs={{0,8},{8,0},{16,24},{24,16},{1,9},{9,1},{17,25},{25,17},{2,10},{10... | collective-permute-start | bytes 4718600 | tf_op jit(solution)/shard_map/ppermute | solution.py:492
  269.8 4.6 %copy-start.3 = (bf16[32,192,128]{2,1,0:T(8,128)(2,1)S(1)}, bf16[32,192,128]{2,1,0:T(8,128)(2,1)}, u32[]{:S(2)}) copy-start(bf16[32,192,128]{2,1,0:T(8,128)(2,1)} %copy-done.2) | copy-start | bytes 4718596
  269.8 4.6 %copy-start.9 = (bf16[32,192,128]{2,1,0:T(8,128)(2,1)S(1)}, bf16[32,192,128]{2,1,0:T(8,128)(2,1)}, u32[]{:S(2)}) copy-start(bf16[32,192,128]{2,1,0:T(8,128)(2,1)} %copy-done.8) | copy-start | bytes 4718596
  269.8 20.7 %collective-permute-start.9 = (bf16[16,192,128]{2,1,0:T(8,128)(2,1)}, bf16[16,192,128]{2,1,0:T(8,128)(2,1)}, u32[]{:S(2)}, u32[]{:S(2)}) collective-permute-start(bf16[16,192,128]{2,1,0:T(8,128)(2,1)} %shard_map.134), channel_id=1, source_target_pairs={{0,16},{8,24},{16,0},{24,8},{1,17},{9,25},{17,1},{25,9},{2,18},{10... | collective-permute-start | bytes 2359304 | tf_op jit(solution)/shard_map/ppermute | solution.py:492
  272.7 30.5 %collective-permute-start.32 = (bf16[12,192,128]{2,1,0:T(8,128)(2,1)}, bf16[12,192,128]{2,1,0:T(8,128)(2,1)}, u32[]{:S(2)}, u32[]{:S(2)}) collective-permute-start(bf16[12,192,128]{2,1,0:T(8,128)(2,1)} %shard_map.145), channel_id=1, source_target_pairs={{0,16},{8,24},{16,0},{24,8},{1,17},{9,25},{17,1},{25,9},{2,18},{10... | collective-permute-start | bytes 1769480 | tf_op jit(solution)/shard_map/ppermute | solution.py:492
  277.2 42.8 %collective-permute-start.19 = (bf16[16,192,128]{2,1,0:T(8,128)(2,1)}, bf16[16,192,128]{2,1,0:T(8,128)(2,1)}, u32[]{:S(2)}, u32[]{:S(2)}) collective-permute-start(bf16[16,192,128]{2,1,0:T(8,128)(2,1)} %shard_map.137), channel_id=1, source_target_pairs={{0,16},{8,24},{16,0},{24,8},{1,17},{9,25},{17,1},{25,9},{2,18},{10... | collective-permute-start | bytes 2359304 | tf_op jit(solution)/shard_map/ppermute | solution.py:492
  280.1 51.9 %collective-permute-start.41 = (bf16[12,192,128]{2,1,0:T(8,128)(2,1)}, bf16[12,192,128]{2,1,0:T(8,128)(2,1)}, u32[]{:S(2)}, u32[]{:S(2)}) collective-permute-start(bf16[12,192,128]{2,1,0:T(8,128)(2,1)} %shard_map.151), channel_id=1, source_target_pairs={{0,16},{8,24},{16,0},{24,8},{1,17},{9,25},{17,1},{25,9},{2,18},{10... | collective-permute-start | bytes 1769480 | tf_op jit(solution)/shard_map/ppermute | solution.py:492
  306.3 25.7 %copy-start.10 = (bf16[32,192,128]{2,1,0:T(8,128)(2,1)S(1)}, bf16[32,192,128]{2,1,0:T(8,128)(2,1)}, u32[]{:S(2)}) copy-start(bf16[32,192,128]{2,1,0:T(8,128)(2,1)} %copy-done.8) | copy-start | bytes 4718596
  310.6 36.0 %collective-permute-start.33 = (bf16[2,192,1024]{2,1,0:T(8,128)(2,1)S(1)}, bf16[2,192,1024]{2,1,0:T(8,128)(2,1)S(1)}, u32[]{:S(2)}, u32[]{:S(2)}) collective-permute-start(bf16[2,192,1024]{2,1,0:T(8,128)(2,1)S(1)} %shard_map.148), channel_id=1, source_target_pairs={{0,8},{8,0},{16,24},{24,16},{1,9},{9,1},{17,25},{25,17},{2,10},{10... | collective-permute-start | bytes 2359304 | tf_op jit(solution)/shard_map/ppermute | solution.py:492
  338.0 10.2 %collective-permute-start.42 = (bf16[2,192,1024]{2,1,0:T(8,128)(2,1)S(1)}, bf16[2,192,1024]{2,1,0:T(8,128)(2,1)S(1)}, u32[]{:S(2)}, u32[]{:S(2)}) collective-permute-start(bf16[2,192,1024]{2,1,0:T(8,128)(2,1)S(1)} %shard_map.154), channel_id=1, source_target_pairs={{0,8},{8,0},{16,24},{24,16},{1,9},{9,1},{17,25},{25,17},{2,10},{10... | collective-permute-start | bytes 2359304 | tf_op jit(solution)/shard_map/ppermute | solution.py:492
  342.3 4.3 %copy-start.16 = (f32[2,192,1024]{2,1,0:T(8,128)}, f32[2,192,1024]{2,1,0:T(8,128)S(1)}, u32[]{:S(2)}) copy-start(f32[2,192,1024]{2,1,0:T(8,128)S(1)} %shard_map.147) | copy-start | bytes 4718596
  347.5 12.1 %collective-permute-start.34 = (bf16[192,1024]{1,0:T(8,128)(2,1)}, bf16[192,1024]{1,0:T(8,128)(2,1)S(1)}, u32[]{:S(2)}, u32[]{:S(2)}) collective-permute-start(bf16[192,1024]{1,0:T(8,128)(2,1)} %fusion.18), channel_id=1, source_target_pairs={{0,16},{8,24},{16,0},{24,8},{1,17},{9,25},{17,1},{25,9},{2,18},{10... | collective-permute-start | bytes 1179656 | tf_op jit(solution)/shard_map/ppermute | solution.py:492
  350.0 17.8 %collective-permute-start.43 = (bf16[192,1024]{1,0:T(8,128)(2,1)}, bf16[192,1024]{1,0:T(8,128)(2,1)}, u32[]{:S(2)}, u32[]{:S(2)}) collective-permute-start(bf16[192,1024]{1,0:T(8,128)(2,1)} %fusion.20), channel_id=1, source_target_pairs={{0,16},{8,24},{16,0},{24,8},{1,17},{9,25},{17,1},{25,9},{2,18},{10... | collective-permute-start | bytes 1179656 | tf_op jit(solution)/shard_map/ppermute | solution.py:492
  359.6 8.1 %copy-start.34 = (bf16[192,1024]{1,0:T(8,128)(2,1)}, bf16[192,1024]{1,0:T(8,128)(2,1)S(1)}, u32[]{:S(2)}) copy-start(bf16[192,1024]{1,0:T(8,128)(2,1)S(1)} %collective-permute-done.34) | copy-start | bytes 1179652
  370.4 4.6 %copy-start.20 = (bf16[192,1024]{1,0:T(8,128)(2,1)}, bf16[192,1024]{1,0:T(8,128)(2,1)S(1)}, u32[]{:S(2)}) copy-start(bf16[192,1024]{1,0:T(8,128)(2,1)S(1)} %get-tuple-element.34.value_ref) | copy-start | bytes 1179652
  375.0 13.2 %collective-permute-start.44 = (bf16[2,192,1024]{2,1,0:T(8,128)(2,1)}, bf16[2,192,1024]{2,1,0:T(8,128)(2,1)}, u32[]{:S(2)}, u32[]{:S(2)}) collective-permute-start(bf16[2,192,1024]{2,1,0:T(8,128)(2,1)} %shard_map.156), channel_id=1, source_target_pairs={{0,8},{8,0},{16,24},{24,16},{1,9},{9,1},{17,25},{25,17},{2,10},{10... | collective-permute-start | bytes 2359304 | tf_op jit(solution)/shard_map/ppermute | solution.py:492
  375.0 5.1 %copy-start.11 = (bf16[32,192,128]{2,1,0:T(8,128)(2,1)S(1)}, bf16[32,192,128]{2,1,0:T(8,128)(2,1)}, u32[]{:S(2)}) copy-start(bf16[32,192,128]{2,1,0:T(8,128)(2,1)} %copy-done.8) | copy-start | bytes 4718596
  379.6 14.9 %collective-permute-start.35 = (bf16[2,192,1024]{2,1,0:T(8,128)(2,1)}, bf16[2,192,1024]{2,1,0:T(8,128)(2,1)}, u32[]{:S(2)}, u32[]{:S(2)}) collective-permute-start(bf16[2,192,1024]{2,1,0:T(8,128)(2,1)} %shard_map.150), channel_id=1, source_target_pairs={{0,8},{8,0},{16,24},{24,16},{1,9},{9,1},{17,25},{25,17},{2,10},{10... | collective-permute-start | bytes 2359304 | tf_op jit(solution)/shard_map/ppermute | solution.py:492
  390.0 12.3 %collective-permute-start.45 = (bf16[192,1024]{1,0:T(8,128)(2,1)}, bf16[192,1024]{1,0:T(8,128)(2,1)}, u32[]{:S(2)}, u32[]{:S(2)}) collective-permute-start(bf16[192,1024]{1,0:T(8,128)(2,1)} %fusion.21), channel_id=1, source_target_pairs={{0,16},{8,24},{16,0},{24,8},{1,17},{9,25},{17,1},{25,9},{2,18},{10... | collective-permute-start | bytes 1179656 | tf_op jit(solution)/shard_map/ppermute | solution.py:492
  394.5 4.7 %copy-start.18 = (f32[2,192,1024]{2,1,0:T(8,128)}, f32[2,192,1024]{2,1,0:T(8,128)S(1)}, u32[]{:S(2)}) copy-start(f32[2,192,1024]{2,1,0:T(8,128)S(1)} %shard_map.149) | copy-start | bytes 4718596
  394.5 3.8 copy-start.28
  394.5 3.8 copy-start.30
  396.9 12.8 %collective-permute-start.36 = (bf16[192,1024]{1,0:T(8,128)(2,1)}, bf16[192,1024]{1,0:T(8,128)(2,1)}, u32[]{:S(2)}, u32[]{:S(2)}) collective-permute-start(bf16[192,1024]{1,0:T(8,128)(2,1)} %fusion.19), channel_id=1, source_target_pairs={{0,16},{8,24},{16,0},{24,8},{1,17},{9,25},{17,1},{25,9},{2,18},{10... | collective-permute-start | bytes 1179656 | tf_op jit(solution)/shard_map/ppermute | solution.py:492
  402.3 7.4 %copy-start.19 = (f32[2,192,1024]{2,1,0:T(8,128)S(1)}, f32[2,192,1024]{2,1,0:T(8,128)}, u32[]{:S(2)}) copy-start(f32[2,192,1024]{2,1,0:T(8,128)} %copy-done.18) | copy-start | bytes 4718596
  (17 other events, 31.6 us)

commit v3 on v2

--- a/solution.py
+++ b/solution.py
@@ -173,16 +173,17 @@
         ("send_root", leaf_slots + slot),
         ("leaf", leaf_slots),
         ("out", slot),
-        ("send_mid", leaf_slots),
+        ("mid_order", local),
+        ("mid_out", slot),
+        ("turn", 1),
     ):
         at[name] = size
         size += count
     at["size"] = size
-    at["mid_base"] = 2 * local + leaf_slots + slot
     return at
 
 
-def plan_kernel(local, slot, leaf_slots, place_ref, bounds_ref, leaf_ref, parents_ref, out_ref, front, ident, where):
+def plan_kernel(local, slot, leaf_slots, place_ref, bounds_ref, leaf_ref, parents_ref, out_ref, front, ident, where, record):
     row, col = place_ref[0], place_ref[1]
     x, h = row // 2, row % 2
     total = 4 * local
@@ -261,10 +262,6 @@
 
     lax.fori_loop(0, 8, per_chip, 0)
 
-    def mid_place(block, bits):
-        inner = block % local
-        return ((block // local) ^ h) * local + place_of(inner // slot, col, bits, slot) + inner % slot
-
     def mid_list(j):
         block = bounds_ref[x, h * local + j]
         for n in chains:
@@ -272,21 +269,76 @@
 
     loop(local, mid_list)
     far = 2 * (1 - x) + h
-    owner = parents_ref[col] == x
-
-    def lists(j):
+    turn = jnp.int32(6)
+    for k in range(7, 0, -1):
+        apart = [(parents_ref[c] != parents_ref[c ^ k]).astype(jnp.int32) for c in range(8)]
+        turn = jnp.where(functools.reduce(jnp.multiply, apart) == 1, k - 1, turn)
+    out_ref[0, at["turn"]] = turn
+    listed = 4 * leaf_slots
+
+    def per_leaf(leaf, _):
+        @pl.when(parents_ref[leaf] == x)
+        def _():
+            def body(j, rank):
+                block = leaf_ref[leaf, j]
+                taken = block >= total
+
+                @pl.when(taken)
+                def _():
+                    record[block - total] = leaf * 4 * slot + rank
+
+                return rank + taken.astype(jnp.int32)
+
+            lax.fori_loop(0, listed, body, jnp.int32(0))
+
+        return 0
+
+    lax.fori_loop(0, 8, per_leaf, 0)
+
+    def spot(block):
+        leaf, rank = record[block] // (4 * slot), record[block] % (4 * slot)
+        chip = jnp.where(rank < 2 * slot, leaf, leaf ^ (turn + 1))
+        return chip, rank // slot % 2, rank % slot
+
+    def mid_orders(block):
+        chip, core, k = spot(block)
+
+        @pl.when(core == h)
+        def _():
+            for n in chains:
+                near = place_of(chip, col, CHAINS[n], slot) + k
+                out_ref[n, at["mid_order"] + near] = (block // local ^ h) * local + block % local
+
+    loop(2 * local, mid_orders)
+
+    def mid_outs(j):
+        chip, core, k = spot(h * local + col * slot + j)
+        for n in chains:
+            out_ref[n, at["mid_out"] + j] = (core ^ h) * local + place_of(chip, col, CHAINS[n], slot) + k
+
+    loop(slot, mid_outs)
+
+    def sends(j):
         asked = leaf_ref[col, far * leaf_slots + j]
+        for n in chains:
+            out_ref[n, at["send_root"] + j] = where[n, jnp.minimum(asked, total - 1)]
+
+    loop(leaf_slots, sends)
+
+    def count(j, rank):
+        return rank + (leaf_ref[col, j] >= total).astype(jnp.int32)
+
+    def lists(j, rank):
         held = leaf_ref[col, row * leaf_slots + j]
         low = jnp.minimum(held, total - 1)
+        near = (rank // slot % 2 ^ h) * 2 * slot + rank // (2 * slot) * slot + rank % slot
         for n in chains:
-            bits = CHAINS[n]
-            out_ref[n, at["send_root"] + j] = where[n, jnp.minimum(asked, total - 1)]
-            out_ref[n, at["send_mid"] + j] = mid_place(jnp.maximum(asked - total, 0), bits)
             from_root = jnp.where(front[low] == x, where[n, low], 2 * local + j)
-            from_mid = jnp.where(owner, mid_place(jnp.maximum(held - total, 0), bits), 2 * local + j)
-            out_ref[n, at["leaf"] + j] = jnp.where(held < total, from_root, from_mid + at["mid_base"])
-
-    loop(leaf_slots, lists)
+            from_mid = 2 * local + leaf_slots + slot + near
+            out_ref[n, at["leaf"] + j] = jnp.where(held < total, from_root, from_mid)
+        return count(row * leaf_slots + j, rank)
+
+    lax.fori_loop(0, leaf_slots, lists, lax.fori_loop(0, row * leaf_slots, count, jnp.int32(0)))
 
     def outs(j):
         asked = far * local + col * slot + j
@@ -298,49 +350,40 @@
     loop(slot, outs)
 
 
-def start_fetch(sources, code, target, sem):
+def start_fetch(sources, code, target, sem, rows=None):
     base = 0
     for source in sources:
         count = source.shape[0]
 
         @pl.when((code >= base) & (code < base + count))
         def _(source=source, base=base):
-            pltpu.make_async_copy(source.at[code - base], target, sem).start()
+            block = source.at[code - base] if rows is None else source.at[code - base, rows]
+            pltpu.make_async_copy(block, target, sem).start()
 
         base += count
 
 
-def lanes(ref, i):
-    return ref.at[:, pl.ds(i * BLOCK, BLOCK)]
-
-
-def gather_kernel(chain, start, count, wide, table_ref, *refs):
-    *sources, out_ref, sems = refs
-    targets = [lanes(out_ref, i) if wide else out_ref.at[i] for i in range(count)]
+def gather_kernel(chain, start, count, total, rows, table_ref, *refs):
+    sources, out_ref, sems = refs[:total], refs[-2], refs[-1]
     for i in range(count):
-        start_fetch(sources, table_ref[chain, start + i], targets[i], sems.at[i])
+        start_fetch(sources, table_ref[chain, start + i], out_ref.at[i], sems.at[i], rows)
     for i in range(count):
-        pltpu.make_async_copy(sources[0].at[0], targets[i], sems.at[i]).wait()
-
-
-def gather(table, chain, start, count, *sources, wide=False):
-    width = sources[0].shape[1]
-    shape = (width, count * BLOCK) if wide else (count, width, BLOCK)
+        pltpu.make_async_copy(sources[0].at[0, rows], out_ref.at[i], sems.at[i]).wait()
+
+
+def gather(table, chain, start, count, sources, after=(), part=None):
+    first, width = (0, sources[0].shape[1]) if part is None else part
     return pl.pallas_call(
-        functools.partial(gather_kernel, chain, start, count, wide),
-        out_shape=jax.ShapeDtypeStruct(shape, BF16),
-        in_specs=[SMEM] + [ANY] * len(sources),
+        functools.partial(gather_kernel, chain, start, count, len(sources), pl.ds(first, width)),
+        out_shape=jax.ShapeDtypeStruct((count, width, BLOCK), BF16),
+        in_specs=[SMEM] + [ANY] * (len(sources) + len(after)),
         out_specs=VMEM,
         scratch_shapes=[pltpu.SemaphoreType.DMA((count,))],
         compiler_params=params(),
-    )(table, *sources)
-
-
-def root_product_kernel(parts, order_ref, value_ref, *refs):
-    blocks, outs = refs[:parts], refs[parts:]
-    step = pl.program_id(0)
-    matrix = jnp.concatenate([b[...] for b in blocks], axis=0)
-    result = lax.dot_general(value_ref[...], matrix, NT, preferred_element_type=F32)
+    )(table, *sources, *after)
+
+
+def store_halves(step, result, parts, outs):
     width = result.shape[0] // 2
     for n, bit in enumerate((2, 1)):
         part = result[n * width : (n + 1) * width]
@@ -360,14 +403,7 @@
             store(outs[2 * n + 1])
 
 
-def root_product(order, value, matrix):
-    width, depth = value.shape
-    local = matrix.shape[0] // BLOCK
-    parts = local // 4
-
-    def spec(i):
-        return pl.BlockSpec((BLOCK, depth), lambda s, order: (order[parts * (3 - s) + i], 0))
-
+def half_specs(local, parts, width):
     out_specs, out_shape = [], []
     for bit in (2, 1):
         for far in (True, False):
@@ -380,13 +416,39 @@
 
             out_specs.append(pl.BlockSpec((parts, width // 2, BLOCK), block))
             out_shape.append(jax.ShapeDtypeStruct((local // 2, width // 2, BLOCK), BF16 if far else F32))
+    return out_specs, out_shape
+
+
+def root_product_kernel(parts, order_ref, value_ref, *refs):
+    blocks, outs, turned = refs[:parts], refs[parts:-1], refs[-1]
+    step = pl.program_id(0)
+
+    @pl.when(step == 0)
+    def _():
+        turned[...] = value_ref[...].T
+
+    matrix = jnp.concatenate([b[...] for b in blocks], axis=0)
+    result = lax.dot_general(turned[...], matrix, NT, preferred_element_type=F32)
+    store_halves(step, result, parts, outs)
+
+
+def root_product(order, value, matrix):
+    depth, width = value.shape
+    local = matrix.shape[0] // BLOCK
+    parts = local // 4
+
+    def spec(i):
+        return pl.BlockSpec((BLOCK, depth), lambda s, order: (order[parts * (3 - s) + i], 0))
+
+    out_specs, out_shape = half_specs(local, parts, width)
     outs = pl.pallas_call(
         functools.partial(root_product_kernel, parts),
         grid_spec=pltpu.PrefetchScalarGridSpec(
             num_scalar_prefetch=1,
             grid=(4,),
-            in_specs=[pl.BlockSpec((width, depth), lambda s, order: (0, 0))] + [spec(i) for i in range(parts)],
+            in_specs=[pl.BlockSpec((depth, width), lambda s, order: (0, 0))] + [spec(i) for i in range(parts)],
             out_specs=out_specs,
+            scratch_shapes=[pltpu.VMEM((width, depth), BF16)],
         ),
         out_shape=out_shape,
         compiler_params=params(),
@@ -395,99 +457,237 @@
     return outs[:2], outs[2:]
 
 
-def mid_product_kernel(parts, order_ref, value_ref, *refs):
-    blocks, (send_ref, keep_ref) = refs[:parts], refs[parts:]
-    step = pl.program_id(0)
-    matrix = jnp.concatenate([b[...] for b in blocks], axis=0)
-    result = lax.dot_general(value_ref[...], matrix, NT, preferred_element_type=F32)
-
-    def store(ref):
-        for i in range(parts):
-            ref[i] = result[:, i * BLOCK : (i + 1) * BLOCK].astype(ref.dtype)
-
-    @pl.when(step < 2)
+def store_blocks(ref, result):
+    for i in range(ref.shape[0]):
+        ref[i] = result[:, i * BLOCK : (i + 1) * BLOCK].astype(ref.dtype)
+
+
+def mid_first_kernel(front_ref, term_ref, got_ref, rhs_ref, matrix_ref, out_ref, shift_ref):
+    @pl.when(pl.program_id(0) == 0)
     def _():
-        store(send_ref)
-
-    @pl.when(step >= 2)
-    def _():
-        store(keep_ref)
-
-
-def mid_product(order, value, matrix):
-    width, depth = value.shape
-    local = matrix.shape[0] // BLOCK
-    parts = local // 4
-
-    def spec(i):
-        return pl.BlockSpec((BLOCK, depth), lambda s, order: (order[parts * ((s + 2) % 4) + i], 0))
-
+        shift_ref[...] = (rhs_ref[0].T.astype(F32) - (term_ref[...] + got_ref[...].astype(F32))).astype(BF16)
+
+    store_blocks(out_ref, lax.dot_general(shift_ref[...], matrix_ref[...], NT, preferred_element_type=F32))
+
+
+def mid_rest_kernel(shift_ref, matrix_ref, out_ref):
+    store_blocks(out_ref, lax.dot_general(shift_ref[...], matrix_ref[...], NT, preferred_element_type=F32))
+
+
+def mid_first(front, term, got, rhs, matrix):
+    width, depth = term.shape
+    half = matrix.shape[0] // BLOCK // 2
+    whole = pl.BlockSpec((width, depth), lambda s, front: (0, 0))
     return pl.pallas_call(
-        functools.partial(mid_product_kernel, parts),
+        mid_first_kernel,
         grid_spec=pltpu.PrefetchScalarGridSpec(
             num_scalar_prefetch=1,
-            grid=(4,),
-            in_specs=[pl.BlockSpec((width, depth), lambda s, order: (0, 0))] + [spec(i) for i in range(parts)],
+            grid=(2,),
+            in_specs=[
+                whole,
+                whole,
+                pl.BlockSpec((1, depth, width), lambda s, front: (front[0], 0, 0)),
+                pl.BlockSpec((half // 2 * BLOCK, depth), lambda s, front: (s, 0)),
+            ],
+            out_specs=[pl.BlockSpec((half // 2, width, BLOCK), lambda s, front: (s, 0, 0)), whole],
+        ),
+        out_shape=[
+            jax.ShapeDtypeStruct((half, width, BLOCK), BF16),
+            jax.ShapeDtypeStruct((width, depth), BF16),
+        ],
+        compiler_params=params(),
+        cost_estimate=cost(half * BLOCK, depth, width),
+    )(front.reshape(1), term, got, rhs, matrix)
+
+
+def mid_rest(shift, matrix):
+    width, depth = shift.shape
+    half = matrix.shape[0] // BLOCK // 2
+    return pl.pallas_call(
+        mid_rest_kernel,
+        grid=(2,),
+        in_specs=[
+            pl.BlockSpec((width, depth), lambda s: (0, 0)),
+            pl.BlockSpec((half // 2 * BLOCK, depth), lambda s: (2 + s, 0)),
+        ],
+        out_specs=pl.BlockSpec((half // 2, width, BLOCK), lambda s: (s, 0, 0)),
+        out_shape=jax.ShapeDtypeStruct((half, width, BLOCK), BF16),
+        compiler_params=params(),
+        cost_estimate=cost(half * BLOCK, depth, width),
+    )(shift, matrix)
+
+
+def mid_coupling_kernel(start, count, table_ref, *refs):
+    sources, (coup_ref, out_ref, send_ref, bound, sems) = refs[:4], refs[4:]
+    width = bound.shape[0] // 2
+
+    def target(n, i):
+        return bound.at[pl.ds(n * width, width), pl.ds(i * BLOCK, BLOCK)]
+
+    @pl.when(pl.program_id(0) == 0)
+    def _():
+        for n in range(2):
+            for i in range(count):
+                start_fetch(sources[2 * n : 2 * n + 2], table_ref[n, start + i], target(n, i), sems.at[n, i])
+        for n in range(2):
+            for i in range(count):
+                pltpu.make_async_copy(sources[0].at[0], target(n, i), sems.at[n, i]).wait()
+
+    product = lax.dot_general(bound[...], coup_ref[...], NN, preferred_element_type=F32)
+    out_ref[...] = product
+    send_ref[...] = product.astype(BF16)
+
+
+def mid_coupling(table, start, sources, coup, steps=4):
+    count, width, _ = sources[0].shape
+    depth, cols = coup.shape
+    tile = pl.BlockSpec((2 * width, cols // steps), lambda s: (0, s))
+    return pl.pallas_call(
+        functools.partial(mid_coupling_kernel, start, count),
+        grid=(steps,),
+        in_specs=[SMEM] + [ANY] * 4 + [pl.BlockSpec((depth, cols // steps), lambda s: (0, s))],
+        out_specs=[tile, tile],
+        out_shape=[
+            jax.ShapeDtypeStruct((2 * width, cols), F32),
+            jax.ShapeDtypeStruct((2 * width, cols), BF16),
+        ],
+        scratch_shapes=[pltpu.VMEM((2 * width, depth), BF16), pltpu.SemaphoreType.DMA((2, count))],
+        compiler_params=params(),
+        cost_estimate=cost(cols, depth, 2 * width),
+    )(table, *sources, coup)
+
+
+def leaf_first_kernel(chain, start, count, total, table_ref, order_ref, *refs):
+    sources, (matrix_ref, *_, out_ref, bound_ref, sems) = refs[:total], refs[total:]
+
+    @pl.when(pl.program_id(0) == 0)
+    def _():
+        targets = [bound_ref.at[:, pl.ds(i * BLOCK, BLOCK)] for i in range(count)]
+        for i in range(count):
+            start_fetch(sources, table_ref[chain, start + i], targets[i], sems.at[i])
+        for i in range(count):
+            pltpu.make_async_copy(sources[0].at[0], targets[i], sems.at[i]).wait()
+
+    out_ref[0] = lax.dot_general(bound_ref[...], matrix_ref[...], NN, preferred_element_type=F32).astype(BF16)
+
+
+def leaf_first(table, chain, start, count, sources, order, matrix, cols, after):
+    width = sources[0].shape[1]
+    depth = matrix.shape[0]
+    return pl.pallas_call(
+        functools.partial(leaf_first_kernel, chain, start, count, len(sources)),
+        grid_spec=pltpu.PrefetchScalarGridSpec(
+            num_scalar_prefetch=2,
+            grid=(2,),
+            in_specs=[ANY] * len(sources)
+            + [pl.BlockSpec((depth, cols), lambda s, table, order: (0, order[s]))]
+            + [ANY] * len(after),
             out_specs=[
-                pl.BlockSpec((parts, width, BLOCK), lambda s, order: (jnp.minimum(s, 1), 0, 0)),
-                pl.BlockSpec((parts, width, BLOCK), lambda s, order: (jnp.maximum(s - 2, 0), 0, 0)),
+                pl.BlockSpec((1, width, cols), lambda s, table, order: (s, 0, 0)),
+                pl.BlockSpec((width, depth), lambda s, table, order: (0, 0)),
+            ],
+            scratch_shapes=[pltpu.SemaphoreType.DMA((count,))],
+        ),
+        out_shape=[
+            jax.ShapeDtypeStruct((2, width, cols), BF16),
+            jax.ShapeDtypeStruct((width, depth), BF16),
+        ],
+        compiler_params=params(),
+        cost_estimate=cost(2 * cols, depth, width),
+    )(table, order, *sources, matrix, *after)
+
+
+def leaf_shift_kernel(chain, order_ref, keep_ref, got_ref, far_ref, rhs_ref, matrix_ref, *refs):
+    out_ref, shift_ref = refs[-2:]
+
+    @pl.when(pl.program_id(0) == 0)
+    def _():
+        width = shift_ref.shape[0]
+        term = keep_ref[0] + got_ref[0].astype(F32) + far_ref[...].astype(F32)
+        rhs = rhs_ref[0].T[chain * width : (chain + 1) * width]
+        shift_ref[...] = (rhs.astype(F32) - term).astype(BF16)
+
+    product = lax.dot_general(shift_ref[...], matrix_ref[...], NT, preferred_element_type=F32)
+    out_ref[0] = product.astype(BF16)
+
+
+def leaf_shift(chain, order, keep, got, far, rhs, matrix, after):
+    _, width, depth = keep.shape
+    one = pl.BlockSpec((1, width, depth), lambda s, order: (0, 0, 0))
+    return pl.pallas_call(
+        functools.partial(leaf_shift_kernel, chain),
+        grid_spec=pltpu.PrefetchScalarGridSpec(
+            num_scalar_prefetch=1,
+            grid=(2,),
+            in_specs=[
+                one,
+                one,
+                pl.BlockSpec((width, depth), lambda s, order: (0, 0)),
+                pl.BlockSpec(rhs.shape, lambda s, order: (0, 0, 0)),
+                pl.BlockSpec((depth, depth), lambda s, order: (order[s], 0)),
+            ]
+            + [ANY] * len(after),
+            out_specs=[
+                pl.BlockSpec((1, width, depth), lambda s, order: (s, 0, 0)),
+                pl.BlockSpec((width, depth), lambda s, order: (0, 0)),
             ],
         ),
         out_shape=[
-            jax.ShapeDtypeStruct((local // 2, width, BLOCK), BF16),
-            jax.ShapeDtypeStruct((local // 2, width, BLOCK), F32),
+            jax.ShapeDtypeStruct((2, width, depth), BF16),
+            jax.ShapeDtypeStruct((width, depth), BF16),
         ],
         compiler_params=params(),
-        cost_estimate=cost(matrix.shape[0], depth, width),
-    )(order, value, *([matrix] * parts))
-
-
-def mid_coupling_kernel(value_ref, coup_ref, out_ref):
-    out_ref[...] = lax.dot_general(value_ref[...], coup_ref[...], NN, preferred_element_type=F32)
-
-
-def mid_coupling(value, coup, steps=4):
-    width, depth = value.shape
-    cols = coup.shape[1]
-    return pl.pallas_call(
-        mid_coupling_kernel,
-        grid=(steps,),
-        in_specs=[
-            pl.BlockSpec((width, depth), lambda s: (0, 0)),
-            pl.BlockSpec((depth, cols // steps), lambda s: (0, s)),
-        ],
-        out_specs=pl.BlockSpec((width, cols // steps), lambda s: (0, s)),
-        out_shape=jax.ShapeDtypeStruct((width, cols), F32),
-        compiler_params=params(),
-        cost_estimate=cost(cols, depth, width),
-    )(value, coup)
-
-
-def leaf_kernel(dims, order_ref, value_ref, matrix_ref, out_ref):
-    product = lax.dot_general(value_ref[...], matrix_ref[...], dims, preferred_element_type=F32)
-    out_ref[0] = product.astype(out_ref.dtype)
-
-
-def leaf_product(order, start, dims, value, matrix, cols, kind):
+        cost_estimate=cost(2 * depth, depth, width),
+    )(order, keep, got, far, rhs, matrix, *after)
+
+
+def leaf_rest_kernel(dims, order_ref, value_ref, matrix_ref, out_ref):
+    out_ref[0] = lax.dot_general(value_ref[...], matrix_ref[...], dims, preferred_element_type=F32)
+
+
+def leaf_rest(order, dims, value, matrix, cols):
     width, depth = value.shape
     if dims is NN:
-        spec = pl.BlockSpec((depth, cols), lambda s, order: (0, order[start + s]))
+        spec = pl.BlockSpec((depth, cols), lambda s, order: (0, order[2 + s]))
     else:
-        spec = pl.BlockSpec((cols, depth), lambda s, order: (order[start + s], 0))
+        spec = pl.BlockSpec((cols, depth), lambda s, order: (order[2 + s], 0))
     return pl.pallas_call(
-        functools.partial(leaf_kernel, dims),
+        functools.partial(leaf_rest_kernel, dims),
         grid_spec=pltpu.PrefetchScalarGridSpec(
             num_scalar_prefetch=1,
             grid=(2,),
             in_specs=[pl.BlockSpec((width, depth), lambda s, order: (0, 0)), spec],
             out_specs=pl.BlockSpec((1, width, cols), lambda s, order: (s, 0, 0)),
         ),
-        out_shape=jax.ShapeDtypeStruct((2, width, cols), kind),
+        out_shape=jax.ShapeDtypeStruct((2, width, cols), F32),
         compiler_params=params(),
         cost_estimate=cost(2 * cols, depth, width),
     )(order, value, matrix)
 
 
+def leaf_finish_kernel(*refs):
+    *terms, out_ref = refs
+    sums = [
+        terms[3 * n][0] + terms[3 * n + 1][0].astype(F32) + terms[3 * n + 2][...].astype(F32)
+        for n in range(len(terms) // 3)
+    ]
+    out_ref[0] = jnp.concatenate([part.astype(BF16) for part in sums], axis=0).T
+
+
+def leaf_finish(terms):
+    _, width, rows = terms[0][0].shape
+    one = pl.BlockSpec((1, width, rows), lambda s: (0, 0, 0))
+    flat = [part for chain in terms for part in chain]
+    return pl.pallas_call(
+        leaf_finish_kernel,
+        grid=(1,),
+        in_specs=[one, one, pl.BlockSpec((width, rows), lambda s: (0, 0))] * len(terms),
+        out_specs=pl.BlockSpec((1, rows, width * len(terms)), lambda s: (0, 0, 0)),
+        out_shape=jax.ShapeDtypeStruct((1, rows, width * len(terms)), BF16),
+        compiler_params=params(),
+    )(*flat)
+
+
 def swap(value, axis, mask):
     return lax.ppermute(value, axis, [(i, i ^ mask) for i in range(lax.axis_size(axis))])
 
@@ -496,14 +696,20 @@
     return functools.reduce(jnp.add, [t.astype(F32) for t in terms])
 
 
-def reduce_columns(send, keep, bits):
-    got = swap(send, "col", bits[0])
-    for bit in bits[1:]:
-        half = got.shape[0] // 2
-        send = add(keep[half:], got[half:]).astype(BF16)
-        keep = add(keep[:half], got[:half])
+def reduce_columns(send, keep, bits, early, step):
+    for i, bit in enumerate(bits):
         got = swap(send, "col", bit)
-    return add(keep, got).astype(BF16)
+        if i == step:
+            got, early = lax.optimization_barrier((got, early))
+        if i < len(bits) - 1:
+            half = got.shape[0] // 2
+            send = add(keep[half:], got[half:]).astype(BF16)
+            keep = add(keep[:half], got[:half])
+    return add(keep, got).astype(BF16), early
+
+
+def turn_columns(values, turn):
+    return lax.switch(turn, [lambda *v, k=k: tuple(swap(part, "col", k) for part in v) for k in range(1, 8)], *values)
 
 
 def gather_columns(value, bits):
@@ -553,52 +759,83 @@
         in_specs=[SMEM] * 4,
         out_specs=SMEM,
         scratch_shapes=[pltpu.SMEM((4 * local,), jnp.int32)] * 2
-        + [pltpu.SMEM((len(CHAINS), 4 * local), jnp.int32)],
+        + [pltpu.SMEM((len(CHAINS), 4 * local), jnp.int32), pltpu.SMEM((2 * local,), jnp.int32)],
     )(place, bounds_mid, bounds_leaf, parents)
 
-    within = jnp.arange(slot, dtype=jnp.int32)
+    half = local // 2
     leaf_order = jnp.stack([2 * x + 1 - h, 2 * (1 - x) + 1 - h, 2 * x + h, 2 * (1 - x) + h]).astype(jnp.int32)
-    mid_rhs = lax.dynamic_index_in_dim(rhs_mid, x, 0, keepdims=False).T
-    leaf_rhs = rhs_leaf[0].T
     leaf_cols = coup_leaf.shape[2] // 4
-    sent = root_product(order, rhs_root.T, dinv_root)
-
-    def reduce_rows(dims, value, matrix):
-        send = leaf_product(leaf_order, 0, dims, value, matrix, leaf_cols, BF16)
-        keep = leaf_product(leaf_order, 2, dims, value, matrix, leaf_cols, F32)
+
+    halves = root_product(order, rhs_root, dinv_root)
+    boundary = []
+    for n in chains:
+        got, plan = reduce_columns(*halves[n], CHAINS[n], plan, 0)
+        picked = gather(plan, n, at["select"], slot, (got, swap(got, "row", 1), swap(got, "row", 2)))
+        own = gather_columns(picked, CHAINS[n])
+        boundary.append((own, swap(own, "row", 1)))
+
+    term, half_term = mid_coupling(plan, at["mid"], [part for pair in boundary for part in pair], coup_mid)
+    asked = [
+        swap(gather(plan, n, at["send_root"], leaf_slots + slot, boundary[n], (half_term,)), "row", 2)
+        for n in chains
+    ]
+    first, shift = mid_first(x, term, swap(half_term, "row", 1), rhs_mid, dinv_mid)
+    rest = mid_rest(shift, dinv_mid)
+    products = (first, rest, swap(first, "row", 1), swap(rest, "row", 1))
+    width = shift.shape[0] // 2
+    root_values, mid_parts, mine, away = [], [], [], []
+    child = parents[col_id] == x
+    for n in chains:
+        part = (n * width, width)
+        send = gather(plan, n, at["mid_order"] + half, half, products, part=part)
+        keep = gather(plan, n, at["mid_order"], half, products, part=part)
+        got, asked[n] = reduce_columns(send, keep, CHAINS[n], asked[n], 2)
+        root_values.append(gather(plan, n, at["out"], slot, (*boundary[n], asked[n])))
+        mid_parts.append(got)
+        other = swap(got, "row", 2)
+        mine.append(jnp.where(child, got, other))
+        away.append(jnp.where(child, other, got))
+    back = turn_columns(away, plan[0, at["turn"]])
+    sources = []
+    for n in chains:
+        own = jnp.concatenate([mine[n], back[n]], axis=0)
+        sources.append((*boundary[n], asked[n], own, swap(own, "row", 1)))
+
+    def spread(step):
+        for n in chains:
+            mid_parts[n] = jnp.concatenate([mid_parts[n], swap(mid_parts[n], "col", CHAINS[n][2 - step])], axis=0)
+
+    def join(value):
+        value, mid_parts[:] = lax.optimization_barrier((value, list(mid_parts)))
+        return value
+
+    coup, inverse = coup_leaf[0], dinv_leaf[0]
+    after = ()
+    sums = []
+    for n in chains:
+        spread(n)
+        send, bound = leaf_first(plan, n, at["leaf"], leaf_slots, sources[n], leaf_order, coup, leaf_cols, after)
+        send = join(send)
         got = swap(send, "row", 1)
-        far = swap(add(keep[1], got[1]).astype(BF16), "row", 2)
-        return add(keep[0], got[0], far)
-
-    def chain(n):
-        bits = CHAINS[n]
-        got = reduce_columns(*sent[n], bits)
-        picked = gather(plan, n, at["select"], slot, got, swap(got, "row", 1), swap(got, "row", 2))
-        own = gather_columns(picked, bits)
-        sib = swap(own, "row", 1)
-        bound = gather(plan, n, at["mid"], local, own, sib, wide=True)
-        asked = swap(gather(plan, n, at["send_root"], leaf_slots + slot, own, sib), "row", 2)
-        root_out = gather(plan, n, at["out"], slot, own, sib, asked)
-
-        term = mid_coupling(bound, coup_mid)
-        width = term.shape[0]
-        rhs = mid_rhs[n * width : (n + 1) * width]
-        shift = (rhs - (term + swap(term, "row", 1))).astype(BF16)
-        mid_order = jnp.concatenate([chip * slot + within for chip in chips_in_order(col_id, bits)])
-        mid_out = reduce_columns(*mid_product(mid_order.astype(jnp.int32), shift, dinv_mid), bits)
-        mid_own = gather_columns(mid_out, bits)
-        mid_sib = swap(mid_own, "row", 1)
-        mid_asked = swap(gather(plan, n, at["send_mid"], leaf_slots, mid_own, mid_sib), "row", 2)
-
-        sources = (own, sib, asked, mid_own, mid_sib, mid_asked)
-        bound = gather(plan, n, at["leaf"], leaf_slots, *sources, wide=True)
-        rhs = leaf_rhs[n * width : (n + 1) * width]
-        shift = (rhs - reduce_rows(NN, bound, coup_leaf[0])).astype(BF16)
-        leaf_out = reduce_rows(NT, shift, dinv_leaf[0]).astype(BF16)
-        return root_out, mid_out, leaf_out
-
-    root_values, mid_values, leaf_values = zip(*[chain(n) for n in chains])
-    return (natural(root_values), natural(mid_values), jnp.concatenate(leaf_values, axis=0).T[None])
+        keep = leaf_rest(leaf_order, NN, bound, coup, leaf_cols)
+        part = add(keep[1], got[1]).astype(BF16)
+        sums.append((keep, got, swap(part, "row", 2)))
+        after = (part,)
+    ends = []
+    for n in chains:
+        if n == 0:
+            spread(2)
+        else:
+            mid_parts[:] = [(own, swap(own, "row", 1)) for own in mid_parts]
+        send, shift = leaf_shift(n, leaf_order, *sums[n], rhs_leaf, inverse, after)
+        send = join(send)
+        got = swap(send, "row", 1)
+        keep = leaf_rest(leaf_order, NT, shift, inverse, leaf_cols)
+        part = add(keep[1], got[1]).astype(BF16)
+        ends.append((keep, got, swap(part, "row", 2)))
+        after = (part,)
+    mid_values = [gather(plan, n, at["mid_out"], slot, mid_parts[n]) for n in chains]
+    return (natural(root_values), natural(mid_values), leaf_finish(ends))
 
 
 def solution(mesh):

time: 413 us -> 350 us (0.85)
  waiting for transfers between devices: 233 us -> 156 us
  starting transfers between devices: 37.1 us -> 46 us
  other arithmetic: 17.8 us -> 25.5 us
  local copies, waits for them, and re-layouts: 18 us -> 11.7 us
    ppermute x46 -> x51, waiting for transfers between devices: 233 us -> 156 us  [swap(): lax.ppermute(value, axis, [(i, i ^ mask) for i in range(lax.axis_size(axi...]
    convert_element_type x12 -> x8, other arithmetic: 14 us -> 4.06 us  [the longest x4 2.82 us: reduce_columns(): return (add(keep, got).astype(BF16), early)]
    concatenate x0 -> x8, other arithmetic: none -> 9.76 us  [the longest x6 7.74 us: spread(): jnp.concatenate([mid_parts[n], swap(mid_parts[n], 'col', CHAINS[n][2 - st...]
    ppermute x46 -> x51, starting transfers between devices: 37.1 us -> 46 us  [swap(): lax.ppermute(value, axis, [(i, i ^ mask) for i in range(lax.axis_size(axi...]
    unnamed x73 -> x64, local copies, waits for them, and re-layouts: 13.5 us -> 7.73 us
    convert_element_type x8, other arithmetic: 1.94 us -> 7.27 us  [reduce_columns(): send = add(keep[half:], got[half:]).astype(BF16)]
  transfers between devices with their start and end apart: 46 -> 51, of which waited for: 31 -> 33; matrix products, arithmetic and copies ran while one was open for 4% -> 8% of each run, Pallas kernels for 19% -> 16%
where the time goes in v3:
time: 350 us
  waiting for transfers between devices  156 us (45%)
  Pallas kernels  109 us (31%)
  starting transfers between devices  46 us (13%)
  other arithmetic  25.5 us (7%)
  local copies, waits for them, and re-layouts  11.7 us (3%)
    ppermute x51, waiting for transfers between devices, swap(): lax.ppermute(value, axis, [(i, i ^ mask) for i in range(lax.axis_size(axi...  156 us
    ppermute x51, starting transfers between devices, swap(): lax.ppermute(value, axis, [(i, i ^ mask) for i in range(lax.axis_size(axi...  46 us
    pallas_call x12, Pallas kernels, gather(): pl.pallas_call(functools.partial(gather_kernel, chain, start, count, len(...  24.4 us
    pallas_call x4, Pallas kernels, leaf_rest(): pl.pallas_call(functools.partial(leaf_rest_kernel, dims), grid_spec=pltpu...  16.2 us
    pallas_call x1, Pallas kernels, root_product(): pl.pallas_call(functools.partial(root_product_kernel, parts), grid_spec=p...  13.5 us
    pallas_call x1, Pallas kernels, shards(): pl.pallas_call(functools.partial(plan_kernel, local, slot, leaf_slots), o...  12.7 us
    pallas_call x2, Pallas kernels, leaf_first(): pl.pallas_call(functools.partial(leaf_first_kernel, chain, start, count,...  11 us
    pallas_call x1, Pallas kernels, mid_coupling(): pl.pallas_call(functools.partial(mid_coupling_kernel, start, count), grid...  9.87 us
  transfers between devices with their start and end apart: 51, of which 33 were waited for; matrix products, arithmetic and copies ran while one was open for 8% of the time, Pallas kernels for 16%

profile of v3, /device:TPU:0, one launch (start us, length us, event | category | flops | bytes accessed | tf_op | source)
XLA Modules:
  0.0 350.5 jit_solution(3470609563007139579)
XLA Ops:
  1.2 2.5 shard_map.130.order_ref
  4.4 13.5 %shard_map.131 = (bf16[16,192,128]{2,1,0:T(8,128)(2,1)}, f32[16,192,128]{2,1,0:T(8,128)S(1)}, bf16[16,192,128]{2,1,0:T(8,128)(2,1)}, f32[16,192,128]{2,1,0:T(8,128)S(1)}) custom-call(s32[32]{0:T(128)S(1)} %copy-done.22, bf16[2048,384]{1,0:T(8,128)(2,1)} %value_ref.1, bf16[4096,2048]{1,0:T(8,128)(2,1)} %refs_7_.1, bf16[4096,2048]{1,0:T(8,128)(2,1)} %refs_7_.1, ...), custom_call_target="tpu_custom_call" | custom-call | flops 6442450944 | bytes 16777216 | tf_op jit(solution)/shard_map/pallas_call | solution.py:444
  17.9 3.0 collective-permute-start.15
  20.9 1.6 collective-permute-start.14
  22.5 12.7 %shard_map.132.table_ref = s32[2,105]{1,0:T(2,128)} custom-call(s32[2]{0:T(128)} %pad_add_fusion.place_ref, s32[2,64]{1,0:T(2,128)} %bounds_ref.3, s32[8,48]{1,0:T(8,128)} %leaf_ref.1, s32[8]{0:T(128)} %parents_ref.1), custom_call_target="tpu_custom_call" | custom-call | tf_op jit(solution)/shard_map/pallas_call | solution.py:756
  35.2 3.8 %collective-permute-done.15 = bf16[16,192,128]{2,1,0:T(8,128)(2,1)} collective-permute-done((bf16[16,192,128]{2,1,0:T(8,128)(2,1)}, bf16[16,192,128]{2,1,0:T(8,128)(2,1)}, u32[]{:S(2)}, u32[]{:S(2)}) %collective-permute-start.15) | collective-permute-done | bytes 786464 | tf_op jit(solution)/shard_map/ppermute | solution.py:692
  41.7 1.6 collective-permute-start.16
  45.2 6.4 %collective-permute-done.16 = bf16[8,192,128]{2,1,0:T(8,128)(2,1)S(1)} collective-permute-done((bf16[8,192,128]{2,1,0:T(8,128)(2,1)S(1)}, bf16[8,192,128]{2,1,0:T(8,128)(2,1)S(1)}, u32[]{:S(2)}, u32[]{:S(2)}) %collective-permute-start.16) | collective-permute-done | bytes 393248 | tf_op jit(solution)/shard_map/ppermute | solution.py:692
  51.7 2.7 collective-permute-start.17
  54.4 2.6 collective-permute-start.25
  57.0 10.0 %collective-permute-done.17 = bf16[4,192,128]{2,1,0:T(8,128)(2,1)S(1)} collective-permute-done((bf16[4,192,128]{2,1,0:T(8,128)(2,1)S(1)}, bf16[4,192,128]{2,1,0:T(8,128)(2,1)S(1)}, u32[]{:S(2)}, u32[]{:S(2)}) %collective-permute-start.17) | collective-permute-done | bytes 196640 | tf_op jit(solution)/shard_map/ppermute | solution.py:692
  67.1 2.0 collective-permute-start.19
  70.1 1.9 collective-permute-start.27
  74.4 2.6 collective-permute-done.27.refs_2_
  78.3 12.4 %collective-permute-done.20 = bf16[4,192,128]{2,1,0:T(8,128)(2,1)S(1)} collective-permute-done((bf16[4,192,128]{2,1,0:T(8,128)(2,1)S(1)}, bf16[4,192,128]{2,1,0:T(8,128)(2,1)S(1)}, u32[]{:S(2)}, u32[]{:S(2)}) %collective-permute-start.20) | collective-permute-done | bytes 196640 | tf_op jit(solution)/shard_map/ppermute | solution.py:692
  90.8 3.2 collective-permute-done.28
  94.8 7.5 %collective-permute-done.21 = bf16[8,192,128]{2,1,0:T(8,128)(2,1)S(1)} collective-permute-done((bf16[8,192,128]{2,1,0:T(8,128)(2,1)S(1)}, bf16[8,192,128]{2,1,0:T(8,128)(2,1)S(1)}, u32[]{:S(2)}, u32[]{:S(2)}) %collective-permute-start.21) | collective-permute-done | bytes 393248 | tf_op jit(solution)/shard_map/ppermute | solution.py:692
  104.3 17.2 %collective-permute-done.22 = bf16[16,192,128]{2,1,0:T(8,128)(2,1)S(1)} collective-permute-done((bf16[16,192,128]{2,1,0:T(8,128)(2,1)S(1)}, bf16[16,192,128]{2,1,0:T(8,128)(2,1)S(1)}, u32[]{:S(2)}, u32[]{:S(2)}) %collective-permute-start.22) | collective-permute-done | bytes 786464 | tf_op jit(solution)/shard_map/ppermute | solution.py:692
  122.5 2.7 collective-permute-done.23.refs_1_
  125.1 2.2 collective-permute-done.31.refs_3_.refs_1_
  128.5 9.9 %shard_map.135 = (f32[384,1024]{1,0:T(8,128)S(1)}, bf16[384,1024]{1,0:T(8,128)(2,1)}) custom-call(s32[2,105]{1,0:T(2,128)S(1)} %copy-done.21, bf16[32,192,128]{2,1,0:T(8,128)(2,1)S(1)} %pad_maximum_fusion.refs_0_, bf16[32,192,128]{2,1,0:T(8,128)(2,1)S(1)} %collective-permute-done.23.refs_1_, bf16[32,192,128]{2,1,0:T(8,128)(2,1)} %copy-done, ...), custom_call_target="tpu_custom_call" | custom-call | flops 3221225472 | bytes 8388608 | tf_op jit(solution)/shard_map/pallas_call | solution.py:545
  139.7 2.4 collective-permute-done.32.got_ref
  143.5 4.2 %shard_map.136 = (bf16[16,384,128]{2,1,0:T(8,128)(2,1)S(1)}, bf16[384,1024]{1,0:T(8,128)(2,1)S(1)}) custom-call(s32[1]{0:T(128)} %bitcast.2.front_ref, f32[384,1024]{1,0:T(8,128)S(1)} %copy-done.20, bf16[384,1024]{1,0:T(8,128)(2,1)S(1)} %collective-permute-done.32.got_ref, bf16[2,1024,384]{2,1,0:T(8,128)(2,1)} %rhs_ref.3, bf16[4096,1024]{1,0:T(8,128)(2,1)} %matrix_ref.3), custom_call_target="tpu_custom_call" | custom-call | flops 1610612736 | bytes 4194304 | tf_op jit(solution)/shard_map/pallas_call | solution.py:481
  147.6 3.7 %shard_map.137.refs_1_ = bf16[16,384,128]{2,1,0:T(8,128)(2,1)S(1)} custom-call(bf16[384,1024]{1,0:T(8,128)(2,1)S(1)} %get-tuple-element.96.shift_ref, bf16[4096,1024]{1,0:T(8,128)(2,1)} %matrix_ref.3), custom_call_target="tpu_custom_call" | custom-call | flops 1610612736 | bytes 4194304 | tf_op jit(solution)/shard_map/pallas_call | solution.py:506
  151.9 2.9 collective-permute-done.34.refs_3_
  154.8 2.2 collective-permute-done.33.refs_2_
  157.0 2.6 shard_map.139
  160.4 2.5 shard_map.143
  163.0 2.9 shard_map.140
  166.0 2.8 shard_map.142
  168.8 2.6 shard_map.138
  171.4 7.7 %collective-permute-done.35 = bf16[16,192,128]{2,1,0:T(8,128)(2,1)S(1)} collective-permute-done((bf16[16,192,128]{2,1,0:T(8,128)(2,1)S(1)}, bf16[16,192,128]{2,1,0:T(8,128)(2,1)S(1)}, u32[]{:S(2)}, u32[]{:S(2)}) %collective-permute-start.35) | collective-permute-done | bytes 786464 | tf_op jit(solution)/shard_map/ppermute | solution.py:692
  184.1 2.8 shard_map.144
  193.9 2.1 collective-permute-start.41
  196.0 10.6 %collective-permute-done.37 = bf16[4,192,128]{2,1,0:T(8,128)(2,1)S(1)} collective-permute-done((bf16[4,192,128]{2,1,0:T(8,128)(2,1)S(1)}, bf16[4,192,128]{2,1,0:T(8,128)(2,1)S(1)}, u32[]{:S(2)}, u32[]{:S(2)}) %collective-permute-start.37) | collective-permute-done | bytes 196640 | tf_op jit(solution)/shard_map/ppermute | solution.py:692
  206.6 1.7 fusion.9
  208.3 1.6 collective-permute-start.44
  211.4 6.3 %collective-permute-start.43 = (bf16[4,192,128]{2,1,0:T(8,128)(2,1)S(1)}, bf16[4,192,128]{2,1,0:T(8,128)(2,1)S(1)}, u32[]{:S(2)}, u32[]{:S(2)}) collective-permute-start(bf16[4,192,128]{2,1,0:T(8,128)(2,1)S(1)} %fusion.11), channel_id=1, source_target_pairs={{0,16},{8,24},{16,0},{24,8},{1,17},{9,25},{17,1},{25,9},{2,18},{10... | collective-permute-start | bytes 589832 | tf_op jit(solution)/shard_map/ppermute | solution.py:692
  217.8 1.7 broadcast_select_fusion
  219.4 3.3 collective-permute-done.43
  223.4 18.7 %conditional.1 = (bf16[4,192,128]{2,1,0:T(8,128)(2,1)}, bf16[4,192,128]{2,1,0:T(8,128)(2,1)}) conditional(s32[]{:T(128)} %bitcast.10, (bf16[4,192,128]{2,1,0:T(8,128)(2,1)S(1)}, bf16[4,192,128]{2,1,0:T(8,128)(2,1)S(1)}) %tuple.48, (bf16[4,192,128]{2,1,0:T(8,128)(2,1)S(1)}, ...), branch_computations={%region_0.1_spmd, %region_1.2_spmd, %region_2.3_spmd, %region_3.4_... | conditional | bytes 1572960 | solution.py:712
  223.4 3.8 %collective-permute-start.9 = (bf16[4,192,128]{2,1,0:T(8,128)(2,1)S(1)}, bf16[4,192,128]{2,1,0:T(8,128)(2,1)}, u32[]{:S(2)}, u32[]{:S(2)}) collective-permute-start(bf16[4,192,128]{2,1,0:T(8,128)(2,1)S(1)} %get-tuple-element.37), channel_id=1, source_target_pairs={{0,5},{1,4},{2,7},{3,6},{4,1},{5,0},{6,3},{7,2},{8,13},{9,12},{10,... | collective-permute-start | bytes 589832 | tf_op jit(solution)/shard_map/cond/branch_4_fun/ppermute | solution.py:692
  227.2 10.8 %collective-permute-done.8 = bf16[4,192,128]{2,1,0:T(8,128)(2,1)} collective-permute-done((bf16[4,192,128]{2,1,0:T(8,128)(2,1)S(1)}, bf16[4,192,128]{2,1,0:T(8,128)(2,1)}, u32[]{:S(2)}, u32[]{:S(2)}) %collective-permute-start.8) | collective-permute-done | bytes 196640 | tf_op jit(solution)/shard_map/cond/branch_4_fun/ppermute | solution.py:692
  238.0 4.1 %collective-permute-done.9 = bf16[4,192,128]{2,1,0:T(8,128)(2,1)} collective-permute-done((bf16[4,192,128]{2,1,0:T(8,128)(2,1)S(1)}, bf16[4,192,128]{2,1,0:T(8,128)(2,1)}, u32[]{:S(2)}, u32[]{:S(2)}) %collective-permute-start.9) | collective-permute-done | bytes 196640 | tf_op jit(solution)/shard_map/cond/branch_4_fun/ppermute | solution.py:692
  244.6 11.0 %collective-permute-done.48 = bf16[4,192,128]{2,1,0:T(8,128)(2,1)S(1)} collective-permute-done((bf16[4,192,128]{2,1,0:T(8,128)(2,1)}, bf16[4,192,128]{2,1,0:T(8,128)(2,1)S(1)}, u32[]{:S(2)}, u32[]{:S(2)}) %collective-permute-start.48) | collective-permute-done | bytes 196640 | tf_op jit(solution)/shard_map/ppermute | solution.py:692
  256.6 5.5 %shard_map.146 = (bf16[2,192,1024]{2,1,0:T(8,128)(2,1)S(1)}, bf16[192,1536]{1,0:T(8,128)(2,1)S(1)}) custom-call(s32[2,105]{1,0:T(2,128)S(1)} %copy-done.21, s32[4]{0:T(128)S(1)} %pad_add_fusion.1.order_ref, bf16[32,192,128]{2,1,0:T(8,128)(2,1)S(1)} %pad_maximum_fusion.refs_0_, bf16[32,192,128]{2,1,0:T(8,128)(2,1)S(1)} %copy-done.4, ...), custom_call_target="tpu_custom_call" | custom-call | flops 1207959552 | bytes 6291456 | tf_op jit(solution)/shard_map/pallas_call | solution.py:577
  264.7 4.2 %shard_map.147.keep_ref = f32[2,192,1024]{2,1,0:T(8,128)S(1)} custom-call(s32[4]{0:T(128)S(1)} %pad_add_fusion.1.order_ref, bf16[192,1536]{1,0:T(8,128)(2,1)S(1)} %get-tuple-element.103.value_ref, bf16[1536,4096]{1,0:T(8,128)(2,1)} %bitcast.26), custom_call_target="tpu_custom_call" | custom-call | flops 1207959552 | bytes 6291456 | tf_op jit(solution)/shard_map/pallas_call | solution.py:654
  268.9 4.8 %collective-permute-done.50 = bf16[8,192,128]{2,1,0:T(8,128)(2,1)S(1)} collective-permute-done((bf16[8,192,128]{2,1,0:T(8,128)(2,1)S(1)}, bf16[8,192,128]{2,1,0:T(8,128)(2,1)S(1)}, u32[]{:S(2)}, u32[]{:S(2)}) %collective-permute-start.50) | collective-permute-done | bytes 393248 | tf_op jit(solution)/shard_map/ppermute | solution.py:692
  275.0 5.5 %shard_map.148 = (bf16[2,192,1024]{2,1,0:T(8,128)(2,1)S(1)}, bf16[192,1536]{1,0:T(8,128)(2,1)S(1)}) custom-call(s32[2,105]{1,0:T(2,128)S(1)} %copy-done.21, s32[4]{0:T(128)S(1)} %pad_add_fusion.1.order_ref, bf16[32,192,128]{2,1,0:T(8,128)(2,1)S(1)} %copy-done.1, bf16[32,192,128]{2,1,0:T(8,128)(2,1)} %copy-done.5, ...), custom_call_target="tpu_custom_call" | custom-call | flops 1207959552 | bytes 6291456 | tf_op jit(solution)/shard_map/pallas_call | solution.py:577
  281.7 1.6 collective-permute-start.56
  284.6 4.2 %shard_map.149.keep_ref = f32[2,192,1024]{2,1,0:T(8,128)S(1)} custom-call(s32[4]{0:T(128)S(1)} %pad_add_fusion.1.order_ref, bf16[192,1536]{1,0:T(8,128)(2,1)S(1)} %get-tuple-element.106.value_ref, bf16[1536,4096]{1,0:T(8,128)(2,1)} %bitcast.28), custom_call_target="tpu_custom_call" | custom-call | flops 1207959552 | bytes 6291456 | tf_op jit(solution)/shard_map/pallas_call | solution.py:654
  288.8 10.8 %collective-permute-done.55 = bf16[16,192,128]{2,1,0:T(8,128)(2,1)} collective-permute-done((bf16[16,192,128]{2,1,0:T(8,128)(2,1)S(1)}, bf16[16,192,128]{2,1,0:T(8,128)(2,1)}, u32[]{:S(2)}, u32[]{:S(2)}) %collective-permute-start.55) | collective-permute-done | bytes 786464 | tf_op jit(solution)/shard_map/ppermute | solution.py:692
  300.9 3.3 pad_maximum_fusion.3.refs_0_
  305.3 4.1 %shard_map.150 = (bf16[2,192,1024]{2,1,0:T(8,128)(2,1)S(1)}, bf16[192,1024]{1,0:T(8,128)(2,1)S(1)}) custom-call(s32[4]{0:T(128)S(1)} %pad_add_fusion.1.order_ref, f32[2,192,1024]{2,1,0:T(8,128)S(1)} %shard_map.147.keep_ref, bf16[2,192,1024]{2,1,0:T(8,128)(2,1)S(1)} %collective-permute-done.49.got_ref, bf16[192,1024]{1,0:T(8,128)(2,1)S(1)} %collective-permute-done.54.far_ref, ...), custom_call_target="tpu_custom_call" | custom-call | flops 805306368 | bytes 4194304 | tf_op jit(solution)/shard_map/pallas_call | solution.py:617
  311.6 3.9 %shard_map.151.refs_0_ = f32[2,192,1024]{2,1,0:T(8,128)S(1)} custom-call(s32[4]{0:T(128)S(1)} %pad_add_fusion.1.order_ref, bf16[192,1024]{1,0:T(8,128)(2,1)S(1)} %get-tuple-element.111.value_ref, bf16[4096,1024]{1,0:T(8,128)(2,1)} %bitcast.30), custom_call_target="tpu_custom_call" | custom-call | flops 805306368 | bytes 4194304 | tf_op jit(solution)/shard_map/pallas_call | solution.py:654
  316.4 5.2 %collective-permute-done.53.far_ref = bf16[192,1024]{1,0:T(8,128)(2,1)S(1)} collective-permute-done((bf16[192,1024]{1,0:T(8,128)(2,1)S(1)}, bf16[192,1024]{1,0:T(8,128)(2,1)S(1)}, u32[]{:S(2)}, u32[]{:S(2)}) %collective-permute-start.53) | collective-permute-done | bytes 393248 | tf_op jit(solution)/shard_map/ppermute | solution.py:692
  321.6 4.1 %shard_map.152 = (bf16[2,192,1024]{2,1,0:T(8,128)(2,1)S(1)}, bf16[192,1024]{1,0:T(8,128)(2,1)S(1)}) custom-call(s32[4]{0:T(128)S(1)} %pad_add_fusion.1.order_ref, f32[2,192,1024]{2,1,0:T(8,128)S(1)} %shard_map.149.keep_ref, bf16[2,192,1024]{2,1,0:T(8,128)(2,1)S(1)} %collective-permute-done.52.got_ref, bf16[192,1024]{1,0:T(8,128)(2,1)S(1)} %collective-permute-done.53.far_ref, ...), custom_call_target="tpu_custom_call" | custom-call | flops 805306368 | bytes 4194304 | tf_op jit(solution)/shard_map/pallas_call | solution.py:617
  325.8 1.5 collective-permute-start.60
  327.4 3.9 %shard_map.155.refs_3_ = f32[2,192,1024]{2,1,0:T(8,128)S(1)} custom-call(s32[4]{0:T(128)S(1)} %pad_add_fusion.1.order_ref, bf16[192,1024]{1,0:T(8,128)(2,1)S(1)} %get-tuple-element.123.value_ref, bf16[4096,1024]{1,0:T(8,128)(2,1)} %bitcast.32), custom_call_target="tpu_custom_call" | custom-call | flops 805306368 | bytes 4194304 | tf_op jit(solution)/shard_map/pallas_call | solution.py:654
  336.8 1.6 shard_map.153
  338.4 1.7 shard_map.154
  340.9 1.9 copy.15
  342.9 3.0 collective-permute-done.62.refs_5_
  348.2 2.3 shard_map.156
  (170 shorter events, 56.4 us)
Async XLA Ops:
  17.9 21.0 %collective-permute-start.15 = (bf16[16,192,128]{2,1,0:T(8,128)(2,1)}, bf16[16,192,128]{2,1,0:T(8,128)(2,1)}, u32[]{:S(2)}, u32[]{:S(2)}) collective-permute-start(bf16[16,192,128]{2,1,0:T(8,128)(2,1)} %get-tuple-element.86), channel_id=1, source_target_pairs={{0,1},{1,0},{2,3},{3,2},{4,5},{5,4},{6,7},{7,6},{8,9},{9,8},{10,11... | collective-permute-start | bytes 2359304 | tf_op jit(solution)/shard_map/ppermute | solution.py:692
  20.9 19.5 %collective-permute-start.14 = (bf16[16,192,128]{2,1,0:T(8,128)(2,1)}, bf16[16,192,128]{2,1,0:T(8,128)(2,1)}, u32[]{:S(2)}, u32[]{:S(2)}) collective-permute-start(bf16[16,192,128]{2,1,0:T(8,128)(2,1)} %get-tuple-element.85), channel_id=1, source_target_pairs={{0,2},{1,3},{2,0},{3,1},{4,6},{5,7},{6,4},{7,5},{8,10},{9,11},{10,... | collective-permute-start | bytes 2359304 | tf_op jit(solution)/shard_map/ppermute | solution.py:692
  41.7 9.9 %collective-permute-start.16 = (bf16[8,192,128]{2,1,0:T(8,128)(2,1)S(1)}, bf16[8,192,128]{2,1,0:T(8,128)(2,1)S(1)}, u32[]{:S(2)}, u32[]{:S(2)}) collective-permute-start(bf16[8,192,128]{2,1,0:T(8,128)(2,1)S(1)} %get-tuple-element.125), channel_id=1, source_target_pairs={{0,2},{1,3},{2,0},{3,1},{4,6},{5,7},{6,4},{7,5},{8,10},{9,11},{10,... | collective-permute-start | bytes 1179656 | tf_op jit(solution)/shard_map/ppermute | solution.py:692
  44.6 9.8 %collective-permute-start.24 = (bf16[8,192,128]{2,1,0:T(8,128)(2,1)S(1)}, bf16[8,192,128]{2,1,0:T(8,128)(2,1)S(1)}, u32[]{:S(2)}, u32[]{:S(2)}) collective-permute-start(bf16[8,192,128]{2,1,0:T(8,128)(2,1)S(1)} %get-tuple-element.127), channel_id=1, source_target_pairs={{0,1},{1,0},{2,3},{3,2},{4,5},{5,4},{6,7},{7,6},{8,9},{9,8},{10,11... | collective-permute-start | bytes 1179656 | tf_op jit(solution)/shard_map/ppermute | solution.py:692
  51.7 21.7 %copy-start.21 = (s32[2,105]{1,0:T(2,128)S(1)}, s32[2,105]{1,0:T(2,128)}, u32[]{:S(2)}) copy-start(s32[2,105]{1,0:T(2,128)} %shard_map.132.table_ref) | copy-start | bytes 2524
  51.7 15.3 %collective-permute-start.17 = (bf16[4,192,128]{2,1,0:T(8,128)(2,1)S(1)}, bf16[4,192,128]{2,1,0:T(8,128)(2,1)S(1)}, u32[]{:S(2)}, u32[]{:S(2)}) collective-permute-start(bf16[4,192,128]{2,1,0:T(8,128)(2,1)S(1)} %fusion.17), channel_id=1, source_target_pairs={{0,4},{1,5},{2,6},{3,7},{4,0},{5,1},{6,2},{7,3},{8,12},{9,13},{10,... | collective-permute-start | bytes 589832 | tf_op jit(solution)/shard_map/ppermute | solution.py:692
  54.4 15.6 %collective-permute-start.25 = (bf16[4,192,128]{2,1,0:T(8,128)(2,1)S(1)}, bf16[4,192,128]{2,1,0:T(8,128)(2,1)S(1)}, u32[]{:S(2)}, u32[]{:S(2)}) collective-permute-start(bf16[4,192,128]{2,1,0:T(8,128)(2,1)S(1)} %fusion.14), channel_id=1, source_target_pairs={{0,4},{1,5},{2,6},{3,7},{4,0},{5,1},{6,2},{7,3},{8,12},{9,13},{10,... | collective-permute-start | bytes 589832 | tf_op jit(solution)/shard_map/ppermute | solution.py:692
  67.1 6.3 %collective-permute-start.19 = (bf16[4,192,128]{2,1,0:T(8,128)(2,1)S(1)}, bf16[4,192,128]{2,1,0:T(8,128)(2,1)S(1)}, u32[]{:S(2)}, u32[]{:S(2)}) collective-permute-start(bf16[4,192,128]{2,1,0:T(8,128)(2,1)S(1)} %fusion.19.refs_0_), channel_id=1, source_target_pairs={{0,16},{8,24},{16,0},{24,8},{1,17},{9,25},{17,1},{25,9},{2,18},{10... | collective-permute-start | bytes 589832 | tf_op jit(solution)/shard_map/ppermute | solution.py:692
  69.0 4.3 %collective-permute-start.18 = (bf16[4,192,128]{2,1,0:T(8,128)(2,1)S(1)}, bf16[4,192,128]{2,1,0:T(8,128)(2,1)S(1)}, u32[]{:S(2)}, u32[]{:S(2)}) collective-permute-start(bf16[4,192,128]{2,1,0:T(8,128)(2,1)S(1)} %fusion.19.refs_0_), channel_id=1, source_target_pairs={{0,8},{8,0},{16,24},{24,16},{1,9},{9,1},{17,25},{25,17},{2,10},{10... | collective-permute-start | bytes 589832 | tf_op jit(solution)/shard_map/ppermute | solution.py:692
  70.1 6.9 %collective-permute-start.27 = (bf16[4,192,128]{2,1,0:T(8,128)(2,1)S(1)}, bf16[4,192,128]{2,1,0:T(8,128)(2,1)S(1)}, u32[]{:S(2)}, u32[]{:S(2)}) collective-permute-start(bf16[4,192,128]{2,1,0:T(8,128)(2,1)S(1)} %fusion.16.refs_0_), channel_id=1, source_target_pairs={{0,16},{8,24},{16,0},{24,8},{1,17},{9,25},{17,1},{25,9},{2,18},{10... | collective-permute-start | bytes 589832 | tf_op jit(solution)/shard_map/ppermute | solution.py:692
  72.0 5.0 %collective-permute-start.26 = (bf16[4,192,128]{2,1,0:T(8,128)(2,1)S(1)}, bf16[4,192,128]{2,1,0:T(8,128)(2,1)S(1)}, u32[]{:S(2)}, u32[]{:S(2)}) collective-permute-start(bf16[4,192,128]{2,1,0:T(8,128)(2,1)S(1)} %fusion.16.refs_0_), channel_id=1, source_target_pairs={{0,8},{8,0},{16,24},{24,16},{1,9},{9,1},{17,25},{25,17},{2,10},{10... | collective-permute-start | bytes 589832 | tf_op jit(solution)/shard_map/ppermute | solution.py:692
  74.3 16.4 %collective-permute-start.20 = (bf16[4,192,128]{2,1,0:T(8,128)(2,1)S(1)}, bf16[4,192,128]{2,1,0:T(8,128)(2,1)S(1)}, u32[]{:S(2)}, u32[]{:S(2)}) collective-permute-start(bf16[4,192,128]{2,1,0:T(8,128)(2,1)S(1)} %shard_map.133), channel_id=1, source_target_pairs={{0,4},{1,5},{2,6},{3,7},{4,0},{5,1},{6,2},{7,3},{8,12},{9,13},{10,... | collective-permute-start | bytes 589832 | tf_op jit(solution)/shard_map/ppermute | solution.py:692
  77.9 16.1 %collective-permute-start.28 = (bf16[4,192,128]{2,1,0:T(8,128)(2,1)S(1)}, bf16[4,192,128]{2,1,0:T(8,128)(2,1)S(1)}, u32[]{:S(2)}, u32[]{:S(2)}) collective-permute-start(bf16[4,192,128]{2,1,0:T(8,128)(2,1)S(1)} %shard_map.134), channel_id=1, source_target_pairs={{0,4},{1,5},{2,6},{3,7},{4,0},{5,1},{6,2},{7,3},{8,12},{9,13},{10,... | collective-permute-start | bytes 589832 | tf_op jit(solution)/shard_map/ppermute | solution.py:692
  90.7 11.6 %collective-permute-start.21 = (bf16[8,192,128]{2,1,0:T(8,128)(2,1)S(1)}, bf16[8,192,128]{2,1,0:T(8,128)(2,1)S(1)}, u32[]{:S(2)}, u32[]{:S(2)}) collective-permute-start(bf16[8,192,128]{2,1,0:T(8,128)(2,1)S(1)} %pad_maximum_fusion.8), channel_id=1, source_target_pairs={{0,2},{1,3},{2,0},{3,1},{4,6},{5,7},{6,4},{7,5},{8,10},{9,11},{10,... | collective-permute-start | bytes 1179656 | tf_op jit(solution)/shard_map/ppermute | solution.py:692
  94.0 10.1 %collective-permute-start.29 = (bf16[8,192,128]{2,1,0:T(8,128)(2,1)S(1)}, bf16[8,192,128]{2,1,0:T(8,128)(2,1)S(1)}, u32[]{:S(2)}, u32[]{:S(2)}) collective-permute-start(bf16[8,192,128]{2,1,0:T(8,128)(2,1)S(1)} %pad_maximum_fusion.9), channel_id=1, source_target_pairs={{0,1},{1,0},{2,3},{3,2},{4,5},{5,4},{6,7},{7,6},{8,9},{9,8},{10,11... | collective-permute-start | bytes 1179656 | tf_op jit(solution)/shard_map/ppermute | solution.py:692
  102.4 19.1 %collective-permute-start.22 = (bf16[16,192,128]{2,1,0:T(8,128)(2,1)S(1)}, bf16[16,192,128]{2,1,0:T(8,128)(2,1)S(1)}, u32[]{:S(2)}, u32[]{:S(2)}) collective-permute-start(bf16[16,192,128]{2,1,0:T(8,128)(2,1)S(1)} %pad_maximum_fusion.4), channel_id=1, source_target_pairs={{0,1},{1,0},{2,3},{3,2},{4,5},{5,4},{6,7},{7,6},{8,9},{9,8},{10,11... | collective-permute-start | bytes 2359304 | tf_op jit(solution)/shard_map/ppermute | solution.py:692
  104.2 17.9 %collective-permute-start.30 = (bf16[16,192,128]{2,1,0:T(8,128)(2,1)S(1)}, bf16[16,192,128]{2,1,0:T(8,128)(2,1)S(1)}, u32[]{:S(2)}, u32[]{:S(2)}) collective-permute-start(bf16[16,192,128]{2,1,0:T(8,128)(2,1)S(1)} %pad_maximum_fusion.5), channel_id=1, source_target_pairs={{0,2},{1,3},{2,0},{3,1},{4,6},{5,7},{6,4},{7,5},{8,10},{9,11},{10,... | collective-permute-start | bytes 2359304 | tf_op jit(solution)/shard_map/ppermute | solution.py:692
  121.6 3.5 collective-permute-start.23
  122.2 5.1 %collective-permute-start.31 = (bf16[32,192,128]{2,1,0:T(8,128)(2,1)S(1)}, bf16[32,192,128]{2,1,0:T(8,128)(2,1)S(1)}, u32[]{:S(2)}, u32[]{:S(2)}) collective-permute-start(bf16[32,192,128]{2,1,0:T(8,128)(2,1)S(1)} %pad_maximum_fusion.1.refs_2_.refs_0_), channel_id=1, source_target_pairs={{0,8},{8,0},{16,24},{24,16},{1,9},{9,1},{17,25},{25,17},{2,10},{10... | collective-permute-start | bytes 4718600 | tf_op jit(solution)/shard_map/ppermute | solution.py:692
  125.1 13.3 %copy-start.2 = (bf16[32,192,128]{2,1,0:T(8,128)(2,1)}, bf16[32,192,128]{2,1,0:T(8,128)(2,1)S(1)}, u32[]{:S(2)}) copy-start(bf16[32,192,128]{2,1,0:T(8,128)(2,1)S(1)} %collective-permute-done.23.refs_1_) | copy-start | bytes 4718596
  139.5 2.5 collective-permute-start.32
  151.3 3.5 collective-permute-start.34
  151.5 5.5 %collective-permute-start.33 = (bf16[16,384,128]{2,1,0:T(8,128)(2,1)S(1)}, bf16[16,384,128]{2,1,0:T(8,128)(2,1)S(1)}, u32[]{:S(2)}, u32[]{:S(2)}) collective-permute-start(bf16[16,384,128]{2,1,0:T(8,128)(2,1)S(1)} %get-tuple-element.95.refs_0_), channel_id=1, source_target_pairs={{0,8},{8,0},{16,24},{24,16},{1,9},{9,1},{17,25},{25,17},{2,10},{10... | collective-permute-start | bytes 4718600 | tf_op jit(solution)/shard_map/ppermute | solution.py:692
  159.7 19.4 %collective-permute-start.35 = (bf16[16,192,128]{2,1,0:T(8,128)(2,1)S(1)}, bf16[16,192,128]{2,1,0:T(8,128)(2,1)S(1)}, u32[]{:S(2)}, u32[]{:S(2)}) collective-permute-start(bf16[16,192,128]{2,1,0:T(8,128)(2,1)S(1)} %shard_map.139), channel_id=1, source_target_pairs={{0,1},{1,0},{2,3},{3,2},{4,5},{5,4},{6,7},{7,6},{8,9},{9,8},{10,11... | collective-permute-start | bytes 2359304 | tf_op jit(solution)/shard_map/ppermute | solution.py:692
  162.9 18.9 %collective-permute-start.39 = (bf16[16,192,128]{2,1,0:T(8,128)(2,1)S(1)}, bf16[16,192,128]{2,1,0:T(8,128)(2,1)S(1)}, u32[]{:S(2)}, u32[]{:S(2)}) collective-permute-start(bf16[16,192,128]{2,1,0:T(8,128)(2,1)S(1)} %shard_map.143), channel_id=1, source_target_pairs={{0,2},{1,3},{2,0},{3,1},{4,6},{5,7},{6,4},{7,5},{8,10},{9,11},{10,... | collective-permute-start | bytes 2359304 | tf_op jit(solution)/shard_map/ppermute | solution.py:692
  165.9 30.1 %collective-permute-start.38 = (bf16[16,192,128]{2,1,0:T(8,128)(2,1)}, bf16[16,192,128]{2,1,0:T(8,128)(2,1)}, u32[]{:S(2)}, u32[]{:S(2)}) collective-permute-start(bf16[16,192,128]{2,1,0:T(8,128)(2,1)} %shard_map.140), channel_id=1, source_target_pairs={{0,16},{8,24},{16,0},{24,8},{1,17},{9,25},{17,1},{25,9},{2,18},{10... | collective-permute-start | bytes 2359304 | tf_op jit(solution)/shard_map/ppermute | solution.py:692
  180.3 10.5 %collective-permute-start.36 = (bf16[8,192,128]{2,1,0:T(8,128)(2,1)}, bf16[8,192,128]{2,1,0:T(8,128)(2,1)}, u32[]{:S(2)}, u32[]{:S(2)}) collective-permute-start(bf16[8,192,128]{2,1,0:T(8,128)(2,1)} %get-tuple-element.129), channel_id=1, source_target_pairs={{0,2},{1,3},{2,0},{3,1},{4,6},{5,7},{6,4},{7,5},{8,10},{9,11},{10,... | collective-permute-start | bytes 1179656 | tf_op jit(solution)/shard_map/ppermute | solution.py:692
  183.0 9.8 %collective-permute-start.40 = (bf16[8,192,128]{2,1,0:T(8,128)(2,1)}, bf16[8,192,128]{2,1,0:T(8,128)(2,1)S(1)}, u32[]{:S(2)}, u32[]{:S(2)}) collective-permute-start(bf16[8,192,128]{2,1,0:T(8,128)(2,1)} %get-tuple-element.131), channel_id=1, source_target_pairs={{0,1},{1,0},{2,3},{3,2},{4,5},{5,4},{6,7},{7,6},{8,9},{9,8},{10,11... | collective-permute-start | bytes 1179656 | tf_op jit(solution)/shard_map/ppermute | solution.py:692
  186.9 23.0 %collective-permute-start.42 = (bf16[16,192,128]{2,1,0:T(8,128)(2,1)}, bf16[16,192,128]{2,1,0:T(8,128)(2,1)}, u32[]{:S(2)}, u32[]{:S(2)}) collective-permute-start(bf16[16,192,128]{2,1,0:T(8,128)(2,1)} %shard_map.144), channel_id=1, source_target_pairs={{0,16},{8,24},{16,0},{24,8},{1,17},{9,25},{17,1},{25,9},{2,18},{10... | collective-permute-start | bytes 2359304 | tf_op jit(solution)/shard_map/ppermute | solution.py:692
  188.5 18.2 %copy-start.27 = (f32[8,192,128]{2,1,0:T(8,128)S(1)}, f32[8,192,128]{2,1,0:T(8,128)}, u32[]{:S(2)}) copy-start(f32[8,192,128]{2,1,0:T(8,128)} %get-tuple-element.130) | copy-start | bytes 2359300
  188.5 21.9 %copy-start.26 = (f32[8,192,128]{2,1,0:T(8,128)S(1)}, f32[8,192,128]{2,1,0:T(8,128)}, u32[]{:S(2)}) copy-start(f32[8,192,128]{2,1,0:T(8,128)} %get-tuple-element.132) | copy-start | bytes 2359300
  191.8 14.8 %collective-permute-start.37 = (bf16[4,192,128]{2,1,0:T(8,128)(2,1)S(1)}, bf16[4,192,128]{2,1,0:T(8,128)(2,1)S(1)}, u32[]{:S(2)}, u32[]{:S(2)}) collective-permute-start(bf16[4,192,128]{2,1,0:T(8,128)(2,1)S(1)} %fusion.13), channel_id=1, source_target_pairs={{0,4},{1,5},{2,6},{3,7},{4,0},{5,1},{6,2},{7,3},{8,12},{9,13},{10,... | collective-permute-start | bytes 589832 | tf_op jit(solution)/shard_map/ppermute | solution.py:692
  192.8 17.2 %copy-start.30 = (bf16[8,192,128]{2,1,0:T(8,128)(2,1)}, bf16[8,192,128]{2,1,0:T(8,128)(2,1)S(1)}, u32[]{:S(2)}) copy-start(bf16[8,192,128]{2,1,0:T(8,128)(2,1)S(1)} %collective-permute-done.40) | copy-start | bytes 1179652
  193.9 16.5 %collective-permute-start.41 = (bf16[4,192,128]{2,1,0:T(8,128)(2,1)S(1)}, bf16[4,192,128]{2,1,0:T(8,128)(2,1)S(1)}, u32[]{:S(2)}, u32[]{:S(2)}) collective-permute-start(bf16[4,192,128]{2,1,0:T(8,128)(2,1)S(1)} %fusion.12), channel_id=1, source_target_pairs={{0,4},{1,5},{2,6},{3,7},{4,0},{5,1},{6,2},{7,3},{8,12},{9,13},{10,... | collective-permute-start | bytes 589832 | tf_op jit(solution)/shard_map/ppermute | solution.py:692
  208.3 35.1 %collective-permute-start.47 = (bf16[4,192,128]{2,1,0:T(8,128)(2,1)}, bf16[4,192,128]{2,1,0:T(8,128)(2,1)}, u32[]{:S(2)}, u32[]{:S(2)}) collective-permute-start(bf16[4,192,128]{2,1,0:T(8,128)(2,1)} %fusion.9), channel_id=1, source_target_pairs={{0,4},{1,5},{2,6},{3,7},{4,0},{5,1},{6,2},{7,3},{8,12},{9,13},{10,... | collective-permute-start | bytes 589832 | tf_op jit(solution)/shard_map/ppermute | solution.py:692
  208.3 9.4 %collective-permute-start.44 = (bf16[4,192,128]{2,1,0:T(8,128)(2,1)}, bf16[4,192,128]{2,1,0:T(8,128)(2,1)S(1)}, u32[]{:S(2)}, u32[]{:S(2)}) collective-permute-start(bf16[4,192,128]{2,1,0:T(8,128)(2,1)} %fusion.9), channel_id=1, source_target_pairs={{0,16},{8,24},{16,0},{24,8},{1,17},{9,25},{17,1},{25,9},{2,18},{10... | collective-permute-start | bytes 589832 | tf_op jit(solution)/shard_map/ppermute | solution.py:692
  211.4 30.7 %copy-start.28 = (bf16[4,192,128]{2,1,0:T(8,128)(2,1)}, bf16[4,192,128]{2,1,0:T(8,128)(2,1)S(1)}, u32[]{:S(2)}) copy-start(bf16[4,192,128]{2,1,0:T(8,128)(2,1)S(1)} %fusion.11) | copy-start | bytes 589828
  211.4 11.2 %collective-permute-start.43 = (bf16[4,192,128]{2,1,0:T(8,128)(2,1)S(1)}, bf16[4,192,128]{2,1,0:T(8,128)(2,1)S(1)}, u32[]{:S(2)}, u32[]{:S(2)}) collective-permute-start(bf16[4,192,128]{2,1,0:T(8,128)(2,1)S(1)} %fusion.11), channel_id=1, source_target_pairs={{0,16},{8,24},{16,0},{24,8},{1,17},{9,25},{17,1},{25,9},{2,18},{10... | collective-permute-start | bytes 589832 | tf_op jit(solution)/shard_map/ppermute | solution.py:692
  223.4 14.6 %collective-permute-start.8 = (bf16[4,192,128]{2,1,0:T(8,128)(2,1)S(1)}, bf16[4,192,128]{2,1,0:T(8,128)(2,1)}, u32[]{:S(2)}, u32[]{:S(2)}) collective-permute-start(bf16[4,192,128]{2,1,0:T(8,128)(2,1)S(1)} %get-tuple-element.36), channel_id=1, source_target_pairs={{0,5},{1,4},{2,7},{3,6},{4,1},{5,0},{6,3},{7,2},{8,13},{9,12},{10,... | collective-permute-start | bytes 589832 | tf_op jit(solution)/shard_map/cond/branch_4_fun/ppermute | solution.py:692
  223.4 18.7 %collective-permute-start.9 = (bf16[4,192,128]{2,1,0:T(8,128)(2,1)S(1)}, bf16[4,192,128]{2,1,0:T(8,128)(2,1)}, u32[]{:S(2)}, u32[]{:S(2)}) collective-permute-start(bf16[4,192,128]{2,1,0:T(8,128)(2,1)S(1)} %get-tuple-element.37), channel_id=1, source_target_pairs={{0,5},{1,4},{2,7},{3,6},{4,1},{5,0},{6,3},{7,2},{8,13},{9,12},{10,... | collective-permute-start | bytes 589832 | tf_op jit(solution)/shard_map/cond/branch_4_fun/ppermute | solution.py:692
  243.1 13.4 %collective-permute-start.46 = (bf16[8,192,128]{2,1,0:T(8,128)(2,1)S(1)}, bf16[8,192,128]{2,1,0:T(8,128)(2,1)}, u32[]{:S(2)}, u32[]{:S(2)}) collective-permute-start(bf16[8,192,128]{2,1,0:T(8,128)(2,1)S(1)} %pad_maximum_fusion.11.refs_3_), channel_id=1, source_target_pairs={{0,8},{8,0},{16,24},{24,16},{1,9},{9,1},{17,25},{25,17},{2,10},{10... | collective-permute-start | bytes 1179656 | tf_op jit(solution)/shard_map/ppermute | solution.py:692
  243.2 13.3 %copy-start.4 = (bf16[32,192,128]{2,1,0:T(8,128)(2,1)S(1)}, bf16[32,192,128]{2,1,0:T(8,128)(2,1)}, u32[]{:S(2)}) copy-start(bf16[32,192,128]{2,1,0:T(8,128)(2,1)} %copy-done.2) | copy-start | bytes 4718596
  243.2 12.3 %collective-permute-start.48 = (bf16[4,192,128]{2,1,0:T(8,128)(2,1)}, bf16[4,192,128]{2,1,0:T(8,128)(2,1)S(1)}, u32[]{:S(2)}, u32[]{:S(2)}) collective-permute-start(bf16[4,192,128]{2,1,0:T(8,128)(2,1)} %copy-done.28), channel_id=1, source_target_pairs={{0,4},{1,5},{2,6},{3,7},{4,0},{5,1},{6,2},{7,3},{8,12},{9,13},{10,... | collective-permute-start | bytes 589832 | tf_op jit(solution)/shard_map/ppermute | solution.py:692
  262.1 12.8 %collective-permute-start.49 = (bf16[2,192,1024]{2,1,0:T(8,128)(2,1)S(1)}, bf16[2,192,1024]{2,1,0:T(8,128)(2,1)S(1)}, u32[]{:S(2)}, u32[]{:S(2)}) collective-permute-start(bf16[2,192,1024]{2,1,0:T(8,128)(2,1)S(1)} %get-tuple-element.105), channel_id=1, source_target_pairs={{0,8},{8,0},{16,24},{24,16},{1,9},{9,1},{17,25},{25,17},{2,10},{10... | collective-permute-start | bytes 2359304 | tf_op jit(solution)/shard_map/ppermute | solution.py:692
  262.2 11.5 %collective-permute-start.50 = (bf16[8,192,128]{2,1,0:T(8,128)(2,1)S(1)}, bf16[8,192,128]{2,1,0:T(8,128)(2,1)S(1)}, u32[]{:S(2)}, u32[]{:S(2)}) collective-permute-start(bf16[8,192,128]{2,1,0:T(8,128)(2,1)S(1)} %pad_maximum_fusion.12), channel_id=1, source_target_pairs={{0,2},{1,3},{2,0},{3,1},{4,6},{5,7},{6,4},{7,5},{8,10},{9,11},{10,... | collective-permute-start | bytes 1179656 | tf_op jit(solution)/shard_map/ppermute | solution.py:692
  262.2 11.5 %collective-permute-start.51 = (bf16[8,192,128]{2,1,0:T(8,128)(2,1)S(1)}, bf16[8,192,128]{2,1,0:T(8,128)(2,1)S(1)}, u32[]{:S(2)}, u32[]{:S(2)}) collective-permute-start(bf16[8,192,128]{2,1,0:T(8,128)(2,1)S(1)} %pad_maximum_fusion.13), channel_id=1, source_target_pairs={{0,1},{1,0},{2,3},{3,2},{4,5},{5,4},{6,7},{7,6},{8,9},{9,8},{10,11... | collective-permute-start | bytes 1179656 | tf_op jit(solution)/shard_map/ppermute | solution.py:692
  264.5 10.4 %collective-permute-start.45 = (bf16[8,192,128]{2,1,0:T(8,128)(2,1)S(1)}, bf16[8,192,128]{2,1,0:T(8,128)(2,1)S(1)}, u32[]{:S(2)}, u32[]{:S(2)}) collective-permute-start(bf16[8,192,128]{2,1,0:T(8,128)(2,1)S(1)} %pad_maximum_fusion.10.refs_3_), channel_id=1, source_target_pairs={{0,8},{8,0},{16,24},{24,16},{1,9},{9,1},{17,25},{25,17},{2,10},{10... | collective-permute-start | bytes 1179656 | tf_op jit(solution)/shard_map/ppermute | solution.py:692
  280.5 19.1 %collective-permute-start.55 = (bf16[16,192,128]{2,1,0:T(8,128)(2,1)S(1)}, bf16[16,192,128]{2,1,0:T(8,128)(2,1)}, u32[]{:S(2)}, u32[]{:S(2)}) collective-permute-start(bf16[16,192,128]{2,1,0:T(8,128)(2,1)S(1)} %pad_maximum_fusion.6), channel_id=1, source_target_pairs={{0,1},{1,0},{2,3},{3,2},{4,5},{5,4},{6,7},{7,6},{8,9},{9,8},{10,11... | collective-permute-start | bytes 2359304 | tf_op jit(solution)/shard_map/ppermute | solution.py:692
  281.7 19.2 %collective-permute-start.56 = (bf16[16,192,128]{2,1,0:T(8,128)(2,1)}, bf16[16,192,128]{2,1,0:T(8,128)(2,1)}, u32[]{:S(2)}, u32[]{:S(2)}) collective-permute-start(bf16[16,192,128]{2,1,0:T(8,128)(2,1)} %pad_maximum_fusion.7), channel_id=1, source_target_pairs={{0,2},{1,3},{2,0},{3,1},{4,6},{5,7},{6,4},{7,5},{8,10},{9,11},{10,... | collective-permute-start | bytes 2359304 | tf_op jit(solution)/shard_map/ppermute | solution.py:692
  283.3 20.9 %collective-permute-start.52 = (bf16[2,192,1024]{2,1,0:T(8,128)(2,1)S(1)}, bf16[2,192,1024]{2,1,0:T(8,128)(2,1)S(1)}, u32[]{:S(2)}, u32[]{:S(2)}) collective-permute-start(bf16[2,192,1024]{2,1,0:T(8,128)(2,1)S(1)} %get-tuple-element.110), channel_id=1, source_target_pairs={{0,8},{8,0},{16,24},{24,16},{1,9},{9,1},{17,25},{25,17},{2,10},{10... | collective-permute-start | bytes 2359304 | tf_op jit(solution)/shard_map/ppermute | solution.py:692
  283.3 21.0 %collective-permute-start.54 = (bf16[192,1024]{1,0:T(8,128)(2,1)S(1)}, bf16[192,1024]{1,0:T(8,128)(2,1)S(1)}, u32[]{:S(2)}, u32[]{:S(2)}) collective-permute-start(bf16[192,1024]{1,0:T(8,128)(2,1)S(1)} %fusion.4.refs_6_), channel_id=1, source_target_pairs={{0,16},{8,24},{16,0},{24,8},{1,17},{9,25},{17,1},{25,9},{2,18},{10... | collective-permute-start | bytes 1179656 | tf_op jit(solution)/shard_map/ppermute | solution.py:692
  284.6 15.1 %copy-start.25 = (bf16[16,192,128]{2,1,0:T(8,128)(2,1)S(1)}, bf16[16,192,128]{2,1,0:T(8,128)(2,1)}, u32[]{:S(2)}) copy-start(bf16[16,192,128]{2,1,0:T(8,128)(2,1)} %copy-done.24) | copy-start | bytes 2359300
  300.9 8.5 %copy-start.12 = (bf16[32,192,128]{2,1,0:T(8,128)(2,1)}, bf16[32,192,128]{2,1,0:T(8,128)(2,1)S(1)}, u32[]{:S(2)}) copy-start(bf16[32,192,128]{2,1,0:T(8,128)(2,1)S(1)} %pad_maximum_fusion.2.refs_0_) | copy-start | bytes 4718596
  309.4 16.3 %collective-permute-start.58 = (bf16[32,192,128]{2,1,0:T(8,128)(2,1)S(1)}, bf16[32,192,128]{2,1,0:T(8,128)(2,1)}, u32[]{:S(2)}, u32[]{:S(2)}) collective-permute-start(bf16[32,192,128]{2,1,0:T(8,128)(2,1)S(1)} %pad_maximum_fusion.2.refs_0_), channel_id=1, source_target_pairs={{0,8},{8,0},{16,24},{24,16},{1,9},{9,1},{17,25},{25,17},{2,10},{10... | collective-permute-start | bytes 4718600 | tf_op jit(solution)/shard_map/ppermute | solution.py:692
  309.5 16.2 %collective-permute-start.59 = (bf16[32,192,128]{2,1,0:T(8,128)(2,1)}, bf16[32,192,128]{2,1,0:T(8,128)(2,1)}, u32[]{:S(2)}, u32[]{:S(2)}) collective-permute-start(bf16[32,192,128]{2,1,0:T(8,128)(2,1)} %pad_maximum_fusion.3.refs_0_), channel_id=1, source_target_pairs={{0,8},{8,0},{16,24},{24,16},{1,9},{9,1},{17,25},{25,17},{2,10},{10... | collective-permute-start | bytes 4718600 | tf_op jit(solution)/shard_map/ppermute | solution.py:692
  310.0 6.3 %collective-permute-start.57 = (bf16[2,192,1024]{2,1,0:T(8,128)(2,1)S(1)}, bf16[2,192,1024]{2,1,0:T(8,128)(2,1)S(1)}, u32[]{:S(2)}, u32[]{:S(2)}) collective-permute-start(bf16[2,192,1024]{2,1,0:T(8,128)(2,1)S(1)} %get-tuple-element.115), channel_id=1, source_target_pairs={{0,8},{8,0},{16,24},{24,16},{1,9},{9,1},{17,25},{25,17},{2,10},{10... | collective-permute-start | bytes 2359304 | tf_op jit(solution)/shard_map/ppermute | solution.py:692
  310.1 11.5 %collective-permute-start.53 = (bf16[192,1024]{1,0:T(8,128)(2,1)S(1)}, bf16[192,1024]{1,0:T(8,128)(2,1)S(1)}, u32[]{:S(2)}, u32[]{:S(2)}) collective-permute-start(bf16[192,1024]{1,0:T(8,128)(2,1)S(1)} %fusion.5.refs_0_), channel_id=1, source_target_pairs={{0,16},{8,24},{16,0},{24,8},{1,17},{9,25},{17,1},{25,9},{2,18},{10... | collective-permute-start | bytes 1179656 | tf_op jit(solution)/shard_map/ppermute | solution.py:692
  315.4 10.3 %copy-start.8 = (f32[2,192,1024]{2,1,0:T(8,128)}, f32[2,192,1024]{2,1,0:T(8,128)S(1)}, u32[]{:S(2)}) copy-start(f32[2,192,1024]{2,1,0:T(8,128)S(1)} %shard_map.151.refs_0_) | copy-start | bytes 4718596
  316.3 9.4 %copy-start.15 = (bf16[2,192,1024]{2,1,0:T(8,128)(2,1)}, bf16[2,192,1024]{2,1,0:T(8,128)(2,1)S(1)}, u32[]{:S(2)}) copy-start(bf16[2,192,1024]{2,1,0:T(8,128)(2,1)S(1)} %collective-permute-done.57.refs_1_) | copy-start | bytes 2359300
  325.7 5.5 %collective-permute-start.61 = (bf16[2,192,1024]{2,1,0:T(8,128)(2,1)S(1)}, bf16[2,192,1024]{2,1,0:T(8,128)(2,1)S(1)}, u32[]{:S(2)}, u32[]{:S(2)}) collective-permute-start(bf16[2,192,1024]{2,1,0:T(8,128)(2,1)S(1)} %get-tuple-element.124), channel_id=1, source_target_pairs={{0,8},{8,0},{16,24},{24,16},{1,9},{9,1},{17,25},{25,17},{2,10},{10... | collective-permute-start | bytes 2359304 | tf_op jit(solution)/shard_map/ppermute | solution.py:692
  325.8 17.0 %collective-permute-start.60 = (bf16[192,1024]{1,0:T(8,128)(2,1)S(1)}, bf16[192,1024]{1,0:T(8,128)(2,1)}, u32[]{:S(2)}, u32[]{:S(2)}) collective-permute-start(bf16[192,1024]{1,0:T(8,128)(2,1)S(1)} %fusion.6.refs_0_), channel_id=1, source_target_pairs={{0,16},{8,24},{16,0},{24,8},{1,17},{9,25},{17,1},{25,9},{2,18},{10... | collective-permute-start | bytes 1179656 | tf_op jit(solution)/shard_map/ppermute | solution.py:692
  332.2 13.7 %collective-permute-start.62 = (bf16[192,1024]{1,0:T(8,128)(2,1)}, bf16[192,1024]{1,0:T(8,128)(2,1)}, u32[]{:S(2)}, u32[]{:S(2)}) collective-permute-start(bf16[192,1024]{1,0:T(8,128)(2,1)} %fusion.7), channel_id=1, source_target_pairs={{0,16},{8,24},{16,0},{24,8},{1,17},{9,25},{17,1},{25,9},{2,18},{10... | collective-permute-start | bytes 1179656 | tf_op jit(solution)/shard_map/ppermute | solution.py:692
  338.4 7.5 %copy-start.9 = (f32[2,192,1024]{2,1,0:T(8,128)S(1)}, f32[2,192,1024]{2,1,0:T(8,128)}, u32[]{:S(2)}) copy-start(f32[2,192,1024]{2,1,0:T(8,128)} %copy-done.8) | copy-start | bytes 4718596
  338.4 7.5 %copy-start.11 = (f32[2,192,1024]{2,1,0:T(8,128)S(1)}, f32[2,192,1024]{2,1,0:T(8,128)}, u32[]{:S(2)}) copy-start(f32[2,192,1024]{2,1,0:T(8,128)} %copy-done.10) | copy-start | bytes 4718596
  (19 other events, 56.0 us)

commit v4 on v3

v4 whole, which is shorter than its diff:
```python
import functools

import jax
import jax.numpy as jnp
from jax import lax
from jax.experimental import pallas as pl
from jax.experimental.pallas import tpu as pltpu
from jax.sharding import PartitionSpec as P

BLOCK = 128
F32 = jnp.float32
BF16 = jnp.bfloat16
NT = (((1,), (1,)), ((), ()))
NN = (((1,), (0,)), ((), ()))


def partner(value, axis, distance):
    mask = 2**distance
    pairs = [(source, source ^ mask) for source in range(lax.axis_size(axis))]
    return lax.ppermute(value, axis, pairs)


def pick_blocks(shard_rows, wanted):
    block_count = shard_rows.shape[0] // BLOCK
    flat_blocks = shard_rows.reshape(block_count, BLOCK * shard_rows.shape[1])
    present = jnp.arange(block_count, dtype=jnp.int32)
    select = (wanted[:, None] == present[None, :]).astype(shard_rows.dtype)
    return jnp.dot(select, flat_blocks, preferred_element_type=F32)


def transposed_product(coupling, boundary):
    return lax.dot_general(coupling, boundary, (((0,), (0,)), ((), ())), preferred_element_type=F32)


def general_shards(
    dinv_root,
    rhs_root,
    dinv_mid,
    coup_mid,
    rhs_mid,
    dinv_leaf,
    coup_leaf,
    rhs_leaf,
    bounds_mid,
    bounds_leaf,
    parents,
):
    row_total = lax.axis_size("row")
    row_id = lax.axis_index("row")
    col_id = lax.axis_index("col")
    rhs_width = rhs_root.shape[1]
    root_total = dinv_root.shape[0] * row_total // BLOCK
    front_mid = row_id // 2
    half_index = row_id % 2
    half_blocks = bounds_mid.shape[1] // 2
    mid_all = lax.dynamic_slice_in_dim(bounds_mid, front_mid, 1, 0)[0]
    mid_list = lax.dynamic_slice_in_dim(mid_all, half_index * half_blocks, half_blocks, 0)
    leaf_all = lax.dynamic_slice_in_dim(bounds_leaf, col_id, 1, 0)[0]
    leaf_slots = leaf_all.shape[0] // row_total
    leaf_list = lax.dynamic_slice_in_dim(leaf_all, row_id * leaf_slots, leaf_slots, 0)
    wanted = jnp.concatenate([mid_list, leaf_list])
    root_values = lax.psum_scatter(
        jnp.dot(dinv_root, rhs_root, preferred_element_type=F32),
        "col",
        scatter_dimension=0,
        tiled=True,
    ).astype(BF16)
    picked = pick_blocks(lax.all_gather(root_values, ("row", "col"), axis=0, tiled=True), wanted)
    bound_mid = picked[:half_blocks].reshape(half_blocks * BLOCK, rhs_width).astype(BF16)
    root_side = picked[half_blocks:]
    mid_part = transposed_product(coup_mid, bound_mid)
    mid_terms = mid_part + partner(mid_part, "row", 0)
    rhs_here = lax.dynamic_slice_in_dim(rhs_mid, front_mid, 1, 0)[0]
    shift_mid = (rhs_here - mid_terms).astype(BF16)
    mid_values = lax.psum_scatter(
        jnp.dot(dinv_mid, shift_mid, preferred_element_type=F32),
        "col",
        scatter_dimension=0,
        tiled=True,
    ).astype(BF16)
    half_rows = lax.all_gather(mid_values, "col", axis=0, tiled=True)
    half_count = half_rows.shape[0] // BLOCK
    half_flat = half_rows.reshape(half_count, BLOCK * rhs_width)
    local_ids = leaf_all - root_total - half_index * half_count
    owns_parent = lax.dynamic_slice_in_dim(parents, col_id, 1, 0)[0] == front_mid
    choose = (
        (local_ids[:, None] == jnp.arange(half_count, dtype=jnp.int32)[None, :]) & owns_parent
    ).astype(BF16)
    from_parent = lax.psum_scatter(
        jnp.dot(choose, half_flat, preferred_element_type=F32).astype(BF16),
        "row",
        scatter_dimension=0,
        tiled=True,
    ).astype(F32)
    bound_leaf = (root_side + from_parent).reshape(leaf_slots * BLOCK, rhs_width).astype(BF16)
    leaf_sum = lax.psum_scatter(
        transposed_product(coup_leaf[0], bound_leaf), "row", scatter_dimension=0, tiled=True
    )
    shift_leaf = (rhs_leaf[0] - leaf_sum).astype(BF16)
    leaf_values = lax.psum_scatter(
        jnp.dot(dinv_leaf[0], shift_leaf, preferred_element_type=F32),
        "row",
        scatter_dimension=0,
        tiled=True,
    ).astype(BF16)
    return (root_values, mid_values, leaf_values[None])


SMEM = pl.BlockSpec(memory_space=pltpu.SMEM)
VMEM = pl.BlockSpec(memory_space=pltpu.VMEM)
ANY = pl.BlockSpec(memory_space=pl.ANY)
MIB = 1024 * 1024
ORDERS = ((1, 2, 4), (2, 1, 4))
CHAINS = (0, 1)


def params(mib):
    return pltpu.CompilerParams(vmem_limit_bytes=mib * MIB)


def cost(rows, depth, width):
    return pl.CostEstimate(flops=2 * rows * depth * width, bytes_accessed=2 * rows * depth, transcendentals=0)


def loop(count, body):
    def step(i, carry):
        body(i)
        return carry

    lax.fori_loop(0, count, step, 0)


def place_of(chip, col, bits, slot):
    far = chip ^ col
    high, mid, low = (((far & bit) != 0).astype(jnp.int32) for bit in bits)
    return (4 * high + 2 * mid + low) * slot


def chips_in_order(col, bits):
    return [col ^ sum(bit for bit, shift in zip(bits, (4, 2, 1)) if t & shift) for t in range(8)]


def mark_fronts(bounds_ref, front):
    def body(j):
        front[bounds_ref[0, j]] = 0
        front[bounds_ref[1, j]] = 1

    loop(bounds_ref.shape[1], body)


def order_kernel(local, slot, place_ref, bounds_ref, out_ref, front):
    row, col = place_ref[0], place_ref[1]
    first = row * local
    mark_fronts(bounds_ref, front)
    before = lax.fori_loop(0, first, lambda v, s: s + 1 - front[v], jnp.int32(0))
    zeros = lax.fori_loop(0, local, lambda i, s: s + 1 - front[first + i], jnp.int32(0))

    def body(i, carry):
        low, high = carry
        kind = front[first + i]
        rank = jnp.where(kind == 0, low, zeros + high)
        out_ref[place_of((before + rank) & 7, col, ORDERS[0], slot) + (rank >> 3)] = i
        return low + 1 - kind, high + kind

    lax.fori_loop(0, local, body, (jnp.int32(0), jnp.int32(0)))


def plan_layout(local, slot, leaf_slots):
    at = {}
    size = 0
    for name, count in (
        ("select", slot),
        ("mid", local),
        ("send_root", leaf_slots + slot),
        ("leaf", leaf_slots),
        ("out", slot),
        ("mid_order", local),
        ("mid_out", slot),
        ("mid_send", slot),
        ("turn", 1),
    ):
        at[name] = size
        size += count
    at["size"] = size
    return at


def plan_kernel(local, slot, leaf_slots, place_ref, bounds_ref, leaf_ref, parents_ref, out_ref, front, ident, where, record):
    row, col = place_ref[0], place_ref[1]
    x, h = row // 2, row % 2
    total = 4 * local
    mark_fronts(bounds_ref, front)
    chains = range(len(ORDERS))
    at = plan_layout(local, slot, leaf_slots)

    def per_row(r, before):
        zeros = lax.fori_loop(0, local, lambda i, s: s + 1 - front[r * local + i], jnp.int32(0))

        def body(i, carry):
            low, high = carry
            kind = front[r * local + i]
            rank = jnp.where(kind == 0, low, zeros + high)
            chip = (before + rank) & 7
            ident[r * local + chip * slot + (rank >> 3)] = r * local + i
            return low + 1 - kind, high + kind

        lax.fori_loop(0, local, body, (jnp.int32(0), jnp.int32(0)))
        return before + zeros

    lax.fori_loop(0, 4, per_row, jnp.int32(0))

    def clear(v):
        for n in chains:
            where[n, v] = 0

    loop(total, clear)

    def per_chip(chip, _):
        here = chip == col
        near = [place_of(chip, col, bits, slot) for bits in ORDERS]

        def put(core, count, block, code):
            for n in chains:
                where[n, block] = (core ^ h) * local + near[n] + count

            @pl.when(here & (core == h))
            def _():
                for n in chains:
                    out_ref[n, count] = code

        def from_far(step, carry):
            count0, count1 = carry
            core, k = step // slot, step % slot
            block = ident[(2 * (1 - x) + core) * local + chip * slot + k]
            taken = front[block] == x
            count = jnp.where(core == 0, count0, count1)

            @pl.when(taken)
            def _():
                put(core, count, block, 2 * slot + k)

            add = taken.astype(jnp.int32)
            return count0 + jnp.where(core == 0, add, 0), count1 + jnp.where(core == 0, 0, add)

        counts = lax.fori_loop(0, 2 * slot, from_far, (jnp.int32(0), jnp.int32(0)))

        def from_near(step, carry):
            count0, count1 = carry
            owner, k = step // slot, step % slot
            block = ident[(2 * x + owner) * local + chip * slot + k]
            taken = front[block] == x
            core = (count0 >= slot).astype(jnp.int32)
            count = jnp.where(core == 0, count0, count1)

            @pl.when(taken)
            def _():
                put(core, count, block, (owner ^ core) * slot + k)

            add = taken.astype(jnp.int32)
            return count0 + jnp.where(core == 0, add, 0), count1 + jnp.where(core == 0, 0, add)

        lax.fori_loop(0, 2 * slot, from_near, counts)
        return 0

    lax.fori_loop(0, 8, per_chip, 0)

    def mid_list(j):
        block = bounds_ref[x, h * local + j]
        for n in chains:
            out_ref[n, at["mid"] + j] = where[n, block]

    loop(local, mid_list)
    far = 2 * (1 - x) + h
    turn = jnp.int32(6)
    for k in range(7, 0, -1):
        apart = [(parents_ref[c] != parents_ref[c ^ k]).astype(jnp.int32) for c in range(8)]
        turn = jnp.where(functools.reduce(jnp.multiply, apart) == 1, k - 1, turn)
    out_ref[0, at["turn"]] = turn
    listed = 4 * leaf_slots

    def per_leaf(leaf, _):
        @pl.when(parents_ref[leaf] == x)
        def _():
            def body(j, rank):
                block = leaf_ref[leaf, j]
                taken = block >= total

                @pl.when(taken)
                def _():
                    record[block - total] = leaf * 4 * slot + rank

                return rank + taken.astype(jnp.int32)

            lax.fori_loop(0, listed, body, jnp.int32(0))

        return 0

    lax.fori_loop(0, 8, per_leaf, 0)

    def spot(block):
        leaf, rank = record[block] // (4 * slot), record[block] % (4 * slot)
        chip = jnp.where(rank < 2 * slot, leaf, leaf ^ (turn + 1))
        return chip, rank // slot % 2, rank % slot

    def mid_orders(block):
        chip, core, k = spot(block)

        @pl.when(core == h)
        def _():
            for n in chains:
                place = place_of(chip, col, ORDERS[n], slot) + k
                out_ref[n, at["mid_order"] + place] = (block // local ^ h) * local + block % local

    loop(2 * local, mid_orders)

    def mid_outs(j):
        chip, core, k = spot(h * local + col * slot + j)
        out_ref[0, at["mid_out"] + j] = jnp.where(core == h, chip * slot + k, local + j)
        chip, core, k = spot((1 - h) * local + col * slot + j)
        out_ref[0, at["mid_send"] + j] = chip * slot + k

    loop(slot, mid_outs)

    def sends(j):
        asked = leaf_ref[col, far * leaf_slots + j]
        for n in chains:
            out_ref[n, at["send_root"] + j] = where[n, jnp.minimum(asked, total - 1)]

    loop(leaf_slots, sends)

    def count(j, rank):
        return rank + (leaf_ref[col, j] >= total).astype(jnp.int32)

    def lists(j, rank):
        held = leaf_ref[col, row * leaf_slots + j]
        low = jnp.minimum(held, total - 1)
        place = (rank // slot % 2 ^ h) * 2 * slot + rank // (2 * slot) * slot + rank % slot
        for n in chains:
            from_root = jnp.where(front[low] == x, where[n, low], 2 * local + j)
            from_mid = 2 * local + leaf_slots + slot + place
            out_ref[n, at["leaf"] + j] = jnp.where(held < total, from_root, from_mid)
        return count(row * leaf_slots + j, rank)

    lax.fori_loop(0, leaf_slots, lists, lax.fori_loop(0, row * leaf_slots, count, jnp.int32(0)))

    def outs(j):
        asked = far * local + col * slot + j
        held = row * local + col * slot + j
        for n in chains:
            out_ref[n, at["send_root"] + leaf_slots + j] = where[n, asked]
            out_ref[n, at["out"] + j] = jnp.where(front[held] == x, where[n, held], 2 * local + leaf_slots + j)

    loop(slot, outs)


def start_fetch(sources, code, target, sem):
    base = 0
    for source, rows in sources:
        count = source.shape[0]

        @pl.when((code >= base) & (code < base + count))
        def _(source=source, base=base, rows=rows):
            pltpu.make_async_copy(source.at[code - base, rows], target, sem).start()

        base += count


def flatten(parts):
    arrays, plans = [], []
    for order, width, sources in parts:
        plan = []
        for array, first in sources:
            number = next((i for i, known in enumerate(arrays) if known is array), len(arrays))
            if number == len(arrays):
                arrays.append(array)
            plan.append((number, first))
        plans.append((order, width, tuple(plan)))
    return arrays, tuple(plans)


def fetch_all(plans, start, count, table_ref, refs, target, sems):
    def each(act):
        first = 0
        for p, (order, width, plan) in enumerate(plans):
            for i in range(count):
                place = target(i, p, first, width)
                act(p, i, order, [(refs[k], pl.ds(row, width)) for k, row in plan], place)
            first += width

    def begin(p, i, order, sources, place):
        start_fetch(sources, table_ref[order, start + i], place, sems.at[p, i])

    def end(p, i, order, sources, place):
        blocks, rows = sources[0]
        pltpu.make_async_copy(blocks.at[0, rows], place, sems.at[p, i]).wait()

    each(begin)
    each(end)


def gather_kernel(plans, start, count, total, split, table_ref, *refs):
    outs, sems = refs[-1 - (len(plans) if split else 1) : -1], refs[-1]

    def target(i, p, first, width):
        return outs[p].at[i] if split else outs[0].at[i, pl.ds(first, width)]

    fetch_all(plans, start, count, table_ref, refs[:total], target, sems)


def gather(table, start, count, parts, after=(), split=False):
    arrays, plans = flatten(parts)
    widths = [part[1] for part in plans] if split else [sum(part[1] for part in plans)]
    outs = pl.pallas_call(
        functools.partial(gather_kernel, plans, start, count, len(arrays), split),
        out_shape=[jax.ShapeDtypeStruct((count, width, BLOCK), BF16) for width in widths],
        in_specs=[SMEM] + [ANY] * (len(arrays) + len(after)),
        out_specs=[VMEM] * len(widths),
        scratch_shapes=[pltpu.SemaphoreType.DMA((len(plans), count))],
        compiler_params=params(10),
    )(table, *arrays, *after)
    return outs if split else outs[0]


def store_blocks(ref, result):
    for i in range(ref.shape[0]):
        ref[i] = result[:, i * BLOCK : (i + 1) * BLOCK].astype(ref.dtype)


def root_product_kernel(parts, last, order_ref, value_ref, *refs):
    blocks, outs, turned = refs[:parts], refs[parts:-1], refs[-1]
    step = pl.program_id(0)

    @pl.when(step == 0)
    def _():
        turned[...] = value_ref[...].T

    matrix = jnp.concatenate([b[...] for b in blocks], axis=0)
    result = lax.dot_general(turned[...], matrix, NT, preferred_element_type=F32)
    width = result.shape[0] // len(CHAINS)
    for n, order in enumerate(CHAINS):
        part = result[n * width : (n + 1) * width]
        if last:
            store_blocks(outs[n], part)
            continue
        next_step = 2 - order

        @pl.when(step != next_step)
        def _(n=n, part=part):
            store_blocks(outs[2 * n], part)

        @pl.when(step == next_step)
        def _(n=n, part=part):
            store_blocks(outs[2 * n + 1], part)


def root_product(order, value, matrix, last):
    depth, width = value.shape
    local = matrix.shape[0] // BLOCK
    parts = local // 4
    base = 0 if last else 3

    def spec(i):
        return pl.BlockSpec((BLOCK, depth), lambda s, order: (order[parts * (base - s) + i], 0))

    part = width // len(CHAINS)
    block = (parts, part, BLOCK)
    fixed = pl.BlockSpec(block, lambda s, order: (0, 0, 0))
    rest = jax.ShapeDtypeStruct(block, F32)
    if last:
        out_specs, out_shape = [fixed] * len(CHAINS), [rest] * len(CHAINS)
    else:
        first = pl.BlockSpec(block, lambda s, order: (jnp.where(s == 0, 1, 0), 0, 0))
        out_specs = [first, fixed] * len(CHAINS)
        out_shape = [jax.ShapeDtypeStruct((local // 2, part, BLOCK), BF16), rest] * len(CHAINS)
    return pl.pallas_call(
        functools.partial(root_product_kernel, parts, last),
        grid_spec=pltpu.PrefetchScalarGridSpec(
            num_scalar_prefetch=1,
            grid=(1 if last else 3,),
            in_specs=[pl.BlockSpec((depth, width), lambda s, order: (0, 0))] + [spec(i) for i in range(parts)],
            out_specs=out_specs,
            scratch_shapes=[pltpu.VMEM((width, depth), BF16)],
        ),
        out_shape=out_shape,
        compiler_params=params(60),
        cost_estimate=cost(matrix.shape[0] // 4 * (1 if last else 3), depth, width),
    )(order, value, *([matrix] * parts))


def mid_first_kernel(front_ref, term_ref, got_ref, rhs_ref, matrix_ref, *refs):
    out_ref, shift_ref = refs[-2:]

    @pl.when(pl.program_id(0) == 0)
    def _():
        shift_ref[...] = (rhs_ref[0].T.astype(F32) - (term_ref[...] + got_ref[...].astype(F32))).astype(BF16)

    store_blocks(out_ref, lax.dot_general(shift_ref[...], matrix_ref[...], NT, preferred_element_type=F32))


def mid_rest_kernel(shift_ref, matrix_ref, out_ref):
    store_blocks(out_ref, lax.dot_general(shift_ref[...], matrix_ref[...], NT, preferred_element_type=F32))


def mid_first(front, term, got, rhs, matrix, after):
    width, depth = term.shape
    half = matrix.shape[0] // BLOCK // 2
    whole = pl.BlockSpec((width, depth), lambda s, front: (0, 0))
    return pl.pallas_call(
        mid_first_kernel,
        grid_spec=pltpu.PrefetchScalarGridSpec(
            num_scalar_prefetch=1,
            grid=(2,),
            in_specs=[
                whole,
                whole,
                pl.BlockSpec((1, depth, width), lambda s, front: (front[0], 0, 0)),
                pl.BlockSpec((half // 2 * BLOCK, depth), lambda s, front: (s, 0)),
            ]
            + [ANY] * len(after),
            out_specs=[pl.BlockSpec((half // 2, width, BLOCK), lambda s, front: (s, 0, 0)), whole],
        ),
        out_shape=[
            jax.ShapeDtypeStruct((half, width, BLOCK), BF16),
            jax.ShapeDtypeStruct((width, depth), BF16),
        ],
        compiler_params=params(60),
        cost_estimate=cost(half * BLOCK, depth, width),
    )(front.reshape(1), term, got, rhs, matrix, *after)


def mid_rest(shift, matrix):
    width, depth = shift.shape
    half = matrix.shape[0] // BLOCK // 2
    return pl.pallas_call(
        mid_rest_kernel,
        grid=(2,),
        in_specs=[
            pl.BlockSpec((width, depth), lambda s: (0, 0)),
            pl.BlockSpec((half // 2 * BLOCK, depth), lambda s: (2 + s, 0)),
        ],
        out_specs=pl.BlockSpec((half // 2, width, BLOCK), lambda s: (s, 0, 0)),
        out_shape=jax.ShapeDtypeStruct((half, width, BLOCK), BF16),
        compiler_params=params(60),
        cost_estimate=cost(half * BLOCK, depth, width),
    )(shift, matrix)


def mid_coupling_kernel(plans, start, count, total, table_ref, *refs):
    coup_ref, out_ref, send_ref, bound, sems = refs[total:]

    def target(i, p, first, width):
        return bound.at[pl.ds(first, width), pl.ds(i * BLOCK, BLOCK)]

    @pl.when(pl.program_id(0) == 0)
    def _():
        fetch_all(plans, start, count, table_ref, refs[:total], target, sems)

    product = lax.dot_general(bound[...], coup_ref[...], NN, preferred_element_type=F32)
    out_ref[...] = product
    send_ref[...] = product.astype(BF16)


def mid_coupling(table, start, parts, coup, steps=4):
    arrays, plans = flatten(parts)
    width = sum(part[1] for part in plans)
    depth, cols = coup.shape
    count = depth // BLOCK
    tile = pl.BlockSpec((width, cols // steps), lambda s: (0, s))
    return pl.pallas_call(
        functools.partial(mid_coupling_kernel, plans, start, count, len(arrays)),
        grid=(steps,),
        in_specs=[SMEM] + [ANY] * len(arrays) + [pl.BlockSpec((depth, cols // steps), lambda s: (0, s))],
        out_specs=[tile, tile],
        out_shape=[jax.ShapeDtypeStruct((width, cols), F32), jax.ShapeDtypeStruct((width, cols), BF16)],
        scratch_shapes=[pltpu.VMEM((width, depth), BF16), pltpu.SemaphoreType.DMA((len(plans), count))],
        compiler_params=params(24),
        cost_estimate=cost(cols, depth, width),
    )(table, *arrays, coup)


def leaf_first_kernel(plans, start, count, total, table_ref, order_ref, *refs):
    matrix_ref, out_ref, bound_ref, sems = refs[total:]

    def target(i, p, first, width):
        return bound_ref.at[pl.ds(first, width), pl.ds(i * BLOCK, BLOCK)]

    @pl.when(pl.program_id(0) == 0)
    def _():
        fetch_all(plans, start, count, table_ref, refs[:total], target, sems)

    out_ref[0] = lax.dot_general(bound_ref[...], matrix_ref[...], NN, preferred_element_type=F32).astype(BF16)


def leaf_first(table, start, parts, order, matrix, cols):
    arrays, plans = flatten(parts)
    width = sum(part[1] for part in plans)
    depth = matrix.shape[0]
    count = depth // BLOCK
    return pl.pallas_call(
        functools.partial(leaf_first_kernel, plans, start, count, len(arrays)),
        grid_spec=pltpu.PrefetchScalarGridSpec(
            num_scalar_prefetch=2,
            grid=(2,),
            in_specs=[ANY] * len(arrays) + [pl.BlockSpec((depth, cols), lambda s, table, order: (0, order[s]))],
            out_specs=[
                pl.BlockSpec((1, width, cols), lambda s, table, order: (s, 0, 0)),
                pl.BlockSpec((width, depth), lambda s, table, order: (0, 0)),
            ],
            scratch_shapes=[pltpu.SemaphoreType.DMA((len(plans), count))],
        ),
        out_shape=[
            jax.ShapeDtypeStruct((2, width, cols), BF16),
            jax.ShapeDtypeStruct((width, depth), BF16),
        ],
        compiler_params=params(60),
        cost_estimate=cost(2 * cols, depth, width),
    )(table, order, *arrays, matrix)


def leaf_shift_kernel(order_ref, keep_ref, got_ref, far_ref, rhs_ref, matrix_ref, *refs):
    out_ref, shift_ref = refs[-2:]

    @pl.when(pl.program_id(0) == 0)
    def _():
        term = keep_ref[0] + got_ref[0].astype(F32) + far_ref[...].astype(F32)
        shift_ref[...] = (rhs_ref[0].T.astype(F32) - term).astype(BF16)

    product = lax.dot_general(shift_ref[...], matrix_ref[...], NT, preferred_element_type=F32)
    out_ref[0] = product.astype(BF16)


def leaf_shift(order, keep, got, far, rhs, matrix, after):
    _, width, depth = keep.shape
    one = pl.BlockSpec((1, width, depth), lambda s, order: (0, 0, 0))
    flat = pl.BlockSpec((width, depth), lambda s, order: (0, 0))
    return pl.pallas_call(
        leaf_shift_kernel,
        grid_spec=pltpu.PrefetchScalarGridSpec(
            num_scalar_prefetch=1,
            grid=(2,),
            in_specs=[
                one,
                one,
                flat,
                pl.BlockSpec(rhs.shape, lambda s, order: (0, 0, 0)),
                pl.BlockSpec((depth, depth), lambda s, order: (order[s], 0)),
            ]
            + [ANY] * len(after),
            out_specs=[pl.BlockSpec((1, width, depth), lambda s, order: (s, 0, 0)), flat],
        ),
        out_shape=[
            jax.ShapeDtypeStruct((2, width, depth), BF16),
            jax.ShapeDtypeStruct((width, depth), BF16),
        ],
        compiler_params=params(60),
        cost_estimate=cost(2 * depth, depth, width),
    )(order, keep, got, far, rhs, matrix, *after)


def leaf_rest_kernel(dims, order_ref, value_ref, matrix_ref, out_ref):
    out_ref[0] = lax.dot_general(value_ref[...], matrix_ref[...], dims, preferred_element_type=F32)


def leaf_rest(order, dims, value, matrix, cols, mib):
    width, depth = value.shape
    if dims is NN:
        spec = pl.BlockSpec((depth, cols), lambda s, order: (0, order[2 + s]))
    else:
        spec = pl.BlockSpec((cols, depth), lambda s, order: (order[2 + s], 0))
    return pl.pallas_call(
        functools.partial(leaf_rest_kernel, dims),
        grid_spec=pltpu.PrefetchScalarGridSpec(
            num_scalar_prefetch=1,
            grid=(2,),
            in_specs=[pl.BlockSpec((width, depth), lambda s, order: (0, 0)), spec],
            out_specs=pl.BlockSpec((1, width, cols), lambda s, order: (s, 0, 0)),
        ),
        out_shape=jax.ShapeDtypeStruct((2, width, cols), F32),
        compiler_params=params(mib),
        cost_estimate=cost(2 * cols, depth, width),
    )(order, value, matrix)


def leaf_finish_kernel(keep_ref, got_ref, far_ref, *refs):
    total = keep_ref[0] + got_ref[0].astype(F32) + far_ref[...].astype(F32)
    refs[-1][0] = total.astype(BF16).T


def leaf_finish(keep, got, far, after):
    _, width, rows = keep.shape
    one = pl.BlockSpec((1, width, rows), lambda s: (0, 0, 0))
    return pl.pallas_call(
        leaf_finish_kernel,
        grid=(1,),
        in_specs=[one, one, pl.BlockSpec((width, rows), lambda s: (0, 0))] + [ANY] * len(after),
        out_specs=pl.BlockSpec((1, rows, width), lambda s: (0, 0, 0)),
        out_shape=jax.ShapeDtypeStruct((1, rows, width), BF16),
        compiler_params=params(60),
    )(keep, got, far, *after)


def swap(value, axis, mask):
    return lax.ppermute(value, axis, [(i, i ^ mask) for i in range(lax.axis_size(axis))])


def add(*terms):
    return functools.reduce(jnp.add, [t.astype(F32) for t in terms])


def tie(value, others):
    value, others[:] = lax.optimization_barrier((value, list(others)))
    return value


def reduce_columns(send, hold, keep, bits, early, step):
    for i, bit in enumerate(bits):
        got = swap(send, "col", bit)
        if i == step:
            got = tie(got, early)
        if i < len(bits) - 1:
            half = got.shape[0] // 2
            send = add(hold, got[half:]).astype(BF16)
            keep = add(keep, got[:half])
        if i < len(bits) - 2:
            hold, keep = keep[half // 2 :], keep[: half // 2]
    return add(keep, got).astype(BF16)


def turn_columns(value, turn):
    return lax.switch(turn, [lambda v, k=k: swap(v, "col", k) for k in range(1, 8)], value)


def gather_columns(value, bits):
    for bit in (bits[2], bits[1]):
        value = jnp.concatenate([value, swap(value, "col", bit)], axis=0)
    far = swap(value, "col", bits[0])
    return [value, far, swap(value, "row", 1), swap(far, "row", 1)]


def natural(blocks):
    return jnp.swapaxes(blocks, 1, 2).reshape(-1, blocks.shape[1])


def shards(
    dinv_root,
    rhs_root,
    dinv_mid,
    coup_mid,
    rhs_mid,
    dinv_leaf,
    coup_leaf,
    rhs_leaf,
    bounds_mid,
    bounds_leaf,
    parents,
):
    row_id = lax.axis_index("row")
    col_id = lax.axis_index("col")
    x, h = row_id // 2, row_id % 2
    place = jnp.stack([row_id, col_id]).astype(jnp.int32)
    local = dinv_root.shape[0] // BLOCK
    slot = local // 8
    leaf_slots = bounds_leaf.shape[1] // 4
    at = plan_layout(local, slot, leaf_slots)

    order = pl.pallas_call(
        functools.partial(order_kernel, local, slot),
        out_shape=jax.ShapeDtypeStruct((local,), jnp.int32),
        in_specs=[SMEM] * 2,
        out_specs=SMEM,
        scratch_shapes=[pltpu.SMEM((4 * local,), jnp.int32)],
    )(place, bounds_mid)
    plan = pl.pallas_call(
        functools.partial(plan_kernel, local, slot, leaf_slots),
        out_shape=jax.ShapeDtypeStruct((len(ORDERS), at["size"]), jnp.int32),
        in_specs=[SMEM] * 4,
        out_specs=SMEM,
        scratch_shapes=[pltpu.SMEM((4 * local,), jnp.int32)] * 2
        + [pltpu.SMEM((len(ORDERS), 4 * local), jnp.int32), pltpu.SMEM((2 * local,), jnp.int32)],
    )(place, bounds_mid, bounds_leaf, parents)

    half, quarter = local // 2, local // 4
    leaf_order = jnp.stack([2 * x + 1 - h, 2 * (1 - x) + 1 - h, 2 * x + h, 2 * (1 - x) + h]).astype(jnp.int32)
    leaf_cols = coup_leaf.shape[2] // 4
    width = rhs_root.shape[1] // len(CHAINS)
    chains = range(len(CHAINS))

    def whole(arrays):
        return [(array, 0) for array in arrays]

    def rows(arrays, n):
        return [(array, n * width) for array in arrays]

    first = root_product(order, rhs_root, dinv_root, False)
    last = root_product(order, rhs_root, dinv_root, True)
    tables = [plan]
    boundary = []
    for n, kind in enumerate(CHAINS):
        got = reduce_columns(*first[2 * n : 2 * n + 2], last[n], ORDERS[kind], tables, 0)
        picked = [(kind, width, whole((got, swap(got, "row", 1), swap(got, "row", 2))))]
        boundary.append(gather_columns(gather(tables[0], at["select"], slot, picked), ORDERS[kind]))
    plan = tables[0]
    parts = [(kind, width, whole(boundary[n])) for n, kind in enumerate(CHAINS)]

    term, half_term = mid_coupling(plan, at["mid"], parts, coup_mid)
    front, shift = mid_first(x, term, swap(half_term, "row", 1), rhs_mid, dinv_mid, ())
    back = mid_rest(shift, dinv_mid)
    asking = gather(plan, at["send_root"], leaf_slots + slot, parts, (back,), split=True)
    asked = [[swap(part, "row", 2)] for part in asking]
    products = (front, back, swap(front, "row", 1), swap(back, "row", 1))
    parts = [(kind, width, rows(products, n)) for n, kind in enumerate(CHAINS)]
    sends = gather(plan, at["mid_order"] + half, half, parts, split=True)
    keeps = gather(plan, at["mid_order"], half, parts, (sends[0],), split=True)
    got = []
    for n, kind in enumerate(CHAINS):
        hold, keep = keeps[n][quarter:], keeps[n][:quarter]
        early = [] if n == 0 else asked[0]
        got.append(reduce_columns(sends[n], hold, keep, ORDERS[kind], early, 1))
    got = tie(jnp.concatenate(got, axis=1), asked[1])
    other = swap(got, "row", 2)
    child = parents[col_id] == x
    mine, away = jnp.where(child, got, other), jnp.where(child, other, got)
    own = jnp.concatenate([mine, turn_columns(away, plan[0, at["turn"]])], axis=0)
    sib = swap(own, "row", 1)
    sources = [(kind, width, whole((*boundary[n], *asked[n])) + rows((own, sib), n)) for n, kind in enumerate(CHAINS)]
    mid = lax.all_gather(got, "col", axis=0, tiled=True)

    def reduce_rows(send, keep):
        got = swap(send, "row", 1)
        far = swap(add(keep[1], got[1]).astype(BF16), "row", 2)
        return keep, got, far

    send, bound = leaf_first(plan, at["leaf"], sources, leaf_order, coup_leaf[0], leaf_cols)
    terms = reduce_rows(send, leaf_rest(leaf_order, NN, bound, coup_leaf[0], leaf_cols, 60))
    held = [(kind, width, whole((*boundary[n], *asked[n]))) for n, kind in enumerate(CHAINS)]
    root_values = gather(plan, at["out"], slot, held)
    root_values = natural(root_values)
    send, shift = leaf_shift(leaf_order, *terms, rhs_leaf, dinv_leaf[0], (root_values,))
    terms = reduce_rows(send, leaf_rest(leaf_order, NT, shift, dinv_leaf[0], leaf_cols, 60))
    joint = len(CHAINS) * width
    wanted = gather(plan, at["mid_send"], slot, [(0, joint, whole((mid,)))])
    mid_values = gather(plan, at["mid_out"], slot, [(0, joint, whole((mid, swap(wanted, "row", 1))))])
    mid_values = natural(mid_values)
    return (root_values, mid_values, leaf_finish(*terms, (mid_values,)))


def solution(mesh):
    sizes = dict(mesh.shape)
    in_specs = (
        P("row", "col"),
        P("col", None),
        P("row", "col"),
        P("row", "col"),
        P(None, "col", None),
        P("col", None, "row"),
        P("col", "row", None),
        P("col", "row", None),
        P(),
        P(),
        P(),
    )
    out_specs = (P(("row", "col"), None), P(("row", "col"), None), P("col", "row", None))

    def run(*args):
        fronts, listed = args[8].shape
        blocks = args[0].shape[0] // BLOCK
        whole = fronts == 2 and fronts * listed == blocks and args[2].shape[0] == args[0].shape[0]
        fits = sizes["row"] == 4 and sizes["col"] == 8 and whole
        body = shards if fits else general_shards
        return jax.shard_map(body, mesh=mesh, in_specs=in_specs, out_specs=out_specs, check_vma=False)(*args)

    return run
```

time: 350 us -> 336 us (0.960); the launches traced: 350 us -> 330 us
  between operations: 2.7 us -> 16 us
  other arithmetic: 25.5 us -> 12.3 us
  starting transfers between devices: 46 us -> 33.6 us
  waiting for transfers between devices: 156 us -> 148 us
  Pallas kernels: 109 us -> 102 us
  local copies, waits for them, and re-layouts: 11.7 us -> 18.1 us
    ppermute x51 -> x39, waiting for transfers between devices: 156 us -> 143 us  [swap(): lax.ppermute(value, axis, [(i, i ^ mask) for i in range(lax.axis_size(axi...]
    ppermute x51 -> x39, starting transfers between devices: 46 us -> 33.5 us  [swap(): lax.ppermute(value, axis, [(i, i ^ mask) for i in range(lax.axis_size(axi...]
    concatenate x8 -> x2, other arithmetic: 9.76 us -> 1.09 us  [the longest x1 1.07 us: shards(): jnp.concatenate([mine, turn_columns(away, plan[0, at['turn']])], axis=0)]
    pallas_call x18 -> x13, Pallas kernels: 67 us -> 60.1 us  [the longest x2 18.4 us: root_product(): pl.pallas_call(functools.partial(root_product_kernel, parts, last), grid_...]
    unnamed x64 -> x86, local copies, waits for them, and re-layouts: 7.73 us -> 14.1 us
    all_gather x0 -> x1, waiting for transfers between devices: none -> 5.08 us  [shards(): mid = lax.all_gather(got, 'col', axis=0, tiled=True)]
    pallas_call x4 -> x2, Pallas kernels: 16.2 us -> 13.2 us  [leaf_rest(): pl.pallas_call(functools.partial(leaf_rest_kernel, dims), grid_spec=pltpu...]
    convert_element_type x16 -> x13, other arithmetic: 11.3 us -> 9.39 us  [the longest x2 6.04 us: reduce_rows(): far = swap(add(keep[1], got[1]).astype(BF16), 'row', 2)]
  transfers between devices with their start and end apart: 51 -> 40, of which waited for: 33 -> 27; matrix products, arithmetic and copies ran while one was open for 8% -> 4% of each run, Pallas kernels for 16% -> 19%
where the time goes in v4:
time: 336 us; the launch traced here: 330 us
  waiting for transfers between devices  148 us (44%)
  Pallas kernels  102 us (30%)
  starting transfers between devices  33.6 us (10%)
  local copies, waits for them, and re-layouts  18.1 us (5%)
  between operations  16 us (5%)
  other arithmetic  12.3 us (4%)
    ppermute x39, waiting for transfers between devices, swap(): lax.ppermute(value, axis, [(i, i ^ mask) for i in range(lax.axis_size(axi...  143 us
    ppermute x39, starting transfers between devices, swap(): lax.ppermute(value, axis, [(i, i ^ mask) for i in range(lax.axis_size(axi...  33.5 us
    pallas_call x2, Pallas kernels, root_product(): pl.pallas_call(functools.partial(root_product_kernel, parts, last), grid_...  18.4 us
    pallas_call x8, Pallas kernels, gather(): pl.pallas_call(functools.partial(gather_kernel, plans, start, count, len(...  17.9 us
    unnamed x86, local copies, waits for them, and re-layouts  14.1 us
    pallas_call x2, Pallas kernels, leaf_rest(): pl.pallas_call(functools.partial(leaf_rest_kernel, dims), grid_spec=pltpu...  13.2 us
    pallas_call x1, Pallas kernels, shards(): pl.pallas_call(functools.partial(plan_kernel, local, slot, leaf_slots), o...  12.7 us
    pallas_call x1, Pallas kernels, mid_coupling(): pl.pallas_call(functools.partial(mid_coupling_kernel, plans, start, count...  9.02 us
  transfers between devices with their start and end apart: 40, of which 27 were waited for; matrix products, arithmetic and copies ran while one was open for 4% of the time, Pallas kernels for 19%

profile of v4, /device:TPU:0, one launch (start us, length us, event | category | flops | bytes accessed | tf_op | source)
XLA Modules:
  0.0 329.7 jit_solution(3054028695022871807)
XLA Ops:
  7.9 2.5 shard_map.130.order_ref
  10.4 12.1 %shard_map.131 = (bf16[16,192,128]{2,1,0:T(8,128)(2,1)}, f32[8,192,128]{2,1,0:T(8,128)}, bf16[16,192,128]{2,1,0:T(8,128)(2,1)}, f32[8,192,128]{2,1,0:T(8,128)}) custom-call(s32[32]{0:T(128)} %shard_map.130.order_ref, bf16[2048,384]{1,0:T(8,128)(2,1)} %value_ref.3, bf16[4096,2048]{1,0:T(8,128)(2,1)} %refs_7_.3, bf16[4096,2048]{1,0:T(8,128)(2,1)} %refs_7_.3, ...), custom_call_target="tpu_custom_call" | custom-call | flops 4831838208 | bytes 12582912 | tf_op jit(solution)/shard_map/pallas_call | solution.py:475
  22.4 3.0 collective-permute-start.8
  25.5 1.6 collective-permute-start.7
  27.0 12.7 %shard_map.132.table_ref = s32[2,109]{1,0:T(2,128)} custom-call(s32[2]{0:T(128)} %pad_add_fusion.place_ref, s32[2,64]{1,0:T(2,128)} %bounds_ref.3, s32[8,48]{1,0:T(8,128)} %leaf_ref.1, s32[8]{0:T(128)} %parents_ref.1), custom_call_target="tpu_custom_call" | custom-call | tf_op jit(solution)/shard_map/pallas_call | solution.py:773
  39.7 6.4 %shard_map.133 = (f32[8,192,128]{2,1,0:T(8,128)}, f32[8,192,128]{2,1,0:T(8,128)}) custom-call(s32[32]{0:T(128)} %shard_map.130.order_ref, bf16[2048,384]{1,0:T(8,128)(2,1)} %value_ref.3, bf16[4096,2048]{1,0:T(8,128)(2,1)} %refs_7_.3, bf16[4096,2048]{1,0:T(8,128)(2,1)} %refs_7_.3, bf16[4096,2048]{1,0:T(8,128)(2,1)} %refs_7_.3, bf16[4096,2048]{1,0:T(8,128)(2,1)} %refs_7_.3, ...), custom_call_target="tpu_custom_call" | custom-call | flops 1610612736 | bytes 4194304 | tf_op jit(solution)/shard_map/pallas_call | solution.py:475
  46.1 1.4 add_convert_fusion.3
  48.1 1.3 add_convert_fusion.2
  49.8 8.4 %collective-permute-done.9 = bf16[8,192,128]{2,1,0:T(8,128)(2,1)S(1)} collective-permute-done((bf16[8,192,128]{2,1,0:T(8,128)(2,1)S(1)}, bf16[8,192,128]{2,1,0:T(8,128)(2,1)S(1)}, u32[]{:S(2)}, u32[]{:S(2)}) %collective-permute-start.9) | collective-permute-done | bytes 393248 | tf_op jit(solution)/shard_map/ppermute | solution.py:703
  58.3 2.6 collective-permute-start.10
  61.0 1.5 collective-permute-start.19
  62.4 10.8 %collective-permute-done.10 = bf16[4,192,128]{2,1,0:T(8,128)(2,1)S(1)} collective-permute-done((bf16[4,192,128]{2,1,0:T(8,128)(2,1)S(1)}, bf16[4,192,128]{2,1,0:T(8,128)(2,1)S(1)}, u32[]{:S(2)}, u32[]{:S(2)}) %collective-permute-start.10) | collective-permute-done | bytes 196640 | tf_op jit(solution)/shard_map/ppermute | solution.py:703
  73.4 2.1 collective-permute-start.12
  75.5 1.7 collective-permute-done.19
  77.4 2.1 collective-permute-start.21
  79.5 1.6 collective-permute-done.12.refs_2_
  82.2 3.0 collective-permute-done.21.refs_2_
  86.4 12.6 %collective-permute-done.13 = bf16[4,192,128]{2,1,0:T(8,128)(2,1)S(1)} collective-permute-done((bf16[4,192,128]{2,1,0:T(8,128)(2,1)S(1)}, bf16[4,192,128]{2,1,0:T(8,128)(2,1)S(1)}, u32[]{:S(2)}, u32[]{:S(2)}) %collective-permute-start.13) | collective-permute-done | bytes 196640 | tf_op jit(solution)/shard_map/ppermute | solution.py:703
  99.1 3.2 collective-permute-done.22
  102.9 7.7 %collective-permute-done.14 = bf16[8,192,128]{2,1,0:T(8,128)(2,1)S(1)} collective-permute-done((bf16[8,192,128]{2,1,0:T(8,128)(2,1)S(1)}, bf16[8,192,128]{2,1,0:T(8,128)(2,1)S(1)}, u32[]{:S(2)}, u32[]{:S(2)}) %collective-permute-start.14) | collective-permute-done | bytes 393248 | tf_op jit(solution)/shard_map/ppermute | solution.py:703
  113.1 16.6 %collective-permute-done.15.refs_1_ = bf16[16,192,128]{2,1,0:T(8,128)(2,1)S(1)} collective-permute-done((bf16[16,192,128]{2,1,0:T(8,128)(2,1)S(1)}, bf16[16,192,128]{2,1,0:T(8,128)(2,1)S(1)}, u32[]{:S(2)}, u32[]{:S(2)}) %collective-permute-start.15) | collective-permute-done | bytes 786464 | tf_op jit(solution)/shard_map/ppermute | solution.py:703
  130.3 1.7 collective-permute-done.17.refs_3_
  133.2 9.0 %shard_map.136 = (f32[384,1024]{1,0:T(8,128)S(1)}, bf16[384,1024]{1,0:T(8,128)(2,1)}) custom-call(s32[2,109]{1,0:T(2,128)S(1)} %copy-done.31, bf16[16,192,128]{2,1,0:T(8,128)(2,1)S(1)} %pad_maximum_fusion.refs_0_, bf16[16,192,128]{2,1,0:T(8,128)(2,1)S(1)} %collective-permute-done.15.refs_1_, bf16[16,192,128]{2,1,0:T(8,128)(2,1)S(1)} %collective-permute-done.16.refs_2_, ...), custom_call_target="tpu_custom_call" | custom-call | flops 3221225472 | bytes 8388608 | tf_op jit(solution)/shard_map/pallas_call | solution.py:569
  142.3 1.1 copy-done.30
  143.5 2.5 collective-permute-done.27.got_ref
  146.0 5.7 %shard_map.137 = (bf16[16,384,128]{2,1,0:T(8,128)(2,1)}, bf16[384,1024]{1,0:T(8,128)(2,1)}) custom-call(s32[1]{0:T(128)} %bitcast.2.front_ref, f32[384,1024]{1,0:T(8,128)} %copy-done.30, bf16[384,1024]{1,0:T(8,128)(2,1)} %collective-permute-done.27.got_ref, bf16[2,1024,384]{2,1,0:T(8,128)(2,1)} %rhs_ref.2, bf16[4096,1024]{1,0:T(8,128)(2,1)} %matrix_ref.3), custom_call_target="tpu_custom_call" | custom-call | flops 1610612736 | bytes 4194304 | tf_op jit(solution)/shard_map/pallas_call | solution.py:508
  151.8 4.7 %shard_map.138.refs_1_.refs_8_ = bf16[16,384,128]{2,1,0:T(8,128)(2,1)} custom-call(bf16[384,1024]{1,0:T(8,128)(2,1)} %get-tuple-element.59.shift_ref, bf16[4096,1024]{1,0:T(8,128)(2,1)} %matrix_ref.3), custom_call_target="tpu_custom_call" | custom-call | flops 1610612736 | bytes 4194304 | tf_op jit(solution)/shard_map/pallas_call | solution.py:534
  157.0 3.1 collective-permute-done.28.refs_2_
  160.1 2.2 collective-permute-done.29.refs_3_
  162.3 1.4 copy-done
  163.7 1.4 copy-done.23
  165.2 3.7 %shard_map.139 = (bf16[16,192,128]{2,1,0:T(8,128)(2,1)S(1)}, bf16[16,192,128]{2,1,0:T(8,128)(2,1)S(1)}) custom-call(s32[2,109]{1,0:T(2,128)S(1)} %copy-done.31, bf16[16,384,128]{2,1,0:T(8,128)(2,1)S(1)} %copy-done.23, bf16[16,384,128]{2,1,0:T(8,128)(2,1)S(1)} %copy-done, bf16[16,384,128]{2,1,0:T(8,128)(2,1)S(1)} %collective-permute-done.28.refs_2_, ...), custom_call_target="tpu_custom_call" | custom-call | tf_op jit(solution)/shard_map/pallas_call | solution.py:413
  174.6 4.6 %shard_map.141 = (bf16[16,192,128]{2,1,0:T(8,128)(2,1)S(1)}, bf16[16,192,128]{2,1,0:T(8,128)(2,1)}) custom-call(s32[2,109]{1,0:T(2,128)S(1)} %copy-done.31, bf16[16,192,128]{2,1,0:T(8,128)(2,1)S(1)} %pad_maximum_fusion.refs_0_, bf16[16,192,128]{2,1,0:T(8,128)(2,1)S(1)} %collective-permute-done.15.refs_1_, bf16[16,192,128]{2,1,0:T(8,128)(2,1)S(1)} %copy-done.11, ...), custom_call_target="tpu_custom_call" | custom-call | tf_op jit(solution)/shard_map/pallas_call | solution.py:413
  179.2 1.6 collective-permute-start.32
  180.8 3.9 %shard_map.140 = (bf16[16,192,128]{2,1,0:T(8,128)(2,1)S(1)}, bf16[16,192,128]{2,1,0:T(8,128)(2,1)S(1)}) custom-call(s32[2,109]{1,0:T(2,128)S(1)} %copy-done.31, bf16[16,384,128]{2,1,0:T(8,128)(2,1)S(1)} %copy-done.24, bf16[16,384,128]{2,1,0:T(8,128)(2,1)S(1)} %copy-done.1, bf16[16,384,128]{2,1,0:T(8,128)(2,1)S(1)} %collective-permute-done.28.refs_2_, ...), custom_call_target="tpu_custom_call" | custom-call | tf_op jit(solution)/shard_map/pallas_call | solution.py:413
  184.7 3.8 %collective-permute-done.30 = bf16[16,192,128]{2,1,0:T(8,128)(2,1)S(1)} collective-permute-done((bf16[16,192,128]{2,1,0:T(8,128)(2,1)S(1)}, bf16[16,192,128]{2,1,0:T(8,128)(2,1)S(1)}, u32[]{:S(2)}, u32[]{:S(2)}) %collective-permute-start.30) | collective-permute-done | bytes 786464 | tf_op jit(solution)/shard_map/ppermute | solution.py:703
  190.5 1.5 collective-permute-start.37
  192.1 7.6 %collective-permute-done.32.refs_4_ = bf16[16,192,128]{2,1,0:T(8,128)(2,1)S(1)} collective-permute-done((bf16[16,192,128]{2,1,0:T(8,128)(2,1)S(1)}, bf16[16,192,128]{2,1,0:T(8,128)(2,1)S(1)}, u32[]{:S(2)}, u32[]{:S(2)}) %collective-permute-start.32) | collective-permute-done | bytes 786464 | tf_op jit(solution)/shard_map/ppermute | solution.py:703
  199.8 2.4 collective-permute-start.36
  202.9 11.6 %collective-permute-done.36 = bf16[4,192,128]{2,1,0:T(8,128)(2,1)S(1)} collective-permute-done((bf16[4,192,128]{2,1,0:T(8,128)(2,1)S(1)}, bf16[4,192,128]{2,1,0:T(8,128)(2,1)S(1)}, u32[]{:S(2)}, u32[]{:S(2)}) %collective-permute-start.36) | collective-permute-done | bytes 196640 | tf_op jit(solution)/shard_map/ppermute | solution.py:703
  214.6 3.4 %collective-permute-done.35 = bf16[4,192,128]{2,1,0:T(8,128)(2,1)S(1)} collective-permute-done((bf16[4,192,128]{2,1,0:T(8,128)(2,1)S(1)}, bf16[4,192,128]{2,1,0:T(8,128)(2,1)S(1)}, u32[]{:S(2)}, u32[]{:S(2)}) %collective-permute-start.35) | collective-permute-done | bytes 196640 | tf_op jit(solution)/shard_map/ppermute | solution.py:703
  218.1 1.6 collective-permute-start.39
  222.2 6.3 %collective-permute-done.39 = bf16[4,384,128]{2,1,0:T(8,128)(2,1)S(1)} collective-permute-done((bf16[4,384,128]{2,1,0:T(8,128)(2,1)S(1)}, bf16[4,384,128]{2,1,0:T(8,128)(2,1)S(1)}, u32[]{:S(2)}, u32[]{:S(2)}) %collective-permute-start.39) | collective-permute-done | bytes 393248 | tf_op jit(solution)/shard_map/ppermute | solution.py:703
  228.6 11.5 %conditional.1 = (bf16[4,384,128]{2,1,0:T(8,128)(2,1)}) conditional(s32[]{:T(128)} %bitcast.12, bf16[4,384,128]{2,1,0:T(8,128)(2,1)S(1)} %get-tuple-element.79, bf16[4,384,128]{2,1,0:T(8,128)(2,1)S(1)} %get-tuple-element.79, bf16[4,384,128]{2,1,0:T(8,128)(2,1)S(1)} %get-tuple-element.79, ...), branch_computations={%region_0.1_spmd, %region_1.2_spmd, %region_2.3_spmd, %region_3.4_... | conditional | bytes 1572912 | solution.py:730
  228.6 2.6 collective-permute-start.5
  231.3 8.9 %collective-permute-done.5 = bf16[4,384,128]{2,1,0:T(8,128)(2,1)} collective-permute-done((bf16[4,384,128]{2,1,0:T(8,128)(2,1)S(1)}, bf16[4,384,128]{2,1,0:T(8,128)(2,1)}, u32[]{:S(2)}, u32[]{:S(2)}) %collective-permute-start.5) | collective-permute-done | bytes 393248 | tf_op jit(solution)/shard_map/cond/branch_5_fun/ppermute | solution.py:703
  242.1 1.5 collective-permute-done.40.refs_6_
  244.5 7.9 %shard_map.145 = (bf16[2,384,1024]{2,1,0:T(8,128)(2,1)}, bf16[384,1536]{1,0:T(8,128)(2,1)}) custom-call(s32[2,109]{1,0:T(2,128)} %shard_map.132.table_ref, s32[4]{0:T(128)} %pad_add_fusion.1.order_ref, bf16[16,192,128]{2,1,0:T(8,128)(2,1)} %copy-done.2, bf16[16,192,128]{2,1,0:T(8,128)(2,1)} %copy-done.6, bf16[16,192,128]{2,1,0:T(8,128)(2,1)} %copy-done.10, ...), custom_call_target="tpu_custom_call" | custom-call | flops 2415919104 | bytes 6291456 | tf_op jit(solution)/shard_map/pallas_call | solution.py:599
  252.6 7.5 %shard_map.146.keep_ref = f32[2,384,1024]{2,1,0:T(8,128)} custom-call(s32[4]{0:T(128)} %pad_add_fusion.1.order_ref, bf16[384,1536]{1,0:T(8,128)(2,1)} %get-tuple-element.70.value_ref, bf16[1536,4096]{1,0:T(8,128)(2,1)} %bitcast.24), custom_call_target="tpu_custom_call" | custom-call | flops 2415919104 | bytes 6291456 | tf_op jit(solution)/shard_map/pallas_call | solution.py:670
  260.2 2.9 fusion.2
  263.1 1.6 collective-permute-start.42
  265.9 1.4 shard_map.142
  268.0 1.9 copy.16
  270.0 13.3 %collective-permute-done.42.far_ref = bf16[384,1024]{1,0:T(8,128)(2,1)} collective-permute-done((bf16[384,1024]{1,0:T(8,128)(2,1)}, bf16[384,1024]{1,0:T(8,128)(2,1)}, u32[]{:S(2)}, u32[]{:S(2)}) %collective-permute-start.42) | collective-permute-done | bytes 786464 | tf_op jit(solution)/shard_map/ppermute | solution.py:703
  283.2 6.8 %shard_map.147 = (bf16[2,384,1024]{2,1,0:T(8,128)(2,1)}, bf16[384,1024]{1,0:T(8,128)(2,1)}) custom-call(s32[4]{0:T(128)} %pad_add_fusion.1.order_ref, f32[2,384,1024]{2,1,0:T(8,128)} %shard_map.146.keep_ref, bf16[2,384,1024]{2,1,0:T(8,128)(2,1)} %collective-permute-done.41.got_ref, bf16[384,1024]{1,0:T(8,128)(2,1)} %collective-permute-done.42.far_ref, ...), custom_call_target="tpu_custom_call" | custom-call | flops 1610612736 | bytes 4194304 | tf_op jit(solution)/shard_map/pallas_call | solution.py:636
  290.0 5.7 %shard_map.148.keep_ref = f32[2,384,1024]{2,1,0:T(8,128)} custom-call(s32[4]{0:T(128)} %pad_add_fusion.1.order_ref, bf16[384,1024]{1,0:T(8,128)(2,1)} %get-tuple-element.72.value_ref, bf16[4096,1024]{1,0:T(8,128)(2,1)} %bitcast.26), custom_call_target="tpu_custom_call" | custom-call | flops 1610612736 | bytes 4194304 | tf_op jit(solution)/shard_map/pallas_call | solution.py:670
  295.6 3.1 fusion.3
  298.8 1.6 collective-permute-start.44
  300.3 5.1 %all-gather.2.cloned.1.call-done.refs_0_ = bf16[32,384,128]{2,1,0:T(8,128)(2,1)} async-done(((bf16[4,384,128]{2,1,0:T(8,128)(2,1)}), bf16[32,384,128]{2,1,0:T(8,128)(2,1)}) %all-gather.2.cloned.1.call-update) | async-done | bytes 3145744 | tf_op jit(solution)/shard_map/all_gather | solution.py:826
  305.4 1.9 copy-done.22
  308.5 1.7 collective-permute-done.38.refs_1_
  310.2 1.1 shard_map.144
  312.3 6.6 %collective-permute-done.44.far_ref = bf16[384,1024]{1,0:T(8,128)(2,1)S(1)} collective-permute-done((bf16[384,1024]{1,0:T(8,128)(2,1)}, bf16[384,1024]{1,0:T(8,128)(2,1)S(1)}, u32[]{:S(2)}, u32[]{:S(2)}) %collective-permute-start.44) | collective-permute-done | bytes 786464 | tf_op jit(solution)/shard_map/ppermute | solution.py:703
  319.8 3.0 shard_map.149
  (152 shorter events, 27.5 us)
Async XLA Ops:
  7.2 298.3 %all-gather.2.cloned.1.call-start = ((), (), s32[]{:S(2)}) async-start(), calls=%async_computation | async-start | bytes 3538944 | tf_op jit(solution)/shard_map/all_gather | solution.py:826
  22.4 23.7 %collective-permute-start.8 = (bf16[16,192,128]{2,1,0:T(8,128)(2,1)}, bf16[16,192,128]{2,1,0:T(8,128)(2,1)S(1)}, u32[]{:S(2)}, u32[]{:S(2)}) collective-permute-start(bf16[16,192,128]{2,1,0:T(8,128)(2,1)} %get-tuple-element.47), channel_id=1, source_target_pairs={{0,1},{1,0},{2,3},{3,2},{4,5},{5,4},{6,7},{7,6},{8,9},{9,8},{10,11... | collective-permute-start | bytes 2359304 | tf_op jit(solution)/shard_map/ppermute | solution.py:703
  25.5 20.6 %collective-permute-start.7 = (bf16[16,192,128]{2,1,0:T(8,128)(2,1)}, bf16[16,192,128]{2,1,0:T(8,128)(2,1)S(1)}, u32[]{:S(2)}, u32[]{:S(2)}) collective-permute-start(bf16[16,192,128]{2,1,0:T(8,128)(2,1)} %get-tuple-element.46), channel_id=1, source_target_pairs={{0,2},{1,3},{2,0},{3,1},{4,6},{5,7},{6,4},{7,5},{8,10},{9,11},{10,... | collective-permute-start | bytes 2359304 | tf_op jit(solution)/shard_map/ppermute | solution.py:703
  39.7 6.4 %copy-start.38 = (f32[8,192,128]{2,1,0:T(8,128)S(1)}, f32[8,192,128]{2,1,0:T(8,128)}, u32[]{:S(2)}) copy-start(f32[8,192,128]{2,1,0:T(8,128)} %get-tuple-element.52) | copy-start | bytes 2359300
  39.7 8.3 %copy-start.37 = (f32[8,192,128]{2,1,0:T(8,128)S(1)}, f32[8,192,128]{2,1,0:T(8,128)}, u32[]{:S(2)}) copy-start(f32[8,192,128]{2,1,0:T(8,128)} %get-tuple-element.55) | copy-start | bytes 2359300
  46.1 87.1 %slice-start = ((s8[8388608]{0:T(1024)(128)(4,1)}), s8[4194304]{0:T(1024)(128)(4,1)S(1)}, s32[]{:S(2)}) async-start(s8[8388608]{0:T(1024)(128)(4,1)} %bitcast.19), calls=%async_computation.1 | async-start | bytes 8388608
  47.6 10.6 %collective-permute-start.9 = (bf16[8,192,128]{2,1,0:T(8,128)(2,1)S(1)}, bf16[8,192,128]{2,1,0:T(8,128)(2,1)S(1)}, u32[]{:S(2)}, u32[]{:S(2)}) collective-permute-start(bf16[8,192,128]{2,1,0:T(8,128)(2,1)S(1)} %get-tuple-element.82), channel_id=1, source_target_pairs={{0,2},{1,3},{2,0},{3,1},{4,6},{5,7},{6,4},{7,5},{8,10},{9,11},{10,... | collective-permute-start | bytes 1179656 | tf_op jit(solution)/shard_map/ppermute | solution.py:703
  49.4 11.6 %collective-permute-start.18 = (bf16[8,192,128]{2,1,0:T(8,128)(2,1)S(1)}, bf16[8,192,128]{2,1,0:T(8,128)(2,1)S(1)}, u32[]{:S(2)}, u32[]{:S(2)}) collective-permute-start(bf16[8,192,128]{2,1,0:T(8,128)(2,1)S(1)} %get-tuple-element.80), channel_id=1, source_target_pairs={{0,1},{1,0},{2,3},{3,2},{4,5},{5,4},{6,7},{7,6},{8,9},{9,8},{10,11... | collective-permute-start | bytes 1179656 | tf_op jit(solution)/shard_map/ppermute | solution.py:703
  58.2 22.9 %copy-start.31 = (s32[2,109]{1,0:T(2,128)S(1)}, s32[2,109]{1,0:T(2,128)}, u32[]{:S(2)}) copy-start(s32[2,109]{1,0:T(2,128)} %shard_map.132.table_ref) | copy-start | bytes 2620
  58.3 14.9 %collective-permute-start.10 = (bf16[4,192,128]{2,1,0:T(8,128)(2,1)S(1)}, bf16[4,192,128]{2,1,0:T(8,128)(2,1)S(1)}, u32[]{:S(2)}, u32[]{:S(2)}) collective-permute-start(bf16[4,192,128]{2,1,0:T(8,128)(2,1)S(1)} %fusion.13), channel_id=1, source_target_pairs={{0,4},{1,5},{2,6},{3,7},{4,0},{5,1},{6,2},{7,3},{8,12},{9,13},{10,... | collective-permute-start | bytes 589832 | tf_op jit(solution)/shard_map/ppermute | solution.py:703
  60.9 72.3 %slice-start.1 = ((s8[8388608]{0:T(1024)(128)(4,1)}), s8[4194304]{0:T(1024)(128)(4,1)S(1)}, s32[]{:S(2)}) async-start(s8[8388608]{0:T(1024)(128)(4,1)} %bitcast.19), calls=%async_computation.2 | async-start | bytes 8388608
  61.0 16.2 %collective-permute-start.19 = (bf16[4,192,128]{2,1,0:T(8,128)(2,1)S(1)}, bf16[4,192,128]{2,1,0:T(8,128)(2,1)S(1)}, u32[]{:S(2)}, u32[]{:S(2)}) collective-permute-start(bf16[4,192,128]{2,1,0:T(8,128)(2,1)S(1)} %fusion.10), channel_id=1, source_target_pairs={{0,4},{1,5},{2,6},{3,7},{4,0},{5,1},{6,2},{7,3},{8,12},{9,13},{10,... | collective-permute-start | bytes 589832 | tf_op jit(solution)/shard_map/ppermute | solution.py:703
  73.3 6.2 %collective-permute-start.11 = (bf16[4,192,128]{2,1,0:T(8,128)(2,1)S(1)}, bf16[4,192,128]{2,1,0:T(8,128)(2,1)S(1)}, u32[]{:S(2)}, u32[]{:S(2)}) collective-permute-start(bf16[4,192,128]{2,1,0:T(8,128)(2,1)S(1)} %fusion.15.refs_0_), channel_id=1, source_target_pairs={{0,8},{8,0},{16,24},{24,16},{1,9},{9,1},{17,25},{25,17},{2,10},{10... | collective-permute-start | bytes 589832 | tf_op jit(solution)/shard_map/ppermute | solution.py:703
  73.4 7.8 %collective-permute-start.12 = (bf16[4,192,128]{2,1,0:T(8,128)(2,1)S(1)}, bf16[4,192,128]{2,1,0:T(8,128)(2,1)S(1)}, u32[]{:S(2)}, u32[]{:S(2)}) collective-permute-start(bf16[4,192,128]{2,1,0:T(8,128)(2,1)S(1)} %fusion.15.refs_0_), channel_id=1, source_target_pairs={{0,16},{8,24},{16,0},{24,8},{1,17},{9,25},{17,1},{25,9},{2,18},{10... | collective-permute-start | bytes 589832 | tf_op jit(solution)/shard_map/ppermute | solution.py:703
  77.3 4.9 %collective-permute-start.20 = (bf16[4,192,128]{2,1,0:T(8,128)(2,1)S(1)}, bf16[4,192,128]{2,1,0:T(8,128)(2,1)S(1)}, u32[]{:S(2)}, u32[]{:S(2)}) collective-permute-start(bf16[4,192,128]{2,1,0:T(8,128)(2,1)S(1)} %fusion.12.refs_0_), channel_id=1, source_target_pairs={{0,8},{8,0},{16,24},{24,16},{1,9},{9,1},{17,25},{25,17},{2,10},{10... | collective-permute-start | bytes 589832 | tf_op jit(solution)/shard_map/ppermute | solution.py:703
  77.4 7.8 %collective-permute-start.21 = (bf16[4,192,128]{2,1,0:T(8,128)(2,1)S(1)}, bf16[4,192,128]{2,1,0:T(8,128)(2,1)S(1)}, u32[]{:S(2)}, u32[]{:S(2)}) collective-permute-start(bf16[4,192,128]{2,1,0:T(8,128)(2,1)S(1)} %fusion.12.refs_0_), channel_id=1, source_target_pairs={{0,16},{8,24},{16,0},{24,8},{1,17},{9,25},{17,1},{25,9},{2,18},{10... | collective-permute-start | bytes 589832 | tf_op jit(solution)/shard_map/ppermute | solution.py:703
  82.1 16.9 %collective-permute-start.13 = (bf16[4,192,128]{2,1,0:T(8,128)(2,1)S(1)}, bf16[4,192,128]{2,1,0:T(8,128)(2,1)S(1)}, u32[]{:S(2)}, u32[]{:S(2)}) collective-permute-start(bf16[4,192,128]{2,1,0:T(8,128)(2,1)S(1)} %shard_map.134), channel_id=1, source_target_pairs={{0,4},{1,5},{2,6},{3,7},{4,0},{5,1},{6,2},{7,3},{8,12},{9,13},{10,... | collective-permute-start | bytes 589832 | tf_op jit(solution)/shard_map/ppermute | solution.py:703
  86.3 16.0 %collective-permute-start.22 = (bf16[4,192,128]{2,1,0:T(8,128)(2,1)S(1)}, bf16[4,192,128]{2,1,0:T(8,128)(2,1)S(1)}, u32[]{:S(2)}, u32[]{:S(2)}) collective-permute-start(bf16[4,192,128]{2,1,0:T(8,128)(2,1)S(1)} %shard_map.135), channel_id=1, source_target_pairs={{0,4},{1,5},{2,6},{3,7},{4,0},{5,1},{6,2},{7,3},{8,12},{9,13},{10,... | collective-permute-start | bytes 589832 | tf_op jit(solution)/shard_map/ppermute | solution.py:703
  99.1 11.6 %collective-permute-start.14 = (bf16[8,192,128]{2,1,0:T(8,128)(2,1)S(1)}, bf16[8,192,128]{2,1,0:T(8,128)(2,1)S(1)}, u32[]{:S(2)}, u32[]{:S(2)}) collective-permute-start(bf16[8,192,128]{2,1,0:T(8,128)(2,1)S(1)} %pad_maximum_fusion.3), channel_id=1, source_target_pairs={{0,2},{1,3},{2,0},{3,1},{4,6},{5,7},{6,4},{7,5},{8,10},{9,11},{10,... | collective-permute-start | bytes 1179656 | tf_op jit(solution)/shard_map/ppermute | solution.py:703
  102.3 10.0 %collective-permute-start.23 = (bf16[8,192,128]{2,1,0:T(8,128)(2,1)S(1)}, bf16[8,192,128]{2,1,0:T(8,128)(2,1)S(1)}, u32[]{:S(2)}, u32[]{:S(2)}) collective-permute-start(bf16[8,192,128]{2,1,0:T(8,128)(2,1)S(1)} %pad_maximum_fusion.4), channel_id=1, source_target_pairs={{0,1},{1,0},{2,3},{3,2},{4,5},{5,4},{6,7},{7,6},{8,9},{9,8},{10,11... | collective-permute-start | bytes 1179656 | tf_op jit(solution)/shard_map/ppermute | solution.py:703
  110.7 59.3 %copy-start.2 = (bf16[16,192,128]{2,1,0:T(8,128)(2,1)}, bf16[16,192,128]{2,1,0:T(8,128)(2,1)S(1)}, u32[]{:S(2)}) copy-start(bf16[16,192,128]{2,1,0:T(8,128)(2,1)S(1)} %pad_maximum_fusion.refs_0_) | copy-start | bytes 2359300
  110.7 19.1 %collective-permute-start.15 = (bf16[16,192,128]{2,1,0:T(8,128)(2,1)S(1)}, bf16[16,192,128]{2,1,0:T(8,128)(2,1)S(1)}, u32[]{:S(2)}, u32[]{:S(2)}) collective-permute-start(bf16[16,192,128]{2,1,0:T(8,128)(2,1)S(1)} %pad_maximum_fusion.refs_0_), channel_id=1, source_target_pairs={{0,1},{1,0},{2,3},{3,2},{4,5},{5,4},{6,7},{7,6},{8,9},{9,8},{10,11... | collective-permute-start | bytes 2359304 | tf_op jit(solution)/shard_map/ppermute | solution.py:703
  112.4 57.6 %copy-start.4 = (bf16[16,192,128]{2,1,0:T(8,128)(2,1)}, bf16[16,192,128]{2,1,0:T(8,128)(2,1)S(1)}, u32[]{:S(2)}) copy-start(bf16[16,192,128]{2,1,0:T(8,128)(2,1)S(1)} %pad_maximum_fusion.1.refs_4_.refs_5_.refs_7_) | copy-start | bytes 2359300
  112.5 17.7 %collective-permute-start.24 = (bf16[16,192,128]{2,1,0:T(8,128)(2,1)S(1)}, bf16[16,192,128]{2,1,0:T(8,128)(2,1)S(1)}, u32[]{:S(2)}, u32[]{:S(2)}) collective-permute-start(bf16[16,192,128]{2,1,0:T(8,128)(2,1)S(1)} %pad_maximum_fusion.1.refs_4_.refs_5_.refs_7_), channel_id=1, source_target_pairs={{0,2},{1,3},{2,0},{3,1},{4,6},{5,7},{6,4},{7,5},{8,10},{9,11},{10,... | collective-permute-start | bytes 2359304 | tf_op jit(solution)/shard_map/ppermute | solution.py:703
  112.5 17.7 %collective-permute-start.16 = (bf16[16,192,128]{2,1,0:T(8,128)(2,1)S(1)}, bf16[16,192,128]{2,1,0:T(8,128)(2,1)S(1)}, u32[]{:S(2)}, u32[]{:S(2)}) collective-permute-start(bf16[16,192,128]{2,1,0:T(8,128)(2,1)S(1)} %pad_maximum_fusion.refs_0_), channel_id=1, source_target_pairs={{0,8},{8,0},{16,24},{24,16},{1,9},{9,1},{17,25},{25,17},{2,10},{10... | collective-permute-start | bytes 2359304 | tf_op jit(solution)/shard_map/ppermute | solution.py:703
  112.6 17.7 %collective-permute-start.25 = (bf16[16,192,128]{2,1,0:T(8,128)(2,1)S(1)}, bf16[16,192,128]{2,1,0:T(8,128)(2,1)S(1)}, u32[]{:S(2)}, u32[]{:S(2)}) collective-permute-start(bf16[16,192,128]{2,1,0:T(8,128)(2,1)S(1)} %pad_maximum_fusion.1.refs_4_.refs_5_.refs_7_), channel_id=1, source_target_pairs={{0,8},{8,0},{16,24},{24,16},{1,9},{9,1},{17,25},{25,17},{2,10},{10... | collective-permute-start | bytes 2359304 | tf_op jit(solution)/shard_map/ppermute | solution.py:703
  129.8 40.3 %copy-start.6 = (bf16[16,192,128]{2,1,0:T(8,128)(2,1)}, bf16[16,192,128]{2,1,0:T(8,128)(2,1)S(1)}, u32[]{:S(2)}) copy-start(bf16[16,192,128]{2,1,0:T(8,128)(2,1)S(1)} %collective-permute-done.15.refs_1_) | copy-start | bytes 2359300
  129.8 2.3 collective-permute-start.17
  130.1 39.9 %copy-start.8 = (bf16[16,192,128]{2,1,0:T(8,128)(2,1)}, bf16[16,192,128]{2,1,0:T(8,128)(2,1)S(1)}, u32[]{:S(2)}) copy-start(bf16[16,192,128]{2,1,0:T(8,128)(2,1)S(1)} %collective-permute-done.24.refs_5_.refs_6_.refs_8_) | copy-start | bytes 2359300
  130.1 3.0 collective-permute-start.26
  130.3 11.9 %copy-start.10 = (bf16[16,192,128]{2,1,0:T(8,128)(2,1)}, bf16[16,192,128]{2,1,0:T(8,128)(2,1)S(1)}, u32[]{:S(2)}) copy-start(bf16[16,192,128]{2,1,0:T(8,128)(2,1)S(1)} %collective-permute-done.16.refs_2_) | copy-start | bytes 2359300
  130.3 11.9 %copy-start.13 = (bf16[16,192,128]{2,1,0:T(8,128)(2,1)}, bf16[16,192,128]{2,1,0:T(8,128)(2,1)S(1)}, u32[]{:S(2)}) copy-start(bf16[16,192,128]{2,1,0:T(8,128)(2,1)S(1)} %collective-permute-done.25.refs_6_.refs_7_.refs_9_) | copy-start | bytes 2359300
  132.0 10.2 %copy-start.16 = (bf16[16,192,128]{2,1,0:T(8,128)(2,1)}, bf16[16,192,128]{2,1,0:T(8,128)(2,1)S(1)}, u32[]{:S(2)}) copy-start(bf16[16,192,128]{2,1,0:T(8,128)(2,1)S(1)} %collective-permute-done.17.refs_3_) | copy-start | bytes 2359300
  133.2 9.1 %copy-start.19 = (bf16[16,192,128]{2,1,0:T(8,128)(2,1)}, bf16[16,192,128]{2,1,0:T(8,128)(2,1)S(1)}, u32[]{:S(2)}) copy-start(bf16[16,192,128]{2,1,0:T(8,128)(2,1)S(1)} %collective-permute-done.26.refs_7_.refs_8_.refs_10_) | copy-start | bytes 2359300
  143.4 2.6 collective-permute-start.27
  156.5 3.6 %collective-permute-start.28 = (bf16[16,384,128]{2,1,0:T(8,128)(2,1)}, bf16[16,384,128]{2,1,0:T(8,128)(2,1)S(1)}, u32[]{:S(2)}, u32[]{:S(2)}) collective-permute-start(bf16[16,384,128]{2,1,0:T(8,128)(2,1)} %get-tuple-element.58.refs_0_), channel_id=1, source_target_pairs={{0,8},{8,0},{16,24},{24,16},{1,9},{9,1},{17,25},{25,17},{2,10},{10... | collective-permute-start | bytes 4718600 | tf_op jit(solution)/shard_map/ppermute | solution.py:703
  156.6 5.7 %collective-permute-start.29 = (bf16[16,384,128]{2,1,0:T(8,128)(2,1)}, bf16[16,384,128]{2,1,0:T(8,128)(2,1)S(1)}, u32[]{:S(2)}, u32[]{:S(2)}) collective-permute-start(bf16[16,384,128]{2,1,0:T(8,128)(2,1)} %shard_map.138.refs_1_.refs_8_), channel_id=1, source_target_pairs={{0,8},{8,0},{16,24},{24,16},{1,9},{9,1},{17,25},{25,17},{2,10},{10... | collective-permute-start | bytes 4718600 | tf_op jit(solution)/shard_map/ppermute | solution.py:703
  168.9 19.6 %collective-permute-start.30 = (bf16[16,192,128]{2,1,0:T(8,128)(2,1)S(1)}, bf16[16,192,128]{2,1,0:T(8,128)(2,1)S(1)}, u32[]{:S(2)}, u32[]{:S(2)}) collective-permute-start(bf16[16,192,128]{2,1,0:T(8,128)(2,1)S(1)} %get-tuple-element.62), channel_id=1, source_target_pairs={{0,2},{1,3},{2,0},{3,1},{4,6},{5,7},{6,4},{7,5},{8,10},{9,11},{10,... | collective-permute-start | bytes 2359304 | tf_op jit(solution)/shard_map/ppermute | solution.py:703
  169.0 20.6 %collective-permute-start.33 = (bf16[16,192,128]{2,1,0:T(8,128)(2,1)S(1)}, bf16[16,192,128]{2,1,0:T(8,128)(2,1)S(1)}, u32[]{:S(2)}, u32[]{:S(2)}) collective-permute-start(bf16[16,192,128]{2,1,0:T(8,128)(2,1)S(1)} %get-tuple-element.60.refs_4_), channel_id=1, source_target_pairs={{0,1},{1,0},{2,3},{3,2},{4,5},{5,4},{6,7},{7,6},{8,9},{9,8},{10,11... | collective-permute-start | bytes 2359304 | tf_op jit(solution)/shard_map/ppermute | solution.py:703
  174.6 6.2 %copy-start.24 = (bf16[16,384,128]{2,1,0:T(8,128)(2,1)S(1)}, bf16[16,384,128]{2,1,0:T(8,128)(2,1)}, u32[]{:S(2)}) copy-start(bf16[16,384,128]{2,1,0:T(8,128)(2,1)} %get-tuple-element.58.refs_0_) | copy-start | bytes 4718596
  179.2 20.5 %collective-permute-start.32 = (bf16[16,192,128]{2,1,0:T(8,128)(2,1)S(1)}, bf16[16,192,128]{2,1,0:T(8,128)(2,1)S(1)}, u32[]{:S(2)}, u32[]{:S(2)}) collective-permute-start(bf16[16,192,128]{2,1,0:T(8,128)(2,1)S(1)} %get-tuple-element.63), channel_id=1, source_target_pairs={{0,16},{8,24},{16,0},{24,8},{1,17},{9,25},{17,1},{25,9},{2,18},{10... | collective-permute-start | bytes 2359304 | tf_op jit(solution)/shard_map/ppermute | solution.py:703
  188.7 11.0 %collective-permute-start.31 = (bf16[8,192,128]{2,1,0:T(8,128)(2,1)S(1)}, bf16[8,192,128]{2,1,0:T(8,128)(2,1)S(1)}, u32[]{:S(2)}, u32[]{:S(2)}) collective-permute-start(bf16[8,192,128]{2,1,0:T(8,128)(2,1)S(1)} %get-tuple-element.77), channel_id=1, source_target_pairs={{0,1},{1,0},{2,3},{3,2},{4,5},{5,4},{6,7},{7,6},{8,9},{9,8},{10,11... | collective-permute-start | bytes 1179656 | tf_op jit(solution)/shard_map/ppermute | solution.py:703
  189.8 12.4 %collective-permute-start.34 = (bf16[8,192,128]{2,1,0:T(8,128)(2,1)S(1)}, bf16[8,192,128]{2,1,0:T(8,128)(2,1)S(1)}, u32[]{:S(2)}, u32[]{:S(2)}) collective-permute-start(bf16[8,192,128]{2,1,0:T(8,128)(2,1)S(1)} %get-tuple-element.74), channel_id=1, source_target_pairs={{0,2},{1,3},{2,0},{3,1},{4,6},{5,7},{6,4},{7,5},{8,10},{9,11},{10,... | collective-permute-start | bytes 1179656 | tf_op jit(solution)/shard_map/ppermute | solution.py:703
  190.5 27.6 %collective-permute-start.37 = (bf16[16,192,128]{2,1,0:T(8,128)(2,1)}, bf16[16,192,128]{2,1,0:T(8,128)(2,1)S(1)}, u32[]{:S(2)}, u32[]{:S(2)}) collective-permute-start(bf16[16,192,128]{2,1,0:T(8,128)(2,1)} %get-tuple-element.67), channel_id=1, source_target_pairs={{0,16},{8,24},{16,0},{24,8},{1,17},{9,25},{17,1},{25,9},{2,18},{10... | collective-permute-start | bytes 2359304 | tf_op jit(solution)/shard_map/ppermute | solution.py:703
  199.7 18.3 %copy-start.25 = (bf16[16,192,128]{2,1,0:T(8,128)(2,1)}, bf16[16,192,128]{2,1,0:T(8,128)(2,1)S(1)}, u32[]{:S(2)}) copy-start(bf16[16,192,128]{2,1,0:T(8,128)(2,1)S(1)} %collective-permute-done.32.refs_4_) | copy-start | bytes 2359300
  199.8 14.7 %collective-permute-start.36 = (bf16[4,192,128]{2,1,0:T(8,128)(2,1)S(1)}, bf16[4,192,128]{2,1,0:T(8,128)(2,1)S(1)}, u32[]{:S(2)}, u32[]{:S(2)}) collective-permute-start(bf16[4,192,128]{2,1,0:T(8,128)(2,1)S(1)} %fusion.4), channel_id=1, source_target_pairs={{0,4},{1,5},{2,6},{3,7},{4,0},{5,1},{6,2},{7,3},{8,12},{9,13},{10,... | collective-permute-start | bytes 589832 | tf_op jit(solution)/shard_map/ppermute | solution.py:703
  202.2 17.5 %copy-start.40 = (s32[8]{0:T(128)S(1)}, s32[8]{0:T(128)}, u32[]{:S(2)}) copy-start(s32[8]{0:T(128)} %parents_ref.1) | copy-start | bytes 100
  202.2 15.8 %collective-permute-start.35 = (bf16[4,192,128]{2,1,0:T(8,128)(2,1)S(1)}, bf16[4,192,128]{2,1,0:T(8,128)(2,1)S(1)}, u32[]{:S(2)}, u32[]{:S(2)}) collective-permute-start(bf16[4,192,128]{2,1,0:T(8,128)(2,1)S(1)} %fusion.7), channel_id=1, source_target_pairs={{0,4},{1,5},{2,6},{3,7},{4,0},{5,1},{6,2},{7,3},{8,12},{9,13},{10,... | collective-permute-start | bytes 589832 | tf_op jit(solution)/shard_map/ppermute | solution.py:703
  218.1 23.1 %copy-start.33 = (bf16[4,384,128]{2,1,0:T(8,128)(2,1)}, bf16[4,384,128]{2,1,0:T(8,128)(2,1)S(1)}, u32[]{:S(2)}) copy-start(bf16[4,384,128]{2,1,0:T(8,128)(2,1)S(1)} %pad_maximum_fusion.5) | copy-start | bytes 1179652
  218.1 23.1 %copy-start.27 = (bf16[16,192,128]{2,1,0:T(8,128)(2,1)}, bf16[16,192,128]{2,1,0:T(8,128)(2,1)S(1)}, u32[]{:S(2)}) copy-start(bf16[16,192,128]{2,1,0:T(8,128)(2,1)S(1)} %collective-permute-done.37.refs_9_.refs_11_) | copy-start | bytes 2359300
  218.1 10.4 %collective-permute-start.39 = (bf16[4,384,128]{2,1,0:T(8,128)(2,1)S(1)}, bf16[4,384,128]{2,1,0:T(8,128)(2,1)S(1)}, u32[]{:S(2)}, u32[]{:S(2)}) collective-permute-start(bf16[4,384,128]{2,1,0:T(8,128)(2,1)S(1)} %pad_maximum_fusion.5), channel_id=1, source_target_pairs={{0,16},{8,24},{16,0},{24,8},{1,17},{9,25},{17,1},{25,9},{2,18},{10... | collective-permute-start | bytes 1179656 | tf_op jit(solution)/shard_map/ppermute | solution.py:703
  228.6 11.5 %collective-permute-start.5 = (bf16[4,384,128]{2,1,0:T(8,128)(2,1)S(1)}, bf16[4,384,128]{2,1,0:T(8,128)(2,1)}, u32[]{:S(2)}, u32[]{:S(2)}) collective-permute-start(bf16[4,384,128]{2,1,0:T(8,128)(2,1)S(1)} %param.5), channel_id=1, source_target_pairs={{0,6},{1,7},{2,4},{3,5},{4,2},{5,3},{6,0},{7,1},{8,14},{9,15},{10,... | collective-permute-start | bytes 1179656 | tf_op jit(solution)/shard_map/cond/branch_5_fun/ppermute | solution.py:703
  241.2 2.4 collective-permute-start.40
  252.4 7.8 %collective-permute-start.41 = (bf16[2,384,1024]{2,1,0:T(8,128)(2,1)}, bf16[2,384,1024]{2,1,0:T(8,128)(2,1)}, u32[]{:S(2)}, u32[]{:S(2)}) collective-permute-start(bf16[2,384,1024]{2,1,0:T(8,128)(2,1)} %get-tuple-element.71), channel_id=1, source_target_pairs={{0,8},{8,0},{16,24},{24,16},{1,9},{9,1},{17,25},{25,17},{2,10},{10... | collective-permute-start | bytes 4718600 | tf_op jit(solution)/shard_map/ppermute | solution.py:703
  252.6 12.1 %copy-start.12 = (bf16[16,192,128]{2,1,0:T(8,128)(2,1)S(1)}, bf16[16,192,128]{2,1,0:T(8,128)(2,1)}, u32[]{:S(2)}) copy-start(bf16[16,192,128]{2,1,0:T(8,128)(2,1)} %copy-done.10) | copy-start | bytes 2359300
  252.6 12.1 %copy-start.15 = (bf16[16,192,128]{2,1,0:T(8,128)(2,1)S(1)}, bf16[16,192,128]{2,1,0:T(8,128)(2,1)}, u32[]{:S(2)}) copy-start(bf16[16,192,128]{2,1,0:T(8,128)(2,1)} %copy-done.13) | copy-start | bytes 2359300
  252.6 12.1 %copy-start.18 = (bf16[16,192,128]{2,1,0:T(8,128)(2,1)S(1)}, bf16[16,192,128]{2,1,0:T(8,128)(2,1)}, u32[]{:S(2)}) copy-start(bf16[16,192,128]{2,1,0:T(8,128)(2,1)} %copy-done.16) | copy-start | bytes 2359300
  252.6 12.1 %copy-start.21 = (bf16[16,192,128]{2,1,0:T(8,128)(2,1)S(1)}, bf16[16,192,128]{2,1,0:T(8,128)(2,1)}, u32[]{:S(2)}) copy-start(bf16[16,192,128]{2,1,0:T(8,128)(2,1)} %copy-done.19) | copy-start | bytes 2359300
  252.6 12.1 %copy-start.26 = (bf16[16,192,128]{2,1,0:T(8,128)(2,1)S(1)}, bf16[16,192,128]{2,1,0:T(8,128)(2,1)}, u32[]{:S(2)}) copy-start(bf16[16,192,128]{2,1,0:T(8,128)(2,1)} %copy-done.25) | copy-start | bytes 2359300
  252.6 12.1 %copy-start.32 = (s32[2,109]{1,0:T(2,128)S(1)}, s32[2,109]{1,0:T(2,128)}, u32[]{:S(2)}) copy-start(s32[2,109]{1,0:T(2,128)} %shard_map.132.table_ref) | copy-start | bytes 2620
  263.1 20.1 %collective-permute-start.42 = (bf16[384,1024]{1,0:T(8,128)(2,1)}, bf16[384,1024]{1,0:T(8,128)(2,1)}, u32[]{:S(2)}, u32[]{:S(2)}) collective-permute-start(bf16[384,1024]{1,0:T(8,128)(2,1)} %fusion.2), channel_id=1, source_target_pairs={{0,16},{8,24},{16,0},{24,8},{1,17},{9,25},{17,1},{25,9},{2,18},{10... | collective-permute-start | bytes 2359304 | tf_op jit(solution)/shard_map/ppermute | solution.py:703
  290.0 5.7 %collective-permute-start.43 = (bf16[2,384,1024]{2,1,0:T(8,128)(2,1)}, bf16[2,384,1024]{2,1,0:T(8,128)(2,1)S(1)}, u32[]{:S(2)}, u32[]{:S(2)}) collective-permute-start(bf16[2,384,1024]{2,1,0:T(8,128)(2,1)} %get-tuple-element.73), channel_id=1, source_target_pairs={{0,8},{8,0},{16,24},{24,16},{1,9},{9,1},{17,25},{25,17},{2,10},{10... | collective-permute-start | bytes 4718600 | tf_op jit(solution)/shard_map/ppermute | solution.py:703
  298.8 20.2 %collective-permute-start.44 = (bf16[384,1024]{1,0:T(8,128)(2,1)}, bf16[384,1024]{1,0:T(8,128)(2,1)S(1)}, u32[]{:S(2)}, u32[]{:S(2)}) collective-permute-start(bf16[384,1024]{1,0:T(8,128)(2,1)} %fusion.3), channel_id=1, source_target_pairs={{0,16},{8,24},{16,0},{24,8},{1,17},{9,25},{17,1},{25,9},{2,18},{10... | collective-permute-start | bytes 2359304 | tf_op jit(solution)/shard_map/ppermute | solution.py:703
  308.4 1.8 collective-permute-start.38
  (19 other events, 42.8 us)
Sparse Core Ops, SparseCore 0:
  241.4 63.9 all-gather.1

commit v5 on v4

--- a/solution.py
+++ b/solution.py
@@ -465,7 +465,7 @@
     part = width // len(CHAINS)
     block = (parts, part, BLOCK)
     fixed = pl.BlockSpec(block, lambda s, order: (0, 0, 0))
-    rest = jax.ShapeDtypeStruct(block, F32)
+    rest = jax.ShapeDtypeStruct(block, BF16)
     if last:
         out_specs, out_shape = [fixed] * len(CHAINS), [rest] * len(CHAINS)
     else:
@@ -492,7 +492,7 @@
 
     @pl.when(pl.program_id(0) == 0)
     def _():
-        shift_ref[...] = (rhs_ref[0].T.astype(F32) - (term_ref[...] + got_ref[...].astype(F32))).astype(BF16)
+        shift_ref[...] = (rhs_ref[0].T.astype(F32) - (term_ref[...].astype(F32) + got_ref[...].astype(F32))).astype(BF16)
 
     store_blocks(out_ref, lax.dot_general(shift_ref[...], matrix_ref[...], NT, preferred_element_type=F32))
 
@@ -546,7 +546,7 @@
 
 
 def mid_coupling_kernel(plans, start, count, total, table_ref, *refs):
-    coup_ref, out_ref, send_ref, bound, sems = refs[total:]
+    coup_ref, out_ref, bound, sems = refs[total:]
 
     def target(i, p, first, width):
         return bound.at[pl.ds(first, width), pl.ds(i * BLOCK, BLOCK)]
@@ -556,8 +556,7 @@
         fetch_all(plans, start, count, table_ref, refs[:total], target, sems)
 
     product = lax.dot_general(bound[...], coup_ref[...], NN, preferred_element_type=F32)
-    out_ref[...] = product
-    send_ref[...] = product.astype(BF16)
+    out_ref[...] = product.astype(BF16)
 
 
 def mid_coupling(table, start, parts, coup, steps=4):
@@ -570,8 +569,8 @@
         functools.partial(mid_coupling_kernel, plans, start, count, len(arrays)),
         grid=(steps,),
         in_specs=[SMEM] + [ANY] * len(arrays) + [pl.BlockSpec((depth, cols // steps), lambda s: (0, s))],
-        out_specs=[tile, tile],
-        out_shape=[jax.ShapeDtypeStruct((width, cols), F32), jax.ShapeDtypeStruct((width, cols), BF16)],
+        out_specs=tile,
+        out_shape=jax.ShapeDtypeStruct((width, cols), BF16),
         scratch_shapes=[pltpu.VMEM((width, depth), BF16), pltpu.SemaphoreType.DMA((len(plans), count))],
         compiler_params=params(24),
         cost_estimate=cost(cols, depth, width),
@@ -802,8 +801,8 @@
     plan = tables[0]
     parts = [(kind, width, whole(boundary[n])) for n, kind in enumerate(CHAINS)]
 
-    term, half_term = mid_coupling(plan, at["mid"], parts, coup_mid)
-    front, shift = mid_first(x, term, swap(half_term, "row", 1), rhs_mid, dinv_mid, ())
+    term = mid_coupling(plan, at["mid"], parts, coup_mid)
+    front, shift = mid_first(x, term, swap(term, "row", 1), rhs_mid, dinv_mid, ())
     back = mid_rest(shift, dinv_mid)
     asking = gather(plan, at["send_root"], leaf_slots + slot, parts, (back,), split=True)
     asked = [[swap(part, "row", 2)] for part in asking]

time: 336 us -> 331 us (0.985)
    ppermute x39, waiting for transfers between devices: 143 us -> 149 us  [swap(): lax.ppermute(value, axis, [(i, i ^ mask) for i in range(lax.axis_size(axi...]
    all_gather x1, waiting for transfers between devices: 5.08 us -> 1.45 us  [shards(): mid = lax.all_gather(got, 'col', axis=0, tiled=True)]
    unnamed x86 -> x84, local copies, waits for them, and re-layouts: 14.1 us -> 13 us
where the time goes in v5:
time: 331 us; the launch traced here: 326 us
  waiting for transfers between devices  151 us (46%)
  Pallas kernels  101 us (31%)
  starting transfers between devices  30.4 us (9%)
  local copies, waits for them, and re-layouts  17 us (5%)
  between operations  16 us (5%)
  other arithmetic  10.9 us (3%)
    ppermute x39, waiting for transfers between devices, swap(): lax.ppermute(value, axis, [(i, i ^ mask) for i in range(lax.axis_size(axi...  149 us
    ppermute x39, starting transfers between devices, swap(): lax.ppermute(value, axis, [(i, i ^ mask) for i in range(lax.axis_size(axi...  30.4 us
    pallas_call x8, Pallas kernels, gather(): pl.pallas_call(functools.partial(gather_kernel, plans, start, count, len(...  17.9 us
    pallas_call x2, Pallas kernels, root_product(): pl.pallas_call(functools.partial(root_product_kernel, parts, last), grid_...  17.9 us
    pallas_call x2, Pallas kernels, leaf_rest(): pl.pallas_call(functools.partial(leaf_rest_kernel, dims), grid_spec=pltpu...  13 us
    unnamed x84, local copies, waits for them, and re-layouts  13 us
    pallas_call x1, Pallas kernels, shards(): pl.pallas_call(functools.partial(plan_kernel, local, slot, leaf_slots), o...  12.7 us
    pallas_call x1, Pallas kernels, mid_coupling(): pl.pallas_call(functools.partial(mid_coupling_kernel, plans, start, count...  8.92 us
  transfers between devices with their start and end apart: 40, of which 27 were waited for; matrix products, arithmetic and copies ran while one was open for 4% of the time, Pallas kernels for 19%

profile of v5, /device:TPU:0, one launch (start us, length us, event | category | flops | bytes accessed | tf_op | source)
XLA Modules:
  0.0 326.2 jit_solution(3396776506029263129)
XLA Ops:
  7.8 2.5 shard_map.130.order_ref
  10.3 11.8 %shard_map.131 = (bf16[16,192,128]{2,1,0:T(8,128)(2,1)}, bf16[8,192,128]{2,1,0:T(8,128)(2,1)}, bf16[16,192,128]{2,1,0:T(8,128)(2,1)}, bf16[8,192,128]{2,1,0:T(8,128)(2,1)}) custom-call(s32[32]{0:T(128)} %shard_map.130.order_ref, bf16[2048,384]{1,0:T(8,128)(2,1)} %value_ref.3, bf16[4096,2048]{1,0:T(8,128)(2,1)} %refs_7_.3, bf16[4096,2048]{1,0:T(8,128)(2,1)} %refs_7_.3, ...), custom_call_target="tpu_custom_call" | custom-call | flops 4831838208 | bytes 12582912 | tf_op jit(solution)/shard_map/pallas_call | solution.py:475
  22.1 3.0 collective-permute-start.8
  25.1 1.6 collective-permute-start.7
  26.7 12.7 %shard_map.132.table_ref = s32[2,109]{1,0:T(2,128)} custom-call(s32[2]{0:T(128)} %pad_add_fusion.place_ref, s32[2,64]{1,0:T(2,128)} %bounds_ref.3, s32[8,48]{1,0:T(8,128)} %leaf_ref.1, s32[8]{0:T(128)} %parents_ref.1), custom_call_target="tpu_custom_call" | custom-call | tf_op jit(solution)/shard_map/pallas_call | solution.py:772
  39.4 6.1 %shard_map.133 = (bf16[8,192,128]{2,1,0:T(8,128)(2,1)}, bf16[8,192,128]{2,1,0:T(8,128)(2,1)}) custom-call(s32[32]{0:T(128)} %shard_map.130.order_ref, bf16[2048,384]{1,0:T(8,128)(2,1)} %value_ref.3, bf16[4096,2048]{1,0:T(8,128)(2,1)} %refs_7_.3, bf16[4096,2048]{1,0:T(8,128)(2,1)} %refs_7_.3, bf16[4096,2048]{1,0:T(8,128)(2,1)} %refs_7_.3, ...), custom_call_target="tpu_custom_call" | custom-call | flops 1610612736 | bytes 4194304 | tf_op jit(solution)/shard_map/pallas_call | solution.py:475
  45.5 1.2 add_convert_fusion.3
  48.1 9.3 %collective-permute-done.9 = bf16[8,192,128]{2,1,0:T(8,128)(2,1)S(1)} collective-permute-done((bf16[8,192,128]{2,1,0:T(8,128)(2,1)S(1)}, bf16[8,192,128]{2,1,0:T(8,128)(2,1)S(1)}, u32[]{:S(2)}, u32[]{:S(2)}) %collective-permute-start.9) | collective-permute-done | bytes 393248 | tf_op jit(solution)/shard_map/ppermute | solution.py:702
  57.4 2.7 collective-permute-start.10
  60.6 11.8 %collective-permute-done.10 = bf16[4,192,128]{2,1,0:T(8,128)(2,1)S(1)} collective-permute-done((bf16[4,192,128]{2,1,0:T(8,128)(2,1)S(1)}, bf16[4,192,128]{2,1,0:T(8,128)(2,1)S(1)}, u32[]{:S(2)}, u32[]{:S(2)}) %collective-permute-start.10) | collective-permute-done | bytes 196640 | tf_op jit(solution)/shard_map/ppermute | solution.py:702
  72.5 2.2 collective-permute-start.12
  74.7 1.6 collective-permute-done.19
  76.4 2.2 collective-permute-start.21
  78.7 1.6 collective-permute-done.12.refs_2_
  81.3 3.1 collective-permute-done.21.refs_2_
  85.6 12.6 %collective-permute-done.13 = bf16[4,192,128]{2,1,0:T(8,128)(2,1)S(1)} collective-permute-done((bf16[4,192,128]{2,1,0:T(8,128)(2,1)S(1)}, bf16[4,192,128]{2,1,0:T(8,128)(2,1)S(1)}, u32[]{:S(2)}, u32[]{:S(2)}) %collective-permute-start.13) | collective-permute-done | bytes 196640 | tf_op jit(solution)/shard_map/ppermute | solution.py:702
  98.3 3.2 collective-permute-done.22
  102.1 7.7 %collective-permute-done.14 = bf16[8,192,128]{2,1,0:T(8,128)(2,1)S(1)} collective-permute-done((bf16[8,192,128]{2,1,0:T(8,128)(2,1)S(1)}, bf16[8,192,128]{2,1,0:T(8,128)(2,1)S(1)}, u32[]{:S(2)}, u32[]{:S(2)}) %collective-permute-start.14) | collective-permute-done | bytes 393248 | tf_op jit(solution)/shard_map/ppermute | solution.py:702
  112.3 16.6 %collective-permute-done.15.refs_1_ = bf16[16,192,128]{2,1,0:T(8,128)(2,1)S(1)} collective-permute-done((bf16[16,192,128]{2,1,0:T(8,128)(2,1)S(1)}, bf16[16,192,128]{2,1,0:T(8,128)(2,1)S(1)}, u32[]{:S(2)}, u32[]{:S(2)}) %collective-permute-start.15) | collective-permute-done | bytes 786464 | tf_op jit(solution)/shard_map/ppermute | solution.py:702
  129.5 1.7 collective-permute-done.17.refs_3_
  132.4 8.9 %shard_map.136.term_ref = bf16[384,1024]{1,0:T(8,128)(2,1)} custom-call(s32[2,109]{1,0:T(2,128)S(1)} %copy-done.31, bf16[16,192,128]{2,1,0:T(8,128)(2,1)S(1)} %pad_maximum_fusion.refs_0_, bf16[16,192,128]{2,1,0:T(8,128)(2,1)S(1)} %collective-permute-done.15.refs_1_, bf16[16,192,128]{2,1,0:T(8,128)(2,1)S(1)} %collective-permute-done.16.refs_2_, ...), custom_call_target="tpu_custom_call" | custom-call | flops 3221225472 | bytes 8388608 | tf_op jit(solution)/shard_map/pallas_call | solution.py:568
  141.5 2.5 collective-permute-done.27.got_ref
  144.0 5.5 %shard_map.137 = (bf16[16,384,128]{2,1,0:T(8,128)(2,1)}, bf16[384,1024]{1,0:T(8,128)(2,1)}) custom-call(s32[1]{0:T(128)} %bitcast.2.front_ref, bf16[384,1024]{1,0:T(8,128)(2,1)} %shard_map.136.term_ref, bf16[384,1024]{1,0:T(8,128)(2,1)} %collective-permute-done.27.got_ref, bf16[2,1024,384]{2,1,0:T(8,128)(2,1)} %rhs_ref.2, bf16[4096,1024]{1,0:T(8,128)(2,1)} %matrix_ref.3), custom_call_target="tpu_custom_call" | custom-call | flops 1610612736 | bytes 4194304 | tf_op jit(solution)/shard_map/pallas_call | solution.py:508
  149.5 4.7 %shard_map.138.refs_1_.refs_8_ = bf16[16,384,128]{2,1,0:T(8,128)(2,1)} custom-call(bf16[384,1024]{1,0:T(8,128)(2,1)} %get-tuple-element.55.shift_ref, bf16[4096,1024]{1,0:T(8,128)(2,1)} %matrix_ref.3), custom_call_target="tpu_custom_call" | custom-call | flops 1610612736 | bytes 4194304 | tf_op jit(solution)/shard_map/pallas_call | solution.py:534
  154.8 3.1 collective-permute-done.28.refs_2_
  157.9 2.2 collective-permute-done.29.refs_3_
  160.1 1.4 copy-done
  161.5 1.4 copy-done.24
  162.9 3.7 %shard_map.139 = (bf16[16,192,128]{2,1,0:T(8,128)(2,1)S(1)}, bf16[16,192,128]{2,1,0:T(8,128)(2,1)S(1)}) custom-call(s32[2,109]{1,0:T(2,128)S(1)} %copy-done.31, bf16[16,384,128]{2,1,0:T(8,128)(2,1)S(1)} %copy-done.24, bf16[16,384,128]{2,1,0:T(8,128)(2,1)S(1)} %copy-done, bf16[16,384,128]{2,1,0:T(8,128)(2,1)S(1)} %collective-permute-done.28.refs_2_, ...), custom_call_target="tpu_custom_call" | custom-call | tf_op jit(solution)/shard_map/pallas_call | solution.py:413
  167.8 1.1 copy-done.11
  169.0 1.1 copy-done.14
  170.1 1.1 copy-done.17
  171.2 1.1 copy-done.20
  172.4 4.6 %shard_map.141 = (bf16[16,192,128]{2,1,0:T(8,128)(2,1)S(1)}, bf16[16,192,128]{2,1,0:T(8,128)(2,1)}) custom-call(s32[2,109]{1,0:T(2,128)S(1)} %copy-done.31, bf16[16,192,128]{2,1,0:T(8,128)(2,1)S(1)} %pad_maximum_fusion.refs_0_, bf16[16,192,128]{2,1,0:T(8,128)(2,1)S(1)} %collective-permute-done.15.refs_1_, bf16[16,192,128]{2,1,0:T(8,128)(2,1)S(1)} %copy-done.11, ...), custom_call_target="tpu_custom_call" | custom-call | tf_op jit(solution)/shard_map/pallas_call | solution.py:413
  177.0 1.6 collective-permute-start.32
  178.6 3.9 %shard_map.140 = (bf16[16,192,128]{2,1,0:T(8,128)(2,1)S(1)}, bf16[16,192,128]{2,1,0:T(8,128)(2,1)S(1)}) custom-call(s32[2,109]{1,0:T(2,128)S(1)} %copy-done.31, bf16[16,384,128]{2,1,0:T(8,128)(2,1)S(1)} %copy-done.25, bf16[16,384,128]{2,1,0:T(8,128)(2,1)S(1)} %copy-done.1, bf16[16,384,128]{2,1,0:T(8,128)(2,1)S(1)} %collective-permute-done.28.refs_2_, ...), custom_call_target="tpu_custom_call" | custom-call | tf_op jit(solution)/shard_map/pallas_call | solution.py:413
  182.5 3.8 %collective-permute-done.30 = bf16[16,192,128]{2,1,0:T(8,128)(2,1)S(1)} collective-permute-done((bf16[16,192,128]{2,1,0:T(8,128)(2,1)S(1)}, bf16[16,192,128]{2,1,0:T(8,128)(2,1)S(1)}, u32[]{:S(2)}, u32[]{:S(2)}) %collective-permute-start.30) | collective-permute-done | bytes 786464 | tf_op jit(solution)/shard_map/ppermute | solution.py:702
  188.3 1.5 collective-permute-start.37
  189.9 7.6 %collective-permute-done.32.refs_4_ = bf16[16,192,128]{2,1,0:T(8,128)(2,1)S(1)} collective-permute-done((bf16[16,192,128]{2,1,0:T(8,128)(2,1)S(1)}, bf16[16,192,128]{2,1,0:T(8,128)(2,1)S(1)}, u32[]{:S(2)}, u32[]{:S(2)}) %collective-permute-start.32) | collective-permute-done | bytes 786464 | tf_op jit(solution)/shard_map/ppermute | solution.py:702
  197.5 2.4 collective-permute-start.36
  200.7 11.7 %collective-permute-done.36 = bf16[4,192,128]{2,1,0:T(8,128)(2,1)S(1)} collective-permute-done((bf16[4,192,128]{2,1,0:T(8,128)(2,1)S(1)}, bf16[4,192,128]{2,1,0:T(8,128)(2,1)S(1)}, u32[]{:S(2)}, u32[]{:S(2)}) %collective-permute-start.36) | collective-permute-done | bytes 196640 | tf_op jit(solution)/shard_map/ppermute | solution.py:702
  212.4 3.3 %collective-permute-done.35 = bf16[4,192,128]{2,1,0:T(8,128)(2,1)S(1)} collective-permute-done((bf16[4,192,128]{2,1,0:T(8,128)(2,1)S(1)}, bf16[4,192,128]{2,1,0:T(8,128)(2,1)S(1)}, u32[]{:S(2)}, u32[]{:S(2)}) %collective-permute-start.35) | collective-permute-done | bytes 196640 | tf_op jit(solution)/shard_map/ppermute | solution.py:702
  215.9 1.6 collective-permute-start.39
  220.0 6.3 %collective-permute-done.39 = bf16[4,384,128]{2,1,0:T(8,128)(2,1)S(1)} collective-permute-done((bf16[4,384,128]{2,1,0:T(8,128)(2,1)S(1)}, bf16[4,384,128]{2,1,0:T(8,128)(2,1)S(1)}, u32[]{:S(2)}, u32[]{:S(2)}) %collective-permute-start.39) | collective-permute-done | bytes 393248 | tf_op jit(solution)/shard_map/ppermute | solution.py:702
  226.3 10.5 %conditional.1 = (bf16[4,384,128]{2,1,0:T(8,128)(2,1)}) conditional(s32[]{:T(128)} %bitcast.12, bf16[4,384,128]{2,1,0:T(8,128)(2,1)S(1)} %get-tuple-element.75, bf16[4,384,128]{2,1,0:T(8,128)(2,1)S(1)} %get-tuple-element.75, bf16[4,384,128]{2,1,0:T(8,128)(2,1)S(1)} %get-tuple-element.75, ...), branch_computations={%region_0.1_spmd, %region_1.2_spmd, %region_2.3_spmd, %region_3.4_... | conditional | bytes 1572912 | solution.py:729
  226.4 10.4 %collective-permute-done.2 = bf16[4,384,128]{2,1,0:T(8,128)(2,1)} collective-permute-done((bf16[4,384,128]{2,1,0:T(8,128)(2,1)S(1)}, bf16[4,384,128]{2,1,0:T(8,128)(2,1)}, u32[]{:S(2)}, u32[]{:S(2)}) %collective-permute-start.2) | collective-permute-done | bytes 393248 | tf_op jit(solution)/shard_map/cond/branch_2_fun/ppermute | solution.py:702
  238.7 1.5 collective-permute-done.40.refs_6_
  241.1 7.9 %shard_map.145 = (bf16[2,384,1024]{2,1,0:T(8,128)(2,1)}, bf16[384,1536]{1,0:T(8,128)(2,1)}) custom-call(s32[2,109]{1,0:T(2,128)} %shard_map.132.table_ref, s32[4]{0:T(128)} %pad_add_fusion.1.order_ref, bf16[16,192,128]{2,1,0:T(8,128)(2,1)} %copy-done.2, bf16[16,192,128]{2,1,0:T(8,128)(2,1)} %copy-done.6, bf16[16,192,128]{2,1,0:T(8,128)(2,1)} %copy-done.10, ...), custom_call_target="tpu_custom_call" | custom-call | flops 2415919104 | bytes 6291456 | tf_op jit(solution)/shard_map/pallas_call | solution.py:598
  249.3 7.3 %shard_map.146.keep_ref = f32[2,384,1024]{2,1,0:T(8,128)} custom-call(s32[4]{0:T(128)} %pad_add_fusion.1.order_ref, bf16[384,1536]{1,0:T(8,128)(2,1)} %get-tuple-element.66.value_ref, bf16[1536,4096]{1,0:T(8,128)(2,1)} %bitcast.22), custom_call_target="tpu_custom_call" | custom-call | flops 2415919104 | bytes 6291456 | tf_op jit(solution)/shard_map/pallas_call | solution.py:669
  256.7 2.9 fusion.2
  259.6 1.6 collective-permute-start.42
  262.4 1.4 shard_map.142
  264.5 1.9 copy.16
  266.4 13.3 %collective-permute-done.42.far_ref = bf16[384,1024]{1,0:T(8,128)(2,1)} collective-permute-done((bf16[384,1024]{1,0:T(8,128)(2,1)}, bf16[384,1024]{1,0:T(8,128)(2,1)}, u32[]{:S(2)}, u32[]{:S(2)}) %collective-permute-start.42) | collective-permute-done | bytes 786464 | tf_op jit(solution)/shard_map/ppermute | solution.py:702
  279.8 6.8 %shard_map.147 = (bf16[2,384,1024]{2,1,0:T(8,128)(2,1)}, bf16[384,1024]{1,0:T(8,128)(2,1)}) custom-call(s32[4]{0:T(128)} %pad_add_fusion.1.order_ref, f32[2,384,1024]{2,1,0:T(8,128)} %shard_map.146.keep_ref, bf16[2,384,1024]{2,1,0:T(8,128)(2,1)} %collective-permute-done.41.got_ref, bf16[384,1024]{1,0:T(8,128)(2,1)} %collective-permute-done.42.far_ref, ...), custom_call_target="tpu_custom_call" | custom-call | flops 1610612736 | bytes 4194304 | tf_op jit(solution)/shard_map/pallas_call | solution.py:635
  286.6 5.7 %shard_map.148.keep_ref = f32[2,384,1024]{2,1,0:T(8,128)} custom-call(s32[4]{0:T(128)} %pad_add_fusion.1.order_ref, bf16[384,1024]{1,0:T(8,128)(2,1)} %get-tuple-element.68.value_ref, bf16[4096,1024]{1,0:T(8,128)(2,1)} %bitcast.24), custom_call_target="tpu_custom_call" | custom-call | flops 1610612736 | bytes 4194304 | tf_op jit(solution)/shard_map/pallas_call | solution.py:669
  292.3 3.1 fusion.3
  295.4 1.6 collective-permute-start.44
  297.0 1.5 all-gather.2.cloned.1.call-done.refs_0_
  298.4 1.9 copy-done.22
  301.5 1.7 collective-permute-done.38.refs_1_
  303.2 1.1 shard_map.144
  305.3 10.2 %collective-permute-done.44.far_ref = bf16[384,1024]{1,0:T(8,128)(2,1)S(1)} collective-permute-done((bf16[384,1024]{1,0:T(8,128)(2,1)}, bf16[384,1024]{1,0:T(8,128)(2,1)S(1)}, u32[]{:S(2)}, u32[]{:S(2)}) %collective-permute-start.44) | collective-permute-done | bytes 786464 | tf_op jit(solution)/shard_map/ppermute | solution.py:702
  316.4 3.0 shard_map.149
  (149 shorter events, 23.7 us)
Async XLA Ops:
  7.2 291.2 %all-gather.2.cloned.1.call-start = ((), (), s32[]{:S(2)}) async-start(), calls=%async_computation | async-start | bytes 3538944 | tf_op jit(solution)/shard_map/all_gather | solution.py:825
  22.1 23.4 %collective-permute-start.8 = (bf16[16,192,128]{2,1,0:T(8,128)(2,1)}, bf16[16,192,128]{2,1,0:T(8,128)(2,1)S(1)}, u32[]{:S(2)}, u32[]{:S(2)}) collective-permute-start(bf16[16,192,128]{2,1,0:T(8,128)(2,1)} %get-tuple-element.45), channel_id=1, source_target_pairs={{0,1},{1,0},{2,3},{3,2},{4,5},{5,4},{6,7},{7,6},{8,9},{9,8},{10,11... | collective-permute-start | bytes 2359304 | tf_op jit(solution)/shard_map/ppermute | solution.py:702
  25.1 20.4 %collective-permute-start.7 = (bf16[16,192,128]{2,1,0:T(8,128)(2,1)}, bf16[16,192,128]{2,1,0:T(8,128)(2,1)S(1)}, u32[]{:S(2)}, u32[]{:S(2)}) collective-permute-start(bf16[16,192,128]{2,1,0:T(8,128)(2,1)} %get-tuple-element.44), channel_id=1, source_target_pairs={{0,2},{1,3},{2,0},{3,1},{4,6},{5,7},{6,4},{7,5},{8,10},{9,11},{10,... | collective-permute-start | bytes 2359304 | tf_op jit(solution)/shard_map/ppermute | solution.py:702
  39.4 6.1 %copy-start.39 = (bf16[8,192,128]{2,1,0:T(8,128)(2,1)S(1)}, bf16[8,192,128]{2,1,0:T(8,128)(2,1)}, u32[]{:S(2)}) copy-start(bf16[8,192,128]{2,1,0:T(8,128)(2,1)} %get-tuple-element.50) | copy-start | bytes 1179652
  45.5 34.8 %copy-start.31 = (s32[2,109]{1,0:T(2,128)S(1)}, s32[2,109]{1,0:T(2,128)}, u32[]{:S(2)}) copy-start(s32[2,109]{1,0:T(2,128)} %shard_map.132.table_ref) | copy-start | bytes 2620
  46.8 10.6 %collective-permute-start.9 = (bf16[8,192,128]{2,1,0:T(8,128)(2,1)S(1)}, bf16[8,192,128]{2,1,0:T(8,128)(2,1)S(1)}, u32[]{:S(2)}, u32[]{:S(2)}) collective-permute-start(bf16[8,192,128]{2,1,0:T(8,128)(2,1)S(1)} %get-tuple-element.78), channel_id=1, source_target_pairs={{0,2},{1,3},{2,0},{3,1},{4,6},{5,7},{6,4},{7,5},{8,10},{9,11},{10,... | collective-permute-start | bytes 1179656 | tf_op jit(solution)/shard_map/ppermute | solution.py:702
  47.4 84.9 %copy-start.23 = (bf16[4096,1024]{1,0:T(8,128)(2,1)S(1)}, bf16[4096,1024]{1,0:T(8,128)(2,1)}, u32[]{:S(2)}) copy-start(bf16[4096,1024]{1,0:T(8,128)(2,1)} %refs_8_.1) | copy-start | bytes 25165828
  47.6 12.5 %collective-permute-start.18 = (bf16[8,192,128]{2,1,0:T(8,128)(2,1)S(1)}, bf16[8,192,128]{2,1,0:T(8,128)(2,1)S(1)}, u32[]{:S(2)}, u32[]{:S(2)}) collective-permute-start(bf16[8,192,128]{2,1,0:T(8,128)(2,1)S(1)} %get-tuple-element.76), channel_id=1, source_target_pairs={{0,1},{1,0},{2,3},{3,2},{4,5},{5,4},{6,7},{7,6},{8,9},{9,8},{10,11... | collective-permute-start | bytes 1179656 | tf_op jit(solution)/shard_map/ppermute | solution.py:702
  57.4 14.9 %collective-permute-start.10 = (bf16[4,192,128]{2,1,0:T(8,128)(2,1)S(1)}, bf16[4,192,128]{2,1,0:T(8,128)(2,1)S(1)}, u32[]{:S(2)}, u32[]{:S(2)}) collective-permute-start(bf16[4,192,128]{2,1,0:T(8,128)(2,1)S(1)} %fusion.13), channel_id=1, source_target_pairs={{0,4},{1,5},{2,6},{3,7},{4,0},{5,1},{6,2},{7,3},{8,12},{9,13},{10,... | collective-permute-start | bytes 589832 | tf_op jit(solution)/shard_map/ppermute | solution.py:702
  60.2 16.1 %collective-permute-start.19 = (bf16[4,192,128]{2,1,0:T(8,128)(2,1)S(1)}, bf16[4,192,128]{2,1,0:T(8,128)(2,1)S(1)}, u32[]{:S(2)}, u32[]{:S(2)}) collective-permute-start(bf16[4,192,128]{2,1,0:T(8,128)(2,1)S(1)} %fusion.10), channel_id=1, source_target_pairs={{0,4},{1,5},{2,6},{3,7},{4,0},{5,1},{6,2},{7,3},{8,12},{9,13},{10,... | collective-permute-start | bytes 589832 | tf_op jit(solution)/shard_map/ppermute | solution.py:702
  72.4 6.2 %collective-permute-start.11 = (bf16[4,192,128]{2,1,0:T(8,128)(2,1)S(1)}, bf16[4,192,128]{2,1,0:T(8,128)(2,1)S(1)}, u32[]{:S(2)}, u32[]{:S(2)}) collective-permute-start(bf16[4,192,128]{2,1,0:T(8,128)(2,1)S(1)} %fusion.15.refs_0_), channel_id=1, source_target_pairs={{0,8},{8,0},{16,24},{24,16},{1,9},{9,1},{17,25},{25,17},{2,10},{10... | collective-permute-start | bytes 589832 | tf_op jit(solution)/shard_map/ppermute | solution.py:702
  72.5 7.8 %collective-permute-start.12 = (bf16[4,192,128]{2,1,0:T(8,128)(2,1)S(1)}, bf16[4,192,128]{2,1,0:T(8,128)(2,1)S(1)}, u32[]{:S(2)}, u32[]{:S(2)}) collective-permute-start(bf16[4,192,128]{2,1,0:T(8,128)(2,1)S(1)} %fusion.15.refs_0_), channel_id=1, source_target_pairs={{0,16},{8,24},{16,0},{24,8},{1,17},{9,25},{17,1},{25,9},{2,18},{10... | collective-permute-start | bytes 589832 | tf_op jit(solution)/shard_map/ppermute | solution.py:702
  76.4 5.0 %collective-permute-start.20 = (bf16[4,192,128]{2,1,0:T(8,128)(2,1)S(1)}, bf16[4,192,128]{2,1,0:T(8,128)(2,1)S(1)}, u32[]{:S(2)}, u32[]{:S(2)}) collective-permute-start(bf16[4,192,128]{2,1,0:T(8,128)(2,1)S(1)} %fusion.12.refs_0_), channel_id=1, source_target_pairs={{0,8},{8,0},{16,24},{24,16},{1,9},{9,1},{17,25},{25,17},{2,10},{10... | collective-permute-start | bytes 589832 | tf_op jit(solution)/shard_map/ppermute | solution.py:702
  76.4 7.9 %collective-permute-start.21 = (bf16[4,192,128]{2,1,0:T(8,128)(2,1)S(1)}, bf16[4,192,128]{2,1,0:T(8,128)(2,1)S(1)}, u32[]{:S(2)}, u32[]{:S(2)}) collective-permute-start(bf16[4,192,128]{2,1,0:T(8,128)(2,1)S(1)} %fusion.12.refs_0_), channel_id=1, source_target_pairs={{0,16},{8,24},{16,0},{24,8},{1,17},{9,25},{17,1},{25,9},{2,18},{10... | collective-permute-start | bytes 589832 | tf_op jit(solution)/shard_map/ppermute | solution.py:702
  81.2 17.0 %collective-permute-start.13 = (bf16[4,192,128]{2,1,0:T(8,128)(2,1)S(1)}, bf16[4,192,128]{2,1,0:T(8,128)(2,1)S(1)}, u32[]{:S(2)}, u32[]{:S(2)}) collective-permute-start(bf16[4,192,128]{2,1,0:T(8,128)(2,1)S(1)} %shard_map.134), channel_id=1, source_target_pairs={{0,4},{1,5},{2,6},{3,7},{4,0},{5,1},{6,2},{7,3},{8,12},{9,13},{10,... | collective-permute-start | bytes 589832 | tf_op jit(solution)/shard_map/ppermute | solution.py:702
  85.5 16.0 %collective-permute-start.22 = (bf16[4,192,128]{2,1,0:T(8,128)(2,1)S(1)}, bf16[4,192,128]{2,1,0:T(8,128)(2,1)S(1)}, u32[]{:S(2)}, u32[]{:S(2)}) collective-permute-start(bf16[4,192,128]{2,1,0:T(8,128)(2,1)S(1)} %shard_map.135), channel_id=1, source_target_pairs={{0,4},{1,5},{2,6},{3,7},{4,0},{5,1},{6,2},{7,3},{8,12},{9,13},{10,... | collective-permute-start | bytes 589832 | tf_op jit(solution)/shard_map/ppermute | solution.py:702
  98.2 11.6 %collective-permute-start.14 = (bf16[8,192,128]{2,1,0:T(8,128)(2,1)S(1)}, bf16[8,192,128]{2,1,0:T(8,128)(2,1)S(1)}, u32[]{:S(2)}, u32[]{:S(2)}) collective-permute-start(bf16[8,192,128]{2,1,0:T(8,128)(2,1)S(1)} %pad_maximum_fusion.3), channel_id=1, source_target_pairs={{0,2},{1,3},{2,0},{3,1},{4,6},{5,7},{6,4},{7,5},{8,10},{9,11},{10,... | collective-permute-start | bytes 1179656 | tf_op jit(solution)/shard_map/ppermute | solution.py:702
  101.5 10.0 %collective-permute-start.23 = (bf16[8,192,128]{2,1,0:T(8,128)(2,1)S(1)}, bf16[8,192,128]{2,1,0:T(8,128)(2,1)S(1)}, u32[]{:S(2)}, u32[]{:S(2)}) collective-permute-start(bf16[8,192,128]{2,1,0:T(8,128)(2,1)S(1)} %pad_maximum_fusion.4), channel_id=1, source_target_pairs={{0,1},{1,0},{2,3},{3,2},{4,5},{5,4},{6,7},{7,6},{8,9},{9,8},{10,11... | collective-permute-start | bytes 1179656 | tf_op jit(solution)/shard_map/ppermute | solution.py:702
  109.9 57.9 %copy-start.2 = (bf16[16,192,128]{2,1,0:T(8,128)(2,1)}, bf16[16,192,128]{2,1,0:T(8,128)(2,1)S(1)}, u32[]{:S(2)}) copy-start(bf16[16,192,128]{2,1,0:T(8,128)(2,1)S(1)} %pad_maximum_fusion.refs_0_) | copy-start | bytes 2359300
  109.9 19.1 %collective-permute-start.15 = (bf16[16,192,128]{2,1,0:T(8,128)(2,1)S(1)}, bf16[16,192,128]{2,1,0:T(8,128)(2,1)S(1)}, u32[]{:S(2)}, u32[]{:S(2)}) collective-permute-start(bf16[16,192,128]{2,1,0:T(8,128)(2,1)S(1)} %pad_maximum_fusion.refs_0_), channel_id=1, source_target_pairs={{0,1},{1,0},{2,3},{3,2},{4,5},{5,4},{6,7},{7,6},{8,9},{9,8},{10,11... | collective-permute-start | bytes 2359304 | tf_op jit(solution)/shard_map/ppermute | solution.py:702
  111.6 56.2 %copy-start.4 = (bf16[16,192,128]{2,1,0:T(8,128)(2,1)}, bf16[16,192,128]{2,1,0:T(8,128)(2,1)S(1)}, u32[]{:S(2)}) copy-start(bf16[16,192,128]{2,1,0:T(8,128)(2,1)S(1)} %pad_maximum_fusion.1.refs_4_.refs_5_.refs_7_) | copy-start | bytes 2359300
  111.6 17.7 %collective-permute-start.24 = (bf16[16,192,128]{2,1,0:T(8,128)(2,1)S(1)}, bf16[16,192,128]{2,1,0:T(8,128)(2,1)S(1)}, u32[]{:S(2)}, u32[]{:S(2)}) collective-permute-start(bf16[16,192,128]{2,1,0:T(8,128)(2,1)S(1)} %pad_maximum_fusion.1.refs_4_.refs_5_.refs_7_), channel_id=1, source_target_pairs={{0,2},{1,3},{2,0},{3,1},{4,6},{5,7},{6,4},{7,5},{8,10},{9,11},{10,... | collective-permute-start | bytes 2359304 | tf_op jit(solution)/shard_map/ppermute | solution.py:702
  111.7 17.7 %collective-permute-start.16 = (bf16[16,192,128]{2,1,0:T(8,128)(2,1)S(1)}, bf16[16,192,128]{2,1,0:T(8,128)(2,1)S(1)}, u32[]{:S(2)}, u32[]{:S(2)}) collective-permute-start(bf16[16,192,128]{2,1,0:T(8,128)(2,1)S(1)} %pad_maximum_fusion.refs_0_), channel_id=1, source_target_pairs={{0,8},{8,0},{16,24},{24,16},{1,9},{9,1},{17,25},{25,17},{2,10},{10... | collective-permute-start | bytes 2359304 | tf_op jit(solution)/shard_map/ppermute | solution.py:702
  111.8 17.7 %collective-permute-start.25 = (bf16[16,192,128]{2,1,0:T(8,128)(2,1)S(1)}, bf16[16,192,128]{2,1,0:T(8,128)(2,1)S(1)}, u32[]{:S(2)}, u32[]{:S(2)}) collective-permute-start(bf16[16,192,128]{2,1,0:T(8,128)(2,1)S(1)} %pad_maximum_fusion.1.refs_4_.refs_5_.refs_7_), channel_id=1, source_target_pairs={{0,8},{8,0},{16,24},{24,16},{1,9},{9,1},{17,25},{25,17},{2,10},{10... | collective-permute-start | bytes 2359304 | tf_op jit(solution)/shard_map/ppermute | solution.py:702
  128.9 38.9 %copy-start.6 = (bf16[16,192,128]{2,1,0:T(8,128)(2,1)}, bf16[16,192,128]{2,1,0:T(8,128)(2,1)S(1)}, u32[]{:S(2)}) copy-start(bf16[16,192,128]{2,1,0:T(8,128)(2,1)S(1)} %collective-permute-done.15.refs_1_) | copy-start | bytes 2359300
  128.9 2.3 collective-permute-start.17
  129.3 38.5 %copy-start.8 = (bf16[16,192,128]{2,1,0:T(8,128)(2,1)}, bf16[16,192,128]{2,1,0:T(8,128)(2,1)S(1)}, u32[]{:S(2)}) copy-start(bf16[16,192,128]{2,1,0:T(8,128)(2,1)S(1)} %collective-permute-done.24.refs_5_.refs_6_.refs_8_) | copy-start | bytes 2359300
  129.3 3.0 collective-permute-start.26
  129.5 11.8 %copy-start.10 = (bf16[16,192,128]{2,1,0:T(8,128)(2,1)}, bf16[16,192,128]{2,1,0:T(8,128)(2,1)S(1)}, u32[]{:S(2)}) copy-start(bf16[16,192,128]{2,1,0:T(8,128)(2,1)S(1)} %collective-permute-done.16.refs_2_) | copy-start | bytes 2359300
  129.5 11.8 %copy-start.13 = (bf16[16,192,128]{2,1,0:T(8,128)(2,1)}, bf16[16,192,128]{2,1,0:T(8,128)(2,1)S(1)}, u32[]{:S(2)}) copy-start(bf16[16,192,128]{2,1,0:T(8,128)(2,1)S(1)} %collective-permute-done.25.refs_6_.refs_7_.refs_9_) | copy-start | bytes 2359300
  131.2 10.1 %copy-start.16 = (bf16[16,192,128]{2,1,0:T(8,128)(2,1)}, bf16[16,192,128]{2,1,0:T(8,128)(2,1)S(1)}, u32[]{:S(2)}) copy-start(bf16[16,192,128]{2,1,0:T(8,128)(2,1)S(1)} %collective-permute-done.17.refs_3_) | copy-start | bytes 2359300
  132.4 9.0 %copy-start.19 = (bf16[16,192,128]{2,1,0:T(8,128)(2,1)}, bf16[16,192,128]{2,1,0:T(8,128)(2,1)S(1)}, u32[]{:S(2)}) copy-start(bf16[16,192,128]{2,1,0:T(8,128)(2,1)S(1)} %collective-permute-done.26.refs_7_.refs_8_.refs_10_) | copy-start | bytes 2359300
  141.3 2.7 collective-permute-start.27
  154.3 3.6 %collective-permute-start.28 = (bf16[16,384,128]{2,1,0:T(8,128)(2,1)}, bf16[16,384,128]{2,1,0:T(8,128)(2,1)S(1)}, u32[]{:S(2)}, u32[]{:S(2)}) collective-permute-start(bf16[16,384,128]{2,1,0:T(8,128)(2,1)} %get-tuple-element.54.refs_0_), channel_id=1, source_target_pairs={{0,8},{8,0},{16,24},{24,16},{1,9},{9,1},{17,25},{25,17},{2,10},{10... | collective-permute-start | bytes 4718600 | tf_op jit(solution)/shard_map/ppermute | solution.py:702
  154.4 5.7 %collective-permute-start.29 = (bf16[16,384,128]{2,1,0:T(8,128)(2,1)}, bf16[16,384,128]{2,1,0:T(8,128)(2,1)S(1)}, u32[]{:S(2)}, u32[]{:S(2)}) collective-permute-start(bf16[16,384,128]{2,1,0:T(8,128)(2,1)} %shard_map.138.refs_1_.refs_8_), channel_id=1, source_target_pairs={{0,8},{8,0},{16,24},{24,16},{1,9},{9,1},{17,25},{25,17},{2,10},{10... | collective-permute-start | bytes 4718600 | tf_op jit(solution)/shard_map/ppermute | solution.py:702
  162.9 4.9 %copy-start.1 = (bf16[16,384,128]{2,1,0:T(8,128)(2,1)S(1)}, bf16[16,384,128]{2,1,0:T(8,128)(2,1)}, u32[]{:S(2)}) copy-start(bf16[16,384,128]{2,1,0:T(8,128)(2,1)} %shard_map.138.refs_1_.refs_8_) | copy-start | bytes 4718596
  166.7 19.6 %collective-permute-start.30 = (bf16[16,192,128]{2,1,0:T(8,128)(2,1)S(1)}, bf16[16,192,128]{2,1,0:T(8,128)(2,1)S(1)}, u32[]{:S(2)}, u32[]{:S(2)}) collective-permute-start(bf16[16,192,128]{2,1,0:T(8,128)(2,1)S(1)} %get-tuple-element.58), channel_id=1, source_target_pairs={{0,2},{1,3},{2,0},{3,1},{4,6},{5,7},{6,4},{7,5},{8,10},{9,11},{10,... | collective-permute-start | bytes 2359304 | tf_op jit(solution)/shard_map/ppermute | solution.py:702
  166.7 20.6 %collective-permute-start.33 = (bf16[16,192,128]{2,1,0:T(8,128)(2,1)S(1)}, bf16[16,192,128]{2,1,0:T(8,128)(2,1)S(1)}, u32[]{:S(2)}, u32[]{:S(2)}) collective-permute-start(bf16[16,192,128]{2,1,0:T(8,128)(2,1)S(1)} %get-tuple-element.56.refs_4_), channel_id=1, source_target_pairs={{0,1},{1,0},{2,3},{3,2},{4,5},{5,4},{6,7},{7,6},{8,9},{9,8},{10,11... | collective-permute-start | bytes 2359304 | tf_op jit(solution)/shard_map/ppermute | solution.py:702
  172.4 6.2 %copy-start.25 = (bf16[16,384,128]{2,1,0:T(8,128)(2,1)S(1)}, bf16[16,384,128]{2,1,0:T(8,128)(2,1)}, u32[]{:S(2)}) copy-start(bf16[16,384,128]{2,1,0:T(8,128)(2,1)} %get-tuple-element.54.refs_0_) | copy-start | bytes 4718596
  177.0 20.5 %collective-permute-start.32 = (bf16[16,192,128]{2,1,0:T(8,128)(2,1)S(1)}, bf16[16,192,128]{2,1,0:T(8,128)(2,1)S(1)}, u32[]{:S(2)}, u32[]{:S(2)}) collective-permute-start(bf16[16,192,128]{2,1,0:T(8,128)(2,1)S(1)} %get-tuple-element.59), channel_id=1, source_target_pairs={{0,16},{8,24},{16,0},{24,8},{1,17},{9,25},{17,1},{25,9},{2,18},{10... | collective-permute-start | bytes 2359304 | tf_op jit(solution)/shard_map/ppermute | solution.py:702
  186.5 11.0 %collective-permute-start.31 = (bf16[8,192,128]{2,1,0:T(8,128)(2,1)S(1)}, bf16[8,192,128]{2,1,0:T(8,128)(2,1)S(1)}, u32[]{:S(2)}, u32[]{:S(2)}) collective-permute-start(bf16[8,192,128]{2,1,0:T(8,128)(2,1)S(1)} %get-tuple-element.73), channel_id=1, source_target_pairs={{0,1},{1,0},{2,3},{3,2},{4,5},{5,4},{6,7},{7,6},{8,9},{9,8},{10,11... | collective-permute-start | bytes 1179656 | tf_op jit(solution)/shard_map/ppermute | solution.py:702
  187.6 12.4 %collective-permute-start.34 = (bf16[8,192,128]{2,1,0:T(8,128)(2,1)S(1)}, bf16[8,192,128]{2,1,0:T(8,128)(2,1)S(1)}, u32[]{:S(2)}, u32[]{:S(2)}) collective-permute-start(bf16[8,192,128]{2,1,0:T(8,128)(2,1)S(1)} %get-tuple-element.70), channel_id=1, source_target_pairs={{0,2},{1,3},{2,0},{3,1},{4,6},{5,7},{6,4},{7,5},{8,10},{9,11},{10,... | collective-permute-start | bytes 1179656 | tf_op jit(solution)/shard_map/ppermute | solution.py:702
  188.3 27.5 %collective-permute-start.37 = (bf16[16,192,128]{2,1,0:T(8,128)(2,1)}, bf16[16,192,128]{2,1,0:T(8,128)(2,1)S(1)}, u32[]{:S(2)}, u32[]{:S(2)}) collective-permute-start(bf16[16,192,128]{2,1,0:T(8,128)(2,1)} %get-tuple-element.63), channel_id=1, source_target_pairs={{0,16},{8,24},{16,0},{24,8},{1,17},{9,25},{17,1},{25,9},{2,18},{10... | collective-permute-start | bytes 2359304 | tf_op jit(solution)/shard_map/ppermute | solution.py:702
  197.5 18.3 %copy-start.26 = (bf16[16,192,128]{2,1,0:T(8,128)(2,1)}, bf16[16,192,128]{2,1,0:T(8,128)(2,1)S(1)}, u32[]{:S(2)}) copy-start(bf16[16,192,128]{2,1,0:T(8,128)(2,1)S(1)} %collective-permute-done.32.refs_4_) | copy-start | bytes 2359300
  197.5 14.8 %collective-permute-start.36 = (bf16[4,192,128]{2,1,0:T(8,128)(2,1)S(1)}, bf16[4,192,128]{2,1,0:T(8,128)(2,1)S(1)}, u32[]{:S(2)}, u32[]{:S(2)}) collective-permute-start(bf16[4,192,128]{2,1,0:T(8,128)(2,1)S(1)} %fusion.4), channel_id=1, source_target_pairs={{0,4},{1,5},{2,6},{3,7},{4,0},{5,1},{6,2},{7,3},{8,12},{9,13},{10,... | collective-permute-start | bytes 589832 | tf_op jit(solution)/shard_map/ppermute | solution.py:702
  200.0 17.5 %copy-start.41 = (s32[8]{0:T(128)S(1)}, s32[8]{0:T(128)}, u32[]{:S(2)}) copy-start(s32[8]{0:T(128)} %parents_ref.1) | copy-start | bytes 100
  200.0 15.7 %collective-permute-start.35 = (bf16[4,192,128]{2,1,0:T(8,128)(2,1)S(1)}, bf16[4,192,128]{2,1,0:T(8,128)(2,1)S(1)}, u32[]{:S(2)}, u32[]{:S(2)}) collective-permute-start(bf16[4,192,128]{2,1,0:T(8,128)(2,1)S(1)} %fusion.7), channel_id=1, source_target_pairs={{0,4},{1,5},{2,6},{3,7},{4,0},{5,1},{6,2},{7,3},{8,12},{9,13},{10,... | collective-permute-start | bytes 589832 | tf_op jit(solution)/shard_map/ppermute | solution.py:702
  215.9 22.0 %copy-start.33 = (bf16[4,384,128]{2,1,0:T(8,128)(2,1)}, bf16[4,384,128]{2,1,0:T(8,128)(2,1)S(1)}, u32[]{:S(2)}) copy-start(bf16[4,384,128]{2,1,0:T(8,128)(2,1)S(1)} %pad_maximum_fusion.5) | copy-start | bytes 1179652
  215.9 22.0 %copy-start.28 = (bf16[16,192,128]{2,1,0:T(8,128)(2,1)}, bf16[16,192,128]{2,1,0:T(8,128)(2,1)S(1)}, u32[]{:S(2)}) copy-start(bf16[16,192,128]{2,1,0:T(8,128)(2,1)S(1)} %collective-permute-done.37.refs_9_.refs_11_) | copy-start | bytes 2359300
  215.9 10.4 %collective-permute-start.39 = (bf16[4,384,128]{2,1,0:T(8,128)(2,1)S(1)}, bf16[4,384,128]{2,1,0:T(8,128)(2,1)S(1)}, u32[]{:S(2)}, u32[]{:S(2)}) collective-permute-start(bf16[4,384,128]{2,1,0:T(8,128)(2,1)S(1)} %pad_maximum_fusion.5), channel_id=1, source_target_pairs={{0,16},{8,24},{16,0},{24,8},{1,17},{9,25},{17,1},{25,9},{2,18},{10... | collective-permute-start | bytes 1179656 | tf_op jit(solution)/shard_map/ppermute | solution.py:702
  226.3 10.5 %collective-permute-start.2 = (bf16[4,384,128]{2,1,0:T(8,128)(2,1)S(1)}, bf16[4,384,128]{2,1,0:T(8,128)(2,1)}, u32[]{:S(2)}, u32[]{:S(2)}) collective-permute-start(bf16[4,384,128]{2,1,0:T(8,128)(2,1)S(1)} %param.2), channel_id=1, source_target_pairs={{0,3},{1,2},{2,1},{3,0},{4,7},{5,6},{6,5},{7,4},{8,11},{9,10},{10,... | collective-permute-start | bytes 1179656 | tf_op jit(solution)/shard_map/cond/branch_2_fun/ppermute | solution.py:702
  237.9 2.4 collective-permute-start.40
  249.1 7.6 %collective-permute-start.41 = (bf16[2,384,1024]{2,1,0:T(8,128)(2,1)}, bf16[2,384,1024]{2,1,0:T(8,128)(2,1)}, u32[]{:S(2)}, u32[]{:S(2)}) collective-permute-start(bf16[2,384,1024]{2,1,0:T(8,128)(2,1)} %get-tuple-element.67), channel_id=1, source_target_pairs={{0,8},{8,0},{16,24},{24,16},{1,9},{9,1},{17,25},{25,17},{2,10},{10... | collective-permute-start | bytes 4718600 | tf_op jit(solution)/shard_map/ppermute | solution.py:702
  249.3 11.9 %copy-start.12 = (bf16[16,192,128]{2,1,0:T(8,128)(2,1)S(1)}, bf16[16,192,128]{2,1,0:T(8,128)(2,1)}, u32[]{:S(2)}) copy-start(bf16[16,192,128]{2,1,0:T(8,128)(2,1)} %copy-done.10) | copy-start | bytes 2359300
  249.3 11.9 %copy-start.15 = (bf16[16,192,128]{2,1,0:T(8,128)(2,1)S(1)}, bf16[16,192,128]{2,1,0:T(8,128)(2,1)}, u32[]{:S(2)}) copy-start(bf16[16,192,128]{2,1,0:T(8,128)(2,1)} %copy-done.13) | copy-start | bytes 2359300
  249.3 11.9 %copy-start.18 = (bf16[16,192,128]{2,1,0:T(8,128)(2,1)S(1)}, bf16[16,192,128]{2,1,0:T(8,128)(2,1)}, u32[]{:S(2)}) copy-start(bf16[16,192,128]{2,1,0:T(8,128)(2,1)} %copy-done.16) | copy-start | bytes 2359300
  249.3 11.9 %copy-start.21 = (bf16[16,192,128]{2,1,0:T(8,128)(2,1)S(1)}, bf16[16,192,128]{2,1,0:T(8,128)(2,1)}, u32[]{:S(2)}) copy-start(bf16[16,192,128]{2,1,0:T(8,128)(2,1)} %copy-done.19) | copy-start | bytes 2359300
  249.3 11.9 %copy-start.27 = (bf16[16,192,128]{2,1,0:T(8,128)(2,1)S(1)}, bf16[16,192,128]{2,1,0:T(8,128)(2,1)}, u32[]{:S(2)}) copy-start(bf16[16,192,128]{2,1,0:T(8,128)(2,1)} %copy-done.26) | copy-start | bytes 2359300
  249.3 11.9 %copy-start.32 = (s32[2,109]{1,0:T(2,128)S(1)}, s32[2,109]{1,0:T(2,128)}, u32[]{:S(2)}) copy-start(s32[2,109]{1,0:T(2,128)} %shard_map.132.table_ref) | copy-start | bytes 2620
  256.6 4.6 %copy-start.9 = (bf16[16,192,128]{2,1,0:T(8,128)(2,1)S(1)}, bf16[16,192,128]{2,1,0:T(8,128)(2,1)}, u32[]{:S(2)}) copy-start(bf16[16,192,128]{2,1,0:T(8,128)(2,1)} %copy-done.8) | copy-start | bytes 2359300
  259.6 20.2 %collective-permute-start.42 = (bf16[384,1024]{1,0:T(8,128)(2,1)}, bf16[384,1024]{1,0:T(8,128)(2,1)}, u32[]{:S(2)}, u32[]{:S(2)}) collective-permute-start(bf16[384,1024]{1,0:T(8,128)(2,1)} %fusion.2), channel_id=1, source_target_pairs={{0,16},{8,24},{16,0},{24,8},{1,17},{9,25},{17,1},{25,9},{2,18},{10... | collective-permute-start | bytes 2359304 | tf_op jit(solution)/shard_map/ppermute | solution.py:702
  286.6 5.7 %collective-permute-start.43 = (bf16[2,384,1024]{2,1,0:T(8,128)(2,1)}, bf16[2,384,1024]{2,1,0:T(8,128)(2,1)S(1)}, u32[]{:S(2)}, u32[]{:S(2)}) collective-permute-start(bf16[2,384,1024]{2,1,0:T(8,128)(2,1)} %get-tuple-element.69), channel_id=1, source_target_pairs={{0,8},{8,0},{16,24},{24,16},{1,9},{9,1},{17,25},{25,17},{2,10},{10... | collective-permute-start | bytes 4718600 | tf_op jit(solution)/shard_map/ppermute | solution.py:702
  295.4 20.1 %collective-permute-start.44 = (bf16[384,1024]{1,0:T(8,128)(2,1)}, bf16[384,1024]{1,0:T(8,128)(2,1)S(1)}, u32[]{:S(2)}, u32[]{:S(2)}) collective-permute-start(bf16[384,1024]{1,0:T(8,128)(2,1)} %fusion.3), channel_id=1, source_target_pairs={{0,16},{8,24},{16,0},{24,8},{1,17},{9,25},{17,1},{25,9},{2,18},{10... | collective-permute-start | bytes 2359304 | tf_op jit(solution)/shard_map/ppermute | solution.py:702
  301.4 1.8 collective-permute-start.38
  (18 other events, 36.0 us)
Sparse Core Ops, SparseCore 0:
  238.1 60.2 all-gather.1
